TPU v7x, 32 devices: a whole 2x2x4 slice. The times are simulated.
32 devices in a mesh: dp: 16 (over z, x, core), rep: 2 (over y).
Axes of the slice: x: 2, y: 2, z: 4, core: 2. Of those that a mesh axis runs over, the one named last changes fastest.
Arguments:
- tokens: bfloat16 [2, 4096, 2048], P('rep', 'dp'), may hold values from -6 to 6
- attention_gain: float32 [2048], replicated, may hold values from 0.1 to 1.9
- query_weight: bfloat16 [2048, 2048], P('dp'), may hold values from -0.125 to 0.125
- key_weight: bfloat16 [2048, 2048], P('dp'), may hold values from -0.125 to 0.125
- value_weight: bfloat16 [2048, 2048], P('dp'), may hold values from -0.125 to 0.125
- output_weight: bfloat16 [2048, 2048], P('dp'), may hold values from -0.5 to 0.5
- dense_gain: float32 [2048], replicated, may hold values from 0.1 to 1.9
- gate_weight: bfloat16 [8192, 2048], P('dp'), may hold values from -0.125 to 0.125
- up_weight: bfloat16 [8192, 2048], P('dp'), may hold values from -0.125 to 0.125
- down_weight: bfloat16 [8192, 2048], P('dp'), may hold values from -0.0625 to 0.0625
- block_document: int32 [2, 32], P('rep'), may hold values from 0 to 7, never falling along the last dimension, each value on 1 to 16 neighbouring positions
- document_tail: int32 [2, 8], P('rep'), may hold values from 1 to 128
- cotangent: bfloat16 [2, 4096, 2048], P('rep', 'dp'), may hold values from -6 to 6
Outputs:
- layer_out: bfloat16 [2, 4096, 2048], P('rep', 'dp')
- input_grad: float32 [2, 4096, 2048], P('rep', 'dp')
- attention_gain_grad: float32 [2048], replicated
- query_grad: float32 [2048, 2048], P('dp')
- key_grad: float32 [2048, 2048], P('dp')
- value_grad: float32 [2048, 2048], P('dp')
- output_grad: float32 [2048, 2048], P('dp')
- dense_gain_grad: float32 [2048], replicated
- gate_grad: float32 [8192, 2048], P('dp')
- up_grad: float32 [8192, 2048], P('dp')
- down_grad: float32 [8192, 2048], P('dp')
Inputs may be any that keep to these rules, and one draw needn't show every extreme that they name: `block_document`: document numbers of a pack start at 0, never fall from block to block, and every document covers 1 to 16 whole blocks; each number of 0 to 7 appears.
All inputs are finite; a program needn't handle non-finite values.
Results may differ from a plain program's by a relative error of at most 0.02.
Values may be sent and summed in bfloat16 or wider, within the bound.
A program may use at most 576 MiB of HBM per device.

v0:
```python
import math

import jax
import jax.numpy as jnp
from jax import lax
from jax.sharding import PartitionSpec as P

D = 2048
HEADS = 32
HEAD_DIM = 64
BLOCK = 128
DOC_MOST = 16


EPSILON = 1e-05
ROPE_BASE = 130000.0
MASKED_SCORE = -1e30


def document_layout(block_document, document_tail):
    pack_blocks = block_document.shape[0]
    doc_count = document_tail.shape[0]
    doc_ids = jnp.arange(doc_count, dtype=jnp.int32)
    member = (block_document[None, :] == doc_ids[:, None]).astype(jnp.int32)
    counts = jnp.sum(member, axis=1)
    first_block = jnp.cumsum(counts) - counts
    token_doc = jnp.repeat(block_document, BLOCK, total_repeat_length=pack_blocks * BLOCK)
    chosen = (token_doc[:, None] == doc_ids[None, :]).astype(jnp.int32)
    doc_start = jnp.sum(chosen * first_block[None, :], axis=1) * BLOCK
    length = jnp.sum(chosen * ((counts - 1) * BLOCK + document_tail)[None, :], axis=1)
    position = jnp.arange(pack_blocks * BLOCK, dtype=jnp.int32) - doc_start
    return (token_doc, position, position < length)


def rope_tables(position):
    half_dim = HEAD_DIM // 2
    frequency = ROPE_BASE ** (-(jnp.arange(half_dim, dtype=jnp.float32) * (2.0 / HEAD_DIM)))
    angles = position.astype(jnp.float32)[:, None] * frequency[None, :]
    cosine = jnp.cos(angles)
    sine = jnp.sin(angles)
    return (jnp.concatenate([cosine, cosine], 1), jnp.concatenate([sine, sine], 1))


def rotate(values, cosine, sine):
    half_dim = values.shape[-1] // 2
    turned = jnp.concatenate([-values[..., half_dim:], values[..., :half_dim]], -1)
    return values * cosine[:, None, :] + turned * sine[:, None, :]


def rotate_back(grads, cosine, sine):
    half_dim = grads.shape[-1] // 2
    turned = grads * sine[:, None, :]
    return grads * cosine[:, None, :] + jnp.concatenate(
        [turned[..., half_dim:], -turned[..., :half_dim]], -1
    )


def rms(values, norm_gain):
    return (
        values * lax.rsqrt(jnp.mean(values * values, axis=-1, keepdims=True) + EPSILON) * norm_gain
    )


def rms_back(values, norm_gain, grads):
    _, pullback = jax.vjp(rms, values, norm_gain)
    return pullback(grads)


def project(left, weight):
    return lax.dot_general(
        left, weight, (((1,), (1,)), ((), ())), preferred_element_type=jnp.float32
    )


def column_product(left, right):
    return lax.dot_general(
        left, right, (((0,), (0,)), ((), ())), preferred_element_type=jnp.float32
    )


def weight_term(left, right, row_count):
    return column_product(lax.slice_in_dim(left, 0, row_count, axis=1), right)


def attention_weight_sum(left, right, row_count):
    return lax.psum_scatter(
        weight_term(left, right, lax.axis_size("dp") * row_count).astype(jnp.bfloat16),
        "dp",
        scatter_dimension=0,
        tiled=True,
    ).astype(jnp.float32)


def dense_weight_sum(left, right, row_count):
    return lax.psum_scatter(
        weight_term(left, right, lax.axis_size("dp") * row_count).astype(jnp.bfloat16),
        "dp",
        scatter_dimension=0,
        tiled=True,
    ).astype(jnp.float32)


def silu_back(gate, up_part, grad_hidden):
    sigma = jax.nn.sigmoid(gate)
    grad_gate = grad_hidden * up_part * sigma * (1.0 + gate * (1.0 - sigma))
    grad_up = grad_hidden * gate * sigma
    return (grad_gate.astype(jnp.bfloat16), grad_up.astype(jnp.bfloat16))


def window_sizes(pack_tok):
    block_rows = min(512, pack_tok)
    return (block_rows, min(pack_tok, DOC_MOST * BLOCK + block_rows))


def block_scores(query_rows, key_rows, first_row, key_start, token_doc, valid):
    block_rows = query_rows.shape[0]
    window = key_rows.shape[0]
    query_doc = lax.dynamic_slice_in_dim(token_doc, first_row, block_rows, 0)
    key_doc = lax.dynamic_slice_in_dim(token_doc, key_start, window, 0)
    key_valid = lax.dynamic_slice_in_dim(valid, key_start, window, 0)
    query_index = first_row + jnp.arange(block_rows, dtype=jnp.int32)
    key_index = key_start + jnp.arange(window, dtype=jnp.int32)
    allowed = (
        (query_doc[:, None] == key_doc[None, :])
        & (key_index[None, :] <= query_index[:, None])
        & key_valid[None, :]
    )
    raw_scores = jnp.einsum(
        "qhd,khd->hqk", query_rows, key_rows, preferred_element_type=jnp.float32
    )
    score_scale = 1.0 / math.sqrt(query_rows.shape[2])
    return jnp.where(allowed[None], raw_scores * score_scale, MASKED_SCORE)


def attend(query, key, value, token_doc, valid):
    pack_tok = query.shape[0]
    block_rows, window = window_sizes(pack_tok)

    def block_fn(first_row):
        key_start = jnp.maximum(first_row + block_rows - window, 0)
        query_rows = lax.dynamic_slice_in_dim(query, first_row, block_rows, 0)
        key_rows = lax.dynamic_slice_in_dim(key, key_start, window, 0)
        value_rows = lax.dynamic_slice_in_dim(value, key_start, window, 0)
        scores = block_scores(query_rows, key_rows, first_row, key_start, token_doc, valid)
        row_max = jnp.max(scores, axis=2, keepdims=True)
        weights = jnp.exp(scores - row_max)
        row_total = jnp.sum(weights, axis=2, keepdims=True)
        weights_low = (weights / row_total).astype(jnp.bfloat16)
        result = jnp.einsum(
            "hqk,khd->qhd", weights_low, value_rows, preferred_element_type=jnp.float32
        )
        return (result, (row_max + jnp.log(row_total))[..., 0])

    starts = jnp.arange(pack_tok // block_rows, dtype=jnp.int32) * block_rows
    results, log_total = lax.map(block_fn, starts)
    return (results.reshape(query.shape), log_total)


def attend_back(query, key, value, grad_out, log_total, token_doc, valid):
    pack_tok = query.shape[0]
    block_rows, window = window_sizes(pack_tok)
    score_scale = 1.0 / math.sqrt(query.shape[2])

    def step(running, block_item):
        first_row, log_rows = block_item
        grad_key, grad_value = running
        key_start = jnp.maximum(first_row + block_rows - window, 0).astype(jnp.int32)
        query_rows = lax.dynamic_slice_in_dim(query, first_row, block_rows, 0)
        key_rows = lax.dynamic_slice_in_dim(key, key_start, window, 0)
        value_rows = lax.dynamic_slice_in_dim(value, key_start, window, 0)
        grad_rows = lax.dynamic_slice_in_dim(grad_out, first_row, block_rows, 0)
        scores = block_scores(query_rows, key_rows, first_row, key_start, token_doc, valid)
        weights = jnp.exp(scores - log_rows[..., None])
        weights_low = weights.astype(jnp.bfloat16)
        grad_weights = jnp.einsum(
            "qhd,khd->hqk", grad_rows, value_rows, preferred_element_type=jnp.float32
        )
        delta = jnp.sum(weights * grad_weights, axis=2, keepdims=True)
        grad_scores = (weights * (grad_weights - delta) * score_scale).astype(jnp.bfloat16)
        grad_query = jnp.einsum(
            "hqk,khd->qhd", grad_scores, key_rows, preferred_element_type=jnp.float32
        )
        key_part = jnp.einsum(
            "hqk,qhd->khd", grad_scores, query_rows, preferred_element_type=jnp.float32
        )
        value_part = jnp.einsum(
            "hqk,qhd->khd", weights_low, grad_rows, preferred_element_type=jnp.float32
        )
        grad_key = lax.dynamic_update_slice_in_dim(
            grad_key,
            lax.dynamic_slice_in_dim(grad_key, key_start, window, 0) + key_part,
            key_start,
            0,
        )
        grad_value = lax.dynamic_update_slice_in_dim(
            grad_value,
            lax.dynamic_slice_in_dim(grad_value, key_start, window, 0) + value_part,
            key_start,
            0,
        )
        return ((grad_key, grad_value), grad_query)

    starts = jnp.arange(pack_tok // block_rows, dtype=jnp.int32) * block_rows
    zeros = jnp.zeros(query.shape, jnp.float32)
    (grad_key, grad_value), grad_query = lax.scan(step, (zeros, zeros), (starts, log_total))
    return (grad_query.reshape(query.shape), grad_key, grad_value)


def body(
    tokens,
    attention_gain,
    query_weight,
    key_weight,
    value_weight,
    output_weight,
    dense_gain,
    gate_weight,
    up_weight,
    down_weight,
    block_document,
    document_tail,
    cotangent,
):
    hidden_in = tokens[0].astype(jnp.float32)
    tok_dev = hidden_in.shape[0]
    token_doc, position, valid = document_layout(block_document[0], document_tail[0])
    cosine_all, sine_all = rope_tables(position)
    cosine_here = lax.dynamic_slice_in_dim(cosine_all, lax.axis_index("dp") * tok_dev, tok_dev, 0)
    sine_here = lax.dynamic_slice_in_dim(sine_all, lax.axis_index("dp") * tok_dev, tok_dev, 0)
    full_query, full_key, full_value, full_output = (
        lax.all_gather(query_weight, "dp", axis=0, tiled=True),
        lax.all_gather(key_weight, "dp", axis=0, tiled=True),
        lax.all_gather(value_weight, "dp", axis=0, tiled=True),
        lax.all_gather(output_weight, "dp", axis=0, tiled=True),
    )
    normed = rms(hidden_in, attention_gain).astype(jnp.bfloat16)
    local_shape = (tok_dev, HEADS, HEAD_DIM)
    query = rotate(project(normed, full_query).reshape(local_shape), cosine_here, sine_here)
    key = rotate(project(normed, full_key).reshape(local_shape), cosine_here, sine_here)
    query = query.reshape(tok_dev, D).astype(jnp.bfloat16)
    key = key.reshape(tok_dev, D).astype(jnp.bfloat16)
    value = project(normed, full_value).astype(jnp.bfloat16)
    query_heads, key_heads, value_heads = (
        lax.all_to_all(query, "dp", split_axis=1, concat_axis=0, tiled=True),
        lax.all_to_all(key, "dp", split_axis=1, concat_axis=0, tiled=True),
        lax.all_to_all(value, "dp", split_axis=1, concat_axis=0, tiled=True),
    )
    pack_tok = query_heads.shape[0]
    head_shape = (pack_tok, query_heads.shape[1] // HEAD_DIM, HEAD_DIM)
    query_heads = query_heads.reshape(head_shape)
    key_heads = key_heads.reshape(head_shape)
    value_heads = value_heads.reshape(head_shape)
    attended, log_total = attend(query_heads, key_heads, value_heads, token_doc, valid)
    attended_low = attended.reshape(pack_tok, -1).astype(jnp.bfloat16)
    attended_here = lax.all_to_all(attended_low, "dp", split_axis=0, concat_axis=1, tiled=True)
    mixed = hidden_in + jnp.dot(attended_here, full_output, preferred_element_type=jnp.float32)
    normed_two = rms(mixed, dense_gain).astype(jnp.bfloat16)
    grad_low = cotangent[0]
    full_gate, full_up, full_down = (
        lax.all_gather(gate_weight, "dp", axis=0, tiled=True),
        lax.all_gather(up_weight, "dp", axis=0, tiled=True),
        lax.all_gather(down_weight, "dp", axis=0, tiled=True),
    )
    gate = project(normed_two, full_gate)
    up_part = project(normed_two, full_up)
    hidden = (jax.nn.silu(gate) * up_part).astype(jnp.bfloat16)
    layer_out = mixed + jnp.dot(hidden, full_down, preferred_element_type=jnp.float32)
    grad_hidden = project(grad_low, full_down)
    grad_gate, grad_up = silu_back(gate, up_part, grad_hidden)
    down_grad = dense_weight_sum(hidden, grad_low, down_weight.shape[0])
    gate_grad = dense_weight_sum(grad_gate, normed_two, gate_weight.shape[0])
    up_grad = dense_weight_sum(grad_up, normed_two, up_weight.shape[0])
    grad_normed_two = jnp.dot(grad_gate, full_gate, preferred_element_type=jnp.float32) + jnp.dot(
        grad_up, full_up, preferred_element_type=jnp.float32
    )
    grad_mixed_norm, dense_gain_part = rms_back(mixed, dense_gain, grad_normed_two)
    grad_mixed = grad_low.astype(jnp.float32) + grad_mixed_norm
    grad_mixed_low = grad_mixed.astype(jnp.bfloat16)
    output_grad = attention_weight_sum(attended_here, grad_mixed_low, output_weight.shape[0])
    grad_attended = project(grad_mixed_low, full_output).astype(jnp.bfloat16)
    grad_heads = lax.all_to_all(
        grad_attended, "dp", split_axis=1, concat_axis=0, tiled=True
    ).reshape(head_shape)
    grad_query, grad_key, grad_value = attend_back(
        query_heads, key_heads, value_heads, grad_heads, log_total, token_doc, valid
    )
    grad_query = (
        rotate_back(grad_query, cosine_all, sine_all).reshape(pack_tok, -1).astype(jnp.bfloat16)
    )
    grad_key = (
        rotate_back(grad_key, cosine_all, sine_all).reshape(pack_tok, -1).astype(jnp.bfloat16)
    )
    grad_value = grad_value.reshape(pack_tok, -1).astype(jnp.bfloat16)
    query_back, key_back, value_back = (
        lax.all_to_all(grad_query, "dp", split_axis=0, concat_axis=1, tiled=True),
        lax.all_to_all(grad_key, "dp", split_axis=0, concat_axis=1, tiled=True),
        lax.all_to_all(grad_value, "dp", split_axis=0, concat_axis=1, tiled=True),
    )
    query_grad = attention_weight_sum(query_back, normed, query_weight.shape[0])
    key_grad = attention_weight_sum(key_back, normed, key_weight.shape[0])
    value_grad = attention_weight_sum(value_back, normed, value_weight.shape[0])
    grad_normed = (
        jnp.dot(query_back, full_query, preferred_element_type=jnp.float32)
        + jnp.dot(key_back, full_key, preferred_element_type=jnp.float32)
        + jnp.dot(value_back, full_value, preferred_element_type=jnp.float32)
    )
    grad_in_norm, attention_gain_part = rms_back(hidden_in, attention_gain, grad_normed)
    input_grad = grad_mixed + grad_in_norm
    summed = (
        lax.psum(query_grad.astype(jnp.bfloat16), "rep").astype(jnp.float32),
        lax.psum(key_grad.astype(jnp.bfloat16), "rep").astype(jnp.float32),
        lax.psum(value_grad.astype(jnp.bfloat16), "rep").astype(jnp.float32),
        lax.psum(output_grad.astype(jnp.bfloat16), "rep").astype(jnp.float32),
        lax.psum(gate_grad.astype(jnp.bfloat16), "rep").astype(jnp.float32),
        lax.psum(up_grad.astype(jnp.bfloat16), "rep").astype(jnp.float32),
        lax.psum(down_grad.astype(jnp.bfloat16), "rep").astype(jnp.float32),
    )
    gain_totals = lax.psum((attention_gain_part, dense_gain_part), ("dp", "rep"))
    return (
        layer_out[None].astype(jnp.bfloat16),
        input_grad[None],
        gain_totals[0],
        summed[0],
        summed[1],
        summed[2],
        summed[3],
        gain_totals[1],
        summed[4],
        summed[5],
        summed[6],
    )


def solution(mesh):
    return jax.shard_map(
        body,
        mesh=mesh,
        in_specs=(
            P("rep", "dp", None),
            P(),
            P("dp", None),
            P("dp", None),
            P("dp", None),
            P("dp", None),
            P(),
            P("dp", None),
            P("dp", None),
            P("dp", None),
            P("rep", None),
            P("rep", None),
            P("rep", "dp", None),
        ),
        out_specs=(
            P("rep", "dp", None),
            P("rep", "dp", None),
            P(),
            P("dp", None),
            P("dp", None),
            P("dp", None),
            P("dp", None),
            P(),
            P("dp", None),
            P("dp", None),
            P("dp", None),
        ),
        check_vma=False,
    )
```

profile of v0, /device:TPU:0, one launch (start us, length us, event | category | flops | bytes accessed | tf_op | source)
XLA Modules:
  0.0 3216.5 jit_solution(9727195749167520506)
XLA Ops:
  38.7 49.1 %all-gather.12.cloned.1.call-done = bf16[2048,2048]{1,0:T(8,128)(2,1)} async-done(((bf16[128,2048]{1,0:T(8,128)(2,1)}), bf16[2048,2048]{1,0:T(8,128)(2,1)}) %all-gather.12.cloned.1.call-update) | async-done | bytes 8388624 | tf_op jit(solution)/shard_map/all_gather | solution.py:232
  95.1 68.0 %all-gather.10.cloned.1.call-done = bf16[2048,2048]{1,0:T(8,128)(2,1)} async-done(((bf16[128,2048]{1,0:T(8,128)(2,1)}), bf16[2048,2048]{1,0:T(8,128)(2,1)}) %all-gather.10.cloned.1.call-update) | async-done | bytes 8388624 | tf_op jit(solution)/shard_map/all_gather | solution.py:231
  172.8 41.0 %all_to_all.122 = bf16[256,16,128]{0,2,1:T(8,128)(2,1)S(1)} all-to-all(bf16[256,16,128]{0,2,1:T(8,128)(2,1)S(1)} %bitcast.278), channel_id=1, replica_groups=mesh['dp'=16,'rep'=2] {'dp'}, dimensions={1} | all-to-all | bytes 2097152 | tf_op jit(solution)/shard_map/all_to_all | solution.py:244
  218.5 57.6 %all-gather.8.cloned.1.call-done = bf16[2048,2048]{1,0:T(8,128)(2,1)} async-done(((bf16[128,2048]{1,0:T(8,128)(2,1)}), bf16[2048,2048]{1,0:T(8,128)(2,1)}) %all-gather.8.cloned.1.call-update) | async-done | bytes 8388624 | tf_op jit(solution)/shard_map/all_gather | solution.py:233
  293.3 31.9 all-to-all-done
  328.4 146.0 %while.35 = (s32[]{:T(128)}, bf16[8,512,2,64]{1,3,2,0:T(8,128)(2,1)S(1)}, f32[8,2,512]{2,1,0:T(2,128)S(1)}, s32[8]{0:T(128)S(1)}, bf16[4096,2,64]{0,2,1:T(8,128)...) while((s32[]{:T(128)}, ...), condition=%wide.region_8.9_spmd, body=%wide.region_5.8_spmd.sunk | while | flops 707790848 | bytes 38506724 | solution.py:155
  483.7 39.8 %all-to-all-done.3 = bf16[16,256,128]{1,2,0:T(8,128)(2,1)S(1)} async-done(((bf16[16,256,128]{1,2,0:T(8,128)(2,1)}), bf16[16,256,128]{1,2,0:T(8,128)(2,1)S(1)}, u32[]{:S(2)}, u32[]{:S(2)}) %all-to-all-start.3) | async-done | bytes 1048608 | tf_op jit(solution)/shard_map/all_to_all | solution.py:255
  531.2 24.0 all-gather.16.cloned.1.call-done
  555.2 17.4 fusion.116
  572.6 156.9 %all-gather.18.cloned.1.call-done = bf16[8192,2048]{1,0:T(8,128)(2,1)} async-done(((bf16[512,2048]{1,0:T(8,128)(2,1)}), bf16[8192,2048]{1,0:T(8,128)(2,1)}) %all-gather.18.cloned.1.call-update) | async-done | bytes 33554448 | tf_op jit(solution)/shard_map/all_gather | solution.py:261
  729.5 18.9 fusion.117
  748.3 150.8 %all-gather.20.cloned.1.call-done = bf16[8192,2048]{1,0:T(8,128)(2,1)} async-done(((bf16[512,2048]{1,0:T(8,128)(2,1)}), bf16[8192,2048]{1,0:T(8,128)(2,1)}) %all-gather.20.cloned.1.call-update) | async-done | bytes 33554448 | tf_op jit(solution)/shard_map/all_gather | solution.py:262
  899.2 24.0 multiply_convert_fusion.1
  923.1 17.6 fusion.118
  940.7 17.5 multiply_reduce_fusion.1
  1001.8 591.6 %while.36 = (s32[]{:T(128)}, f32[4096,2,64]{0,2,1:T(8,128)}, f32[4096,2,64]{0,2,1:T(8,128)S(1)}, f32[8,512,2,64]{1,0,3,2:T(8,128)}, s32[8]{0:T(128)S(1)}, /*inde...) while((s32[]{:T(128)}, f32[4096,2,64]{0,2,1:T(8,128)}, ...), condition=%wide.region_13.14_spmd, body=%wide.region_11.13_spmd.sunk | while | flops 1720330240 | bytes 132333336 | solution.py:205
  1023.6 16.2 fusion.185
  1543.2 16.1 fusion.185
  1603.1 31.3 all_to_all.123
  1653.1 38.5 %all_to_all.124 = bf16[16,256,128]{1,2,0:T(8,128)(2,1)S(1)} all-to-all(bf16[16,256,128]{1,2,0:T(8,128)(2,1)S(1)} %copy.86), channel_id=1, replica_groups=mesh['dp'=16,'rep'=2] {'dp'}, dimensions={0} | all-to-all | bytes 2097152 | tf_op jit(solution)/shard_map/all_to_all | solution.py:295
  1699.0 40.3 %all_to_all.125 = bf16[16,256,128]{1,2,0:T(8,128)(2,1)S(1)} all-to-all(bf16[16,256,128]{1,2,0:T(8,128)(2,1)S(1)} %copy.88), channel_id=1, replica_groups=mesh['dp'=16,'rep'=2] {'dp'}, dimensions={0} | all-to-all | bytes 2097152 | tf_op jit(solution)/shard_map/all_to_all | solution.py:297
  1747.2 16.1 convolution_convert_fusion.2
  1763.4 16.8 convolution_convert_fusion.1
  1781.5 17.3 convolution_convert_fusion
  1798.9 75.4 %reduce-scatter.8.cloned.1.call-done = bf16[128,2048]{1,0:T(8,128)(2,1)} async-done(((bf16[2048,2048]{1,0:T(8,128)(2,1)}), bf16[128,2048]{1,0:T(8,128)(2,1)}) %reduce-scatter.8.cloned.1.call-update) | async-done | bytes 524304 | tf_op jit(solution)/shard_map/reduce_scatter | solution.py:86
  1874.4 108.5 %reduce-scatter.12.cloned.1.call-done = bf16[128,2048]{1,0:T(8,128)(2,1)} async-done(((bf16[2048,2048]{1,0:T(8,128)(2,1)}), bf16[128,2048]{1,0:T(8,128)(2,1)}) %reduce-scatter.12.cloned.1.call-update) | async-done | bytes 524304 | tf_op jit(solution)/shard_map/reduce_scatter | solution.py:86
  1982.8 336.6 %reduce-scatter.16.cloned.1.call-done = bf16[512,2048]{1,0:T(8,128)(2,1)} async-done(((bf16[8192,2048]{1,0:T(8,128)(2,1)}), bf16[512,2048]{1,0:T(8,128)(2,1)}) %reduce-scatter.16.cloned.1.call-update) | async-done | bytes 2097168 | tf_op jit(solution)/shard_map/reduce_scatter | solution.py:95
  2319.4 336.0 %reduce-scatter.18.cloned.1.call-done = bf16[512,2048]{1,0:T(8,128)(2,1)} async-done(((bf16[8192,2048]{1,0:T(8,128)(2,1)}), bf16[512,2048]{1,0:T(8,128)(2,1)}) %reduce-scatter.18.cloned.1.call-update) | async-done | bytes 2097168 | tf_op jit(solution)/shard_map/reduce_scatter | solution.py:95
  2655.4 335.8 %reduce-scatter.20.cloned.1.call-done = bf16[512,2048]{1,0:T(8,128)(2,1)} async-done(((bf16[8192,2048]{1,0:T(8,128)(2,1)}), bf16[512,2048]{1,0:T(8,128)(2,1)}) %reduce-scatter.20.cloned.1.call-update) | async-done | bytes 2097168 | tf_op jit(solution)/shard_map/reduce_scatter | solution.py:95
  2992.8 18.3 fusion.65
  3027.2 39.8 %all-reduce = (f32[2048]{0:T(1024)}, f32[2048]{0:T(1024)}) all-reduce(f32[2048]{0:T(1024)S(1)} %get-tuple-element.469, f32[2048]{0:T(1024)S(1)} %copy-done.42), channel_id=1, replica_groups=mesh['dp'=16,'rep'=2] {'dp','rep'}, use_global_device_ids=true, to_apply=%region_16.17 | all-reduce | flops 4096 | bytes 32768 | tf_op jit(solution)/shard_map/psum | solution.py:318
  3070.5 125.3 %all-reduce.4.cloned.1.call-done = (bf16[128,2048]{1,0:T(8,128)(2,1)}, bf16[128,2048]{1,0:T(8,128)(2,1)}, bf16[128,2048]{1,0:T(8,128)(2,1)}, bf16[128,2048]{1,0:...) async-done(((bf16[128,2048]{1,0:T(8,128)(2,1)}, bf16[128,2048]{1,0:T(8,128)(2,1)}, bf16[128,2048]{1,0:T(8,128)(2,1)}, ...) | async-done | bytes 8388624 | tf_op jit(solution)/shard_map/psum | solution.py:310
  (438 shorter events, 875.7 us)
Async XLA Ops:
  7.2 80.6 %all-gather.12.cloned.1.call-start = ((), (), s32[]{:S(2)}) async-start(), calls=%async_computation.17 | async-start | bytes 8912896 | tf_op jit(solution)/shard_map/all_gather | solution.py:232
  7.9 155.2 %all-gather.10.cloned.1.call-start = ((), (), s32[]{:S(2)}) async-start(), calls=%async_computation.16 | async-start | bytes 8912896 | tf_op jit(solution)/shard_map/all_gather | solution.py:231
  8.7 267.4 %all-gather.8.cloned.1.call-start = ((), (), s32[]{:S(2)}) async-start(), calls=%async_computation.15 | async-start | bytes 8912896 | tf_op jit(solution)/shard_map/all_gather | solution.py:233
  9.4 474.3 %all-gather.14.cloned.1.call-start = ((), (), s32[]{:S(2)}) async-start(), calls=%async_computation.18 | async-start | bytes 8912896 | tf_op jit(solution)/shard_map/all_gather | solution.py:234
  10.0 545.2 %all-gather.16.cloned.1.call-start = ((), (), s32[]{:S(2)}) async-start(), calls=%async_computation.19 | async-start | bytes 35651584 | tf_op jit(solution)/shard_map/all_gather | solution.py:260
  10.6 718.9 %all-gather.18.cloned.1.call-start = ((), (), s32[]{:S(2)}) async-start(), calls=%async_computation.20 | async-start | bytes 35651584 | tf_op jit(solution)/shard_map/all_gather | solution.py:261
  11.2 27.3 copy-start
  11.2 888.0 %all-gather.20.cloned.1.call-start = ((), (), s32[]{:S(2)}) async-start(), calls=%async_computation.21 | async-start | bytes 35651584 | tf_op jit(solution)/shard_map/all_gather | solution.py:262
  11.9 75.9 %copy-start.35 = (f32[2048]{0:T(1024)S(1)}, f32[2048]{0:T(1024)}, u32[]{:S(2)}) copy-start(f32[2048]{0:T(1024)} %param.20) | copy-start | bytes 24580
  38.7 54.9 %copy-start.40 = (f32[256]{0:T(256)}, f32[256]{0:T(256)S(1)}, u32[]{:S(2)}) copy-start(f32[256]{0:T(256)S(1)} %fusion.68) | copy-start | bytes 3076
  38.7 237.4 %copy-start.37 = (f32[256]{0:T(256)}, f32[256]{0:T(256)S(1)}, u32[]{:S(2)}) copy-start(f32[256]{0:T(256)S(1)} %fusion.104) | copy-start | bytes 3076
  213.8 69.3 %all-to-all-start.2 = ((bf16[256,16,128]{0,2,1:T(8,128)(2,1)}), bf16[256,16,128]{0,2,1:T(8,128)(2,1)S(1)}, u32[]{:S(2)}, u32[]{:S(2)}) async-start(bf16[256,16,128]{0,2,1:T(8,128)(2,1)} %bitcast.277), calls=%async_computation.2 | async-start | bytes 2097152 | tf_op jit(solution)/shard_map/all_to_all | solution.py:245
  283.1 42.1 %all-to-all-start = ((bf16[256,16,128]{2,0,1:T(8,128)(2,1)}), bf16[256,16,128]{2,0,1:T(8,128)(2,1)}, u32[]{:S(2)}, u32[]{:S(2)}) async-start(bf16[256,16,128]{2,0,1:T(8,128)(2,1)} %bitcast.273), calls=%async_computation | async-start | bytes 2097152 | tf_op jit(solution)/shard_map/all_to_all | solution.py:246
  476.8 46.7 %all-to-all-start.3 = ((bf16[16,256,128]{1,2,0:T(8,128)(2,1)}), bf16[16,256,128]{1,2,0:T(8,128)(2,1)S(1)}, u32[]{:S(2)}, u32[]{:S(2)}) async-start(bf16[16,256,128]{1,2,0:T(8,128)(2,1)} %copy.81), calls=%async_computation.3 | async-start | bytes 2097152 | tf_op jit(solution)/shard_map/all_to_all | solution.py:255
  530.9 409.8 %copy-start.4 = (f32[256,2048]{1,0:T(8,128)}, f32[256,2048]{1,0:T(8,128)S(1)}, u32[]{:S(2)}) copy-start(f32[256,2048]{1,0:T(8,128)S(1)} %get-tuple-element.603) | copy-start | bytes 6291460
  531.2 198.3 %copy-start.15 = (bf16[256,2048]{1,0:T(8,128)(2,1)}, bf16[256,2048]{1,0:T(8,128)(2,1)S(1)}, u32[]{:S(2)}) copy-start(bf16[256,2048]{1,0:T(8,128)(2,1)S(1)} %multiply_convert_fusion.4) | copy-start | bytes 3145732
  923.1 17.6 copy-start.20
  969.1 27.8 all-to-all-start.4
  973.8 825.1 %reduce-scatter.14.cloned.1.call-start = ((), (), s32[]{:S(2)}) async-start(), calls=%async_computation.25 | async-start | bytes 8912896 | tf_op jit(solution)/shard_map/reduce_scatter | solution.py:86
  982.5 816.4 %reduce-scatter.10.cloned.1.call-start = ((), (), s32[]{:S(2)}) async-start(), calls=%async_computation.23 | async-start | bytes 8912896 | tf_op jit(solution)/shard_map/reduce_scatter | solution.py:86
  1602.7 32.7 %copy-start.1 = (bf16[1,256,2048]{2,1,0:T(8,128)(2,1)S(1)}, bf16[1,256,2048]{2,1,0:T(8,128)(2,1)}, u32[]{:S(2)}) copy-start(bf16[1,256,2048]{2,1,0:T(8,128)(2,1)} %param.19) | copy-start | bytes 3145732
  1602.8 32.7 %copy-start.36 = (f32[2048]{0:T(1024)S(1)}, f32[2048]{0:T(1024)}, u32[]{:S(2)}) copy-start(f32[2048]{0:T(1024)} %param.20) | copy-start | bytes 24580
  1602.8 32.7 %copy-start.38 = (f32[256]{0:T(256)S(1)}, f32[256]{0:T(256)}, u32[]{:S(2)}) copy-start(f32[256]{0:T(256)} %copy-done.37) | copy-start | bytes 3076
  1641.1 233.3 %reduce-scatter.8.cloned.1.call-start = ((), (), s32[]{:S(2)}) async-start(), calls=%async_computation.22 | async-start | bytes 8912896 | tf_op jit(solution)/shard_map/reduce_scatter | solution.py:86
  1698.2 284.6 %reduce-scatter.12.cloned.1.call-start = ((), (), s32[]{:S(2)}) async-start(), calls=%async_computation.24 | async-start | bytes 8912896 | tf_op jit(solution)/shard_map/reduce_scatter | solution.py:86
  1746.0 573.4 %reduce-scatter.16.cloned.1.call-start = ((), (), s32[]{:S(2)}) async-start(), calls=%async_computation.26 | async-start | bytes 35651584 | tf_op jit(solution)/shard_map/reduce_scatter | solution.py:95
  1763.3 892.1 %reduce-scatter.18.cloned.1.call-start = ((), (), s32[]{:S(2)}) async-start(), calls=%async_computation.27 | async-start | bytes 35651584 | tf_op jit(solution)/shard_map/reduce_scatter | solution.py:95
  1780.2 1211.0 %reduce-scatter.20.cloned.1.call-start = ((), (), s32[]{:S(2)}) async-start(), calls=%async_computation.28 | async-start | bytes 35651584 | tf_op jit(solution)/shard_map/reduce_scatter | solution.py:95
  1798.8 1397.0 %all-reduce.4.cloned.1.call-start = ((), (), s32[]{:S(2)}) async-start(), calls=%async_computation.29 | async-start | bytes 16777216 | tf_op jit(solution)/shard_map/psum | solution.py:310
  2992.8 18.3 copy-start.10
  3023.2 43.8 %copy-start.41 = (f32[256]{0:T(256)S(1)}, f32[256]{0:T(256)}, u32[]{:S(2)}) copy-start(f32[256]{0:T(256)} %copy-done.40) | copy-start | bytes 3076
  3023.2 43.8 %copy-start.3 = (f32[256,2048]{1,0:T(8,128)S(1)}, f32[256,2048]{1,0:T(8,128)}, u32[]{:S(2)}) copy-start(f32[256,2048]{1,0:T(8,128)} %copy-done.2) | copy-start | bytes 6291460
  (33 other events, 115.2 us)
Sparse Core Ops, SparseCore 0:
  10.2 77.5 all-gather.11
  90.0 73.1 all-gather.9
  165.3 110.7 all-gather.7
  278.1 92.3 all-gather.13
  372.0 183.1 all-gather.15
  556.7 172.7 all-gather.17
  731.1 168.0 all-gather.19
  982.7 105.9 reduce-scatter.13
  1641.2 124.7 reduce-scatter.9
  1770.0 104.3 reduce-scatter.7
  1878.4 104.3 reduce-scatter.11
  1986.9 332.4 reduce-scatter.15
  2323.7 331.7 reduce-scatter.17
  2659.6 331.6 reduce-scatter.19
  2994.1 201.6 all-reduce.3
where the time goes:
time: 3230 us; the launch traced here: 3220 us
  waiting for transfers between devices  1910 us (59%)
  matrix products  713 us (22%)
  local copies, waits for them, and re-layouts  192 us (6%)
  blocking collectives  191 us (6%)
  other arithmetic  126 us (4%)
  loops' own time  43 us (1%)
    reduce_scatter x3, waiting for transfers between devices, dense_weight_sum(): lax.psum_scatter(weight_term(left, right, lax.axis_size('dp') * row_count...  1010 us
    reduce_scatter x4, waiting for transfers between devices, attention_weight_sum(): lax.psum_scatter(weight_term(left, right, lax.axis_size('dp') * row_count...  184 us
    all_gather x1, waiting for transfers between devices, body(): lax.all_gather(up_weight, 'dp', axis=0, tiled=True)  157 us
    all_gather x1, waiting for transfers between devices, body(): lax.all_gather(down_weight, 'dp', axis=0, tiled=True)  151 us
    dot_general x8, matrix products, step(): jnp.einsum('hqk,qhd->khd', grad_scores, query_rows, preferred_element_typ...  128 us
    psum x1, waiting for transfers between devices, body(): lax.psum(query_grad.astype(jnp.bfloat16), 'rep').astype(jnp.float32)  125 us
    dot_general x8, matrix products, step(): jnp.einsum('hqk,khd->qhd', grad_scores, key_rows, preferred_element_type=...  118 us
    dot_general x16, matrix products, block_scores(): jnp.einsum('qhd,khd->hqk', query_rows, key_rows, preferred_element_type=j...  99.4 us
  transfers between devices with their start and end apart: 19, of which 15 were waited for; matrix products, arithmetic and copies ran while one was open for 29% of the time, Pallas kernels for 0%

commit v1 on v0

v1 whole, which is shorter than its diff:
```python
import functools
import math

import jax
import jax.numpy as jnp
from jax import lax
from jax.experimental import pallas as pl
from jax.experimental.pallas import tpu as pltpu
from jax.sharding import PartitionSpec as P

HEAD_DIM = 64
HALF = HEAD_DIM // 2
BLOCK = 128
CHUNK = 512
FF_TILE = 256
EPSILON = 1e-05
ROPE_BASE = 130000.0
MASKED_SCORE = -1e30
MESH = pl.DeviceIdType.MESH
MIB = 2**20
LOW = jnp.bfloat16
F32 = jnp.float32


def dot_nn(a, b):
    return lax.dot_general(a, b, (((1,), (0,)), ((), ())), preferred_element_type=F32)


def dot_nt(a, b):
    return lax.dot_general(a, b, (((1,), (1,)), ((), ())), preferred_element_type=F32)


def dot_tn(a, b):
    return lax.dot_general(a, b, (((0,), (0,)), ((), ())), preferred_element_type=F32)


def grid_of(chips):
    depth = 4 if chips % 8 == 0 else 2
    return depth, chips // depth


def chip_at(place, chips):
    depth, width = grid_of(chips)
    place = lax.rem(place + chips, chips)
    later = place - depth
    row, column = later // (width - 1), later % (width - 1)
    odd = row % 2
    far = (depth - 1 - row) * width + 1 + column + odd * (width - 2 - 2 * column)
    return jnp.where(place < depth, place * width, far)


def place_of(chip, chips):
    depth, width = grid_of(chips)
    z, x = chip // width, chip % width
    row = depth - 1 - z
    odd = row % 2
    column = x - 1 + odd * (width - 2 * x)
    return jnp.where(x == 0, z, depth + row * (width - 1) + column)


class Ring:
    def __init__(self):
        self.chips = lax.axis_size("dp") // 2
        me = lax.axis_index("dp")
        self.core = me % 2
        self.chip = me // 2
        self.partner = self.chip * 2 + 1 - self.core
        self.place = place_of(self.chip, self.chips)
        self.next = (self.device(1), self.device(-1))
        self.back = (self.next[1], self.next[0])

    def chip_far(self, steps):
        return chip_at(self.place + steps, self.chips)

    def device(self, steps):
        return self.chip_far(steps) * 2 + self.core

    def greet(self, others):
        barrier = pltpu.get_barrier_semaphore()
        for other in others:
            pl.semaphore_signal(barrier, inc=1, device_id={"dp": other}, device_id_type=MESH)
        pl.semaphore_wait(barrier, len(others))


def remote(src, dst, send_sem, recv_sem, device):
    return pltpu.make_async_remote_copy(
        src_ref=src,
        dst_ref=dst,
        send_sem=send_sem,
        recv_sem=recv_sem,
        device_id={"dp": device},
        device_id_type=MESH,
    )


def half_rows(direction, rows):
    return pl.ds(direction * (rows // 2), rows // 2)


def gather_project_kernel(
    normed, weights, cosine, sine, qkv, gathered,
    partner_weights, x_buf, staged,
    ag_send, ag_recv, w_send, w_recv, q_send, q_recv, local_sem,
):
    ring = Ring()
    n = ring.chips
    rows = normed.shape[0]
    r = qkv.shape[2]
    ring.greet((ring.next[0], ring.next[1], ring.partner))
    swap = remote(weights, partner_weights, w_send, w_recv, ring.partner)
    swap.start()
    keep = pltpu.make_async_copy(normed, gathered.at[ring.chip], local_sem.at[2])
    keep.start()

    def hop(t, d):
        chip = ring.chip_far((1 - t) if d == 0 else (t - 1))
        return chip, half_rows(d, rows)

    def send(t, d, first):
        chip, part = hop(t, d)
        src = normed.at[part] if first else gathered.at[chip, part]
        return remote(src, gathered.at[chip, part], ag_send.at[d, t - 1], ag_recv.at[d, t - 1], ring.next[d])

    for d in (0, 1):
        send(1, d, True).start()

    def project_block(t, from_input):
        x = normed[...] if from_input else x_buf[...]
        places = [ring.chip_far(-t), ring.chip_far(t)]
        cos = jnp.concatenate([cosine[places[d], half_rows(d, rows), :] for d in (0, 1)], 0)
        sin = jnp.concatenate([sine[places[d], half_rows(d, rows), :] for d in (0, 1)], 0)

        def heads(w):
            part = [dot_nt(x, w[i * r : (i + 1) * r, :]) for i in range(5)]
            return (
                (part[0] * cos + part[1] * sin).astype(LOW),
                (part[2] * cos + part[3] * sin).astype(LOW),
                part[4].astype(LOW),
            )

        starts = [
            pl.multiple_of((places[d] * 2 + ring.core) * rows + d * (rows // 2), rows // 2)
            for d in (0, 1)
        ]
        for i, value in enumerate(heads(weights)):
            for d in (0, 1):
                qkv[i, pl.ds(starts[d], rows // 2), :] = value[d * (rows // 2) : (d + 1) * (rows // 2)]
        if from_input:
            swap.wait()
        for i, value in enumerate(heads(partner_weights)):
            staged[t, i] = value
        for d in (0, 1):
            remote(
                staged.at[t, :, half_rows(d, rows)],
                qkv.at[:, pl.ds(starts[d], rows // 2)],
                q_send.at[d, t],
                q_recv.at[d, t],
                ring.partner,
            ).start()

    project_block(0, True)

    def step(t, carry):
        for d in (0, 1):
            send(t, d, False).wait_recv()

        @pl.when(t < n - 1)
        def _():
            for d in (0, 1):
                send(t + 1, d, False).start()

        loads = []
        for d in (0, 1):
            chip, part = hop(t + 1, d)
            loads.append(pltpu.make_async_copy(gathered.at[chip, part], x_buf.at[part], local_sem.at[d]))
        for load in loads:
            load.start()
        for load in loads:
            load.wait()
        project_block(t, False)
        return carry

    lax.fori_loop(1, n, step, 0)

    def finish(t, carry):
        for d in (0, 1):
            send(t, d, False).wait_send()
        return carry

    lax.fori_loop(1, n, finish, 0)

    def finish_heads(t, carry):
        for d in (0, 1):
            done = remote(
                staged.at[t, :, half_rows(d, rows)],
                qkv.at[:, half_rows(d, rows)],
                q_send.at[d, t],
                q_recv.at[d, t],
                ring.partner,
            )
            done.wait_send()
            done.wait_recv()
        return carry

    lax.fori_loop(0, n, finish_heads, 0)
    keep.wait()


def gather_project(normed, weights, cosine, sine):
    rows, features = normed.shape
    r = weights.shape[0] // 5
    devices = lax.axis_size("dp")
    n = devices // 2
    vmem = pl.BlockSpec(memory_space=pltpu.VMEM)
    dma = pltpu.SemaphoreType.DMA
    return pl.pallas_call(
        gather_project_kernel,
        out_shape=(
            jax.ShapeDtypeStruct((3, devices * rows, r), LOW),
            jax.ShapeDtypeStruct((n, rows, features), LOW),
        ),
        in_specs=[vmem] * 4,
        out_specs=(vmem, pl.BlockSpec(memory_space=pl.ANY)),
        scratch_shapes=[
            pltpu.VMEM(weights.shape, LOW),
            pltpu.VMEM((rows, features), LOW),
            pltpu.VMEM((n, 3, rows, r), LOW),
            dma((2, n)), dma((2, n)), dma, dma, dma((2, n)), dma((2, n)), dma((3,)),
        ],
        compiler_params=pltpu.CompilerParams(
            collective_id=1, has_side_effects=True, vmem_limit_bytes=40 * MIB
        ),
        cost_estimate=pl.CostEstimate(
            flops=4 * n * rows * features * 5 * r, bytes_accessed=320 * MIB, transcendentals=0
        ),
        name="gather_project",
    )(normed, weights, cosine, sine)


def split_heads(u):
    heads = u.shape[1] // HEAD_DIM
    if heads == 1:
        return u
    lane = lax.broadcasted_iota(jnp.int32, u.shape, 1) // HEAD_DIM
    zero = jnp.zeros_like(u)
    return jnp.concatenate([jnp.where(lane == h, u, zero) for h in range(heads)], 0)


def join_heads(u):
    heads = u.shape[0] // HEAD_DIM
    return jnp.concatenate(
        [u[h * HEAD_DIM : (h + 1) * HEAD_DIM, h * BLOCK : (h + 1) * BLOCK] for h in range(heads)], 0
    )


def transpose_blocks(source, target):
    def one(b, carry):
        at = pl.multiple_of(b * BLOCK, BLOCK)
        target[:, pl.ds(at, BLOCK)] = source[pl.ds(at, BLOCK), :].astype(F32).T.astype(LOW)
        return carry

    lax.fori_loop(0, source.shape[0] // BLOCK, one, 0)


def window_of(b, first, tail, columns):
    start = pl.multiple_of(jnp.maximum(b - (CHUNK // BLOCK - 1), 0) * BLOCK, BLOCK)
    whole = (b - first) // (CHUNK // BLOCK)
    lowest = (first + whole * (CHUNK // BLOCK)) * BLOCK
    key_index = start + lax.broadcasted_iota(jnp.int32, (CHUNK, columns), 0)
    query_index = b * BLOCK + lax.broadcasted_iota(jnp.int32, (CHUNK, columns), 1) % BLOCK
    allowed = (
        (key_index >= lowest)
        & (key_index <= query_index)
        & (key_index < b * BLOCK + tail)
    )
    return start, whole, allowed


def attend_kernel(first_ref, tail_ref, qkv, attended, log_total, value_t):
    tokens, r = qkv.shape[1:]
    columns = (r // HEAD_DIM) * BLOCK
    scale = 1.0 / math.sqrt(HEAD_DIM)
    transpose_blocks(qkv.at[2], value_t)

    def block(b, carry):
        at = pl.multiple_of(b * BLOCK, BLOCK)
        query = split_heads(qkv[0, pl.ds(at, BLOCK), :])
        start, whole, allowed = window_of(b, first_ref[b], tail_ref[b], columns)
        scores = dot_nt(qkv[1, pl.ds(start, CHUNK), :], query) * scale
        scores = jnp.where(allowed, scores, MASKED_SCORE)
        top = jnp.max(scores, axis=0, keepdims=True)
        weights = jnp.exp(scores - top)
        total = jnp.sum(weights, axis=0, keepdims=True)
        out = dot_nn(value_t[:, pl.ds(start, CHUNK)], weights.astype(LOW))

        def more(i, state):
            top, total, out = state
            start = pl.multiple_of(first_ref[b] * BLOCK + i * CHUNK, BLOCK)
            scores = dot_nt(qkv[1, pl.ds(start, CHUNK), :], query) * scale
            higher = jnp.maximum(top, jnp.max(scores, axis=0, keepdims=True))
            shrink = jnp.exp(top - higher)
            weights = jnp.exp(scores - higher)
            total = total * shrink + jnp.sum(weights, axis=0, keepdims=True)
            out = out * shrink + dot_nn(value_t[:, pl.ds(start, CHUNK)], weights.astype(LOW))
            return higher, total, out

        top, total, out = lax.fori_loop(0, whole, more, (top, total, out))
        log_total[pl.ds(b, 1), :] = top + jnp.log(total)
        attended[pl.ds(at, BLOCK), :] = join_heads(out / total).T.astype(LOW)
        return carry

    lax.fori_loop(0, tokens // BLOCK, block, 0)


def attend(first, tail, qkv):
    tokens, r = qkv.shape[1:]
    smem = pl.BlockSpec(memory_space=pltpu.SMEM)
    vmem = pl.BlockSpec(memory_space=pltpu.VMEM)
    return pl.pallas_call(
        attend_kernel,
        out_shape=(
            jax.ShapeDtypeStruct((tokens, r), LOW),
            jax.ShapeDtypeStruct((tokens // BLOCK, (r // HEAD_DIM) * BLOCK), F32),
        ),
        in_specs=[smem, smem, vmem],
        out_specs=(vmem, vmem),
        scratch_shapes=[pltpu.VMEM((r, tokens), LOW)],
        compiler_params=pltpu.CompilerParams(vmem_limit_bytes=40 * MIB),
        cost_estimate=pl.CostEstimate(
            flops=4 * tokens * 1024 * r * 8, bytes_accessed=120 * MIB, transcendentals=tokens * 1024
        ),
        name="attend",
    )(first, tail, qkv)


def unrotate(g, cos, sin):
    parts = []
    for h in range(g.shape[0] // HEAD_DIM):
        one = g[h * HEAD_DIM : h * HEAD_DIM + HALF]
        two = g[h * HEAD_DIM + HALF : (h + 1) * HEAD_DIM]
        parts += [one * cos + two * sin, two * cos - one * sin]
    return jnp.concatenate(parts, 0)


def attend_back_kernel(
    first_ref, tail_ref, qkv, grad_out, attended, log_total, cos_t, sin_t, grads,
    key_t, grad_key, grad_value,
):
    tokens, r = qkv.shape[1:]
    heads = r // HEAD_DIM
    columns = heads * BLOCK
    scale = 1.0 / math.sqrt(HEAD_DIM)
    transpose_blocks(qkv.at[1], key_t)
    grad_key[...] = jnp.zeros_like(grad_key)
    grad_value[...] = jnp.zeros_like(grad_value)

    def block(b, carry):
        at = pl.multiple_of(b * BLOCK, BLOCK)
        here = pl.ds(at, BLOCK)
        query = split_heads(qkv[0, here, :])
        grad_rows = grad_out[here, :]
        grad = split_heads(grad_rows)
        product = (grad_rows.astype(F32) * attended[here, :].astype(F32)).T
        delta = jnp.concatenate(
            [
                jnp.sum(product[h * HEAD_DIM : (h + 1) * HEAD_DIM], axis=0, keepdims=True)
                for h in range(heads)
            ],
            1,
        )
        log_row = log_total[pl.ds(b, 1), :]

        def chunk(start, allowed, grad_query):
            span = pl.ds(start, CHUNK)
            scores = dot_nt(qkv[1, span, :], query) * scale
            weights = jnp.exp(scores - log_row)
            if allowed is not None:
                weights = jnp.where(allowed, weights, 0.0)
            grad_weights = dot_nt(qkv[2, span, :], grad)
            grad_scores = (weights * (grad_weights - delta)).astype(LOW)
            grad_value[span, :] += dot_nn(weights.astype(LOW), grad)
            grad_key[span, :] += dot_nn(grad_scores, query)
            return grad_query + dot_nn(key_t[:, span], grad_scores)

        start, whole, allowed = window_of(b, first_ref[b], tail_ref[b], columns)
        grad_query = chunk(start, allowed, jnp.zeros((r, columns), F32))
        grad_query = lax.fori_loop(
            0,
            whole,
            lambda i, g: chunk(pl.multiple_of(first_ref[b] * BLOCK + i * CHUNK, BLOCK), None, g),
            grad_query,
        )
        turned = unrotate(join_heads(grad_query) * scale, cos_t[:, here], sin_t[:, here])
        grads[0, here, :] = turned.T.astype(LOW)
        return carry

    lax.fori_loop(0, tokens // BLOCK, block, 0)

    def close(b, carry):
        here = pl.ds(pl.multiple_of(b * BLOCK, BLOCK), BLOCK)
        turned = unrotate(grad_key[here, :].T * scale, cos_t[:, here], sin_t[:, here])
        grads[1, here, :] = turned.T.astype(LOW)
        grads[2, here, :] = grad_value[here, :].astype(LOW)
        return carry

    lax.fori_loop(0, tokens // BLOCK, close, 0)


def attend_back(first, tail, qkv, grad_out, attended, log_total, cos_t, sin_t):
    tokens, r = qkv.shape[1:]
    smem = pl.BlockSpec(memory_space=pltpu.SMEM)
    vmem = pl.BlockSpec(memory_space=pltpu.VMEM)
    return pl.pallas_call(
        attend_back_kernel,
        out_shape=jax.ShapeDtypeStruct((3, tokens, r), LOW),
        in_specs=[smem, smem] + [vmem] * 6,
        out_specs=vmem,
        scratch_shapes=[
            pltpu.VMEM((r, tokens), LOW),
            pltpu.VMEM((tokens, r), F32),
            pltpu.VMEM((tokens, r), F32),
        ],
        compiler_params=pltpu.CompilerParams(vmem_limit_bytes=40 * MIB),
        cost_estimate=pl.CostEstimate(
            flops=10 * tokens * 1024 * r * 8, bytes_accessed=240 * MIB, transcendentals=tokens * 1024
        ),
        name="attend_back",
    )(first, tail, qkv, grad_out, attended, log_total, cos_t, sin_t)


def dense_kernel(
    normed, cotangents, gate_w, up_w, down_w, gate_p, up_p, down_p,
    out_sum, grad_sum, gathered, weight_grads,
    weights, totals, x_buf, g_buf, sent, landed, cast_buf,
    ag_send, ag_recv, rs_send, rs_recv, credit, local_sem, w_sem, cast_sem,
):
    ring = Ring()
    n = ring.chips
    rows, features = normed.shape
    half = rows // 2
    own = gate_w.shape[0]
    tiles = 2 * own // FF_TILE
    loads = []
    for i, (mine, theirs) in enumerate(((gate_w, gate_p), (up_w, up_p), (down_w, down_p))):
        loads.append(pltpu.make_async_copy(mine, weights.at[i, pl.ds(0, own)], w_sem.at[2 * i]))
        loads.append(pltpu.make_async_copy(theirs, weights.at[i, pl.ds(own, own)], w_sem.at[2 * i + 1]))
    for load in loads:
        load.start()
    ring.greet((ring.next[0], ring.next[1]))

    def hop(t, d):
        return ring.chip_far((1 - t) if d == 0 else (t - 1)), half_rows(d, rows)

    def send(t, d, first):
        chip, part = hop(t, d)
        src = normed.at[part] if first else gathered.at[chip, part]
        return remote(src, gathered.at[chip, part], ag_send.at[d, t - 1], ag_recv.at[d, t - 1], ring.next[d])

    def reduce_copy(t, d, k):
        return remote(
            sent.at[d, k], landed.at[d, k, t % 2], rs_send.at[d, k], rs_recv.at[d, k, t % 2], ring.next[d]
        )

    for d in (0, 1):
        send(1, d, True).start()

    def clear(i, carry):
        for k in range(3):
            totals[k, pl.ds(pl.multiple_of(i * FF_TILE, FF_TILE), FF_TILE), :] = jnp.zeros(
                (FF_TILE, features), F32
            )
        return carry

    lax.fori_loop(0, tiles, clear, 0)
    for load in loads:
        load.wait()

    def step(t, carry):
        @pl.when(t < n)
        def _():
            for d in (0, 1):
                send(t, d, False).wait_recv()

            @pl.when(t < n - 1)
            def _():
                for d in (0, 1):
                    send(t + 1, d, False).start()

        copies = []
        for d in (0, 1):
            chip, part = hop(t + 1, d)
            copies.append(pltpu.make_async_copy(cotangents.at[chip, part], g_buf.at[part], local_sem.at[d]))
            copies[-1].start()

        @pl.when(t < n)
        def _():
            more = []
            for d in (0, 1):
                chip, part = hop(t + 1, d)
                more.append(pltpu.make_async_copy(gathered.at[chip, part], x_buf.at[part], local_sem.at[2 + d]))
                more[-1].start()
            for copy in more:
                copy.wait()

        @pl.when(t == n)
        def _():
            x_buf[...] = normed[...]

        for copy in copies:
            copy.wait()

        out_sum[...] = jnp.zeros_like(out_sum)
        grad_sum[...] = jnp.zeros_like(grad_sum)

        def tile(i, carry):
            span = pl.ds(pl.multiple_of(i * FF_TILE, FF_TILE), FF_TILE)
            x = x_buf[...]
            g = g_buf[...]
            gate = dot_nt(x, weights[0, span, :])
            up = dot_nt(x, weights[1, span, :])
            grad_hidden = dot_nt(g, weights[2, span, :])
            sigma = 1.0 / (1.0 + jnp.exp(-gate))
            silu = gate * sigma
            hidden = (silu * up).astype(LOW)
            grad_gate = (grad_hidden * up * sigma * (1.0 + gate * (1.0 - sigma))).astype(LOW)
            grad_up = (grad_hidden * silu).astype(LOW)
            out_sum[...] += dot_nn(hidden, weights[2, span, :])
            grad_sum[...] += dot_nn(grad_gate, weights[0, span, :])
            grad_sum[...] += dot_nn(grad_up, weights[1, span, :])
            totals[0, span, :] += dot_tn(grad_gate, x)
            totals[1, span, :] += dot_tn(grad_up, x)
            totals[2, span, :] += dot_tn(hidden, g)
            return carry

        lax.fori_loop(0, tiles, tile, 0)
        for d in (0, 1):
            for k, total in enumerate((out_sum, grad_sum)):
                part = pl.ds(d * half, half)

                @pl.when(t >= 2)
                def _():
                    reduce_copy(t - 1, d, k).wait_recv()
                    total[part, :] += landed[d, k, (t - 1) % 2].astype(F32)

                    @pl.when(t <= n - 2)
                    def _():
                        pl.semaphore_signal(
                            credit.at[d, k], inc=1, device_id={"dp": ring.back[d]}, device_id_type=MESH
                        )

                    reduce_copy(t - 1, d, k).wait_send()

                @pl.when(t < n)
                def _():
                    sent[d, k] = total[part, :].astype(LOW)

                    @pl.when(t >= 3)
                    def _():
                        pl.semaphore_wait(credit.at[d, k], 1)

                    reduce_copy(t, d, k).start()

        return carry

    lax.fori_loop(1, n + 1, step, 0)

    def cast_copy(i):
        return pltpu.make_async_copy(
            cast_buf.at[i % 2],
            weight_grads.at[i // tiles, pl.ds(pl.multiple_of((i % tiles) * FF_TILE, FF_TILE), FF_TILE)],
            cast_sem.at[i % 2],
        )

    def store(i, carry):
        @pl.when(i >= 2)
        def _():
            cast_copy(i - 2).wait()

        span = pl.ds(pl.multiple_of((i % tiles) * FF_TILE, FF_TILE), FF_TILE)
        cast_buf[i % 2] = totals[i // tiles, span, :].astype(LOW)
        cast_copy(i).start()
        return carry

    lax.fori_loop(0, 3 * tiles, store, 0)
    cast_copy(3 * tiles - 2).wait()
    cast_copy(3 * tiles - 1).wait()

    def finish(t, carry):
        for d in (0, 1):
            send(t, d, False).wait_send()
        return carry

    lax.fori_loop(1, n, finish, 0)


def dense(normed, cotangents, own_weights, partner_weights):
    rows, features = normed.shape
    n = lax.axis_size("dp") // 2
    own = own_weights[0].shape[0]
    half = rows // 2
    vmem = pl.BlockSpec(memory_space=pltpu.VMEM)
    hbm = pl.BlockSpec(memory_space=pl.ANY)
    dma = pltpu.SemaphoreType.DMA
    return pl.pallas_call(
        dense_kernel,
        out_shape=(
            jax.ShapeDtypeStruct((rows, features), F32),
            jax.ShapeDtypeStruct((rows, features), F32),
            jax.ShapeDtypeStruct((n, rows, features), LOW),
            jax.ShapeDtypeStruct((3, 2 * own, features), LOW),
        ),
        in_specs=[vmem] + [hbm] * 7,
        out_specs=(vmem, vmem, hbm, hbm),
        scratch_shapes=[
            pltpu.VMEM((3, 2 * own, features), LOW),
            pltpu.VMEM((3, 2 * own, features), F32),
            pltpu.VMEM((rows, features), LOW),
            pltpu.VMEM((rows, features), LOW),
            pltpu.VMEM((2, 2, half, features), LOW),
            pltpu.VMEM((2, 2, 2, half, features), LOW),
            pltpu.VMEM((2, FF_TILE, features), LOW),
            dma((2, n)), dma((2, n)), dma((2, 2)), dma((2, 2, 2)),
            pltpu.SemaphoreType.REGULAR((2, 2)),
            dma((4,)), dma((6,)), dma((2,)),
        ],
        compiler_params=pltpu.CompilerParams(
            collective_id=2, has_side_effects=True, vmem_limit_bytes=62 * MIB
        ),
        cost_estimate=pl.CostEstimate(
            flops=2 * 9 * n * rows * features * 2 * own, bytes_accessed=800 * MIB, transcendentals=0
        ),
        name="dense",
    )(normed, cotangents, *own_weights, *partner_weights)


def normed_back_kernel(
    grads, weights, partner_weights, out,
    partner_grads, sent, landed,
    p_send, p_recv, rs_send, rs_recv, credit,
):
    ring = Ring()
    n = ring.chips
    rows, features = out.shape
    half = rows // 2
    r = grads.shape[2]
    ring.greet((ring.next[0], ring.next[1], ring.partner))

    def place(t, d):
        return ring.chip_far(-t if d == 0 else t)

    def swap(t, d):
        start = (place(t, d) * 2 + 1 - ring.core) * rows + d * half
        return remote(
            grads.at[:, pl.ds(pl.multiple_of(start, half), half)],
            partner_grads.at[:, t % n, half_rows(d, rows)],
            p_send.at[d, t % n],
            p_recv.at[d, t % n],
            ring.partner,
        )

    def begin(t, carry):
        for d in (0, 1):
            swap(t, d).start()
        return carry

    lax.fori_loop(1, n + 1, begin, 0)

    def reduce_copy(t, d):
        return remote(sent.at[d], landed.at[d, t % 2], rs_send.at[d], rs_recv.at[d, t % 2], ring.next[d])

    def step(t, carry):
        for d in (0, 1):
            start = (place(t, d) * 2 + ring.core) * rows + d * half
            mine = pl.ds(pl.multiple_of(start, half), half)
            part = pl.ds(d * half, half)
            swap(t, d).wait_recv()
            total = dot_nn(grads[0, mine, :], weights[0])
            for i in (1, 2):
                total += dot_nn(grads[i, mine, :], weights[i])
            for i in range(3):
                total += dot_nn(partner_grads[i, t % n, part, :], partner_weights[i])
            out[part, :] = total

        for d in (0, 1):
            part = pl.ds(d * half, half)

            @pl.when(t >= 2)
            def _():
                reduce_copy(t - 1, d).wait_recv()
                out[part, :] += landed[d, (t - 1) % 2].astype(F32)

                @pl.when(t <= n - 2)
                def _():
                    pl.semaphore_signal(
                        credit.at[d], inc=1, device_id={"dp": ring.back[d]}, device_id_type=MESH
                    )

                reduce_copy(t - 1, d).wait_send()

            @pl.when(t < n)
            def _():
                sent[d] = out[part, :].astype(LOW)

                @pl.when(t >= 3)
                def _():
                    pl.semaphore_wait(credit.at[d], 1)

                reduce_copy(t, d).start()

        return carry

    lax.fori_loop(1, n + 1, step, 0)

    def finish(t, carry):
        for d in (0, 1):
            swap(t, d).wait_send()
        return carry

    lax.fori_loop(1, n + 1, finish, 0)


def normed_back(grads, weights, partner_weights):
    tokens, r = grads.shape[1:]
    features = weights.shape[2]
    devices = lax.axis_size("dp")
    n = devices // 2
    rows = tokens // devices
    half = rows // 2
    vmem = pl.BlockSpec(memory_space=pltpu.VMEM)
    dma = pltpu.SemaphoreType.DMA
    return pl.pallas_call(
        normed_back_kernel,
        out_shape=jax.ShapeDtypeStruct((rows, features), F32),
        in_specs=[vmem] * 3,
        out_specs=vmem,
        scratch_shapes=[
            pltpu.VMEM((3, n, rows, r), LOW),
            pltpu.VMEM((2, half, features), LOW),
            pltpu.VMEM((2, 2, half, features), LOW),
            dma((2, n)), dma((2, n)), dma((2,)), dma((2, 2)),
            pltpu.SemaphoreType.REGULAR((2,)),
        ],
        compiler_params=pltpu.CompilerParams(
            collective_id=3, has_side_effects=True, vmem_limit_bytes=40 * MIB
        ),
        cost_estimate=pl.CostEstimate(
            flops=2 * n * rows * features * 6 * r, bytes_accessed=320 * MIB, transcendentals=0
        ),
        name="normed_back",
    )(grads, weights, partner_weights)


def rms(values, norm_gain):
    return (
        values * lax.rsqrt(jnp.mean(values * values, axis=-1, keepdims=True) + EPSILON) * norm_gain
    )


def rms_back(values, norm_gain, grads):
    _, pullback = jax.vjp(rms, values, norm_gain)
    return pullback(grads)


def turned_rows(weight):
    parts = weight.reshape(-1, 2, HALF, weight.shape[1])
    return jnp.concatenate([-parts[:, 1:], parts[:, :1]], 1).reshape(weight.shape)


def from_partner(value):
    devices = lax.axis_size("dp")
    return lax.ppermute(value, "dp", [(i, i ^ 1) for i in range(devices)])


def pack_sum(value):
    low = value.astype(LOW)
    if lax.axis_size("rep") == 2:
        other = lax.ppermute(low, "rep", [(0, 1), (1, 0)])
        return low.astype(F32) + other.astype(F32)
    return lax.psum(low, "rep").astype(F32)


def body(
    tokens,
    attention_gain,
    query_weight,
    key_weight,
    value_weight,
    output_weight,
    dense_gain,
    gate_weight,
    up_weight,
    down_weight,
    block_document,
    document_tail,
    cotangent,
):
    devices = lax.axis_size("dp")
    chips = devices // 2
    core = lax.axis_index("dp") % 2
    hidden_in = tokens[0].astype(F32)
    tok_dev = hidden_in.shape[0]
    pack_tok = tok_dev * devices

    documents, tails = block_document[0], document_tail[0]
    first = jnp.sum((documents[None, :] < documents[:, None]).astype(jnp.int32), axis=1)
    last = jnp.concatenate([documents[1:] != documents[:-1], jnp.ones((1,), bool)])
    doc_ids = jnp.arange(tails.shape[0], dtype=jnp.int32)
    own_tail = jnp.sum((documents[:, None] == doc_ids[None, :]) * tails[None, :], axis=1)
    tail = jnp.where(last, own_tail, BLOCK).astype(jnp.int32)
    block_index = jnp.arange(documents.shape[0], dtype=jnp.int32)
    inside = jnp.arange(BLOCK, dtype=jnp.int32)
    position = ((block_index - first)[:, None] * BLOCK + inside[None, :]).reshape(-1)
    frequency = ROPE_BASE ** (-(jnp.arange(HALF, dtype=F32) * (2.0 / HEAD_DIM)))
    angles = position.astype(F32)[None, :] * frequency[:, None]
    cos_t, sin_t = jnp.cos(angles), jnp.sin(angles)
    r = query_weight.shape[0]

    def rows_of(table):
        mine = lax.dynamic_index_in_dim(
            table.reshape(HALF, chips, 2, tok_dev), core, axis=2, keepdims=False
        )
        return jnp.tile(mine.transpose(1, 2, 0), (1, 1, r // HALF))

    normed = rms(hidden_in, attention_gain).astype(LOW)
    stacked = jnp.concatenate(
        [
            query_weight,
            turned_rows(query_weight),
            key_weight,
            turned_rows(key_weight),
            value_weight,
        ],
        0,
    )
    qkv, normed_all = gather_project(normed, stacked, rows_of(cos_t), rows_of(sin_t))

    full_output = lax.all_gather(output_weight, "dp", axis=0, tiled=True)
    groups = [list(range(c, devices, 2)) for c in (0, 1)]
    grad_low = cotangent[0]
    cotangents = lax.all_gather(
        grad_low, "dp", axis=0, tiled=True, axis_index_groups=groups
    ).reshape(chips, tok_dev, -1)
    gate_other, up_other, down_other = (
        from_partner(gate_weight),
        from_partner(up_weight),
        from_partner(down_weight),
    )
    qkv_weight = jnp.stack([query_weight, key_weight, value_weight])
    qkv_other = from_partner(qkv_weight)

    attended, log_total = attend(first, tail, qkv)
    attended_here = lax.all_to_all(attended, "dp", split_axis=0, concat_axis=1, tiled=True)
    mixed = hidden_in + dot_nn(attended_here, full_output)
    normed_two = rms(mixed, dense_gain).astype(LOW)

    out_sum, grad_normed_two, _, dense_grads = dense(
        normed_two,
        cotangents,
        (gate_weight, up_weight, down_weight),
        (gate_other, up_other, down_other),
    )
    layer_out = mixed + out_sum
    own_rows = gate_weight.shape[0]
    dense_low = (
        dense_grads[:, :own_rows].astype(F32)
        + from_partner(dense_grads[:, own_rows:]).astype(F32)
    ).astype(LOW)
    dense_total = pack_sum(dense_low)

    grad_mixed_norm, dense_gain_part = rms_back(mixed, dense_gain, grad_normed_two)
    grad_mixed = grad_low.astype(F32) + grad_mixed_norm
    grad_mixed_low = grad_mixed.astype(LOW)
    grad_attended = dot_nt(grad_mixed_low, full_output).astype(LOW)
    grad_heads = lax.all_to_all(grad_attended, "dp", split_axis=1, concat_axis=0, tiled=True)
    output_grad = lax.psum_scatter(
        dot_tn(attended_here, grad_mixed_low).astype(LOW), "dp", scatter_dimension=0, tiled=True
    )
    output_total = pack_sum(output_grad)

    grads = attend_back(first, tail, qkv, grad_heads, attended, log_total, cos_t, sin_t)
    swapped = from_partner(
        lax.dynamic_index_in_dim(
            grads.reshape(3, chips, 2, tok_dev, r), 1 - core, axis=2, keepdims=False
        )
    )
    mine = lax.dynamic_index_in_dim(
        grads.reshape(3, chips, 2, tok_dev, r), core, axis=2, keepdims=False
    )
    both = jnp.stack([mine, swapped]).reshape(2, 3, chips * tok_dev, r)
    normed_rows = normed_all.reshape(chips * tok_dev, -1)
    qkv_parts = lax.dot_general(
        both, normed_rows, (((2,), (0,)), ((), ())), preferred_element_type=F32
    ).astype(LOW)
    qkv_low = (qkv_parts[0].astype(F32) + from_partner(qkv_parts[1]).astype(F32)).astype(LOW)
    qkv_total = pack_sum(qkv_low)

    grad_normed = normed_back(grads, qkv_weight, qkv_other)
    grad_in_norm, attention_gain_part = rms_back(hidden_in, attention_gain, grad_normed)
    input_grad = grad_mixed + grad_in_norm
    gain_totals = lax.psum((attention_gain_part, dense_gain_part), ("dp", "rep"))
    return (
        layer_out[None].astype(LOW),
        input_grad[None],
        gain_totals[0],
        qkv_total[0],
        qkv_total[1],
        qkv_total[2],
        output_total,
        gain_totals[1],
        dense_total[0],
        dense_total[1],
        dense_total[2],
    )


def solution(mesh):
    return jax.shard_map(
        body,
        mesh=mesh,
        in_specs=(
            P("rep", "dp", None),
            P(),
            P("dp", None),
            P("dp", None),
            P("dp", None),
            P("dp", None),
            P(),
            P("dp", None),
            P("dp", None),
            P("dp", None),
            P("rep", None),
            P("rep", None),
            P("rep", "dp", None),
        ),
        out_specs=(
            P("rep", "dp", None),
            P("rep", "dp", None),
            P(),
            P("dp", None),
            P("dp", None),
            P("dp", None),
            P("dp", None),
            P(),
            P("dp", None),
            P("dp", None),
            P("dp", None),
        ),
        check_vma=False,
    )
```

time: 3230 us -> 904 us (0.28)
  waiting for transfers between devices: 1910 us -> 44.9 us
  matrix products: 713 us -> 25.4 us
  Pallas kernels: 0 us -> 626 us
  local copies, waits for them, and re-layouts: 192 us -> 38.4 us
  blocking collectives: 191 us -> 83 us
  other arithmetic: 126 us -> 46.9 us
  loops' own time: 43 us -> 0 us
    reduce_scatter x7 -> x1, waiting for transfers between devices: 1190 us -> 0.01 us  [body(): lax.psum_scatter(dot_tn(attended_here, grad_mixed_low).astype(LOW), 'dp',...]
    dot_general x77 -> x4, matrix products: 713 us -> 25.4 us  [the longest x1 9.95 us: body(): lax.dot_general(both, normed_rows, (((2,), (0,)), ((), ())), preferred_el...]
    pallas_call x0 -> x5, Pallas kernels: none -> 626 us  [the longest x1 258 us: dense(): pl.pallas_call(dense_kernel, out_shape=(jax.ShapeDtypeStruct((rows, featu...]
    all_gather x7 -> x2, waiting for transfers between devices: 506 us -> 0.02 us  [the longest x1 0.02 us: body(): lax.all_gather(grad_low, 'dp', axis=0, tiled=True, axis_index_groups=groups)]
    all_to_all x4 -> x0, blocking collectives: 151 us -> none  [the longest x1 41 us: body(): lax.all_to_all(query, 'dp', split_axis=1, concat_axis=0, tiled=True)]
    dynamic_update_slice x32 -> x0, local copies, waits for them, and re-layouts: 134 us -> none  [the longest x16 53.1 us: attend(): results, log_total = lax.map(block_fn, starts)]
    psum x1 -> x0, waiting for transfers between devices: 125 us -> none  [body(): lax.psum(query_grad.astype(jnp.bfloat16), 'rep').astype(jnp.float32)]
    psum x1, blocking collectives: 39.8 us -> 83 us  [body(): lax.psum((attention_gain_part, dense_gain_part), ('dp', 'rep'))]
  transfers between devices with their start and end apart: 19 -> 15, of which waited for: 15 -> 4; matrix products, arithmetic and copies ran while one was open for 29% -> 10% of each run, Pallas kernels for 0% -> 41%
where the time goes in v1:
time: 904 us; the launch traced here: 896 us
  Pallas kernels  626 us (69%)
  blocking collectives  83 us (9%)
  other arithmetic  46.9 us (5%)
  waiting for transfers between devices  44.9 us (5%)
  local copies, waits for them, and re-layouts  38.4 us (4%)
  matrix products  25.4 us (3%)
  starting transfers between devices  16.6 us (2%)
  between operations  14.8 us (2%)
    pallas_call x1, Pallas kernels, dense(): pl.pallas_call(dense_kernel, out_shape=(jax.ShapeDtypeStruct((rows, featu...  258 us
    pallas_call x1, Pallas kernels, gather_project(): pl.pallas_call(gather_project_kernel, out_shape=(jax.ShapeDtypeStruct((3,...  181 us
    pallas_call x1, Pallas kernels, normed_back(): pl.pallas_call(normed_back_kernel, out_shape=jax.ShapeDtypeStruct((rows,...  106 us
    psum x1, blocking collectives, body(): lax.psum((attention_gain_part, dense_gain_part), ('dp', 'rep'))  83 us
    pallas_call x1, Pallas kernels, attend_back(): pl.pallas_call(attend_back_kernel, out_shape=jax.ShapeDtypeStruct((3, tok...  43.2 us
    pallas_call x1, Pallas kernels, attend(): pl.pallas_call(attend_kernel, out_shape=(jax.ShapeDtypeStruct((tokens, r)...  37.9 us
    all_to_all x1, waiting for transfers between devices, body(): lax.all_to_all(attended, 'dp', split_axis=0, concat_axis=1, tiled=True)  34.4 us
  transfers between devices with their start and end apart: 15, of which 4 were waited for; matrix products, arithmetic and copies ran while one was open for 10% of the time, Pallas kernels for 41%

profile of v1, /device:TPU:0, one launch (start us, length us, event | category | flops | bytes accessed | tf_op | source)
XLA Modules:
  0.0 896.3 jit_solution(824116249994317554)
XLA Ops:
  12.6 1.5 copy.37.sine
  14.3 1.5 fusion.15
  18.7 181.2 %gather_project.1 = (bf16[3,4096,128]{2,1,0:T(8,128)(2,1)S(1)}, bf16[8,256,2048]{2,1,0:T(8,128)(2,1)}) custom-call(bf16[256,2048]{1,0:T(8,128)(2,1)S(1)} %fusion.10.normed, bf16[640,2048]{1,0:T(8,128)(2,1)S(1)} %constant_dynamic-update-slice_fusion.weights, f32[8,256,128]{2,1,0:T(8,128)S(1)} %copy.36.cosine, f32[8,256,128]{2,1,0:T(8,128)S(1)} %copy.37.sine), custom_call_target="tpu_custom_call" | custom-call | flops 10737418240 | bytes 335544320 | tf_op jit(solution)/shard_map/gather_project/pallas_call | solution.py:216
  200.0 37.9 %attend.1 = (bf16[4096,128]{1,0:T(8,128)(2,1)S(1)}, f32[32,256]{1,0:T(8,128)S(1)}) custom-call(s32[32]{0:T(128)S(1)} %convert_reduce_fusion.first_ref, s32[32]{0:T(128)S(1)} %add_select_fusion.tail_ref, bf16[3,4096,128]{2,1,0:T(8,128)(2,1)S(1)} %get-tuple-element.18.qkv), custom_call_target="tpu_custom_call" | custom-call | flops 17179869184 | bytes 125829120 | tf_op jit(solution)/shard_map/attend/pallas_call | solution.py:319
  239.3 5.3 all-to-all-start
  245.7 34.4 %all-to-all-done = bf16[16,256,128]{1,2,0:T(8,128)(2,1)} async-done(((bf16[16,256,128]{1,2,0:T(8,128)(2,1)}), bf16[16,256,128]{1,2,0:T(8,128)(2,1)}, u32[]{:S(2)}, u32[]{:S(2)}) %all-to-all-start) | async-done | bytes 1048608 | tf_op jit(solution)/shard_map/all_to_all | solution.py:852
  280.1 6.2 multiply_reduce_fusion.2
  288.9 258.4 %dense.1 = (f32[256,2048]{1,0:T(8,128)}, f32[256,2048]{1,0:T(8,128)}, bf16[8,256,2048]{2,1,0:T(8,128)(2,1)}, bf16[3,1024,2048]{2,1,0:T(8,128)(2,1)}) custom-call(bf16[256,2048]{1,0:T(8,128)(2,1)} %multiply_convert_fusion.normed, bf16[8,256,2048]{2,1,0:T(8,128)(2,1)} %bitcast.103, bf16[512,2048]{1,0:T(8,128)(2,1)} %gate_w.1, bf16[512,2048]{1,0:T(8,128)(2,1)} %up_w.1, ...), custom_call_target="tpu_custom_call" | custom-call | flops 77309411328 | bytes 838860800 | tf_op jit(solution)/shard_map/dense/pallas_call | solution.py:604
  547.3 2.9 multiply_reduce_fusion
  550.8 3.7 fusion.12
  555.5 2.4 fusion.17
  559.1 3.8 all-to-all-start.1
  563.3 6.6 slice.62
  570.3 2.7 multiply_sine_fusion
  573.0 6.8 convolution_convert_fusion
  579.8 6.0 all-to-all-done.1
  586.9 2.1 copy-done.4
  589.0 43.2 %attend_back.1.grads = bf16[3,4096,128]{2,1,0:T(8,128)(2,1)S(1)} custom-call(s32[32]{0:T(128)S(1)} %convert_reduce_fusion.first_ref, s32[32]{0:T(128)S(1)} %add_select_fusion.tail_ref, bf16[3,4096,128]{2,1,0:T(8,128)(2,1)S(1)} %copy-done.4, bf16[4096,128]{1,0:T(8,128)(2,1)S(1)} %bitcast.90, bf16[4096,128]{1,0:T(8,128)(2,1)S(1)} %get-tuple-element.19.attended, ...), custom_call_target="tpu_custom_call" | custom-call | flops 42949672960 | bytes 251658240 | tf_op jit(solution)/shard_map/attend_back/pallas_call | solution.py:413
  632.5 1.4 copy-done
  633.9 1.6 copy.41
  636.9 11.0 %add_convert_fusion = bf16[3,512,2048]{2,1,0:T(8,128)(2,1)} fusion(bf16[3,512,2048]{2,1,0:T(8,128)(2,1)} %collective-permute-done.8, bf16[3,1024,2048]{2,1,0:T(8,128)(2,1)} %get-tuple-element.24), kind=kLoop, calls=%fused_computation.1 | loop fusion | flops 12582912 | bytes 18874368 | tf_op jit(solution)/shard_map/convert_element_type | solution.py:867
  649.3 9.9 %bitcast_convert_fusion = bf16[2,3,128,2048]{3,2,1,0:T(8,128)(2,1)S(1)} fusion(bf16[8,256,2048]{2,1,0:T(8,128)(2,1)} %get-tuple-element.23, bf16[1,3,8,256,128]{3,4,2,1,0:T(8,128)(2,1)} %bitcast.31, bf16[1,3,8,256,128]{3,4,2,1,0:T(8,128)(2,1)S(1)} %bitcast.101), kind=kOutput, calls=%fused_computation.5 | convolution fusion | flops 6445596672 | bytes 14680064 | tf_op jit(solution)/shard_map/dot_general | solution.py:891
  660.8 2.1 collective-permute-done.5
  662.9 1.9 fusion.7
  665.3 105.6 %normed_back.1 = f32[256,2048]{1,0:T(8,128)S(1)} custom-call(bf16[3,4096,128]{2,1,0:T(8,128)(2,1)S(1)} %copy-done.1, bf16[3,128,2048]{2,1,0:T(8,128)(2,1)S(1)} %pad_maximum_fusion.weights, bf16[3,128,2048]{2,1,0:T(8,128)(2,1)S(1)} %collective-permute-done.3.partner_weights), custom_call_target="tpu_custom_call" | custom-call | flops 6442450944 | bytes 335544320 | tf_op jit(solution)/shard_map/normed_back/pallas_call | solution.py:731
  771.7 83.0 %all-reduce = (f32[2048]{0:T(1024)}, f32[2048]{0:T(1024)}) all-reduce(f32[2048]{0:T(1024)S(1)} %get-tuple-element.27, f32[2048]{0:T(1024)S(1)} %get-tuple-element.25), channel_id=1, replica_groups=mesh['dp'=16,'rep'=2] {'dp','rep'}, use_global_device_ids=true, to_apply=%region_7.8 | all-reduce | flops 4096 | bytes 32768 | tf_op jit(solution)/shard_map/psum | solution.py:900
  854.7 3.5 fusion.14
  858.2 2.5 convert_add_fusion.3
  860.7 1.7 slice_bitcast_fusion.5
  862.4 12.2 %convert_add_fusion = f32[3,512,2048]{2,1,0:T(8,128)} fusion(bf16[3,512,2048]{2,1,0:T(8,128)(2,1)} %collective-permute-done.9, bf16[3,512,2048]{2,1,0:T(8,128)(2,1)} %add_convert_fusion), kind=kLoop, calls=%fused_computation | loop fusion | flops 9437184 | bytes 25165824 | tf_op jit(solution)/shard_map/add | solution.py:778
  874.6 2.9 collective-permute-start.7
  877.5 9.8 %slice_bitcast_fusion = (f32[512,2048]{1,0:T(8,128)}, f32[512,2048]{1,0:T(8,128)}, f32[512,2048]{1,0:T(8,128)}) fusion(f32[3,512,2048]{2,1,0:T(8,128)} %convert_add_fusion), kind=kLoop, calls=%fused_computation.6 | loop fusion | bytes 25165824 | tf_op jit(solution)/shard_map/squeeze | solution.py:912
  (128 shorter events, 25.8 us)
Async XLA Ops:
  7.2 273.0 %all-gather.4.cloned.1.call-start = ((), (), s32[]{:S(2)}) async-start(), calls=%async_computation.3 | async-start | bytes 8912896 | tf_op jit(solution)/shard_map/all_gather | solution.py:837
  7.9 281.0 %all-gather.6.cloned.1.call-start = ((), (), s32[]{:S(2)}) async-start(), calls=%async_computation.5 | async-start | bytes 9437184 | tf_op jit(solution)/shard_map/all_gather | solution.py:840
  11.5 2.7 copy-start.28
  11.5 2.7 copy-start.29
  11.5 4.4 copy-start.14
  200.0 38.0 %copy-start.3 = (bf16[3,4096,128]{2,1,0:T(8,128)(2,1)}, bf16[3,4096,128]{2,1,0:T(8,128)(2,1)S(1)}, u32[]{:S(2)}) copy-start(bf16[3,4096,128]{2,1,0:T(8,128)(2,1)S(1)} %get-tuple-element.18.qkv) | copy-start | bytes 9437188
  237.9 42.2 %copy-start.8 = (bf16[1,256,2048]{2,1,0:T(8,128)(2,1)S(1)}, bf16[1,256,2048]{2,1,0:T(8,128)(2,1)}, u32[]{:S(2)}) copy-start(bf16[1,256,2048]{2,1,0:T(8,128)(2,1)} %param.13) | copy-start | bytes 3145732
  239.3 40.9 %all-to-all-start = ((bf16[16,256,128]{1,2,0:T(8,128)(2,1)}), bf16[16,256,128]{1,2,0:T(8,128)(2,1)}, u32[]{:S(2)}, u32[]{:S(2)}) async-start(bf16[16,256,128]{1,2,0:T(8,128)(2,1)} %copy.38), calls=%async_computation | async-start | bytes 2097152 | tf_op jit(solution)/shard_map/all_to_all | solution.py:852
  244.6 44.3 %collective-permute-start = (bf16[512,2048]{1,0:T(8,128)(2,1)}, bf16[512,2048]{1,0:T(8,128)(2,1)}, u32[]{:S(2)}, u32[]{:S(2)}) collective-permute-start(bf16[512,2048]{1,0:T(8,128)(2,1)} %gate_w.1), channel_id=1, source_target_pairs={{0,2},{2,0},{4,6},{6,4},{8,10},{10,8},{12,14},{14,12},{16,18},{18,... | collective-permute-start | bytes 6291464 | tf_op jit(solution)/shard_map/ppermute | solution.py:771
  245.2 43.7 %collective-permute-start.1 = (bf16[512,2048]{1,0:T(8,128)(2,1)}, bf16[512,2048]{1,0:T(8,128)(2,1)}, u32[]{:S(2)}, u32[]{:S(2)}) collective-permute-start(bf16[512,2048]{1,0:T(8,128)(2,1)} %up_w.1), channel_id=1, source_target_pairs={{0,2},{2,0},{4,6},{6,4},{8,10},{10,8},{12,14},{14,12},{16,18},{18,... | collective-permute-start | bytes 6291464 | tf_op jit(solution)/shard_map/ppermute | solution.py:771
  245.3 43.6 %collective-permute-start.2 = (bf16[512,2048]{1,0:T(8,128)(2,1)}, bf16[512,2048]{1,0:T(8,128)(2,1)}, u32[]{:S(2)}, u32[]{:S(2)}) collective-permute-start(bf16[512,2048]{1,0:T(8,128)(2,1)} %down_w.1), channel_id=1, source_target_pairs={{0,2},{2,0},{4,6},{6,4},{8,10},{10,8},{12,14},{14,12},{16,18},{18,... | collective-permute-start | bytes 6291464 | tf_op jit(solution)/shard_map/ppermute | solution.py:771
  280.1 7.5 copy-start.21
  547.3 2.9 copy-start.6
  547.3 3.5 copy-start.13
  550.8 4.7 copy-start.12
  554.5 3.4 copy-start.10
  559.1 26.7 %all-to-all-start.1 = ((bf16[256,16,128]{2,0,1:T(8,128)(2,1)}), bf16[256,16,128]{2,0,1:T(8,128)(2,1)S(1)}, u32[]{:S(2)}, u32[]{:S(2)}) async-start(bf16[256,16,128]{2,0,1:T(8,128)(2,1)} %bitcast.97), calls=%async_computation.1 | async-start | bytes 2097152 | tf_op jit(solution)/shard_map/all_to_all | solution.py:874
  562.9 311.7 %reduce-scatter.2.cloned.1.call-start = ((), (), s32[]{:S(2)}) async-start(), calls=%async_computation.4 | async-start | bytes 8912896 | tf_op jit(solution)/shard_map/reduce_scatter | solution.py:875
  563.3 9.7 %copy-start.11 = (f32[256,2048]{1,0:T(8,128)S(1)}, f32[256,2048]{1,0:T(8,128)}, u32[]{:S(2)}) copy-start(f32[256,2048]{1,0:T(8,128)} %copy-done.10) | copy-start | bytes 6291460
  569.9 67.0 %collective-permute-start.8 = (bf16[3,512,2048]{2,1,0:T(8,128)(2,1)}, bf16[3,512,2048]{2,1,0:T(8,128)(2,1)}, u32[]{:S(2)}, u32[]{:S(2)}) collective-permute-start(bf16[3,512,2048]{2,1,0:T(8,128)(2,1)} %slice.62), channel_id=1, source_target_pairs={{0,2},{2,0},{4,6},{6,4},{8,10},{10,8},{12,14},{14,12},{16,18},{18,... | collective-permute-start | bytes 18874376 | tf_op jit(solution)/shard_map/ppermute | solution.py:771
  635.5 13.8 %collective-permute-start.4 = (bf16[3,8,256,128]{2,3,1,0:T(8,128)(2,1)}, bf16[3,8,256,128]{2,3,1,0:T(8,128)(2,1)}, u32[]{:S(2)}, u32[]{:S(2)}) collective-permute-start(bf16[3,8,256,128]{2,3,1,0:T(8,128)(2,1)} %bitcast.102), channel_id=1, source_target_pairs={{0,2},{2,0},{4,6},{6,4},{8,10},{10,8},{12,14},{14,12},{16,18},{18,... | collective-permute-start | bytes 4718600 | tf_op jit(solution)/shard_map/ppermute | solution.py:771
  647.9 214.6 %collective-permute-start.9 = (bf16[3,512,2048]{2,1,0:T(8,128)(2,1)}, bf16[3,512,2048]{2,1,0:T(8,128)(2,1)}, u32[]{:S(2)}, u32[]{:S(2)}) collective-permute-start(bf16[3,512,2048]{2,1,0:T(8,128)(2,1)} %add_convert_fusion), channel_id=1, source_target_pairs={{0,1},{1,0},{2,3},{3,2},{4,5},{5,4},{6,7},{7,6},{8,9},{9,8},{10,11... | collective-permute-start | bytes 18874376 | tf_op jit(solution)/shard_map/ppermute | solution.py:777
  659.4 3.5 collective-permute-start.5
  660.8 4.5 copy-start.1
  660.8 4.5 collective-permute-start.3
  664.7 106.1 %copy-start.9 = (bf16[1,256,2048]{2,1,0:T(8,128)(2,1)S(1)}, bf16[1,256,2048]{2,1,0:T(8,128)(2,1)}, u32[]{:S(2)}) copy-start(bf16[1,256,2048]{2,1,0:T(8,128)(2,1)} %param.13) | copy-start | bytes 3145732
  664.8 106.1 %copy-start.23 = (f32[2048]{0:T(1024)S(1)}, f32[2048]{0:T(1024)}, u32[]{:S(2)}) copy-start(f32[2048]{0:T(1024)} %param.14) | copy-start | bytes 24580
  664.8 106.1 %copy-start.25 = (f32[256]{0:T(256)S(1)}, f32[256]{0:T(256)}, u32[]{:S(2)}) copy-start(f32[256]{0:T(256)} %copy-done.24) | copy-start | bytes 3076
  664.8 193.4 %collective-permute-start.6 = (bf16[3,128,2048]{2,1,0:T(8,128)(2,1)}, bf16[3,128,2048]{2,1,0:T(8,128)(2,1)}, u32[]{:S(2)}, u32[]{:S(2)}) collective-permute-start(bf16[3,128,2048]{2,1,0:T(8,128)(2,1)} %fusion.7), channel_id=1, source_target_pairs={{0,1},{1,0},{2,3},{3,2},{4,5},{5,4},{6,7},{7,6},{8,9},{9,8},{10,11... | collective-permute-start | bytes 4718600 | tf_op jit(solution)/shard_map/ppermute | solution.py:777
  770.9 83.8 %copy-start.27 = (f32[256]{0:T(256)S(1)}, f32[256]{0:T(256)}, u32[]{:S(2)}) copy-start(f32[256]{0:T(256)} %copy-done.26) | copy-start | bytes 3076
  874.6 13.7 %copy-start.20 = (bf16[128,2048]{1,0:T(8,128)(2,1)S(1)}, bf16[128,2048]{1,0:T(8,128)(2,1)}, u32[]{:S(2)}) copy-start(bf16[128,2048]{1,0:T(8,128)(2,1)} %reduce-scatter.2.cloned.1.call-done) | copy-start | bytes 1572868
  874.6 13.7 %collective-permute-start.7 = (bf16[128,2048]{1,0:T(8,128)(2,1)}, bf16[128,2048]{1,0:T(8,128)(2,1)S(1)}, u32[]{:S(2)}, u32[]{:S(2)}) collective-permute-start(bf16[128,2048]{1,0:T(8,128)(2,1)} %reduce-scatter.2.cloned.1.call-done), channel_id=1, source_target_pairs={{0,1},{1,0},{2,3},{3,2},{4,5},{5,4},{6,7},{7,6},{8,9},{9,8},{10,11... | collective-permute-start | bytes 1572872 | tf_op jit(solution)/shard_map/ppermute | solution.py:777
  (13 other events, 17.2 us)
Sparse Core Ops, SparseCore 0:
  10.2 104.4 all-gather.3
  116.8 164.9 all-gather.5
  580.0 113.4 reduce-scatter.1

commit v2 on v1

--- a/solution.py
+++ b/solution.py
@@ -56,6 +56,15 @@
     odd = row % 2
     column = x - 1 + odd * (width - 2 * x)
     return jnp.where(x == 0, z, depth + row * (width - 1) + column)
+
+
+def ring_order(chips):
+    depth, width = grid_of(chips)
+    order = [z * width for z in range(depth)]
+    for row in range(depth):
+        columns = list(range(1, width))
+        order += [(depth - 1 - row) * width + x for x in (columns[::-1] if row % 2 else columns)]
+    return order
 
 
 class Ring:
@@ -430,9 +439,9 @@
 
 def dense_kernel(
     normed, cotangents, gate_w, up_w, down_w, gate_p, up_p, down_p,
-    out_sum, grad_sum, gathered, weight_grads,
-    weights, totals, x_buf, g_buf, sent, landed, cast_buf,
-    ag_send, ag_recv, rs_send, rs_recv, credit, local_sem, w_sem, cast_sem,
+    grad_sum, out_parts, gathered, weight_grads,
+    weights, totals, x_buf, g_buf, out_acc, grad_acc, sent, landed, cast_buf, pair_land,
+    ag_send, ag_recv, rs_send, rs_recv, credit, local_sem, w_sem, cast_sem, pair_send, pair_recv,
 ):
     ring = Ring()
     n = ring.chips
@@ -446,37 +455,48 @@
         loads.append(pltpu.make_async_copy(theirs, weights.at[i, pl.ds(own, own)], w_sem.at[2 * i + 1]))
     for load in loads:
         load.start()
-    ring.greet((ring.next[0], ring.next[1]))
-
-    def hop(t, d):
-        return ring.chip_far((1 - t) if d == 0 else (t - 1)), half_rows(d, rows)
+    ring.greet((ring.next[0], ring.next[1], ring.partner))
+
+    def source(t, d):
+        return lax.rem(ring.place + (n - t if d == 0 else t), n)
 
     def send(t, d, first):
-        chip, part = hop(t, d)
-        src = normed.at[part] if first else gathered.at[chip, part]
-        return remote(src, gathered.at[chip, part], ag_send.at[d, t - 1], ag_recv.at[d, t - 1], ring.next[d])
-
-    def reduce_copy(t, d, k):
-        return remote(
-            sent.at[d, k], landed.at[d, k, t % 2], rs_send.at[d, k], rs_recv.at[d, k, t % 2], ring.next[d]
-        )
+        place, part = source(t - 1, d), half_rows(d, rows)
+        src = normed.at[part] if first else gathered.at[place, part]
+        return remote(src, gathered.at[place, part], ag_send.at[d, t - 1], ag_recv.at[d, t - 1], ring.next[d])
+
+    def reduce_copy(t, d):
+        return remote(sent.at[d], landed.at[d, t % 2], rs_send.at[d], rs_recv.at[d, t % 2], ring.next[d])
 
     for d in (0, 1):
         send(1, d, True).start()
 
     def clear(i, carry):
+        span = pl.ds(pl.multiple_of(i * FF_TILE, FF_TILE), FF_TILE)
         for k in range(3):
-            totals[k, pl.ds(pl.multiple_of(i * FF_TILE, FF_TILE), FF_TILE), :] = jnp.zeros(
-                (FF_TILE, features), F32
-            )
+            totals[k, span, :] = jnp.zeros((FF_TILE, features), F32)
         return carry
 
     lax.fori_loop(0, tiles, clear, 0)
     for load in loads:
         load.wait()
 
+    def out_copy(t, d):
+        part = half_rows(d, rows)
+        return pltpu.make_async_copy(
+            cast_buf.at[t % 2, part], out_parts.at[source(t, d), part], cast_sem.at[t % 2, d]
+        )
+
     def step(t, carry):
-        @pl.when(t < n)
+        copies = []
+        for d in (0, 1):
+            part = half_rows(d, rows)
+            copies.append(
+                pltpu.make_async_copy(cotangents.at[source(t, d), part], g_buf.at[part], local_sem.at[d])
+            )
+            copies[-1].start()
+
+        @pl.when(t > 0)
         def _():
             for d in (0, 1):
                 send(t, d, False).wait_recv()
@@ -486,31 +506,25 @@
                 for d in (0, 1):
                     send(t + 1, d, False).start()
 
-        copies = []
-        for d in (0, 1):
-            chip, part = hop(t + 1, d)
-            copies.append(pltpu.make_async_copy(cotangents.at[chip, part], g_buf.at[part], local_sem.at[d]))
-            copies[-1].start()
-
-        @pl.when(t < n)
-        def _():
             more = []
             for d in (0, 1):
-                chip, part = hop(t + 1, d)
-                more.append(pltpu.make_async_copy(gathered.at[chip, part], x_buf.at[part], local_sem.at[2 + d]))
+                part = half_rows(d, rows)
+                more.append(
+                    pltpu.make_async_copy(gathered.at[source(t, d), part], x_buf.at[part], local_sem.at[2 + d])
+                )
                 more[-1].start()
             for copy in more:
                 copy.wait()
 
-        @pl.when(t == n)
+        @pl.when(t == 0)
         def _():
             x_buf[...] = normed[...]
 
         for copy in copies:
             copy.wait()
 
-        out_sum[...] = jnp.zeros_like(out_sum)
-        grad_sum[...] = jnp.zeros_like(grad_sum)
+        out_acc[...] = jnp.zeros_like(out_acc)
+        grad_acc[...] = jnp.zeros_like(grad_acc)
 
         def tile(i, carry):
             span = pl.ds(pl.multiple_of(i * FF_TILE, FF_TILE), FF_TILE)
@@ -524,66 +538,111 @@
             hidden = (silu * up).astype(LOW)
             grad_gate = (grad_hidden * up * sigma * (1.0 + gate * (1.0 - sigma))).astype(LOW)
             grad_up = (grad_hidden * silu).astype(LOW)
-            out_sum[...] += dot_nn(hidden, weights[2, span, :])
-            grad_sum[...] += dot_nn(grad_gate, weights[0, span, :])
-            grad_sum[...] += dot_nn(grad_up, weights[1, span, :])
+            out_acc[...] += dot_nn(hidden, weights[2, span, :])
+            grad_acc[...] += dot_nn(grad_gate, weights[0, span, :])
+            grad_acc[...] += dot_nn(grad_up, weights[1, span, :])
             totals[0, span, :] += dot_tn(grad_gate, x)
             totals[1, span, :] += dot_tn(grad_up, x)
             totals[2, span, :] += dot_tn(hidden, g)
             return carry
 
         lax.fori_loop(0, tiles, tile, 0)
-        for d in (0, 1):
-            for k, total in enumerate((out_sum, grad_sum)):
+
+        @pl.when(t >= 2)
+        def _():
+            for d in (0, 1):
+                out_copy(t - 2, d).wait()
+
+        cast_buf[t % 2] = out_acc[...].astype(LOW)
+        for d in (0, 1):
+            out_copy(t, d).start()
+
+        @pl.when(t == 0)
+        def _():
+            grad_sum[...] = grad_acc[...]
+
+        @pl.when(t > 0)
+        def _():
+            for d in (0, 1):
                 part = pl.ds(d * half, half)
 
                 @pl.when(t >= 2)
                 def _():
-                    reduce_copy(t - 1, d, k).wait_recv()
-                    total[part, :] += landed[d, k, (t - 1) % 2].astype(F32)
+                    reduce_copy(t - 1, d).wait_recv()
+                    grad_acc[part, :] += landed[d, (t - 1) % 2].astype(F32)
 
                     @pl.when(t <= n - 2)
                     def _():
                         pl.semaphore_signal(
-                            credit.at[d, k], inc=1, device_id={"dp": ring.back[d]}, device_id_type=MESH
+                            credit.at[d], inc=1, device_id={"dp": ring.back[d]}, device_id_type=MESH
                         )
 
-                    reduce_copy(t - 1, d, k).wait_send()
-
-                @pl.when(t < n)
+                    reduce_copy(t - 1, d).wait_send()
+
+                sent[d] = grad_acc[part, :].astype(LOW)
+
+                @pl.when(t >= 3)
                 def _():
-                    sent[d, k] = total[part, :].astype(LOW)
-
-                    @pl.when(t >= 3)
-                    def _():
-                        pl.semaphore_wait(credit.at[d, k], 1)
-
-                    reduce_copy(t, d, k).start()
-
-        return carry
-
-    lax.fori_loop(1, n + 1, step, 0)
-
-    def cast_copy(i):
-        return pltpu.make_async_copy(
-            cast_buf.at[i % 2],
-            weight_grads.at[i // tiles, pl.ds(pl.multiple_of((i % tiles) * FF_TILE, FF_TILE), FF_TILE)],
-            cast_sem.at[i % 2],
+                    pl.semaphore_wait(credit.at[d], 1)
+
+                reduce_copy(t, d).start()
+
+        return carry
+
+    lax.fori_loop(0, n, step, 0)
+    for t in (n - 2, n - 1):
+        for d in (0, 1):
+            out_copy(t, d).wait()
+
+    own_tiles = 3 * own // FF_TILE
+
+    def tile_of(i, first):
+        return i // (own // FF_TILE), pl.ds(
+            pl.multiple_of(first + (i % (own // FF_TILE)) * FF_TILE, FF_TILE), FF_TILE
         )
 
-    def store(i, carry):
+    def pair_copy(i):
+        return remote(cast_buf.at[i % 2], pair_land.at[i], pair_send.at[i % 2], pair_recv.at[i], ring.partner)
+
+    def give(i, carry):
         @pl.when(i >= 2)
         def _():
-            cast_copy(i - 2).wait()
-
-        span = pl.ds(pl.multiple_of((i % tiles) * FF_TILE, FF_TILE), FF_TILE)
-        cast_buf[i % 2] = totals[i // tiles, span, :].astype(LOW)
-        cast_copy(i).start()
-        return carry
-
-    lax.fori_loop(0, 3 * tiles, store, 0)
-    cast_copy(3 * tiles - 2).wait()
-    cast_copy(3 * tiles - 1).wait()
+            pair_copy(i - 2).wait_send()
+
+        k, span = tile_of(i, own)
+        cast_buf[i % 2] = totals[k, span, :].astype(LOW)
+        pair_copy(i).start()
+        return carry
+
+    lax.fori_loop(0, own_tiles, give, 0)
+    for i in (own_tiles - 2, own_tiles - 1):
+        pair_copy(i).wait_send()
+
+    def total_copy(i):
+        k, span = tile_of(i, 0)
+        return pltpu.make_async_copy(cast_buf.at[i % 2], weight_grads.at[k, span], cast_sem.at[i % 2, 0])
+
+    def take(i, carry):
+        @pl.when(i >= 2)
+        def _():
+            total_copy(i - 2).wait()
+
+        pair_copy(i).wait_recv()
+        k, span = tile_of(i, 0)
+        cast_buf[i % 2] = (totals[k, span, :] + pair_land[i].astype(F32)).astype(LOW)
+        total_copy(i).start()
+        return carry
+
+    lax.fori_loop(0, own_tiles, take, 0)
+
+    for d in (0, 1):
+        part = pl.ds(d * half, half)
+        reduce_copy(n - 1, d).wait_recv()
+        grad_sum[part, :] += landed[d, (n - 1) % 2].astype(F32)
+        reduce_copy(n - 1, d).wait_send()
+
+    for i in (own_tiles - 2, own_tiles - 1):
+        total_copy(i).wait()
 
     def finish(t, carry):
         for d in (0, 1):
@@ -601,40 +660,44 @@
     vmem = pl.BlockSpec(memory_space=pltpu.VMEM)
     hbm = pl.BlockSpec(memory_space=pl.ANY)
     dma = pltpu.SemaphoreType.DMA
+    own_tiles = 3 * own // FF_TILE
     return pl.pallas_call(
         dense_kernel,
         out_shape=(
             jax.ShapeDtypeStruct((rows, features), F32),
-            jax.ShapeDtypeStruct((rows, features), F32),
             jax.ShapeDtypeStruct((n, rows, features), LOW),
-            jax.ShapeDtypeStruct((3, 2 * own, features), LOW),
+            jax.ShapeDtypeStruct((n, rows, features), LOW),
+            jax.ShapeDtypeStruct((3, own, features), LOW),
         ),
         in_specs=[vmem] + [hbm] * 7,
-        out_specs=(vmem, vmem, hbm, hbm),
+        out_specs=(vmem, hbm, hbm, hbm),
         scratch_shapes=[
             pltpu.VMEM((3, 2 * own, features), LOW),
             pltpu.VMEM((3, 2 * own, features), F32),
             pltpu.VMEM((rows, features), LOW),
             pltpu.VMEM((rows, features), LOW),
+            pltpu.VMEM((rows, features), F32),
+            pltpu.VMEM((rows, features), F32),
+            pltpu.VMEM((2, half, features), LOW),
             pltpu.VMEM((2, 2, half, features), LOW),
-            pltpu.VMEM((2, 2, 2, half, features), LOW),
             pltpu.VMEM((2, FF_TILE, features), LOW),
-            dma((2, n)), dma((2, n)), dma((2, 2)), dma((2, 2, 2)),
-            pltpu.SemaphoreType.REGULAR((2, 2)),
-            dma((4,)), dma((6,)), dma((2,)),
+            pltpu.VMEM((own_tiles, FF_TILE, features), LOW),
+            dma((2, n)), dma((2, n)), dma((2,)), dma((2, 2)),
+            pltpu.SemaphoreType.REGULAR((2,)),
+            dma((4,)), dma((6,)), dma((2, 2)), dma((2,)), dma((own_tiles,)),
         ],
         compiler_params=pltpu.CompilerParams(
             collective_id=2, has_side_effects=True, vmem_limit_bytes=62 * MIB
         ),
         cost_estimate=pl.CostEstimate(
-            flops=2 * 9 * n * rows * features * 2 * own, bytes_accessed=800 * MIB, transcendentals=0
+            flops=2 * 9 * n * rows * features * 2 * own, bytes_accessed=500 * MIB, transcendentals=0
         ),
         name="dense",
     )(normed, cotangents, *own_weights, *partner_weights)
 
 
 def normed_back_kernel(
-    grads, weights, partner_weights, out,
+    grads, weights, partner_weights, hidden_in, gain, grad_mixed, out, gain_part,
     partner_grads, sent, landed,
     p_send, p_recv, rs_send, rs_recv, credit,
 ):
@@ -718,8 +781,23 @@
 
     lax.fori_loop(1, n + 1, finish, 0)
 
-
-def normed_back(grads, weights, partner_weights):
+    gain_part[...] = jnp.zeros_like(gain_part)
+
+    def close(i, carry):
+        span = pl.ds(pl.multiple_of(i * 16, 16), 16)
+        value = hidden_in[span, :].astype(F32)
+        grad = out[span, :]
+        scale = lax.rsqrt(jnp.mean(value * value, axis=1, keepdims=True) + EPSILON)
+        scaled = grad * gain[...]
+        shift = jnp.mean(value * scaled, axis=1, keepdims=True)
+        out[span, :] = grad_mixed[span, :] + scale * scaled - value * (scale * scale * scale * shift)
+        gain_part[...] += jnp.sum(grad * value * scale, axis=0, keepdims=True)
+        return carry
+
+    lax.fori_loop(0, rows // 16, close, 0)
+
+
+def normed_back(grads, weights, partner_weights, hidden_in, gain, grad_mixed):
     tokens, r = grads.shape[1:]
     features = weights.shape[2]
     devices = lax.axis_size("dp")
@@ -730,9 +808,12 @@
     dma = pltpu.SemaphoreType.DMA
     return pl.pallas_call(
         normed_back_kernel,
-        out_shape=jax.ShapeDtypeStruct((rows, features), F32),
-        in_specs=[vmem] * 3,
-        out_specs=vmem,
+        out_shape=(
+            jax.ShapeDtypeStruct((rows, features), F32),
+            jax.ShapeDtypeStruct((1, features), F32),
+        ),
+        in_specs=[vmem] * 6,
+        out_specs=(vmem, vmem),
         scratch_shapes=[
             pltpu.VMEM((3, n, rows, r), LOW),
             pltpu.VMEM((2, half, features), LOW),
@@ -747,7 +828,69 @@
             flops=2 * n * rows * features * 6 * r, bytes_accessed=320 * MIB, transcendentals=0
         ),
         name="normed_back",
-    )(grads, weights, partner_weights)
+    )(grads, weights, partner_weights, hidden_in, gain, grad_mixed)
+
+
+def gain_total_kernel(part, out, landed, send_sem, recv_sem, local_sem):
+    columns, packs = lax.axis_size("dp"), lax.axis_size("rep")
+    devices = columns * packs
+    me = lax.axis_index("rep") * columns + lax.axis_index("dp")
+    barrier = pltpu.get_barrier_semaphore()
+
+    def other(k):
+        to = lax.rem(me + k, devices)
+        return {"dp": to % columns, "rep": to // columns}
+
+    def greet(k, carry):
+        pl.semaphore_signal(barrier, inc=1, device_id=other(k), device_id_type=MESH)
+        return carry
+
+    lax.fori_loop(1, devices, greet, 0)
+    pl.semaphore_wait(barrier, devices - 1)
+
+    def copy(k):
+        return pltpu.make_async_remote_copy(
+            src_ref=part,
+            dst_ref=landed.at[me],
+            send_sem=send_sem.at[k],
+            recv_sem=recv_sem.at[k],
+            device_id=other(k),
+            device_id_type=MESH,
+        )
+
+    def begin(k, carry):
+        copy(k).start()
+        return carry
+
+    lax.fori_loop(1, devices, begin, 0)
+    keep = pltpu.make_async_copy(part, landed.at[me], local_sem)
+    keep.start()
+    keep.wait()
+
+    def wait(k, carry):
+        copy(k).wait()
+        return carry
+
+    lax.fori_loop(1, devices, wait, 0)
+    out[...] = lax.fori_loop(1, devices, lambda i, total: total + landed[i], landed[0])
+
+
+def gain_total(part):
+    devices = lax.axis_size("dp") * lax.axis_size("rep")
+    vmem = pl.BlockSpec(memory_space=pltpu.VMEM)
+    dma = pltpu.SemaphoreType.DMA
+    return pl.pallas_call(
+        gain_total_kernel,
+        out_shape=jax.ShapeDtypeStruct(part.shape, F32),
+        in_specs=[vmem],
+        out_specs=vmem,
+        scratch_shapes=[
+            pltpu.VMEM((devices,) + part.shape, F32),
+            dma((devices,)), dma((devices,)), dma,
+        ],
+        compiler_params=pltpu.CompilerParams(collective_id=4, has_side_effects=True),
+        name="gain_total",
+    )(part)
 
 
 def rms(values, norm_gain):
@@ -834,11 +977,13 @@
     )
     qkv, normed_all = gather_project(normed, stacked, rows_of(cos_t), rows_of(sin_t))
 
-    full_output = lax.all_gather(output_weight, "dp", axis=0, tiled=True)
-    groups = [list(range(c, devices, 2)) for c in (0, 1)]
+    order = ring_order(chips)
+    walk = [2 * chip + k for chip in order for k in (0, 1)]
+    lanes = [[2 * chip + k for chip in order] for k in (0, 1)]
+    full_output = lax.all_gather(output_weight, "dp", axis=0, tiled=True, axis_index_groups=[walk])
     grad_low = cotangent[0]
     cotangents = lax.all_gather(
-        grad_low, "dp", axis=0, tiled=True, axis_index_groups=groups
+        grad_low, "dp", axis=0, tiled=True, axis_index_groups=lanes
     ).reshape(chips, tok_dev, -1)
     gate_other, up_other, down_other = (
         from_partner(gate_weight),
@@ -849,55 +994,71 @@
     qkv_other = from_partner(qkv_weight)
 
     attended, log_total = attend(first, tail, qkv)
-    attended_here = lax.all_to_all(attended, "dp", split_axis=0, concat_axis=1, tiled=True)
+    attended_blocks = lax.all_to_all(
+        attended.reshape(devices, tok_dev, r), "dp", split_axis=0, concat_axis=0, tiled=True
+    )
+    attended_here = jnp.concatenate([attended_blocks[i] for i in walk], 1)
     mixed = hidden_in + dot_nn(attended_here, full_output)
     normed_two = rms(mixed, dense_gain).astype(LOW)
 
-    out_sum, grad_normed_two, _, dense_grads = dense(
+    grad_normed_two, out_parts, _, dense_low = dense(
         normed_two,
         cotangents,
         (gate_weight, up_weight, down_weight),
         (gate_other, up_other, down_other),
     )
-    layer_out = mixed + out_sum
-    own_rows = gate_weight.shape[0]
-    dense_low = (
-        dense_grads[:, :own_rows].astype(F32)
-        + from_partner(dense_grads[:, own_rows:]).astype(F32)
-    ).astype(LOW)
     dense_total = pack_sum(dense_low)
 
     grad_mixed_norm, dense_gain_part = rms_back(mixed, dense_gain, grad_normed_two)
     grad_mixed = grad_low.astype(F32) + grad_mixed_norm
     grad_mixed_low = grad_mixed.astype(LOW)
     grad_attended = dot_nt(grad_mixed_low, full_output).astype(LOW)
-    grad_heads = lax.all_to_all(grad_attended, "dp", split_axis=1, concat_axis=0, tiled=True)
+    grad_blocks = jnp.stack(
+        [grad_attended[:, walk.index(i) * r : (walk.index(i) + 1) * r] for i in range(devices)]
+    )
+    grad_heads = lax.all_to_all(
+        grad_blocks, "dp", split_axis=0, concat_axis=0, tiled=True
+    ).reshape(pack_tok, r)
     output_grad = lax.psum_scatter(
-        dot_tn(attended_here, grad_mixed_low).astype(LOW), "dp", scatter_dimension=0, tiled=True
+        dot_tn(attended_here, grad_mixed_low).astype(LOW),
+        "dp",
+        scatter_dimension=0,
+        tiled=True,
+        axis_index_groups=[walk],
     )
     output_total = pack_sum(output_grad)
+    out_sum = lax.psum_scatter(
+        out_parts.reshape(chips * tok_dev, -1),
+        "dp",
+        scatter_dimension=0,
+        tiled=True,
+        axis_index_groups=lanes,
+    )
+    layer_out = mixed + out_sum.astype(F32)
 
     grads = attend_back(first, tail, qkv, grad_heads, attended, log_total, cos_t, sin_t)
-    swapped = from_partner(
-        lax.dynamic_index_in_dim(
-            grads.reshape(3, chips, 2, tok_dev, r), 1 - core, axis=2, keepdims=False
+    by_core = grads.reshape(3, chips, 2, tok_dev, r)
+    swapped = from_partner(lax.dynamic_index_in_dim(by_core, 1 - core, axis=2, keepdims=False))
+    mine = lax.dynamic_index_in_dim(by_core, core, axis=2, keepdims=False)
+    normed_rows = normed_all.reshape(chips * tok_dev, -1)
+
+    def weight_part(value):
+        return lax.dot_general(
+            value.reshape(3, chips * tok_dev, r),
+            normed_rows,
+            (((1,), (0,)), ((), ())),
+            preferred_element_type=F32,
         )
-    )
-    mine = lax.dynamic_index_in_dim(
-        grads.reshape(3, chips, 2, tok_dev, r), core, axis=2, keepdims=False
-    )
-    both = jnp.stack([mine, swapped]).reshape(2, 3, chips * tok_dev, r)
-    normed_rows = normed_all.reshape(chips * tok_dev, -1)
-    qkv_parts = lax.dot_general(
-        both, normed_rows, (((2,), (0,)), ((), ())), preferred_element_type=F32
-    ).astype(LOW)
-    qkv_low = (qkv_parts[0].astype(F32) + from_partner(qkv_parts[1]).astype(F32)).astype(LOW)
+
+    qkv_there = from_partner(weight_part(swapped).astype(LOW))
+    qkv_low = (weight_part(mine) + qkv_there.astype(F32)).astype(LOW)
     qkv_total = pack_sum(qkv_low)
 
-    grad_normed = normed_back(grads, qkv_weight, qkv_other)
-    grad_in_norm, attention_gain_part = rms_back(hidden_in, attention_gain, grad_normed)
-    input_grad = grad_mixed + grad_in_norm
-    gain_totals = lax.psum((attention_gain_part, dense_gain_part), ("dp", "rep"))
+    input_grad, attention_gain_part = normed_back(
+        grads, qkv_weight, qkv_other, tokens[0], attention_gain[None], grad_mixed
+    )
+    gain_parts = jnp.stack([attention_gain_part[0], dense_gain_part])
+    gain_totals = gain_total(gain_parts.reshape(2, -1, 128)).reshape(2, -1)
     return (
         layer_out[None].astype(LOW),
         input_grad[None],

time: 904 us -> 886 us (0.980)
  waiting for transfers between devices: 44.9 us -> 192 us
  blocking collectives: 83 us -> 0 us
  Pallas kernels: 626 us -> 548 us
  other arithmetic: 46.9 us -> 35 us
    reduce_scatter x0 -> x1, waiting for transfers between devices: none -> 84.6 us  [body(): lax.psum_scatter(out_parts.reshape(chips * tok_dev, -1), 'dp', scatter_di...]
    psum x1 -> x0, blocking collectives: 83 us -> none  [body(): lax.psum((attention_gain_part, dense_gain_part), ('dp', 'rep'))]
    pallas_call x1, Pallas kernels: 258 us -> 179 us  [dense(): pl.pallas_call(dense_kernel, out_shape=(jax.ShapeDtypeStruct((rows, featu...]
    ppermute x3, waiting for transfers between devices: 0.99 us -> 57.1 us  [pack_sum(): other = lax.ppermute(low, 'rep', [(0, 1), (1, 0)])]
    unnamed x64 -> x89, local copies, waits for them, and re-layouts: 10.7 us -> 24 us
    convert_element_type x2 -> x1, other arithmetic: 12.8 us -> 3.13 us  [body(): qkv_low = (weight_part(mine) + qkv_there.astype(F32)).astype(LOW)]
    pallas_call x1, Pallas kernels: 181 us -> 172 us  [gather_project(): pl.pallas_call(gather_project_kernel, out_shape=(jax.ShapeDtypeStruct((3,...]
    pallas_call x1 -> x2, Pallas kernels: 106 us -> 115 us  [the longest x1 98.4 us: normed_back(): pl.pallas_call(normed_back_kernel, out_shape=(jax.ShapeDtypeStruct((rows,...]
  transfers between devices with their start and end apart: 15 -> 15, of which waited for: 4 -> 6; matrix products, arithmetic and copies ran while one was open for 10% -> 10% of each run, Pallas kernels for 41% -> 42%
where the time goes in v2:
time: 886 us; the launch traced here: 885 us
  Pallas kernels  548 us (62%)
  waiting for transfers between devices  192 us (22%)
  local copies, waits for them, and re-layouts  46.6 us (5%)
  other arithmetic  35 us (4%)
  matrix products  33 us (4%)
  starting transfers between devices  15.2 us (2%)
  between operations  14.4 us (2%)
    pallas_call x1, Pallas kernels, dense(): pl.pallas_call(dense_kernel, out_shape=(jax.ShapeDtypeStruct((rows, featu...  179 us
    pallas_call x1, Pallas kernels, gather_project(): pl.pallas_call(gather_project_kernel, out_shape=(jax.ShapeDtypeStruct((3,...  172 us
    pallas_call x1, Pallas kernels, normed_back(): pl.pallas_call(normed_back_kernel, out_shape=(jax.ShapeDtypeStruct((rows,...  98.4 us
    reduce_scatter x1, waiting for transfers between devices, body(): lax.psum_scatter(out_parts.reshape(chips * tok_dev, -1), 'dp', scatter_di...  84.6 us
    ppermute x3, waiting for transfers between devices, pack_sum(): other = lax.ppermute(low, 'rep', [(0, 1), (1, 0)])  57.1 us
    pallas_call x1, Pallas kernels, attend_back(): pl.pallas_call(attend_back_kernel, out_shape=jax.ShapeDtypeStruct((3, tok...  43.8 us
    pallas_call x1, Pallas kernels, attend(): pl.pallas_call(attend_kernel, out_shape=(jax.ShapeDtypeStruct((tokens, r)...  38.9 us
    all_to_all x1, waiting for transfers between devices, body(): lax.all_to_all(grad_blocks, 'dp', split_axis=0, concat_axis=0, tiled=True)  25.7 us
  transfers between devices with their start and end apart: 15, of which 6 were waited for; matrix products, arithmetic and copies ran while one was open for 10% of the time, Pallas kernels for 42%

profile of v2, /device:TPU:0, one launch (start us, length us, event | category | flops | bytes accessed | tf_op | source)
XLA Modules:
  0.0 884.6 jit_solution(12947136718993261596)
XLA Ops:
  17.4 171.9 %gather_project.1 = (bf16[3,4096,128]{2,1,0:T(8,128)(2,1)S(1)}, bf16[8,256,2048]{2,1,0:T(8,128)(2,1)}) custom-call(bf16[256,2048]{1,0:T(8,128)(2,1)S(1)} %fusion.6.normed, bf16[640,2048]{1,0:T(8,128)(2,1)S(1)} %constant_dynamic-update-slice_fusion.weights, f32[8,256,128]{2,1,0:T(8,128)S(1)} %copy.33.cosine, f32[8,256,128]{2,1,0:T(8,128)S(1)} %copy.34.sine), custom_call_target="tpu_custom_call" | custom-call | flops 10737418240 | bytes 335544320 | tf_op jit(solution)/shard_map/gather_project/pallas_call | solution.py:225
  189.4 38.9 %attend.1 = (bf16[4096,128]{1,0:T(8,128)(2,1)}, f32[32,256]{1,0:T(8,128)S(1)}) custom-call(s32[32]{0:T(128)S(1)} %convert_reduce_fusion.first_ref, s32[32]{0:T(128)S(1)} %add_select_fusion.tail_ref, bf16[3,4096,128]{2,1,0:T(8,128)(2,1)S(1)} %get-tuple-element.20.qkv), custom_call_target="tpu_custom_call" | custom-call | flops 17179869184 | bytes 125829120 | tf_op jit(solution)/shard_map/attend/pallas_call | solution.py:328
  228.3 3.7 all-to-all-start
  233.3 21.7 %all-to-all-done = bf16[16,256,128]{2,1,0:T(8,128)(2,1)S(1)} async-done(((bf16[16,256,128]{2,1,0:T(8,128)(2,1)}), bf16[16,256,128]{2,1,0:T(8,128)(2,1)S(1)}, u32[]{:S(2)}, u32[]{:S(2)}) %all-to-all-start) | async-done | bytes 1048608 | tf_op jit(solution)/shard_map/all_to_all | solution.py:997
  255.5 7.4 multiply_reduce_fusion.2
  262.9 2.8 multiply_convert_fusion.normed
  265.8 178.6 %dense.1 = (f32[256,2048]{1,0:T(8,128)}, bf16[8,256,2048]{2,1,0:T(8,128)(2,1)}, bf16[8,256,2048]{2,1,0:T(8,128)(2,1)}, bf16[3,512,2048]{2,1,0:T(8,128)(2,1)}) custom-call(bf16[256,2048]{1,0:T(8,128)(2,1)} %multiply_convert_fusion.normed, bf16[8,256,2048]{2,1,0:T(8,128)(2,1)} %bitcast.225, bf16[512,2048]{1,0:T(8,128)(2,1)} %gate_w.1, bf16[512,2048]{1,0:T(8,128)(2,1)} %up_w.1, ...), custom_call_target="tpu_custom_call" | custom-call | flops 77309411328 | bytes 524288000 | tf_op jit(solution)/shard_map/dense/pallas_call | solution.py:664
  445.9 2.2 multiply_reduce_fusion
  448.1 84.6 %reduce-scatter.3.cloned.1.call-done = bf16[256,2048]{1,0:T(8,128)(2,1)} async-done(((bf16[2048,2048]{1,0:T(8,128)(2,1)}), bf16[256,2048]{1,0:T(8,128)(2,1)}) %reduce-scatter.3.cloned.1.call-update) | async-done | bytes 1048592 | tf_op jit(solution)/shard_map/reduce_scatter | solution.py:1030
  532.7 4.2 fusion.7
  537.0 5.7 convolution_convert_fusion
  542.6 5.7 convolution_convert_fusion.1
  558.8 4.7 all-to-all-start.1
  563.6 2.8 multiply_sine_fusion
  567.8 25.7 %all-to-all-done.1 = bf16[16,256,128]{2,1,0:T(8,128)(2,1)S(1)} async-done(((bf16[16,256,128]{2,1,0:T(8,128)(2,1)}), bf16[16,256,128]{2,1,0:T(8,128)(2,1)S(1)}, u32[]{:S(2)}, u32[]{:S(2)}) %all-to-all-start.1) | async-done | bytes 1048608 | tf_op jit(solution)/shard_map/all_to_all | solution.py:1019
  595.7 1.9 copy-done.13
  597.6 43.8 %attend_back.1.grads = bf16[3,4096,128]{2,1,0:T(8,128)(2,1)S(1)} custom-call(s32[32]{0:T(128)S(1)} %convert_reduce_fusion.first_ref, s32[32]{0:T(128)S(1)} %add_select_fusion.tail_ref, bf16[3,4096,128]{2,1,0:T(8,128)(2,1)S(1)} %copy-done.13, bf16[4096,128]{1,0:T(8,128)(2,1)S(1)} %bitcast.208, bf16[4096,128]{1,0:T(8,128)(2,1)} %get-tuple-element.21.attended, ...), custom_call_target="tpu_custom_call" | custom-call | flops 42949672960 | bytes 251658240 | tf_op jit(solution)/shard_map/attend_back/pallas_call | solution.py:422
  641.4 2.0 constant_dynamic-slice_fusion.1
  644.1 2.7 copy.36
  648.6 1.8 collective-permute-done.4
  650.4 7.9 bitcast_convert_fusion
  658.4 46.1 %collective-permute-done.8 = bf16[3,512,2048]{2,1,0:T(8,128)(2,1)} collective-permute-done((bf16[3,512,2048]{2,1,0:T(8,128)(2,1)}, bf16[3,512,2048]{2,1,0:T(8,128)(2,1)}, u32[]{:S(2)}, u32[]{:S(2)}) %collective-permute-start.8) | collective-permute-done | bytes 6291488 | tf_op jit(solution)/shard_map/ppermute | solution.py:920
  704.5 12.3 %convert_add_fusion = f32[3,512,2048]{2,1,0:T(8,128)} fusion(bf16[3,512,2048]{2,1,0:T(8,128)(2,1)} %collective-permute-done.8, bf16[3,512,2048]{2,1,0:T(8,128)(2,1)} %get-tuple-element.28), kind=kLoop, calls=%fused_computation | loop fusion | flops 9437184 | bytes 25165824 | tf_op jit(solution)/shard_map/add | solution.py:921
  716.7 6.3 fusion.12
  723.1 3.1 add_convert_fusion
  727.7 9.8 %slice_bitcast_fusion = (f32[512,2048]{1,0:T(8,128)}, f32[512,2048]{1,0:T(8,128)}, f32[512,2048]{1,0:T(8,128)}) fusion(f32[3,512,2048]{2,1,0:T(8,128)} %convert_add_fusion), kind=kLoop, calls=%fused_computation.4 | loop fusion | bytes 25165824 | tf_op jit(solution)/shard_map/squeeze | solution.py:1073
  737.5 1.9 copy-done.3
  740.8 98.4 %normed_back.1 = (f32[256,2048]{1,0:T(8,128)S(1)}, f32[1,2048]{1,0:T(1,128)S(1)}) custom-call(bf16[3,4096,128]{2,1,0:T(8,128)(2,1)S(1)} %copy-done.3, bf16[3,128,2048]{2,1,0:T(8,128)(2,1)S(1)} %copy-done.7, bf16[3,128,2048]{2,1,0:T(8,128)(2,1)} %collective-permute-done.3.partner_weights, bf16[256,2048]{1,0:T(8,128)(2,1)S(1)} %bitcast.205, ...), custom_call_target="tpu_custom_call" | custom-call | flops 6442450944 | bytes 335544320 | tf_op jit(solution)/shard_map/normed_back/pallas_call | solution.py:809
  841.1 16.4 %gain_total.1 = f32[2,16,128]{2,1,0:T(8,128)} custom-call(f32[2,16,128]{2,1,0:T(8,128)} %pad_maximum_fusion.3.part), custom_call_target="tpu_custom_call" | custom-call | tf_op jit(solution)/shard_map/gain_total/pallas_call | solution.py:882
  858.8 2.5 convert_add_fusion.1
  862.9 1.7 slice_bitcast_fusion.3
  864.6 11.0 %collective-permute-done.7 = bf16[128,2048]{1,0:T(8,128)(2,1)S(1)} collective-permute-done((bf16[128,2048]{1,0:T(8,128)(2,1)}, bf16[128,2048]{1,0:T(8,128)(2,1)S(1)}, u32[]{:S(2)}, u32[]{:S(2)}) %collective-permute-start.7) | collective-permute-done | bytes 524320 | tf_op jit(solution)/shard_map/ppermute | solution.py:920
  (150 shorter events, 39.9 us)
Async XLA Ops:
  7.2 248.3 %all-gather.4.cloned.1.call-start = ((), (), s32[]{:S(2)}) async-start(), calls=%async_computation.4 | async-start | bytes 8912896 | tf_op jit(solution)/shard_map/all_gather | solution.py:983
  7.9 257.8 %all-gather.6.cloned.1.call-start = ((), (), s32[]{:S(2)}) async-start(), calls=%async_computation.7 | async-start | bytes 9437184 | tf_op jit(solution)/shard_map/all_gather | solution.py:985
  11.5 2.7 copy-start.25
  11.5 2.7 copy-start.26
  11.5 2.8 copy-start
  189.4 39.0 %copy-start.12 = (bf16[3,4096,128]{2,1,0:T(8,128)(2,1)}, bf16[3,4096,128]{2,1,0:T(8,128)(2,1)S(1)}, u32[]{:S(2)}) copy-start(bf16[3,4096,128]{2,1,0:T(8,128)(2,1)S(1)} %get-tuple-element.20.qkv) | copy-start | bytes 9437188
  228.3 26.7 %all-to-all-start = ((bf16[16,256,128]{2,1,0:T(8,128)(2,1)}), bf16[16,256,128]{2,1,0:T(8,128)(2,1)S(1)}, u32[]{:S(2)}, u32[]{:S(2)}) async-start(bf16[16,256,128]{2,1,0:T(8,128)(2,1)} %bitcast.14), calls=%async_computation | async-start | bytes 2097152 | tf_op jit(solution)/shard_map/all_to_all | solution.py:997
  232.1 300.7 %reduce-scatter.3.cloned.1.call-start = ((), (), s32[]{:S(2)}) async-start(), calls=%async_computation.5 | async-start | bytes 9437184 | tf_op jit(solution)/shard_map/reduce_scatter | solution.py:1030
  232.3 33.4 %collective-permute-start = (bf16[512,2048]{1,0:T(8,128)(2,1)}, bf16[512,2048]{1,0:T(8,128)(2,1)}, u32[]{:S(2)}, u32[]{:S(2)}) collective-permute-start(bf16[512,2048]{1,0:T(8,128)(2,1)} %gate_w.1), channel_id=1, source_target_pairs={{0,2},{2,0},{4,6},{6,4},{8,10},{10,8},{12,14},{14,12},{16,18},{18,... | collective-permute-start | bytes 6291464 | tf_op jit(solution)/shard_map/ppermute | solution.py:914
  232.8 33.0 %collective-permute-start.1 = (bf16[512,2048]{1,0:T(8,128)(2,1)}, bf16[512,2048]{1,0:T(8,128)(2,1)}, u32[]{:S(2)}, u32[]{:S(2)}) collective-permute-start(bf16[512,2048]{1,0:T(8,128)(2,1)} %up_w.1), channel_id=1, source_target_pairs={{0,2},{2,0},{4,6},{6,4},{8,10},{10,8},{12,14},{14,12},{16,18},{18,... | collective-permute-start | bytes 6291464 | tf_op jit(solution)/shard_map/ppermute | solution.py:914
  232.9 32.9 %collective-permute-start.2 = (bf16[512,2048]{1,0:T(8,128)(2,1)}, bf16[512,2048]{1,0:T(8,128)(2,1)}, u32[]{:S(2)}, u32[]{:S(2)}) collective-permute-start(bf16[512,2048]{1,0:T(8,128)(2,1)} %down_w.1), channel_id=1, source_target_pairs={{0,2},{2,0},{4,6},{6,4},{8,10},{10,8},{12,14},{14,12},{16,18},{18,... | collective-permute-start | bytes 6291464 | tf_op jit(solution)/shard_map/ppermute | solution.py:914
  255.4 7.5 copy-start.20
  255.4 7.5 copy-start.24
  444.4 417.0 %reduce-scatter.5.cloned.1.call-start = ((), (), s32[]{:S(2)}) async-start(), calls=%async_computation.6 | async-start | bytes 8912896 | tf_op jit(solution)/shard_map/reduce_scatter | solution.py:1022
  445.9 86.8 %copy-start.19 = (bf16[1,256,2048]{2,1,0:T(8,128)(2,1)S(1)}, bf16[1,256,2048]{2,1,0:T(8,128)(2,1)}, u32[]{:S(2)}) copy-start(bf16[1,256,2048]{2,1,0:T(8,128)(2,1)} %param.25) | copy-start | bytes 3145732
  532.7 4.2 copy-start.21
  558.8 34.8 %all-to-all-start.1 = ((bf16[16,256,128]{2,1,0:T(8,128)(2,1)}), bf16[16,256,128]{2,1,0:T(8,128)(2,1)S(1)}, u32[]{:S(2)}, u32[]{:S(2)}) async-start(bf16[16,256,128]{2,1,0:T(8,128)(2,1)} %constant_dynamic-update-slice_fusion.21), calls=%async_computation.2 | async-start | bytes 2097152 | tf_op jit(solution)/shard_map/all_to_all | solution.py:1019
  566.3 138.1 %collective-permute-start.8 = (bf16[3,512,2048]{2,1,0:T(8,128)(2,1)}, bf16[3,512,2048]{2,1,0:T(8,128)(2,1)}, u32[]{:S(2)}, u32[]{:S(2)}) collective-permute-start(bf16[3,512,2048]{2,1,0:T(8,128)(2,1)} %get-tuple-element.28), channel_id=1, source_target_pairs={{0,1},{1,0},{2,3},{3,2},{4,5},{5,4},{6,7},{7,6},{8,9},{9,8},{10,11... | collective-permute-start | bytes 18874376 | tf_op jit(solution)/shard_map/ppermute | solution.py:920
  595.7 1.9 copy-start.13
  641.4 2.7 copy-start.2
  644.1 2.7 copy-start.16
  644.1 2.7 copy-start.18
  646.8 3.6 collective-permute-start.4
  648.0 10.3 %copy-start.6 = (bf16[3,128,2048]{2,1,0:T(8,128)(2,1)}, bf16[3,128,2048]{2,1,0:T(8,128)(2,1)S(1)}, u32[]{:S(2)}) copy-start(bf16[3,128,2048]{2,1,0:T(8,128)(2,1)S(1)} %pad_maximum_fusion.weights) | copy-start | bytes 4718596
  648.0 89.5 %collective-permute-start.3 = (bf16[3,128,2048]{2,1,0:T(8,128)(2,1)S(1)}, bf16[3,128,2048]{2,1,0:T(8,128)(2,1)}, u32[]{:S(2)}, u32[]{:S(2)}) collective-permute-start(bf16[3,128,2048]{2,1,0:T(8,128)(2,1)S(1)} %pad_maximum_fusion.weights), channel_id=1, source_target_pairs={{0,2},{2,0},{4,6},{6,4},{8,10},{10,8},{12,14},{14,12},{16,18},{18,... | collective-permute-start | bytes 4718600 | tf_op jit(solution)/shard_map/ppermute | solution.py:914
  658.2 64.8 %collective-permute-start.5 = (bf16[3,128,2048]{2,1,0:T(8,128)(2,1)}, bf16[3,128,2048]{2,1,0:T(8,128)(2,1)}, u32[]{:S(2)}, u32[]{:S(2)}) collective-permute-start(bf16[3,128,2048]{2,1,0:T(8,128)(2,1)} %bitcast_convert_fusion), channel_id=1, source_target_pairs={{0,2},{2,0},{4,6},{6,4},{8,10},{10,8},{12,14},{14,12},{16,18},{18,... | collective-permute-start | bytes 4718600 | tf_op jit(solution)/shard_map/ppermute | solution.py:914
  726.2 11.3 %copy-start.1 = (bf16[1,256,2048]{2,1,0:T(8,128)(2,1)S(1)}, bf16[1,256,2048]{2,1,0:T(8,128)(2,1)}, u32[]{:S(2)}) copy-start(bf16[1,256,2048]{2,1,0:T(8,128)(2,1)} %param.13) | copy-start | bytes 3145732
  726.2 11.3 %copy-start.11 = (f32[2048]{0:T(1024)S(1)}, f32[2048]{0:T(1024)}, u32[]{:S(2)}) copy-start(f32[2048]{0:T(1024)} %param.14) | copy-start | bytes 24580
  726.2 132.6 %collective-permute-start.6 = (bf16[3,128,2048]{2,1,0:T(8,128)(2,1)}, bf16[3,128,2048]{2,1,0:T(8,128)(2,1)}, u32[]{:S(2)}, u32[]{:S(2)}) collective-permute-start(bf16[3,128,2048]{2,1,0:T(8,128)(2,1)} %add_convert_fusion), channel_id=1, source_target_pairs={{0,1},{1,0},{2,3},{3,2},{4,5},{5,4},{6,7},{7,6},{8,9},{9,8},{10,11... | collective-permute-start | bytes 4718600 | tf_op jit(solution)/shard_map/ppermute | solution.py:920
  861.3 14.3 %copy-start.23 = (bf16[128,2048]{1,0:T(8,128)(2,1)S(1)}, bf16[128,2048]{1,0:T(8,128)(2,1)}, u32[]{:S(2)}) copy-start(bf16[128,2048]{1,0:T(8,128)(2,1)} %reduce-scatter.5.cloned.1.call-done) | copy-start | bytes 1572868
  861.3 14.3 %collective-permute-start.7 = (bf16[128,2048]{1,0:T(8,128)(2,1)}, bf16[128,2048]{1,0:T(8,128)(2,1)S(1)}, u32[]{:S(2)}, u32[]{:S(2)}) collective-permute-start(bf16[128,2048]{1,0:T(8,128)(2,1)} %reduce-scatter.5.cloned.1.call-done), channel_id=1, source_target_pairs={{0,1},{1,0},{2,3},{3,2},{4,5},{5,4},{6,7},{7,6},{8,9},{9,8},{10,11... | collective-permute-start | bytes 1572872 | tf_op jit(solution)/shard_map/ppermute | solution.py:920
  864.6 12.1 %copy-start.5 = (f32[256,2048]{1,0:T(8,128)S(1)}, f32[256,2048]{1,0:T(8,128)}, u32[]{:S(2)}) copy-start(f32[256,2048]{1,0:T(8,128)} %copy-done.4) | copy-start | bytes 6291460
  (10 other events, 13.4 us)
Sparse Core Ops, SparseCore 0:
  9.6 84.9 all-gather.3
  96.1 123.9 all-gather.5
  444.5 88.1 reduce-scatter.2
  542.8 75.6 reduce-scatter.4

commit v3 on v2

--- a/solution.py
+++ b/solution.py
@@ -439,7 +439,7 @@
 
 def dense_kernel(
     normed, cotangents, gate_w, up_w, down_w, gate_p, up_p, down_p,
-    grad_sum, out_parts, gathered, weight_grads,
+    grad_sum, out_parts, gathered, gate_grad, up_grad, down_grad,
     weights, totals, x_buf, g_buf, out_acc, grad_acc, sent, landed, cast_buf, pair_land,
     ag_send, ag_recv, rs_send, rs_recv, credit, local_sem, w_sem, cast_sem, pair_send, pair_recv,
 ):
@@ -619,21 +619,17 @@
         pair_copy(i).wait_send()
 
     def total_copy(i):
-        k, span = tile_of(i, 0)
-        return pltpu.make_async_copy(cast_buf.at[i % 2], weight_grads.at[k, span], cast_sem.at[i % 2, 0])
-
-    def take(i, carry):
-        @pl.when(i >= 2)
-        def _():
+        target = (gate_grad, up_grad, down_grad)[i // (own // FF_TILE)]
+        span = pl.ds((i % (own // FF_TILE)) * FF_TILE, FF_TILE)
+        return pltpu.make_async_copy(cast_buf.at[i % 2], target.at[span], cast_sem.at[i % 2, 0])
+
+    for i in range(own_tiles):
+        if i >= 2:
             total_copy(i - 2).wait()
-
         pair_copy(i).wait_recv()
         k, span = tile_of(i, 0)
         cast_buf[i % 2] = (totals[k, span, :] + pair_land[i].astype(F32)).astype(LOW)
         total_copy(i).start()
-        return carry
-
-    lax.fori_loop(0, own_tiles, take, 0)
 
     for d in (0, 1):
         part = pl.ds(d * half, half)
@@ -667,10 +663,12 @@
             jax.ShapeDtypeStruct((rows, features), F32),
             jax.ShapeDtypeStruct((n, rows, features), LOW),
             jax.ShapeDtypeStruct((n, rows, features), LOW),
-            jax.ShapeDtypeStruct((3, own, features), LOW),
+            jax.ShapeDtypeStruct((own, features), LOW),
+            jax.ShapeDtypeStruct((own, features), LOW),
+            jax.ShapeDtypeStruct((own, features), LOW),
         ),
         in_specs=[vmem] + [hbm] * 7,
-        out_specs=(vmem, hbm, hbm, hbm),
+        out_specs=(vmem,) + (hbm,) * 5,
         scratch_shapes=[
             pltpu.VMEM((3, 2 * own, features), LOW),
             pltpu.VMEM((3, 2 * own, features), F32),
@@ -914,12 +912,20 @@
     return lax.ppermute(value, "dp", [(i, i ^ 1) for i in range(devices)])
 
 
-def pack_sum(value):
-    low = value.astype(LOW)
+def pack_swap(low):
     if lax.axis_size("rep") == 2:
-        other = lax.ppermute(low, "rep", [(0, 1), (1, 0)])
+        return lax.ppermute(low, "rep", [(0, 1), (1, 0)])
+    return lax.psum(low, "rep")
+
+
+def pack_add(low, other):
+    if lax.axis_size("rep") == 2:
         return low.astype(F32) + other.astype(F32)
-    return lax.psum(low, "rep").astype(F32)
+    return other.astype(F32)
+
+
+def together(*values):
+    return lax.optimization_barrier(values)
 
 
 def body(
@@ -1001,13 +1007,20 @@
     mixed = hidden_in + dot_nn(attended_here, full_output)
     normed_two = rms(mixed, dense_gain).astype(LOW)
 
-    grad_normed_two, out_parts, _, dense_low = dense(
+    grad_normed_two, out_parts, _, gate_low, up_low, down_low = dense(
         normed_two,
         cotangents,
         (gate_weight, up_weight, down_weight),
         (gate_other, up_other, down_other),
     )
-    dense_total = pack_sum(dense_low)
+    out_sum = lax.psum_scatter(
+        out_parts.reshape(chips * tok_dev, -1),
+        "dp",
+        scatter_dimension=0,
+        tiled=True,
+        axis_index_groups=lanes,
+    )
+    gate_there = pack_swap(gate_low)
 
     grad_mixed_norm, dense_gain_part = rms_back(mixed, dense_gain, grad_normed_two)
     grad_mixed = grad_low.astype(F32) + grad_mixed_norm
@@ -1019,23 +1032,10 @@
     grad_heads = lax.all_to_all(
         grad_blocks, "dp", split_axis=0, concat_axis=0, tiled=True
     ).reshape(pack_tok, r)
-    output_grad = lax.psum_scatter(
-        dot_tn(attended_here, grad_mixed_low).astype(LOW),
-        "dp",
-        scatter_dimension=0,
-        tiled=True,
-        axis_index_groups=[walk],
-    )
-    output_total = pack_sum(output_grad)
-    out_sum = lax.psum_scatter(
-        out_parts.reshape(chips * tok_dev, -1),
-        "dp",
-        scatter_dimension=0,
-        tiled=True,
-        axis_index_groups=lanes,
-    )
-    layer_out = mixed + out_sum.astype(F32)
-
+
+    grad_heads, gate_there = together(grad_heads, gate_there)
+    up_low, _ = together(up_low, gate_there)
+    up_there = pack_swap(up_low)
     grads = attend_back(first, tail, qkv, grad_heads, attended, log_total, cos_t, sin_t)
     by_core = grads.reshape(3, chips, 2, tok_dev, r)
     swapped = from_partner(lax.dynamic_index_in_dim(by_core, 1 - core, axis=2, keepdims=False))
@@ -1052,25 +1052,37 @@
 
     qkv_there = from_partner(weight_part(swapped).astype(LOW))
     qkv_low = (weight_part(mine) + qkv_there.astype(F32)).astype(LOW)
-    qkv_total = pack_sum(qkv_low)
-
+
+    output_part = dot_tn(attended_here, grad_mixed_low).astype(LOW)
+    grads, output_part, out_sum, up_there = together(grads, output_part, out_sum, up_there)
+    output_grad = lax.psum_scatter(
+        output_part, "dp", scatter_dimension=0, tiled=True, axis_index_groups=[walk]
+    )
+    down_low, _ = together(down_low, up_there)
+    down_there = pack_swap(down_low)
+    qkv_other_sum = pack_swap(qkv_low)
     input_grad, attention_gain_part = normed_back(
         grads, qkv_weight, qkv_other, tokens[0], attention_gain[None], grad_mixed
     )
+    input_grad, out_sum, gate_there, up_there, down_there, qkv_other_sum, output_grad = together(
+        input_grad, out_sum, gate_there, up_there, down_there, qkv_other_sum, output_grad
+    )
+    output_there = pack_swap(output_grad)
     gain_parts = jnp.stack([attention_gain_part[0], dense_gain_part])
     gain_totals = gain_total(gain_parts.reshape(2, -1, 128)).reshape(2, -1)
+    layer_out = mixed + out_sum.astype(F32)
     return (
         layer_out[None].astype(LOW),
         input_grad[None],
         gain_totals[0],
-        qkv_total[0],
-        qkv_total[1],
-        qkv_total[2],
-        output_total,
+        pack_add(qkv_low[0], qkv_other_sum[0]),
+        pack_add(qkv_low[1], qkv_other_sum[1]),
+        pack_add(qkv_low[2], qkv_other_sum[2]),
+        pack_add(output_grad, output_there),
         gain_totals[1],
-        dense_total[0],
-        dense_total[1],
-        dense_total[2],
+        pack_add(gate_low, gate_there),
+        pack_add(up_low, up_there),
+        pack_add(down_low, down_there),
     )
 
 

time: 886 us -> 759 us (0.86)
  waiting for transfers between devices: 192 us -> 57.1 us
  Pallas kernels: 548 us -> 562 us
  local copies, waits for them, and re-layouts: 46.6 us -> 37.6 us
    reduce_scatter x1, waiting for transfers between devices: 84.6 us -> 0.01 us  [body(): lax.psum_scatter(out_parts.reshape(chips * tok_dev, -1), 'dp', scatter_di...]
    ppermute x3 -> x5, waiting for transfers between devices: 57.1 us -> 0.19 us  [pack_swap(): return lax.ppermute(low, 'rep', [(0, 1), (1, 0)])]
    pallas_call x1, Pallas kernels: 98.4 us -> 112 us  [normed_back(): pl.pallas_call(normed_back_kernel, out_shape=(jax.ShapeDtypeStruct((rows,...]
    squeeze x2 -> x0, local copies, waits for them, and re-layouts: 11.5 us -> none  [the longest x1 9.81 us: body(): dense_total[2]]
    add x3 -> x4, other arithmetic: 15.9 us -> 18.1 us  [pack_add(): return low.astype(F32) + other.astype(F32)]
    unnamed x89 -> x103, local copies, waits for them, and re-layouts: 24 us -> 24.8 us
  transfers between devices with their start and end apart: 15 -> 17, of which waited for: 6 -> 4; matrix products, arithmetic and copies ran while one was open for 10% -> 11% of each run, Pallas kernels for 42% -> 51%
where the time goes in v3:
time: 759 us; the launch traced here: 749 us
  Pallas kernels  562 us (74%)
  waiting for transfers between devices  57.1 us (8%)
  local copies, waits for them, and re-layouts  37.6 us (5%)
  other arithmetic  31 us (4%)
  matrix products  30.3 us (4%)
  starting transfers between devices  15.9 us (2%)
  between operations  14.9 us (2%)
    pallas_call x1, Pallas kernels, dense(): pl.pallas_call(dense_kernel, out_shape=(jax.ShapeDtypeStruct((rows, featu...  179 us
    pallas_call x1, Pallas kernels, gather_project(): pl.pallas_call(gather_project_kernel, out_shape=(jax.ShapeDtypeStruct((3,...  172 us
    pallas_call x1, Pallas kernels, normed_back(): pl.pallas_call(normed_back_kernel, out_shape=(jax.ShapeDtypeStruct((rows,...  112 us
    pallas_call x1, Pallas kernels, attend_back(): pl.pallas_call(attend_back_kernel, out_shape=jax.ShapeDtypeStruct((3, tok...  43.7 us
    pallas_call x1, Pallas kernels, attend(): pl.pallas_call(attend_kernel, out_shape=(jax.ShapeDtypeStruct((tokens, r)...  38.9 us
    all_to_all x1, waiting for transfers between devices, body(): lax.all_to_all(grad_blocks, 'dp', split_axis=0, concat_axis=0, tiled=True)  30 us
    unnamed x103, local copies, waits for them, and re-layouts  24.8 us
    all_to_all x1, waiting for transfers between devices, body(): lax.all_to_all(attended.reshape(devices, tok_dev, r), 'dp', split_axis=0,...  21.9 us
  transfers between devices with their start and end apart: 17, of which 4 were waited for; matrix products, arithmetic and copies ran while one was open for 11% of the time, Pallas kernels for 51%

profile of v3, /device:TPU:0, one launch (start us, length us, event | category | flops | bytes accessed | tf_op | source)
XLA Modules:
  0.0 748.9 jit_solution(7405865964928887166)
XLA Ops:
  12.6 1.6 copy.34.sine
  17.4 171.9 %gather_project.1 = (bf16[3,4096,128]{2,1,0:T(8,128)(2,1)S(1)}, bf16[8,256,2048]{2,1,0:T(8,128)(2,1)}) custom-call(bf16[256,2048]{1,0:T(8,128)(2,1)S(1)} %fusion.6.normed, bf16[640,2048]{1,0:T(8,128)(2,1)S(1)} %constant_dynamic-update-slice_fusion.weights, f32[8,256,128]{2,1,0:T(8,128)S(1)} %copy.33.cosine, f32[8,256,128]{2,1,0:T(8,128)S(1)} %copy.34.sine), custom_call_target="tpu_custom_call" | custom-call | flops 10737418240 | bytes 335544320 | tf_op jit(solution)/shard_map/gather_project/pallas_call | solution.py:225
  189.4 38.9 %attend.1 = (bf16[4096,128]{1,0:T(8,128)(2,1)}, f32[32,256]{1,0:T(8,128)S(1)}) custom-call(s32[32]{0:T(128)S(1)} %convert_reduce_fusion.first_ref, s32[32]{0:T(128)S(1)} %add_select_fusion.tail_ref, bf16[3,4096,128]{2,1,0:T(8,128)(2,1)S(1)} %get-tuple-element.37.qkv), custom_call_target="tpu_custom_call" | custom-call | flops 17179869184 | bytes 125829120 | tf_op jit(solution)/shard_map/attend/pallas_call | solution.py:328
  228.3 3.7 all-to-all-start
  233.1 21.9 %all-to-all-done = bf16[16,256,128]{2,1,0:T(8,128)(2,1)S(1)} async-done(((bf16[16,256,128]{2,1,0:T(8,128)(2,1)}), bf16[16,256,128]{2,1,0:T(8,128)(2,1)S(1)}, u32[]{:S(2)}, u32[]{:S(2)}) %all-to-all-start) | async-done | bytes 1048608 | tf_op jit(solution)/shard_map/all_to_all | solution.py:1003
  256.4 6.2 multiply_reduce_fusion.2
  265.2 178.6 %dense.1 = (f32[256,2048]{1,0:T(8,128)}, bf16[8,256,2048]{2,1,0:T(8,128)(2,1)}, bf16[8,256,2048]{2,1,0:T(8,128)(2,1)}, bf16[512,2048]{1,0:T(8,128)(2,1)}, bf16[5...) custom-call(bf16[256,2048]{1,0:T(8,128)(2,1)} %multiply_convert_fusion.normed, bf16[8,256,2048]{2,1,0:T(8,128)(2,1)} %bitcast.221, ...), custom_call_target="tpu_custom_call" | custom-call | flops 77309411328 | bytes 524288000 | tf_op jit(solution)/shard_map/dense/pallas_call | solution.py:660
  443.8 1.5 collective-permute-start.3
  445.3 2.3 multiply_reduce_fusion
  448.9 6.5 convolution_convert_fusion.1
  465.7 4.7 all-to-all-start.1
  470.6 3.0 multiply_sine_fusion
  473.6 6.9 convolution_convert_fusion
  480.5 30.0 %all-to-all-done.1 = bf16[16,256,128]{2,1,0:T(8,128)(2,1)S(1)} async-done(((bf16[16,256,128]{2,1,0:T(8,128)(2,1)}), bf16[16,256,128]{2,1,0:T(8,128)(2,1)S(1)}, u32[]{:S(2)}, u32[]{:S(2)}) %all-to-all-start.1) | async-done | bytes 1048608 | tf_op jit(solution)/shard_map/all_to_all | solution.py:1032
  510.4 1.4 collective-permute-start.4
  514.0 1.9 copy-done.11
  515.9 43.7 %attend_back.1.grads = bf16[3,4096,128]{2,1,0:T(8,128)(2,1)S(1)} custom-call(s32[32]{0:T(128)S(1)} %convert_reduce_fusion.first_ref, s32[32]{0:T(128)S(1)} %add_select_fusion.tail_ref, bf16[3,4096,128]{2,1,0:T(8,128)(2,1)S(1)} %copy-done.11, bf16[4096,128]{1,0:T(8,128)(2,1)S(1)} %bitcast.202, bf16[4096,128]{1,0:T(8,128)(2,1)} %get-tuple-element.38.attended, ...), custom_call_target="tpu_custom_call" | custom-call | flops 42949672960 | bytes 251658240 | tf_op jit(solution)/shard_map/attend_back/pallas_call | solution.py:422
  559.7 1.7 copy-done.2
  561.4 3.9 constant_dynamic-slice_fusion.1
  565.3 2.6 copy.36
  567.9 3.6 collective-permute-done.7
  571.5 7.1 bitcast_convert_fusion
  580.1 3.6 fusion.12
  584.4 1.7 add_convert_fusion
  586.1 1.4 collective-permute-start.9
  587.5 111.7 %normed_back.1 = (f32[256,2048]{1,0:T(8,128)S(1)}, f32[1,2048]{1,0:T(1,128)S(1)}) custom-call(bf16[3,4096,128]{2,1,0:T(8,128)(2,1)S(1)} %copy-done.3, bf16[3,128,2048]{2,1,0:T(8,128)(2,1)S(1)} %pad_maximum_fusion.weights, bf16[3,128,2048]{2,1,0:T(8,128)(2,1)S(1)} %collective-permute-done.5.partner_weights, bf16[256,2048]{1,0:T(8,128)(2,1)S(1)} %bitcast.199, ...), custom_call_target="tpu_custom_call" | custom-call | flops 6442450944 | bytes 335544320 | tf_op jit(solution)/shard_map/normed_back/pallas_call | solution.py:807
  699.2 1.3 copy-done.4
  701.1 17.2 %gain_total.1 = f32[2,16,128]{2,1,0:T(8,128)} custom-call(f32[2,16,128]{2,1,0:T(8,128)} %pad_maximum_fusion.3.part), custom_call_target="tpu_custom_call" | custom-call | tf_op jit(solution)/shard_map/gain_total/pallas_call | solution.py:880
  718.3 1.3 slice_bitcast_fusion.32
  719.7 5.1 convert_add_fusion.2
  725.5 3.6 add_bitcast_fusion
  729.1 8.2 %convert_add_fusion = (f32[512,2048]{1,0:T(8,128)}, f32[512,2048]{1,0:T(8,128)}) fusion(bf16[512,2048]{1,0:T(8,128)(2,1)} %collective-permute-done.6, bf16[512,2048]{1,0:T(8,128)(2,1)} %get-tuple-element.52, bf16[512,2048]{1,0:T(8,128)(2,1)} %collective-permute-done.4, bf16[512,2048]{1,0:T(8,128)(2,1)S(1)} %copy-done.26), kind=kLoop, calls=%fused_computation.3 | loop fusion | flops 6291456 | bytes 16777216 | tf_op jit(solution)/shard_map/add | solution.py:923
  (169 shorter events, 35.2 us)
Async XLA Ops:
  7.2 249.2 %all-gather.4.cloned.1.call-start = ((), (), s32[]{:S(2)}) async-start(), calls=%async_computation.4 | async-start | bytes 8912896 | tf_op jit(solution)/shard_map/all_gather | solution.py:989
  7.9 257.2 %all-gather.6.cloned.1.call-start = ((), (), s32[]{:S(2)}) async-start(), calls=%async_computation.7 | async-start | bytes 9437184 | tf_op jit(solution)/shard_map/all_gather | solution.py:991
  189.3 39.0 %copy-start.10 = (bf16[3,4096,128]{2,1,0:T(8,128)(2,1)}, bf16[3,4096,128]{2,1,0:T(8,128)(2,1)S(1)}, u32[]{:S(2)}) copy-start(bf16[3,4096,128]{2,1,0:T(8,128)(2,1)S(1)} %get-tuple-element.37.qkv) | copy-start | bytes 9437188
  228.3 26.7 %all-to-all-start = ((bf16[16,256,128]{2,1,0:T(8,128)(2,1)}), bf16[16,256,128]{2,1,0:T(8,128)(2,1)S(1)}, u32[]{:S(2)}, u32[]{:S(2)}) async-start(bf16[16,256,128]{2,1,0:T(8,128)(2,1)} %bitcast.14), calls=%async_computation | async-start | bytes 2097152 | tf_op jit(solution)/shard_map/all_to_all | solution.py:1003
  232.1 329.3 %reduce-scatter.3.cloned.1.call-start = ((), (), s32[]{:S(2)}) async-start(), calls=%async_computation.5 | async-start | bytes 9437184 | tf_op jit(solution)/shard_map/reduce_scatter | solution.py:1016
  232.1 33.0 %collective-permute-start = (bf16[512,2048]{1,0:T(8,128)(2,1)}, bf16[512,2048]{1,0:T(8,128)(2,1)}, u32[]{:S(2)}, u32[]{:S(2)}) collective-permute-start(bf16[512,2048]{1,0:T(8,128)(2,1)} %gate_w.1), channel_id=1, source_target_pairs={{0,2},{2,0},{4,6},{6,4},{8,10},{10,8},{12,14},{14,12},{16,18},{18,... | collective-permute-start | bytes 6291464 | tf_op jit(solution)/shard_map/ppermute | solution.py:912
  232.6 32.5 %collective-permute-start.1 = (bf16[512,2048]{1,0:T(8,128)(2,1)}, bf16[512,2048]{1,0:T(8,128)(2,1)}, u32[]{:S(2)}, u32[]{:S(2)}) collective-permute-start(bf16[512,2048]{1,0:T(8,128)(2,1)} %up_w.1), channel_id=1, source_target_pairs={{0,2},{2,0},{4,6},{6,4},{8,10},{10,8},{12,14},{14,12},{16,18},{18,... | collective-permute-start | bytes 6291464 | tf_op jit(solution)/shard_map/ppermute | solution.py:912
  232.7 32.4 %collective-permute-start.2 = (bf16[512,2048]{1,0:T(8,128)(2,1)}, bf16[512,2048]{1,0:T(8,128)(2,1)}, u32[]{:S(2)}, u32[]{:S(2)}) collective-permute-start(bf16[512,2048]{1,0:T(8,128)(2,1)} %down_w.1), channel_id=1, source_target_pairs={{0,2},{2,0},{4,6},{6,4},{8,10},{10,8},{12,14},{14,12},{16,18},{18,... | collective-permute-start | bytes 6291464 | tf_op jit(solution)/shard_map/ppermute | solution.py:912
  256.4 7.5 %copy-start.29 = (f32[2048]{0:T(1024)S(1)}, f32[2048]{0:T(1024)}, u32[]{:S(2)}) copy-start(f32[2048]{0:T(1024)} %param.19) | copy-start | bytes 24580
  443.7 3.9 copy-start.22
  443.8 66.7 %collective-permute-start.3 = (bf16[512,2048]{1,0:T(8,128)(2,1)}, bf16[512,2048]{1,0:T(8,128)(2,1)}, u32[]{:S(2)}, u32[]{:S(2)}) collective-permute-start(bf16[512,2048]{1,0:T(8,128)(2,1)} %get-tuple-element.40), channel_id=1, source_target_pairs={{0,1},{1,0},{2,3},{3,2},{4,5},{5,4},{6,7},{7,6},{8,9},{9,8},{10,11... | collective-permute-start | bytes 6291464 | tf_op jit(solution)/shard_map/ppermute | solution.py:917
  465.7 44.7 %all-to-all-start.1 = ((bf16[16,256,128]{2,1,0:T(8,128)(2,1)}), bf16[16,256,128]{2,1,0:T(8,128)(2,1)S(1)}, u32[]{:S(2)}, u32[]{:S(2)}) async-start(bf16[16,256,128]{2,1,0:T(8,128)(2,1)} %constant_dynamic-update-slice_fusion.21), calls=%async_computation.1 | async-start | bytes 2097152 | tf_op jit(solution)/shard_map/all_to_all | solution.py:1032
  470.5 249.2 %reduce-scatter.5.cloned.1.call-start = ((), (), s32[]{:S(2)}) async-start(), calls=%async_computation.6 | async-start | bytes 8912896 | tf_op jit(solution)/shard_map/reduce_scatter | solution.py:1058
  510.4 50.9 %collective-permute-start.4 = (bf16[512,2048]{1,0:T(8,128)(2,1)}, bf16[512,2048]{1,0:T(8,128)(2,1)}, u32[]{:S(2)}, u32[]{:S(2)}) collective-permute-start(bf16[512,2048]{1,0:T(8,128)(2,1)} %get-tuple-element.46), channel_id=1, source_target_pairs={{0,1},{1,0},{2,3},{3,2},{4,5},{5,4},{6,7},{7,6},{8,9},{9,8},{10,11... | collective-permute-start | bytes 6291464 | tf_op jit(solution)/shard_map/ppermute | solution.py:917
  567.9 3.6 collective-permute-start.7
  571.5 8.0 %slice-start = ((s8[8388608]{0:T(1024)(128)(4,1)}), s8[4194304]{0:T(1024)(128)(4,1)S(1)}, s32[]{:S(2)}) async-start(s8[8388608]{0:T(1024)(128)(4,1)} %bitcast.205), calls=%async_computation.8 | async-start | bytes 8388608
  571.5 7.4 copy-start.19
  571.5 7.4 copy-start.21
  571.5 7.4 copy-start.25
  571.5 8.0 %slice-start.1 = ((s8[8388608]{0:T(1024)(128)(4,1)}), s8[4194304]{0:T(1024)(128)(4,1)S(1)}, s32[]{:S(2)}) async-start(s8[8388608]{0:T(1024)(128)(4,1)} %bitcast.205), calls=%async_computation.9 | async-start | bytes 8388608
  578.6 5.8 collective-permute-start.8
  579.0 8.5 %collective-permute-start.5 = (bf16[3,128,2048]{2,1,0:T(8,128)(2,1)S(1)}, bf16[3,128,2048]{2,1,0:T(8,128)(2,1)S(1)}, u32[]{:S(2)}, u32[]{:S(2)}) collective-permute-start(bf16[3,128,2048]{2,1,0:T(8,128)(2,1)S(1)} %pad_maximum_fusion.weights), channel_id=1, source_target_pairs={{0,2},{2,0},{4,6},{6,4},{8,10},{10,8},{12,14},{14,12},{16,18},{18,... | collective-permute-start | bytes 4718600 | tf_op jit(solution)/shard_map/ppermute | solution.py:912
  583.7 3.8 copy-start.1
  583.7 3.8 copy-start.3
  583.7 3.8 copy-start.9
  583.7 135.9 %collective-permute-start.6 = (bf16[512,2048]{1,0:T(8,128)(2,1)}, bf16[512,2048]{1,0:T(8,128)(2,1)}, u32[]{:S(2)}, u32[]{:S(2)}) collective-permute-start(bf16[512,2048]{1,0:T(8,128)(2,1)} %get-tuple-element.52), channel_id=1, source_target_pairs={{0,1},{1,0},{2,3},{3,2},{4,5},{5,4},{6,7},{7,6},{8,9},{9,8},{10,11... | collective-permute-start | bytes 6291464 | tf_op jit(solution)/shard_map/ppermute | solution.py:917
  586.1 133.6 %collective-permute-start.9 = (bf16[3,128,2048]{2,1,0:T(8,128)(2,1)}, bf16[3,128,2048]{2,1,0:T(8,128)(2,1)}, u32[]{:S(2)}, u32[]{:S(2)}) collective-permute-start(bf16[3,128,2048]{2,1,0:T(8,128)(2,1)} %add_convert_fusion), channel_id=1, source_target_pairs={{0,1},{1,0},{2,3},{3,2},{4,5},{5,4},{6,7},{7,6},{8,9},{9,8},{10,11... | collective-permute-start | bytes 4718600 | tf_op jit(solution)/shard_map/ppermute | solution.py:917
  719.7 5.1 copy-start.28
  724.8 4.3 copy-start.26
  724.8 14.0 %collective-permute-start.10 = (bf16[128,2048]{1,0:T(8,128)(2,1)S(1)}, bf16[128,2048]{1,0:T(8,128)(2,1)S(1)}, u32[]{:S(2)}, u32[]{:S(2)}) collective-permute-start(bf16[128,2048]{1,0:T(8,128)(2,1)S(1)} %copy-done.28), channel_id=1, source_target_pairs={{0,1},{1,0},{2,3},{3,2},{4,5},{5,4},{6,7},{7,6},{8,9},{9,8},{10,11... | collective-permute-start | bytes 1572872 | tf_op jit(solution)/shard_map/ppermute | solution.py:917
  729.1 8.2 %copy-start.15 = (f32[256,2048]{1,0:T(8,128)S(1)}, f32[256,2048]{1,0:T(8,128)}, u32[]{:S(2)}) copy-start(f32[256,2048]{1,0:T(8,128)} %copy-done.12) | copy-start | bytes 6291460
  729.1 8.2 %copy-start.27 = (bf16[256,2048]{1,0:T(8,128)(2,1)S(1)}, bf16[256,2048]{1,0:T(8,128)(2,1)}, u32[]{:S(2)}) copy-start(bf16[256,2048]{1,0:T(8,128)(2,1)} %reduce-scatter.3.cloned.1.call-done) | copy-start | bytes 3145732
  (19 other events, 32.8 us)
Sparse Core Ops, SparseCore 0:
  9.6 84.9 all-gather.3
  96.1 123.9 all-gather.5
  443.9 104.7 reduce-scatter.2
  561.5 82.3 reduce-scatter.4

commit v4 on v3

--- a/solution.py
+++ b/solution.py
@@ -106,20 +106,43 @@
     return pl.ds(direction * (rows // 2), rows // 2)
 
 
+def turned(u):
+    parts = []
+    for at in range(0, u.shape[1], HEAD_DIM):
+        parts += [-u[:, at + HALF : at + HEAD_DIM], u[:, at : at + HALF]]
+    return jnp.concatenate(parts, 1)
+
+
 def gather_project_kernel(
-    normed, weights, cosine, sine, qkv, gathered,
-    partner_weights, x_buf, staged,
+    tokens, gain, query_w, key_w, value_w, output_w, cos_t, sin_t, qkv, gathered, output_all,
+    normed, partner_weights, x_buf, staged,
     ag_send, ag_recv, w_send, w_recv, q_send, q_recv, local_sem,
+    o_send, o_recv, pair_send, pair_recv, rep_send, rep_recv, far_send, far_recv,
 ):
     ring = Ring()
     n = ring.chips
+    packs, pack = lax.axis_size("rep"), lax.axis_index("rep")
     rows = normed.shape[0]
+    half = rows // 2
     r = qkv.shape[2]
-    ring.greet((ring.next[0], ring.next[1], ring.partner))
-    swap = remote(weights, partner_weights, w_send, w_recv, ring.partner)
-    swap.start()
-    keep = pltpu.make_async_copy(normed, gathered.at[ring.chip], local_sem.at[2])
-    keep.start()
+    own_weights = (query_w, key_w, value_w)
+    barrier = pltpu.get_barrier_semaphore()
+    for k in range(1, packs):
+        pl.semaphore_signal(
+            barrier, inc=1, device_id={"rep": lax.rem(pack + k, packs)}, device_id_type=MESH
+        )
+    for other in (ring.next[0], ring.next[1], ring.partner):
+        pl.semaphore_signal(barrier, inc=1, device_id={"dp": other}, device_id_type=MESH)
+    pl.semaphore_wait(barrier, 3 + packs - 1)
+
+    def normalize(i, carry):
+        span = pl.ds(pl.multiple_of(i * 32, 32), 32)
+        value = tokens[span, :].astype(F32)
+        scale = lax.rsqrt(jnp.mean(value * value, axis=1, keepdims=True) + EPSILON)
+        normed[span, :] = (value * scale * gain[...]).astype(LOW)
+        return carry
+
+    lax.fori_loop(0, rows // 32, normalize, 0)
 
     def hop(t, d):
         chip = ring.chip_far((1 - t) if d == 0 else (t - 1))
@@ -130,38 +153,102 @@
         src = normed.at[part] if first else gathered.at[chip, part]
         return remote(src, gathered.at[chip, part], ag_send.at[d, t - 1], ag_recv.at[d, t - 1], ring.next[d])
 
+    out_rows, features = output_w.shape
+    share = out_rows // packs
+    spot = ring.place * 2 + ring.core
+
+    def share_of(q, d):
+        return pl.ds(pl.multiple_of(q * share, share), share), pl.ds(d * (features // 2), features // 2)
+
+    def block_at(t, d, q, core):
+        place = lax.rem(ring.place + (n - t if d == 0 else t), n)
+        at_rows, columns = share_of(q, d)
+        return output_all.at[place * 2 + core, at_rows, columns]
+
+    def o_copy(t, d, first):
+        at_rows, columns = share_of(pack, d)
+        src = output_w.at[at_rows, columns] if first else block_at(t - 1, d, pack, ring.core)
+        return remote(
+            src, block_at(t - 1, d, pack, ring.core), o_send.at[d, t], o_recv.at[d, t], ring.next[d]
+        )
+
+    def pair_copy(t, d):
+        block = block_at(t, d, pack, ring.core)
+        return remote(block, block, pair_send.at[d, t], pair_recv.at[d, t], ring.partner)
+
+    def rep_copy(t, d, k):
+        block = block_at(t, d, pack, ring.core)
+        return pltpu.make_async_remote_copy(
+            src_ref=block,
+            dst_ref=block,
+            send_sem=rep_send.at[k - 1, d, t],
+            recv_sem=rep_recv.at[k - 1, d, t],
+            device_id={"rep": lax.rem(pack + k, packs)},
+            device_id_type=MESH,
+        )
+
+    def far_copy(t, d, k):
+        block = block_at(t, d, lax.rem(pack + packs - k, packs), ring.core)
+        return remote(block, block, far_send.at[k - 1, d, t], far_recv.at[k - 1, d, t], ring.partner)
+
+    def forward_far(t):
+        for d in (0, 1):
+            for k in range(1, packs):
+                rep_copy(t, d, k).wait_recv()
+                far_copy(t, d, k).start()
+
     for d in (0, 1):
         send(1, d, True).start()
+    for d in (0, 1):
+        o_copy(1, d, True).start()
+    own_rows = remote(output_w, output_all.at[spot], local_sem.at[3], local_sem.at[4], ring.partner)
+    own_rows.start()
+    own_keep = pltpu.make_async_copy(output_w, output_all.at[spot], local_sem.at[5])
+    own_keep.start()
+    swaps = [
+        remote(own_weights[i], partner_weights.at[i], w_send.at[i], w_recv.at[i], ring.partner)
+        for i in range(3)
+    ]
+    for swap in swaps:
+        swap.start()
+    keep = pltpu.make_async_copy(normed, gathered.at[ring.chip], local_sem.at[2])
+    keep.start()
 
     def project_block(t, from_input):
         x = normed[...] if from_input else x_buf[...]
         places = [ring.chip_far(-t), ring.chip_far(t)]
-        cos = jnp.concatenate([cosine[places[d], half_rows(d, rows), :] for d in (0, 1)], 0)
-        sin = jnp.concatenate([sine[places[d], half_rows(d, rows), :] for d in (0, 1)], 0)
+        starts = [
+            pl.multiple_of((places[d] * 2 + ring.core) * rows + d * half, half) for d in (0, 1)
+        ]
+
+        def table(source):
+            wide = [source[:, pl.ds(starts[d], half)] for d in (0, 1)]
+            return jnp.concatenate(
+                [jnp.concatenate([w] * (r // HALF), 0).T for w in wide], 0
+            )
+
+        cos, sin = table(cos_t), table(sin_t)
 
         def heads(w):
-            part = [dot_nt(x, w[i * r : (i + 1) * r, :]) for i in range(5)]
+            query, key, value = [dot_nt(x, w[i][...]) for i in range(3)]
             return (
-                (part[0] * cos + part[1] * sin).astype(LOW),
-                (part[2] * cos + part[3] * sin).astype(LOW),
-                part[4].astype(LOW),
+                (query * cos + turned(query) * sin).astype(LOW),
+                (key * cos + turned(key) * sin).astype(LOW),
+                value.astype(LOW),
             )
 
-        starts = [
-            pl.multiple_of((places[d] * 2 + ring.core) * rows + d * (rows // 2), rows // 2)
-            for d in (0, 1)
-        ]
-        for i, value in enumerate(heads(weights)):
+        for i, value in enumerate(heads(own_weights)):
             for d in (0, 1):
-                qkv[i, pl.ds(starts[d], rows // 2), :] = value[d * (rows // 2) : (d + 1) * (rows // 2)]
+                qkv[i, pl.ds(starts[d], half), :] = value[d * half : (d + 1) * half]
         if from_input:
-            swap.wait()
-        for i, value in enumerate(heads(partner_weights)):
+            for swap in swaps:
+                swap.wait()
+        for i, value in enumerate(heads([partner_weights.at[i] for i in range(3)])):
             staged[t, i] = value
         for d in (0, 1):
             remote(
                 staged.at[t, :, half_rows(d, rows)],
-                qkv.at[:, pl.ds(starts[d], rows // 2)],
+                qkv.at[:, pl.ds(starts[d], half)],
                 q_send.at[d, t],
                 q_recv.at[d, t],
                 ring.partner,
@@ -177,6 +264,23 @@
         def _():
             for d in (0, 1):
                 send(t + 1, d, False).start()
+
+        for d in (0, 1):
+            o_copy(t, d, False).wait_recv()
+
+        @pl.when(t < n - 1)
+        def _():
+            for d in (0, 1):
+                o_copy(t + 1, d, False).start()
+
+        for d in (0, 1):
+            for k in range(1, packs):
+                rep_copy(t, d, k).start()
+            pair_copy(t, d).start()
+
+        @pl.when(t > 1)
+        def _():
+            forward_far(t - 1)
 
         loads = []
         for d in (0, 1):
@@ -190,13 +294,21 @@
         return carry
 
     lax.fori_loop(1, n, step, 0)
+    forward_far(n - 1)
 
     def finish(t, carry):
         for d in (0, 1):
             send(t, d, False).wait_send()
+            o_copy(t, d, False).wait_send()
+            pair_copy(t, d).wait()
+            for k in range(1, packs):
+                rep_copy(t, d, k).wait_send()
+                far_copy(t, d, k).wait()
         return carry
 
     lax.fori_loop(1, n, finish, 0)
+    own_rows.wait()
+    own_keep.wait()
 
     def finish_heads(t, carry):
         for d in (0, 1):
@@ -215,10 +327,11 @@
     keep.wait()
 
 
-def gather_project(normed, weights, cosine, sine):
-    rows, features = normed.shape
-    r = weights.shape[0] // 5
+def gather_project(tokens, gain, weights, output_weight, cos_t, sin_t):
+    rows, features = tokens.shape
+    r = weights[0].shape[0]
     devices = lax.axis_size("dp")
+    packs = lax.axis_size("rep")
     n = devices // 2
     vmem = pl.BlockSpec(memory_space=pltpu.VMEM)
     dma = pltpu.SemaphoreType.DMA
@@ -227,23 +340,28 @@
         out_shape=(
             jax.ShapeDtypeStruct((3, devices * rows, r), LOW),
             jax.ShapeDtypeStruct((n, rows, features), LOW),
+            jax.ShapeDtypeStruct((devices,) + output_weight.shape, LOW),
         ),
-        in_specs=[vmem] * 4,
-        out_specs=(vmem, pl.BlockSpec(memory_space=pl.ANY)),
+        in_specs=[vmem] * 8,
+        out_specs=(vmem, pl.BlockSpec(memory_space=pl.ANY), pl.BlockSpec(memory_space=pl.ANY)),
         scratch_shapes=[
-            pltpu.VMEM(weights.shape, LOW),
+            pltpu.VMEM((rows, features), LOW),
+            pltpu.VMEM((3, r, features), LOW),
             pltpu.VMEM((rows, features), LOW),
             pltpu.VMEM((n, 3, rows, r), LOW),
-            dma((2, n)), dma((2, n)), dma, dma, dma((2, n)), dma((2, n)), dma((3,)),
+            dma((2, n)), dma((2, n)), dma((3,)), dma((3,)), dma((2, n)), dma((2, n)), dma((6,)),
+            dma((2, n)), dma((2, n)), dma((2, n)), dma((2, n)),
+            dma((packs - 1, 2, n)), dma((packs - 1, 2, n)),
+            dma((packs - 1, 2, n)), dma((packs - 1, 2, n)),
         ],
         compiler_params=pltpu.CompilerParams(
             collective_id=1, has_side_effects=True, vmem_limit_bytes=40 * MIB
         ),
         cost_estimate=pl.CostEstimate(
-            flops=4 * n * rows * features * 5 * r, bytes_accessed=320 * MIB, transcendentals=0
+            flops=4 * n * rows * features * 3 * r, bytes_accessed=320 * MIB, transcendentals=0
         ),
         name="gather_project",
-    )(normed, weights, cosine, sine)
+    )(tokens, gain, *weights, output_weight, cos_t, sin_t)
 
 
 def split_heads(u):
@@ -285,8 +403,15 @@
     return start, whole, allowed
 
 
-def attend_kernel(first_ref, tail_ref, qkv, attended, log_total, value_t):
+def walk_rows(b, tok_dev, chips):
+    device = b * BLOCK // tok_dev
+    spot = place_of(device // 2, chips) * 2 + device % 2
+    return pl.ds(pl.multiple_of(spot * tok_dev + b * BLOCK % tok_dev, BLOCK), BLOCK)
+
+
+def attend_kernel(chips, first_ref, tail_ref, qkv, attended, log_total, value_t):
     tokens, r = qkv.shape[1:]
+    tok_dev = tokens // (2 * chips)
     columns = (r // HEAD_DIM) * BLOCK
     scale = 1.0 / math.sqrt(HEAD_DIM)
     transpose_blocks(qkv.at[2], value_t)
@@ -315,7 +440,7 @@
 
         top, total, out = lax.fori_loop(0, whole, more, (top, total, out))
         log_total[pl.ds(b, 1), :] = top + jnp.log(total)
-        attended[pl.ds(at, BLOCK), :] = join_heads(out / total).T.astype(LOW)
+        attended[walk_rows(b, tok_dev, chips), :] = join_heads(out / total).T.astype(LOW)
         return carry
 
     lax.fori_loop(0, tokens // BLOCK, block, 0)
@@ -326,7 +451,7 @@
     smem = pl.BlockSpec(memory_space=pltpu.SMEM)
     vmem = pl.BlockSpec(memory_space=pltpu.VMEM)
     return pl.pallas_call(
-        attend_kernel,
+        functools.partial(attend_kernel, lax.axis_size("dp") // 2),
         out_shape=(
             jax.ShapeDtypeStruct((tokens, r), LOW),
             jax.ShapeDtypeStruct((tokens // BLOCK, (r // HEAD_DIM) * BLOCK), F32),
@@ -352,10 +477,11 @@
 
 
 def attend_back_kernel(
-    first_ref, tail_ref, qkv, grad_out, attended, log_total, cos_t, sin_t, grads,
+    chips, first_ref, tail_ref, qkv, grad_out, attended, log_total, cos_t, sin_t, grads,
     key_t, grad_key, grad_value,
 ):
     tokens, r = qkv.shape[1:]
+    tok_dev = tokens // (2 * chips)
     heads = r // HEAD_DIM
     columns = heads * BLOCK
     scale = 1.0 / math.sqrt(HEAD_DIM)
@@ -367,9 +493,10 @@
         at = pl.multiple_of(b * BLOCK, BLOCK)
         here = pl.ds(at, BLOCK)
         query = split_heads(qkv[0, here, :])
-        grad_rows = grad_out[here, :]
+        walk = walk_rows(b, tok_dev, chips)
+        grad_rows = grad_out[walk, :]
         grad = split_heads(grad_rows)
-        product = (grad_rows.astype(F32) * attended[here, :].astype(F32)).T
+        product = (grad_rows.astype(F32) * attended[walk, :].astype(F32)).T
         delta = jnp.concatenate(
             [
                 jnp.sum(product[h * HEAD_DIM : (h + 1) * HEAD_DIM], axis=0, keepdims=True)
@@ -420,7 +547,7 @@
     smem = pl.BlockSpec(memory_space=pltpu.SMEM)
     vmem = pl.BlockSpec(memory_space=pltpu.VMEM)
     return pl.pallas_call(
-        attend_back_kernel,
+        functools.partial(attend_back_kernel, lax.axis_size("dp") // 2),
         out_shape=jax.ShapeDtypeStruct((3, tokens, r), LOW),
         in_specs=[smem, smem] + [vmem] * 6,
         out_specs=vmem,
@@ -438,7 +565,7 @@
 
 
 def dense_kernel(
-    normed, cotangents, gate_w, up_w, down_w, gate_p, up_p, down_p,
+    normed, cotangents_a, cotangents_b, gate_w, up_w, down_w, gate_p, up_p, down_p,
     grad_sum, out_parts, gathered, gate_grad, up_grad, down_grad,
     weights, totals, x_buf, g_buf, out_acc, grad_acc, sent, landed, cast_buf, pair_land,
     ag_send, ag_recv, rs_send, rs_recv, credit, local_sem, w_sem, cast_sem, pair_send, pair_recv,
@@ -492,7 +619,7 @@
         for d in (0, 1):
             part = half_rows(d, rows)
             copies.append(
-                pltpu.make_async_copy(cotangents.at[source(t, d), part], g_buf.at[part], local_sem.at[d])
+                pltpu.make_async_copy((cotangents_a, cotangents_b)[d].at[source(t, d)], g_buf.at[part], local_sem.at[d])
             )
             copies[-1].start()
 
@@ -667,7 +794,7 @@
             jax.ShapeDtypeStruct((own, features), LOW),
             jax.ShapeDtypeStruct((own, features), LOW),
         ),
-        in_specs=[vmem] + [hbm] * 7,
+        in_specs=[vmem] + [hbm] * 8,
         out_specs=(vmem,) + (hbm,) * 5,
         scratch_shapes=[
             pltpu.VMEM((3, 2 * own, features), LOW),
@@ -691,20 +818,29 @@
             flops=2 * 9 * n * rows * features * 2 * own, bytes_accessed=500 * MIB, transcendentals=0
         ),
         name="dense",
-    )(normed, cotangents, *own_weights, *partner_weights)
+    )(normed, *cotangents, *own_weights, *partner_weights)
 
 
 def normed_back_kernel(
-    grads, weights, partner_weights, hidden_in, gain, grad_mixed, out, gain_part,
-    partner_grads, sent, landed,
-    p_send, p_recv, rs_send, rs_recv, credit,
+    grads, weights, partner_weights, hidden_in, gain, grad_mixed, normed_all,
+    out, gain_part, query_total, key_total, value_total,
+    partner_grads, sent, landed, x_buf, parts, joined, pair_out, pair_land, rep_land,
+    p_send, p_recv, rs_send, rs_recv, credit, x_sem, pair_sem, rep_send, rep_recv,
 ):
     ring = Ring()
     n = ring.chips
     rows, features = out.shape
     half = rows // 2
     r = grads.shape[2]
-    ring.greet((ring.next[0], ring.next[1], ring.partner))
+    packs, pack = lax.axis_size("rep"), lax.axis_index("rep")
+    barrier = pltpu.get_barrier_semaphore()
+    for k in range(1, packs):
+        pl.semaphore_signal(
+            barrier, inc=1, device_id={"rep": lax.rem(pack + k, packs)}, device_id_type=MESH
+        )
+    for other in (ring.next[0], ring.next[1], ring.partner):
+        pl.semaphore_signal(barrier, inc=1, device_id={"dp": other}, device_id_type=MESH)
+    pl.semaphore_wait(barrier, 3 + packs - 1)
 
     def place(t, d):
         return ring.chip_far(-t if d == 0 else t)
@@ -729,18 +865,58 @@
     def reduce_copy(t, d):
         return remote(sent.at[d], landed.at[d, t % 2], rs_send.at[d], rs_recv.at[d, t % 2], ring.next[d])
 
+    def mine(t, d):
+        start = (place(t, d) * 2 + ring.core) * rows + d * half
+        return pl.ds(pl.multiple_of(start, half), half)
+
+    def load(t, d):
+        part = half_rows(d, rows)
+        return pltpu.make_async_copy(normed_all.at[place(t, d), part], x_buf.at[t % 2, part], x_sem.at[t % 2, d])
+
+    def block_grads(t):
+        return jnp.concatenate(
+            [jnp.concatenate([grads[i, mine(t, d), :] for d in (0, 1)], 0) for i in range(3)]
+            + [partner_grads[i, t % n] for i in range(3)],
+            1,
+        )
+
+    def weight_parts(t):
+        for d in (0, 1):
+            load(t, d).wait()
+        parts[...] += dot_tn(block_grads(t), x_buf[t % 2])
+
+    def pair_copy():
+        return remote(pair_out, pair_land, pair_sem.at[0], pair_sem.at[1], ring.partner)
+
+    def rep_copy(k):
+        return pltpu.make_async_remote_copy(
+            src_ref=pair_out,
+            dst_ref=rep_land.at[k - 1],
+            send_sem=rep_send.at[k - 1],
+            recv_sem=rep_recv.at[k - 1],
+            device_id={"rep": lax.rem(pack + k, packs)},
+            device_id_type=MESH,
+        )
+
+    parts[...] = jnp.zeros_like(parts)
+    for i in range(3):
+        joined[pl.ds(i * r, r), :] = weights[i]
+        joined[pl.ds((3 + i) * r, r), :] = partner_weights[i]
+    middle = n // 2
+
     def step(t, carry):
-        for d in (0, 1):
-            start = (place(t, d) * 2 + ring.core) * rows + d * half
-            mine = pl.ds(pl.multiple_of(start, half), half)
-            part = pl.ds(d * half, half)
-            swap(t, d).wait_recv()
-            total = dot_nn(grads[0, mine, :], weights[0])
-            for i in (1, 2):
-                total += dot_nn(grads[i, mine, :], weights[i])
-            for i in range(3):
-                total += dot_nn(partner_grads[i, t % n, part, :], partner_weights[i])
-            out[part, :] = total
+        @pl.when(t <= middle)
+        def _():
+            for d in (0, 1):
+                load(2 * t - 1, d).start()
+                load(2 * t, d).start()
+
+        @pl.when(t == 1)
+        def _():
+            for d in (0, 1):
+                swap(t, d).wait_recv()
+
+        out[...] = dot_nn(block_grads(t), joined[...])
 
         for d in (0, 1):
             part = pl.ds(d * half, half)
@@ -768,16 +944,38 @@
 
                 reduce_copy(t, d).start()
 
+        @pl.when(t == 1)
+        def _():
+            def arrived(k, carry):
+                for d in (0, 1):
+                    swap(k, d).wait_recv()
+                return carry
+
+            lax.fori_loop(2, n + 1, arrived, 0)
+
+        @pl.when(t <= middle)
+        def _():
+            weight_parts(2 * t - 1)
+            weight_parts(2 * t)
+
+        @pl.when(t == middle)
+        def _():
+            for i in range(3):
+                pair_out[i] = parts[pl.ds((3 + i) * r, r), :].astype(LOW)
+            pair_copy().start()
+
+        @pl.when(t == middle + 1)
+        def _():
+            pair_copy().wait()
+            for i in range(3):
+                pair_out[i] = (parts[pl.ds(i * r, r), :] + pair_land[i].astype(F32)).astype(LOW)
+            for k in range(1, packs):
+                rep_copy(k).start()
+            rep_land[packs - 1] = pair_out[...]
+
         return carry
 
     lax.fori_loop(1, n + 1, step, 0)
-
-    def finish(t, carry):
-        for d in (0, 1):
-            swap(t, d).wait_send()
-        return carry
-
-    lax.fori_loop(1, n + 1, finish, 0)
 
     gain_part[...] = jnp.zeros_like(gain_part)
 
@@ -794,11 +992,26 @@
 
     lax.fori_loop(0, rows // 16, close, 0)
 
-
-def normed_back(grads, weights, partner_weights, hidden_in, gain, grad_mixed):
+    def finish(t, carry):
+        for d in (0, 1):
+            swap(t, d).wait_send()
+        return carry
+
+    lax.fori_loop(1, n + 1, finish, 0)
+    for k in range(1, packs):
+        rep_copy(k).wait()
+    for i, total in enumerate((query_total, key_total, value_total)):
+        value = rep_land[lax.rem(pack + packs - 1, packs), i].astype(F32)
+        for q in range(1, packs):
+            value += rep_land[lax.rem(pack + 2 * packs - q - 1, packs), i].astype(F32)
+        total[...] = value
+
+
+def normed_back(grads, weights, partner_weights, hidden_in, gain, grad_mixed, normed_all):
     tokens, r = grads.shape[1:]
     features = weights.shape[2]
     devices = lax.axis_size("dp")
+    packs = lax.axis_size("rep")
     n = devices // 2
     rows = tokens // devices
     half = rows // 2
@@ -809,72 +1022,84 @@
         out_shape=(
             jax.ShapeDtypeStruct((rows, features), F32),
             jax.ShapeDtypeStruct((1, features), F32),
-        ),
-        in_specs=[vmem] * 6,
-        out_specs=(vmem, vmem),
+        )
+        + (jax.ShapeDtypeStruct((r, features), F32),) * 3,
+        in_specs=[vmem] * 6 + [pl.BlockSpec(memory_space=pl.ANY)],
+        out_specs=(vmem,) * 5,
         scratch_shapes=[
             pltpu.VMEM((3, n, rows, r), LOW),
             pltpu.VMEM((2, half, features), LOW),
             pltpu.VMEM((2, 2, half, features), LOW),
+            pltpu.VMEM((2, rows, features), LOW),
+            pltpu.VMEM((6 * r, features), F32),
+            pltpu.VMEM((6 * r, features), LOW),
+            pltpu.VMEM((3, r, features), LOW),
+            pltpu.VMEM((3, r, features), LOW),
+            pltpu.VMEM((packs, 3, r, features), LOW),
             dma((2, n)), dma((2, n)), dma((2,)), dma((2, 2)),
             pltpu.SemaphoreType.REGULAR((2,)),
+            dma((2, 2)), dma((2,)), dma((packs - 1,)), dma((packs - 1,)),
         ],
         compiler_params=pltpu.CompilerParams(
-            collective_id=3, has_side_effects=True, vmem_limit_bytes=40 * MIB
+            collective_id=3, has_side_effects=True, vmem_limit_bytes=56 * MIB
         ),
         cost_estimate=pl.CostEstimate(
-            flops=2 * n * rows * features * 6 * r, bytes_accessed=320 * MIB, transcendentals=0
+            flops=2 * n * rows * features * 12 * r, bytes_accessed=320 * MIB, transcendentals=0
         ),
         name="normed_back",
-    )(grads, weights, partner_weights, hidden_in, gain, grad_mixed)
-
-
-def gain_total_kernel(part, out, landed, send_sem, recv_sem, local_sem):
-    columns, packs = lax.axis_size("dp"), lax.axis_size("rep")
-    devices = columns * packs
-    me = lax.axis_index("rep") * columns + lax.axis_index("dp")
+    )(grads, weights, partner_weights, hidden_in, gain, grad_mixed, normed_all)
+
+
+def gain_total_kernel(part, out, near_land, near_sum, far_land, near_send, near_recv, far_send, far_recv):
+    packs = lax.axis_size("rep")
+    chips = lax.axis_size("dp") // 2
+    mates = 2 * packs
+    me, pack = lax.axis_index("dp"), lax.axis_index("rep")
+    core, chip = me % 2, me // 2
+    mate = pack * 2 + core
     barrier = pltpu.get_barrier_semaphore()
 
-    def other(k):
-        to = lax.rem(me + k, devices)
-        return {"dp": to % columns, "rep": to // columns}
-
-    def greet(k, carry):
-        pl.semaphore_signal(barrier, inc=1, device_id=other(k), device_id_type=MESH)
-        return carry
-
-    lax.fori_loop(1, devices, greet, 0)
-    pl.semaphore_wait(barrier, devices - 1)
-
-    def copy(k):
-        return pltpu.make_async_remote_copy(
-            src_ref=part,
-            dst_ref=landed.at[me],
-            send_sem=send_sem.at[k],
-            recv_sem=recv_sem.at[k],
-            device_id=other(k),
-            device_id_type=MESH,
-        )
-
-    def begin(k, carry):
-        copy(k).start()
-        return carry
-
-    lax.fori_loop(1, devices, begin, 0)
-    keep = pltpu.make_async_copy(part, landed.at[me], local_sem)
-    keep.start()
-    keep.wait()
-
-    def wait(k, carry):
-        copy(k).wait()
-        return carry
-
-    lax.fori_loop(1, devices, wait, 0)
-    out[...] = lax.fori_loop(1, devices, lambda i, total: total + landed[i], landed[0])
+    def near(k):
+        to = lax.rem(mate + k, mates)
+        return {"dp": chip * 2 + to % 2, "rep": to // 2}
+
+    def far(k):
+        return {"dp": lax.rem(chip + k, chips) * 2 + core}
+
+    for k in range(1, mates):
+        pl.semaphore_signal(barrier, inc=1, device_id=near(k), device_id_type=MESH)
+    for k in range(1, chips):
+        pl.semaphore_signal(barrier, inc=1, device_id=far(k), device_id_type=MESH)
+    pl.semaphore_wait(barrier, mates + chips - 2)
+
+    def exchange(src, landed, own, send_sem, recv_sem, device, count):
+        copies = [
+            pltpu.make_async_remote_copy(
+                src_ref=src,
+                dst_ref=landed.at[own],
+                send_sem=send_sem.at[k],
+                recv_sem=recv_sem.at[k],
+                device_id=device(k),
+                device_id_type=MESH,
+            )
+            for k in range(1, count)
+        ]
+        for copy in copies:
+            copy.start()
+        landed[own] = src[...]
+        for copy in copies:
+            copy.wait()
+        total = landed[0]
+        for k in range(1, count):
+            total += landed[k]
+        return total
+
+    near_sum[...] = exchange(part, near_land, mate, near_send, near_recv, near, mates)
+    out[...] = exchange(near_sum, far_land, chip, far_send, far_recv, far, chips)
 
 
 def gain_total(part):
-    devices = lax.axis_size("dp") * lax.axis_size("rep")
+    mates, chips = 2 * lax.axis_size("rep"), lax.axis_size("dp") // 2
     vmem = pl.BlockSpec(memory_space=pltpu.VMEM)
     dma = pltpu.SemaphoreType.DMA
     return pl.pallas_call(
@@ -883,8 +1108,10 @@
         in_specs=[vmem],
         out_specs=vmem,
         scratch_shapes=[
-            pltpu.VMEM((devices,) + part.shape, F32),
-            dma((devices,)), dma((devices,)), dma,
+            pltpu.VMEM((mates,) + part.shape, F32),
+            pltpu.VMEM(part.shape, F32),
+            pltpu.VMEM((chips,) + part.shape, F32),
+            dma((mates,)), dma((mates,)), dma((chips,)), dma((chips,)),
         ],
         compiler_params=pltpu.CompilerParams(collective_id=4, has_side_effects=True),
         name="gain_total",
@@ -900,11 +1127,6 @@
 def rms_back(values, norm_gain, grads):
     _, pullback = jax.vjp(rms, values, norm_gain)
     return pullback(grads)
-
-
-def turned_rows(weight):
-    parts = weight.reshape(-1, 2, HALF, weight.shape[1])
-    return jnp.concatenate([-parts[:, 1:], parts[:, :1]], 1).reshape(weight.shape)
 
 
 def from_partner(value):
@@ -945,7 +1167,6 @@
 ):
     devices = lax.axis_size("dp")
     chips = devices // 2
-    core = lax.axis_index("dp") % 2
     hidden_in = tokens[0].astype(F32)
     tok_dev = hidden_in.shape[0]
     pack_tok = tok_dev * devices
@@ -964,33 +1185,26 @@
     cos_t, sin_t = jnp.cos(angles), jnp.sin(angles)
     r = query_weight.shape[0]
 
-    def rows_of(table):
-        mine = lax.dynamic_index_in_dim(
-            table.reshape(HALF, chips, 2, tok_dev), core, axis=2, keepdims=False
-        )
-        return jnp.tile(mine.transpose(1, 2, 0), (1, 1, r // HALF))
-
-    normed = rms(hidden_in, attention_gain).astype(LOW)
-    stacked = jnp.concatenate(
-        [
-            query_weight,
-            turned_rows(query_weight),
-            key_weight,
-            turned_rows(key_weight),
-            value_weight,
-        ],
-        0,
-    )
-    qkv, normed_all = gather_project(normed, stacked, rows_of(cos_t), rows_of(sin_t))
+    qkv, normed_all, full_output = gather_project(
+        tokens[0],
+        attention_gain[None],
+        (query_weight, key_weight, value_weight),
+        output_weight,
+        cos_t,
+        sin_t,
+    )
 
     order = ring_order(chips)
     walk = [2 * chip + k for chip in order for k in (0, 1)]
     lanes = [[2 * chip + k for chip in order] for k in (0, 1)]
-    full_output = lax.all_gather(output_weight, "dp", axis=0, tiled=True, axis_index_groups=[walk])
+    full_output = full_output.reshape(-1, output_weight.shape[1])
     grad_low = cotangent[0]
-    cotangents = lax.all_gather(
-        grad_low, "dp", axis=0, tiled=True, axis_index_groups=lanes
-    ).reshape(chips, tok_dev, -1)
+    first_half, second_half = grad_low[: tok_dev // 2], grad_low[tok_dev // 2 :]
+    second_half, _ = together(second_half, qkv)
+    cotangents = [
+        lax.all_gather(part, "dp", axis=0, axis_index_groups=lanes)
+        for part in (first_half, second_half)
+    ]
     gate_other, up_other, down_other = (
         from_partner(gate_weight),
         from_partner(up_weight),
@@ -1001,9 +1215,14 @@
 
     attended, log_total = attend(first, tail, qkv)
     attended_blocks = lax.all_to_all(
-        attended.reshape(devices, tok_dev, r), "dp", split_axis=0, concat_axis=0, tiled=True
-    )
-    attended_here = jnp.concatenate([attended_blocks[i] for i in walk], 1)
+        attended.reshape(devices, tok_dev, r),
+        "dp",
+        split_axis=0,
+        concat_axis=0,
+        tiled=True,
+        axis_index_groups=[walk],
+    )
+    attended_here = attended_blocks.transpose(1, 0, 2).reshape(tok_dev, -1)
     mixed = hidden_in + dot_nn(attended_here, full_output)
     normed_two = rms(mixed, dense_gain).astype(LOW)
 
@@ -1026,59 +1245,80 @@
     grad_mixed = grad_low.astype(F32) + grad_mixed_norm
     grad_mixed_low = grad_mixed.astype(LOW)
     grad_attended = dot_nt(grad_mixed_low, full_output).astype(LOW)
-    grad_blocks = jnp.stack(
-        [grad_attended[:, walk.index(i) * r : (walk.index(i) + 1) * r] for i in range(devices)]
-    )
     grad_heads = lax.all_to_all(
-        grad_blocks, "dp", split_axis=0, concat_axis=0, tiled=True
+        grad_attended.reshape(tok_dev, devices, r).transpose(1, 0, 2),
+        "dp",
+        split_axis=0,
+        concat_axis=0,
+        tiled=True,
+        axis_index_groups=[walk],
     ).reshape(pack_tok, r)
 
+    packs, pack = lax.axis_size("rep"), lax.axis_index("rep")
+    core = lax.axis_index("dp") % 2
+    share = r // packs
+    by_share = attended_here.reshape(tok_dev, chips, 2, packs, share)
+
+    def output_rows(from_core, from_pack):
+        left = lax.dynamic_index_in_dim(by_share, from_core, axis=2, keepdims=False)
+        left = lax.dynamic_index_in_dim(left, from_pack, axis=2, keepdims=False)
+        return dot_tn(left.reshape(tok_dev, chips * share), grad_mixed_low)
+
+    others = [lax.rem(pack + k, packs) for k in range(1, packs)]
+    output_mine = (
+        output_rows(core, pack)
+        + from_partner(output_rows(1 - core, pack).astype(LOW)).astype(F32)
+    ).astype(LOW)
+    output_there = [
+        lax.ppermute(
+            (
+                output_rows(core, other)
+                + from_partner(output_rows(1 - core, other).astype(LOW)).astype(F32)
+            ).astype(LOW),
+            "rep",
+            [(i, (i + k) % packs) for i in range(packs)],
+        )
+        for k, other in enumerate(others, 1)
+    ]
     grad_heads, gate_there = together(grad_heads, gate_there)
-    up_low, _ = together(up_low, gate_there)
+    grads = attend_back(first, tail, qkv, grad_heads, attended, log_total, cos_t, sin_t)
+    grads, output_there, out_sum, up_low, down_low = together(
+        grads, output_there, out_sum, up_low, down_low
+    )
     up_there = pack_swap(up_low)
-    grads = attend_back(first, tail, qkv, grad_heads, attended, log_total, cos_t, sin_t)
-    by_core = grads.reshape(3, chips, 2, tok_dev, r)
-    swapped = from_partner(lax.dynamic_index_in_dim(by_core, 1 - core, axis=2, keepdims=False))
-    mine = lax.dynamic_index_in_dim(by_core, core, axis=2, keepdims=False)
-    normed_rows = normed_all.reshape(chips * tok_dev, -1)
-
-    def weight_part(value):
-        return lax.dot_general(
-            value.reshape(3, chips * tok_dev, r),
-            normed_rows,
-            (((1,), (0,)), ((), ())),
-            preferred_element_type=F32,
+    down_there = pack_swap(down_low)
+    output_grad = lax.psum_scatter(
+        sum((there.astype(F32) for there in output_there), output_mine.astype(F32)).astype(LOW),
+        "dp",
+        scatter_dimension=0,
+        tiled=True,
+        axis_index_groups=lanes,
+    )
+    input_grad, attention_gain_part, query_total, key_total, value_total = normed_back(
+        grads, qkv_weight, qkv_other, tokens[0], attention_gain[None], grad_mixed, normed_all
+    )
+    input_grad, out_sum, gate_there, up_there, down_there, output_grad = together(
+        input_grad, out_sum, gate_there, up_there, down_there, output_grad
+    )
+    output_total = lax.all_gather(output_grad, "rep", axis=0, tiled=True)
+    if packs == 2:
+        output_other = lax.ppermute(output_grad, "rep", [(0, 1), (1, 0)])
+        output_total = jnp.where(
+            pack == 0,
+            jnp.concatenate([output_grad, output_other], 0),
+            jnp.concatenate([output_other, output_grad], 0),
         )
-
-    qkv_there = from_partner(weight_part(swapped).astype(LOW))
-    qkv_low = (weight_part(mine) + qkv_there.astype(F32)).astype(LOW)
-
-    output_part = dot_tn(attended_here, grad_mixed_low).astype(LOW)
-    grads, output_part, out_sum, up_there = together(grads, output_part, out_sum, up_there)
-    output_grad = lax.psum_scatter(
-        output_part, "dp", scatter_dimension=0, tiled=True, axis_index_groups=[walk]
-    )
-    down_low, _ = together(down_low, up_there)
-    down_there = pack_swap(down_low)
-    qkv_other_sum = pack_swap(qkv_low)
-    input_grad, attention_gain_part = normed_back(
-        grads, qkv_weight, qkv_other, tokens[0], attention_gain[None], grad_mixed
-    )
-    input_grad, out_sum, gate_there, up_there, down_there, qkv_other_sum, output_grad = together(
-        input_grad, out_sum, gate_there, up_there, down_there, qkv_other_sum, output_grad
-    )
-    output_there = pack_swap(output_grad)
     gain_parts = jnp.stack([attention_gain_part[0], dense_gain_part])
-    gain_totals = gain_total(gain_parts.reshape(2, -1, 128)).reshape(2, -1)
+    gain_totals = gain_total(gain_parts.reshape(-1, 128)).reshape(2, -1)
     layer_out = mixed + out_sum.astype(F32)
     return (
         layer_out[None].astype(LOW),
         input_grad[None],
         gain_totals[0],
-        pack_add(qkv_low[0], qkv_other_sum[0]),
-        pack_add(qkv_low[1], qkv_other_sum[1]),
-        pack_add(qkv_low[2], qkv_other_sum[2]),
-        pack_add(output_grad, output_there),
+        query_total,
+        key_total,
+        value_total,
+        output_total.astype(F32),
         gain_totals[1],
         pack_add(gate_low, gate_there),
         pack_add(up_low, up_there),

time: 759 us -> 711 us (0.937); the launches traced: 749 us -> 710 us
  Pallas kernels: 562 us -> 516 us
  waiting for transfers between devices: 57.1 us -> 82.6 us
  local copies, waits for them, and re-layouts: 37.6 us -> 25.6 us
    pallas_call x1, Pallas kernels: 172 us -> 114 us  [gather_project(): pl.pallas_call(gather_project_kernel, out_shape=(jax.ShapeDtypeStruct((3,...]
    all_gather x2, waiting for transfers between devices: 0.02 us -> 24.9 us  [body(): lax.all_gather(part, 'dp', axis=0, axis_index_groups=lanes)]
    pallas_call x1, Pallas kernels: 112 us -> 125 us  [normed_back(): pl.pallas_call(normed_back_kernel, out_shape=(jax.ShapeDtypeStruct((rows,...]
    dot_general x2 -> x0, matrix products: 10.7 us -> none  [weight_part(): lax.dot_general(value.reshape(3, chips * tok_dev, r), normed_rows, (((1,)...]
    all_to_all x1, waiting for transfers between devices: 21.9 us -> 30.2 us  [body(): lax.all_to_all(attended.reshape(devices, tok_dev, r), 'dp', split_axis=0,...]
    unnamed x103 -> x66, local copies, waits for them, and re-layouts: 24.8 us -> 18.5 us
    add x4 -> x2, other arithmetic: 18.1 us -> 14.2 us  [pack_add(): return low.astype(F32) + other.astype(F32)]
  transfers between devices with their start and end apart: 17 -> 17, of which waited for: 4 -> 5; matrix products, arithmetic and copies ran while one was open for 11% -> 6% of each run, Pallas kernels for 51% -> 31%
where the time goes in v4:
time: 711 us; the launch traced here: 710 us
  Pallas kernels  516 us (73%)
  waiting for transfers between devices  82.6 us (12%)
  other arithmetic  32.3 us (5%)
  local copies, waits for them, and re-layouts  25.6 us (4%)
  matrix products  23.1 us (3%)
  starting transfers between devices  15.5 us (2%)
  between operations  14.2 us (2%)
    pallas_call x1, Pallas kernels, dense(): pl.pallas_call(dense_kernel, out_shape=(jax.ShapeDtypeStruct((rows, featu...  180 us
    pallas_call x1, Pallas kernels, normed_back(): pl.pallas_call(normed_back_kernel, out_shape=(jax.ShapeDtypeStruct((rows,...  125 us
    pallas_call x1, Pallas kernels, gather_project(): pl.pallas_call(gather_project_kernel, out_shape=(jax.ShapeDtypeStruct((3,...  114 us
    pallas_call x1, Pallas kernels, attend_back(): pl.pallas_call(functools.partial(attend_back_kernel, lax.axis_size('dp')...  44.2 us
    pallas_call x1, Pallas kernels, attend(): pl.pallas_call(functools.partial(attend_kernel, lax.axis_size('dp') // 2)...  38.9 us
    all_to_all x1, waiting for transfers between devices, body(): lax.all_to_all(attended.reshape(devices, tok_dev, r), 'dp', split_axis=0,...  30.2 us
    all_gather x2, waiting for transfers between devices, body(): lax.all_gather(part, 'dp', axis=0, axis_index_groups=lanes)  24.9 us
    all_to_all x1, waiting for transfers between devices, body(): lax.all_to_all(grad_attended.reshape(tok_dev, devices, r).transpose(1, 0,...  23.4 us
  transfers between devices with their start and end apart: 17, of which 5 were waited for; matrix products, arithmetic and copies ran while one was open for 6% of the time, Pallas kernels for 31%

profile of v4, /device:TPU:0, one launch (start us, length us, event | category | flops | bytes accessed | tf_op | source)
XLA Modules:
  0.0 709.7 jit_solution(18213707760060557988)
XLA Ops:
  8.4 2.3 slice_bitcast_fusion
  10.7 1.9 multiply_sine_fusion
  12.6 114.0 %gather_project.1 = (bf16[3,4096,128]{2,1,0:T(8,128)(2,1)S(1)}, bf16[8,256,2048]{2,1,0:T(8,128)(2,1)}, bf16[16,128,2048]{2,1,0:T(8,128)(2,1)}) custom-call(bf16[256,2048]{1,0:T(8,128)(2,1)S(1)} %bitcast.69, f32[1,2048]{1,0:T(1,128)S(1)} %bitcast.71, bf16[128,2048]{1,0:T(8,128)(2,1)S(1)} %copy-done, bf16[128,2048]{1,0:T(8,128)(2,1)S(1)} %copy-done.2, ...), custom_call_target="tpu_custom_call" | custom-call | flops 6442450944 | bytes 335544320 | tf_op jit(solution)/shard_map/gather_project/pallas_call | solution.py:338
  126.6 1.7 copy-done.9
  129.3 1.9 copy-done.10
  131.2 38.9 %attend.1 = (bf16[4096,128]{1,0:T(8,128)(2,1)}, f32[32,256]{1,0:T(8,128)S(1)}) custom-call(s32[32]{0:T(128)S(1)} %convert_reduce_fusion.first_ref, s32[32]{0:T(128)S(1)} %add_select_fusion.tail_ref, bf16[3,4096,128]{2,1,0:T(8,128)(2,1)S(1)} %copy-done.10), custom_call_target="tpu_custom_call" | custom-call | flops 17179869184 | bytes 125829120 | tf_op jit(solution)/shard_map/attend/pallas_call | solution.py:453
  170.1 5.3 all-to-all-start
  176.5 30.2 %all-to-all-done = bf16[16,256,128]{2,1,0:T(8,128)(2,1)} async-done(((bf16[16,256,128]{2,1,0:T(8,128)(2,1)}), bf16[16,256,128]{2,1,0:T(8,128)(2,1)}, u32[]{:S(2)}, u32[]{:S(2)}) %all-to-all-start) | async-done | bytes 1048608 | tf_op jit(solution)/shard_map/all_to_all | solution.py:1217
  206.6 5.4 multiply_reduce_fusion.2
  214.6 24.9 %all-gather.4.cloned.1.call-done.cotangents_a = bf16[8,128,2048]{2,1,0:T(8,128)(2,1)} async-done(((bf16[1,128,2048]{2,1,0:T(8,128)(2,1)}), bf16[8,128,2048]{2,1,0:T(8,128)(2,1)}) %all-gather.4.cloned.1.call-update) | async-done | bytes 4194320 | tf_op jit(solution)/shard_map/all_gather | solution.py:1205
  239.5 179.9 %dense.1 = (f32[256,2048]{1,0:T(8,128)}, bf16[8,256,2048]{2,1,0:T(8,128)(2,1)}, bf16[8,256,2048]{2,1,0:T(8,128)(2,1)}, bf16[512,2048]{1,0:T(8,128)(2,1)}, bf16[5...) custom-call(bf16[256,2048]{1,0:T(8,128)(2,1)} %multiply_convert_fusion.normed, ...), custom_call_target="tpu_custom_call" | custom-call | flops 77309411328 | bytes 524288000 | tf_op jit(solution)/shard_map/dense/pallas_call | solution.py:787
  419.5 1.5 copy.30
  421.1 1.5 copy-done.14
  422.6 2.4 multiply_reduce_fusion
  425.7 2.1 fusion.7
  427.8 2.0 convolution_convert_fusion.1
  430.6 5.8 fusion.2
  437.7 3.9 all-to-all-start.1
  441.6 3.4 convolution_convert_fusion
  445.3 2.7 fusion.9
  448.1 3.8 add_convert_fusion.2
  453.1 23.4 %all-to-all-done.1 = bf16[16,256,128]{2,1,0:T(8,128)(2,1)S(1)} async-done(((bf16[16,256,128]{2,1,0:T(8,128)(2,1)}), bf16[16,256,128]{2,1,0:T(8,128)(2,1)S(1)}, u32[]{:S(2)}, u32[]{:S(2)}) %all-to-all-start.1) | async-done | bytes 1048608 | tf_op jit(solution)/shard_map/all_to_all | solution.py:1248
  476.5 2.1 collective-permute-done.3
  478.6 1.9 copy-done.11
  480.5 44.2 %attend_back.1.grads = bf16[3,4096,128]{2,1,0:T(8,128)(2,1)S(1)} custom-call(s32[32]{0:T(128)S(1)} %convert_reduce_fusion.first_ref, s32[32]{0:T(128)S(1)} %add_select_fusion.tail_ref, bf16[3,4096,128]{2,1,0:T(8,128)(2,1)S(1)} %copy-done.11, bf16[4096,128]{1,0:T(8,128)(2,1)S(1)} %bitcast.64, bf16[4096,128]{1,0:T(8,128)(2,1)} %get-tuple-element.41.attended, ...), custom_call_target="tpu_custom_call" | custom-call | flops 42949672960 | bytes 251658240 | tf_op jit(solution)/shard_map/attend_back/pallas_call | solution.py:549
  524.7 1.7 copy-done.12
  526.4 5.9 add_convert_fusion
  538.4 125.3 %normed_back.1 = (f32[256,2048]{1,0:T(8,128)}, f32[1,2048]{1,0:T(1,128)}, f32[128,2048]{1,0:T(8,128)}, f32[128,2048]{1,0:T(8,128)}, f32[128,2048]{1,0:T(8,128)}) custom-call(bf16[3,4096,128]{2,1,0:T(8,128)(2,1)} %copy-done.12, bf16[3,128,2048]{2,1,0:T(8,128)(2,1)} %copy-done.21, bf16[3,128,2048]{2,1,0:T(8,128)(2,1)} %copy-done.28, ...), custom_call_target="tpu_custom_call" | custom-call | flops 12884901888 | bytes 335544320 | tf_op jit(solution)/shard_map/normed_back/pallas_call | solution.py:1020
  665.0 14.1 %gain_total.1 = f32[32,128]{1,0:T(8,128)} custom-call(f32[32,128]{1,0:T(8,128)} %reshape.141.part), custom_call_target="tpu_custom_call" | custom-call | tf_op jit(solution)/shard_map/gain_total/pallas_call | solution.py:1105
  679.1 1.3 slice_bitcast_fusion.1
  680.5 5.1 convert_add_fusion.2
  686.2 9.1 %convert_add_fusion = (f32[512,2048]{1,0:T(8,128)}, f32[512,2048]{1,0:T(8,128)}) fusion(bf16[512,2048]{1,0:T(8,128)(2,1)} %collective-permute-done.8, bf16[512,2048]{1,0:T(8,128)(2,1)} %get-tuple-element.57, bf16[512,2048]{1,0:T(8,128)(2,1)} %collective-permute-done.7, bf16[512,2048]{1,0:T(8,128)(2,1)} %get-tuple-element.56), kind=kLoop, calls=%fused_computation | loop fusion | flops 6291456 | bytes 16777216 | tf_op jit(solution)/shard_map/add | solution.py:1145
  (110 shorter events, 26.1 us)
Async XLA Ops:
  7.2 5.4 copy-start.8
  7.2 5.4 copy-start
  7.2 5.4 copy-start.2
  7.2 5.4 copy-start.4
  7.2 207.4 %all-gather.6.cloned.1.call-start = ((), (), s32[]{:S(2)}) async-start(), calls=%async_computation.7 | async-start | bytes 4718592 | tf_op jit(solution)/shard_map/all_gather | solution.py:1205
  7.3 5.3 copy-start.5
  7.3 5.3 copy-start.7
  12.6 116.4 %copy-start.29 = (s32[1,8]{1,0:T(1,128)S(1)}, s32[1,8]{1,0:T(1,128)}, u32[]{:S(2)}) copy-start(s32[1,8]{1,0:T(1,128)} %param.24) | copy-start | bytes 100
  12.6 116.4 %copy-start.30 = (s32[1,32]{1,0:T(1,128)S(1)}, s32[1,32]{1,0:T(1,128)}, u32[]{:S(2)}) copy-start(s32[1,32]{1,0:T(1,128)} %param.23) | copy-start | bytes 388
  128.3 111.2 %all-gather.4.cloned.1.call-start = ((), (), s32[]{:S(2)}) async-start(), calls=%async_computation.4 | async-start | bytes 4718592 | tf_op jit(solution)/shard_map/all_gather | solution.py:1205
  170.1 36.5 %copy-start.6 = (bf16[1,256,2048]{2,1,0:T(8,128)(2,1)S(1)}, bf16[1,256,2048]{2,1,0:T(8,128)(2,1)}, u32[]{:S(2)}) copy-start(bf16[1,256,2048]{2,1,0:T(8,128)(2,1)} %param.13) | copy-start | bytes 3145732
  170.1 36.5 %all-to-all-start = ((bf16[16,256,128]{2,1,0:T(8,128)(2,1)}), bf16[16,256,128]{2,1,0:T(8,128)(2,1)}, u32[]{:S(2)}, u32[]{:S(2)}) async-start(bf16[16,256,128]{2,1,0:T(8,128)(2,1)} %bitcast.6), calls=%async_computation | async-start | bytes 2097152 | tf_op jit(solution)/shard_map/all_to_all | solution.py:1217
  175.5 350.9 %reduce-scatter.3.cloned.1.call-start = ((), (), s32[]{:S(2)}) async-start(), calls=%async_computation.5 | async-start | bytes 9437184 | tf_op jit(solution)/shard_map/reduce_scatter | solution.py:1235
  175.5 39.1 %collective-permute-start = (bf16[512,2048]{1,0:T(8,128)(2,1)}, bf16[512,2048]{1,0:T(8,128)(2,1)}, u32[]{:S(2)}, u32[]{:S(2)}) collective-permute-start(bf16[512,2048]{1,0:T(8,128)(2,1)} %gate_w.1), channel_id=1, source_target_pairs={{0,2},{2,0},{4,6},{6,4},{8,10},{10,8},{12,14},{14,12},{16,18},{18,... | collective-permute-start | bytes 6291464 | tf_op jit(solution)/shard_map/ppermute | solution.py:1134
  175.9 38.6 %collective-permute-start.1 = (bf16[512,2048]{1,0:T(8,128)(2,1)}, bf16[512,2048]{1,0:T(8,128)(2,1)}, u32[]{:S(2)}, u32[]{:S(2)}) collective-permute-start(bf16[512,2048]{1,0:T(8,128)(2,1)} %up_w.1), channel_id=1, source_target_pairs={{0,2},{2,0},{4,6},{6,4},{8,10},{10,8},{12,14},{14,12},{16,18},{18,... | collective-permute-start | bytes 6291464 | tf_op jit(solution)/shard_map/ppermute | solution.py:1134
  176.1 38.5 %collective-permute-start.2 = (bf16[512,2048]{1,0:T(8,128)(2,1)}, bf16[512,2048]{1,0:T(8,128)(2,1)}, u32[]{:S(2)}, u32[]{:S(2)}) collective-permute-start(bf16[512,2048]{1,0:T(8,128)(2,1)} %down_w.1), channel_id=1, source_target_pairs={{0,2},{2,0},{4,6},{6,4},{8,10},{10,8},{12,14},{14,12},{16,18},{18,... | collective-permute-start | bytes 6291464 | tf_op jit(solution)/shard_map/ppermute | solution.py:1134
  206.6 6.7 copy-start.27
  427.8 8.6 %copy-start.16 = (bf16[256,2048]{1,0:T(8,128)(2,1)}, bf16[256,2048]{1,0:T(8,128)(2,1)S(1)}, u32[]{:S(2)}) copy-start(bf16[256,2048]{1,0:T(8,128)(2,1)S(1)} %get-tuple-element.71) | copy-start | bytes 3145732
  429.8 18.2 %collective-permute-start.4 = (bf16[512,2048]{1,0:T(8,128)(2,1)}, bf16[512,2048]{1,0:T(8,128)(2,1)}, u32[]{:S(2)}, u32[]{:S(2)}) collective-permute-start(bf16[512,2048]{1,0:T(8,128)(2,1)} %convolution_convert_fusion.1), channel_id=1, source_target_pairs={{0,2},{2,0},{4,6},{6,4},{8,10},{10,8},{12,14},{14,12},{16,18},{18,... | collective-permute-start | bytes 6291464 | tf_op jit(solution)/shard_map/ppermute | solution.py:1134
  429.8 48.7 %collective-permute-start.3 = (bf16[512,2048]{1,0:T(8,128)(2,1)}, bf16[512,2048]{1,0:T(8,128)(2,1)}, u32[]{:S(2)}, u32[]{:S(2)}) collective-permute-start(bf16[512,2048]{1,0:T(8,128)(2,1)} %get-tuple-element.45), channel_id=1, source_target_pairs={{0,1},{1,0},{2,3},{3,2},{4,5},{5,4},{6,7},{7,6},{8,9},{9,8},{10,11... | collective-permute-start | bytes 6291464 | tf_op jit(solution)/shard_map/ppermute | solution.py:1139
  437.7 38.8 %all-to-all-start.1 = ((bf16[16,256,128]{2,1,0:T(8,128)(2,1)}), bf16[16,256,128]{2,1,0:T(8,128)(2,1)S(1)}, u32[]{:S(2)}, u32[]{:S(2)}) async-start(bf16[16,256,128]{2,1,0:T(8,128)(2,1)} %bitcast.74), calls=%async_computation.1 | async-start | bytes 2097152 | tf_op jit(solution)/shard_map/all_to_all | solution.py:1248
  441.6 238.9 %reduce-scatter.5.cloned.1.call-start = ((), (), s32[]{:S(2)}) async-start(), calls=%async_computation.6 | async-start | bytes 2359296 | tf_op jit(solution)/shard_map/reduce_scatter | solution.py:1290
  441.6 3.7 copy-start.17
  445.0 81.4 %collective-permute-start.9 = (bf16[512,2048]{1,0:T(8,128)(2,1)}, bf16[512,2048]{1,0:T(8,128)(2,1)}, u32[]{:S(2)}, u32[]{:S(2)}) collective-permute-start(bf16[512,2048]{1,0:T(8,128)(2,1)} %convolution_convert_fusion), channel_id=1, source_target_pairs={{0,2},{2,0},{4,6},{6,4},{8,10},{10,8},{12,14},{14,12},{16,18},{18,... | collective-permute-start | bytes 6291464 | tf_op jit(solution)/shard_map/ppermute | solution.py:1134
  451.8 74.6 %collective-permute-start.5 = (bf16[512,2048]{1,0:T(8,128)(2,1)}, bf16[512,2048]{1,0:T(8,128)(2,1)}, u32[]{:S(2)}, u32[]{:S(2)}) collective-permute-start(bf16[512,2048]{1,0:T(8,128)(2,1)} %add_convert_fusion.2), channel_id=1, source_target_pairs={{0,1},{1,0},{2,3},{3,2},{4,5},{5,4},{6,7},{7,6},{8,9},{9,8},{10,11... | collective-permute-start | bytes 6291464 | tf_op jit(solution)/shard_map/ppermute | solution.py:1273
  533.7 3.5 collective-permute-start.6
  533.8 146.7 %collective-permute-start.7 = (bf16[512,2048]{1,0:T(8,128)(2,1)}, bf16[512,2048]{1,0:T(8,128)(2,1)}, u32[]{:S(2)}, u32[]{:S(2)}) collective-permute-start(bf16[512,2048]{1,0:T(8,128)(2,1)} %get-tuple-element.56), channel_id=1, source_target_pairs={{0,1},{1,0},{2,3},{3,2},{4,5},{5,4},{6,7},{7,6},{8,9},{9,8},{10,11... | collective-permute-start | bytes 6291464 | tf_op jit(solution)/shard_map/ppermute | solution.py:1139
  534.7 145.7 %collective-permute-start.8 = (bf16[512,2048]{1,0:T(8,128)(2,1)}, bf16[512,2048]{1,0:T(8,128)(2,1)}, u32[]{:S(2)}, u32[]{:S(2)}) collective-permute-start(bf16[512,2048]{1,0:T(8,128)(2,1)} %get-tuple-element.57), channel_id=1, source_target_pairs={{0,1},{1,0},{2,3},{3,2},{4,5},{5,4},{6,7},{7,6},{8,9},{9,8},{10,11... | collective-permute-start | bytes 6291464 | tf_op jit(solution)/shard_map/ppermute | solution.py:1139
  680.5 5.1 copy-start.26
  685.6 9.7 %copy-start.15 = (f32[256,2048]{1,0:T(8,128)S(1)}, f32[256,2048]{1,0:T(8,128)}, u32[]{:S(2)}) copy-start(f32[256,2048]{1,0:T(8,128)} %copy-done.13) | copy-start | bytes 6291460
  685.6 9.7 %copy-start.25 = (bf16[256,2048]{1,0:T(8,128)(2,1)S(1)}, bf16[256,2048]{1,0:T(8,128)(2,1)}, u32[]{:S(2)}) copy-start(bf16[256,2048]{1,0:T(8,128)(2,1)} %reduce-scatter.3.cloned.1.call-done) | copy-start | bytes 3145732
  685.6 11.0 %collective-permute-start.10 = (bf16[64,2048]{1,0:T(8,128)(2,1)S(1)}, bf16[64,2048]{1,0:T(8,128)(2,1)S(1)}, u32[]{:S(2)}, u32[]{:S(2)}) collective-permute-start(bf16[64,2048]{1,0:T(8,128)(2,1)S(1)} %copy-done.26), channel_id=1, source_target_pairs={{0,1},{1,0},{2,3},{3,2},{4,5},{5,4},{6,7},{7,6},{8,9},{9,8},{10,11... | collective-permute-start | bytes 786440 | tf_op jit(solution)/shard_map/ppermute | solution.py:1305
  (16 other events, 31.1 us)
Sparse Core Ops, SparseCore 0:
  128.4 48.2 all-gather.5
  178.8 60.6 all-gather.3
  419.6 103.7 reduce-scatter.2
  532.5 44.8 reduce-scatter.4

commit v5 on v4

--- a/solution.py
+++ b/solution.py
@@ -478,7 +478,7 @@
 
 def attend_back_kernel(
     chips, first_ref, tail_ref, qkv, grad_out, attended, log_total, cos_t, sin_t, grads,
-    key_t, grad_key, grad_value,
+    key_t, grad_key, grad_value, staged, store_sem,
 ):
     tokens, r = qkv.shape[1:]
     tok_dev = tokens // (2 * chips)
@@ -527,19 +527,25 @@
             grad_query,
         )
         turned = unrotate(join_heads(grad_query) * scale, cos_t[:, here], sin_t[:, here])
-        grads[0, here, :] = turned.T.astype(LOW)
+        staged[0, here, :] = turned.T.astype(LOW)
         return carry
 
     lax.fori_loop(0, tokens // BLOCK, block, 0)
+    query_store = pltpu.make_async_copy(staged.at[0], grads.at[0], store_sem.at[0])
+    query_store.start()
 
     def close(b, carry):
         here = pl.ds(pl.multiple_of(b * BLOCK, BLOCK), BLOCK)
         turned = unrotate(grad_key[here, :].T * scale, cos_t[:, here], sin_t[:, here])
-        grads[1, here, :] = turned.T.astype(LOW)
-        grads[2, here, :] = grad_value[here, :].astype(LOW)
+        staged[1, here, :] = turned.T.astype(LOW)
+        staged[2, here, :] = grad_value[here, :].astype(LOW)
         return carry
 
     lax.fori_loop(0, tokens // BLOCK, close, 0)
+    rest_store = pltpu.make_async_copy(staged.at[pl.ds(1, 2)], grads.at[pl.ds(1, 2)], store_sem.at[1])
+    rest_store.start()
+    query_store.wait()
+    rest_store.wait()
 
 
 def attend_back(first, tail, qkv, grad_out, attended, log_total, cos_t, sin_t):
@@ -550,11 +556,13 @@
         functools.partial(attend_back_kernel, lax.axis_size("dp") // 2),
         out_shape=jax.ShapeDtypeStruct((3, tokens, r), LOW),
         in_specs=[smem, smem] + [vmem] * 6,
-        out_specs=vmem,
+        out_specs=pl.BlockSpec(memory_space=pl.ANY),
         scratch_shapes=[
             pltpu.VMEM((r, tokens), LOW),
             pltpu.VMEM((tokens, r), F32),
             pltpu.VMEM((tokens, r), F32),
+            pltpu.VMEM((3, tokens, r), LOW),
+            pltpu.SemaphoreType.DMA((2,)),
         ],
         compiler_params=pltpu.CompilerParams(vmem_limit_bytes=40 * MIB),
         cost_estimate=pl.CostEstimate(
@@ -566,7 +574,7 @@
 
 def dense_kernel(
     normed, cotangents_a, cotangents_b, gate_w, up_w, down_w, gate_p, up_p, down_p,
-    grad_sum, out_parts, gathered, gate_grad, up_grad, down_grad,
+    grad_sum, out_parts, gathered, gate_grad, up_a, up_b, down_grad,
     weights, totals, x_buf, g_buf, out_acc, grad_acc, sent, landed, cast_buf, pair_land,
     ag_send, ag_recv, rs_send, rs_recv, credit, local_sem, w_sem, cast_sem, pair_send, pair_recv,
 ):
@@ -574,6 +582,7 @@
     n = ring.chips
     rows, features = normed.shape
     half = rows // 2
+    early = cotangents_a.shape[1]
     own = gate_w.shape[0]
     tiles = 2 * own // FF_TILE
     loads = []
@@ -615,13 +624,21 @@
         )
 
     def step(t, carry):
-        copies = []
-        for d in (0, 1):
-            part = half_rows(d, rows)
-            copies.append(
-                pltpu.make_async_copy((cotangents_a, cotangents_b)[d].at[source(t, d)], g_buf.at[part], local_sem.at[d])
-            )
-            copies[-1].start()
+        copies = [
+            pltpu.make_async_copy(cotangents_a.at[source(t, 0)], g_buf.at[pl.ds(0, early)], local_sem.at[0]),
+            pltpu.make_async_copy(
+                cotangents_b.at[source(t, 0), pl.ds(0, half - early)],
+                g_buf.at[pl.ds(early, half - early)],
+                local_sem.at[1],
+            ),
+            pltpu.make_async_copy(
+                cotangents_b.at[source(t, 1), pl.ds(half - early, half)],
+                g_buf.at[pl.ds(half, half)],
+                local_sem.at[4],
+            ),
+        ]
+        for copy in copies:
+            copy.start()
 
         @pl.when(t > 0)
         def _():
@@ -745,18 +762,34 @@
     for i in (own_tiles - 2, own_tiles - 1):
         pair_copy(i).wait_send()
 
-    def total_copy(i):
-        target = (gate_grad, up_grad, down_grad)[i // (own // FF_TILE)]
-        span = pl.ds((i % (own // FF_TILE)) * FF_TILE, FF_TILE)
-        return pltpu.make_async_copy(cast_buf.at[i % 2], target.at[span], cast_sem.at[i % 2, 0])
+    pieces = ((gate_grad,), (up_a, up_b), (down_grad,))
+
+    def total_copies(i):
+        matrix, low = i // (own // FF_TILE), (i % (own // FF_TILE)) * FF_TILE
+        copies, begin = [], 0
+        for piece in pieces[matrix]:
+            end = begin + piece.shape[0]
+            first, last = max(begin, low), min(end, low + FF_TILE)
+            if first < last:
+                copies.append(
+                    pltpu.make_async_copy(
+                        cast_buf.at[i % 2, pl.ds(first - low, last - first)],
+                        piece.at[pl.ds(first - begin, last - first)],
+                        cast_sem.at[i % 2, len(copies)],
+                    )
+                )
+            begin = end
+        return copies
 
     for i in range(own_tiles):
         if i >= 2:
-            total_copy(i - 2).wait()
+            for copy in total_copies(i - 2):
+                copy.wait()
         pair_copy(i).wait_recv()
         k, span = tile_of(i, 0)
         cast_buf[i % 2] = (totals[k, span, :] + pair_land[i].astype(F32)).astype(LOW)
-        total_copy(i).start()
+        for copy in total_copies(i):
+            copy.start()
 
     for d in (0, 1):
         part = pl.ds(d * half, half)
@@ -765,7 +798,8 @@
         reduce_copy(n - 1, d).wait_send()
 
     for i in (own_tiles - 2, own_tiles - 1):
-        total_copy(i).wait()
+        for copy in total_copies(i):
+            copy.wait()
 
     def finish(t, carry):
         for d in (0, 1):
@@ -791,11 +825,12 @@
             jax.ShapeDtypeStruct((n, rows, features), LOW),
             jax.ShapeDtypeStruct((n, rows, features), LOW),
             jax.ShapeDtypeStruct((own, features), LOW),
-            jax.ShapeDtypeStruct((own, features), LOW),
+            jax.ShapeDtypeStruct((own // 8, features), LOW),
+            jax.ShapeDtypeStruct((own - own // 8, features), LOW),
             jax.ShapeDtypeStruct((own, features), LOW),
         ),
         in_specs=[vmem] + [hbm] * 8,
-        out_specs=(vmem,) + (hbm,) * 5,
+        out_specs=(vmem,) + (hbm,) * 6,
         scratch_shapes=[
             pltpu.VMEM((3, 2 * own, features), LOW),
             pltpu.VMEM((3, 2 * own, features), F32),
@@ -809,7 +844,7 @@
             pltpu.VMEM((own_tiles, FF_TILE, features), LOW),
             dma((2, n)), dma((2, n)), dma((2,)), dma((2, 2)),
             pltpu.SemaphoreType.REGULAR((2,)),
-            dma((4,)), dma((6,)), dma((2, 2)), dma((2,)), dma((own_tiles,)),
+            dma((5,)), dma((6,)), dma((2, 2)), dma((2,)), dma((own_tiles,)),
         ],
         compiler_params=pltpu.CompilerParams(
             collective_id=2, has_side_effects=True, vmem_limit_bytes=62 * MIB
@@ -821,26 +856,189 @@
     )(normed, *cotangents, *own_weights, *partner_weights)
 
 
+def mixed_back_kernel(
+    packs, mixed_in, grad_in, cotangent_in, gain, output_all, shares, grad_mixed, gain_part, grad_heads, *rest
+):
+    sums = rest[:packs]
+    mixed, grad_two, cotangent, low, weights, staged, given, taken, sem, w_sem, send_sem, recv_sem, g_sem, t_sem = (
+        rest[packs:]
+    )
+    ring = Ring()
+    n = ring.chips
+    devices = 2 * n
+    rows, features = mixed.shape
+    r = grad_heads.shape[1]
+    pack = lax.axis_index("rep")
+    spot = ring.place * 2 + ring.core
+    loads = [
+        pltpu.make_async_copy(src, dst, sem.at[i])
+        for i, (src, dst) in enumerate(((mixed_in, mixed), (grad_in, grad_two), (cotangent_in, cotangent)))
+    ]
+    for load in loads:
+        load.start()
+
+    def chip_weights(k):
+        at = lax.rem(ring.place + k, n) * 2
+        return pltpu.make_async_copy(output_all.at[pl.ds(at, 2)], weights.at[pl.ds(2 * k, 2)], w_sem.at[k])
+
+    def fetch(k, carry):
+        chip_weights(k).start()
+        return carry
+
+    lax.fori_loop(0, n, fetch, 0)
+    barrier = pltpu.get_barrier_semaphore()
+
+    def to(k):
+        other = lax.rem(spot + k, devices)
+        return {"dp": chip_at(other // 2, n) * 2 + other % 2}
+
+    def greet(k, carry):
+        pl.semaphore_signal(barrier, inc=1, device_id=to(k), device_id_type=MESH)
+        return carry
+
+    lax.fori_loop(1, devices, greet, 0)
+    pl.semaphore_wait(barrier, devices - 1)
+    for load in loads:
+        load.wait()
+    gain_part[...] = jnp.zeros_like(gain_part)
+
+    def norm_back(i, carry):
+        span = pl.ds(pl.multiple_of(i * 16, 16), 16)
+        value, grad = mixed[span, :], grad_two[span, :]
+        scale = lax.rsqrt(jnp.mean(value * value, axis=1, keepdims=True) + EPSILON)
+        scaled = grad * gain[...]
+        shift = jnp.mean(value * scaled, axis=1, keepdims=True)
+        total = cotangent[span, :].astype(F32) + scale * scaled - value * (scale * scale * scale * shift)
+        grad_mixed[span, :] = total
+        low[span, :] = total.astype(LOW)
+        gain_part[...] += jnp.sum(grad * value * scale, axis=0, keepdims=True)
+        return carry
+
+    lax.fori_loop(0, rows // 16, norm_back, 0)
+
+    def copy(k):
+        return remote(
+            staged.at[k],
+            grad_heads.at[pl.ds(pl.multiple_of(spot * rows, rows), rows)],
+            send_sem.at[k],
+            recv_sem.at[k],
+            to(k)["dp"],
+        )
+
+    def project(k, carry):
+        chip_weights(k).wait()
+        both = dot_nt(low[...], weights[pl.ds(2 * k, 2)].reshape(2 * r, features))
+        for core in (0, 1):
+            step = lax.rem(2 * k + core - ring.core + devices, devices)
+            staged[step] = both[:, core * r : (core + 1) * r].astype(LOW)
+
+            @pl.when(step > 0)
+            def _():
+                copy(step).start()
+
+        return carry
+
+    lax.fori_loop(0, n, project, 0)
+    grad_heads[pl.ds(pl.multiple_of(spot * rows, rows), rows), :] = staged[0]
+
+    def give(k):
+        return remote(given.at[k], taken.at[k], g_sem.at[k], t_sem.at[k], ring.partner)
+
+    for k in range(packs):
+        given[k] = dot_tn(shares[1 - ring.core, lax.rem(pack + k, packs)], low[...]).astype(LOW)
+        give(k).start()
+    for k in range(packs):
+        own = dot_tn(shares[ring.core, lax.rem(pack + k, packs)], low[...])
+        give(k).wait_recv()
+        sums[k][...] = (own + taken[k].astype(F32)).astype(LOW)
+
+    def finish(k, carry):
+        copy(k).wait_send()
+        copy(k).wait_recv()
+        return carry
+
+    lax.fori_loop(1, devices, finish, 0)
+    for k in range(packs):
+        give(k).wait_send()
+
+
+def mixed_back(mixed, grad_two, cotangent, gain, output_all, shares):
+    rows, features = mixed.shape
+    devices, r = output_all.shape[:2]
+    packs = lax.axis_size("rep")
+    n = devices // 2
+    total = shares.shape[3]
+    vmem = pl.BlockSpec(memory_space=pltpu.VMEM)
+    hbm = pl.BlockSpec(memory_space=pl.ANY)
+    dma = pltpu.SemaphoreType.DMA
+    return pl.pallas_call(
+        functools.partial(mixed_back_kernel, packs),
+        out_shape=(
+            jax.ShapeDtypeStruct((rows, features), F32),
+            jax.ShapeDtypeStruct((1, features), F32),
+            jax.ShapeDtypeStruct((devices * rows, r), LOW),
+        )
+        + (jax.ShapeDtypeStruct((total, features), LOW),) * packs,
+        in_specs=[hbm] * 3 + [vmem, hbm, vmem],
+        out_specs=(vmem,) * (3 + packs),
+        scratch_shapes=[
+            pltpu.VMEM((rows, features), F32),
+            pltpu.VMEM((rows, features), F32),
+            pltpu.VMEM((rows, features), LOW),
+            pltpu.VMEM((rows, features), LOW),
+            pltpu.VMEM((devices, r, features), LOW),
+            pltpu.VMEM((devices, rows, r), LOW),
+            pltpu.VMEM((packs, total, features), LOW),
+            pltpu.VMEM((packs, total, features), LOW),
+            dma((3,)), dma((n,)), dma((devices,)), dma((devices,)), dma((packs,)), dma((packs,)),
+        ],
+        compiler_params=pltpu.CompilerParams(
+            collective_id=4, has_side_effects=True, vmem_limit_bytes=56 * MIB
+        ),
+        cost_estimate=pl.CostEstimate(
+            flops=4 * rows * features * features, bytes_accessed=130 * MIB, transcendentals=0
+        ),
+        name="mixed_back",
+    )(mixed, grad_two, cotangent, gain, output_all, shares)
+
+
 def normed_back_kernel(
-    grads, weights, partner_weights, hidden_in, gain, grad_mixed, normed_all,
-    out, gain_part, query_total, key_total, value_total,
-    partner_grads, sent, landed, x_buf, parts, joined, pair_out, pair_land, rep_land,
-    p_send, p_recv, rs_send, rs_recv, credit, x_sem, pair_sem, rep_send, rep_recv,
+    packs, grads_in, joined, hidden_in, gain, grad_mixed, dense_gain_part, normed_all, output_mine, *rest
 ):
+    output_there = rest[: packs - 1]
+    (
+        out, gains, query_total, key_total, value_total, output_grad,
+        grads, partner_grads, sent, landed, x_buf, parts, pair_out, pair_land, rep_land,
+        o_sent, o_landed, near_part, near_land, near_sum, far_land,
+        in_sem, p_send, p_recv, rs_send, rs_recv, credit, x_sem, pair_sem, rep_send, rep_recv,
+        o_send, o_recv, o_credit, near_send, near_recv, far_send, far_recv,
+    ) = rest[packs - 1 :]
     ring = Ring()
     n = ring.chips
     rows, features = out.shape
     half = rows // 2
     r = grads.shape[2]
-    packs, pack = lax.axis_size("rep"), lax.axis_index("rep")
+    share = output_grad.shape[0]
+    pack = lax.axis_index("rep")
+    mates = 2 * packs
+    mate = pack * 2 + ring.core
     barrier = pltpu.get_barrier_semaphore()
-    for k in range(1, packs):
-        pl.semaphore_signal(
-            barrier, inc=1, device_id={"rep": lax.rem(pack + k, packs)}, device_id_type=MESH
-        )
-    for other in (ring.next[0], ring.next[1], ring.partner):
-        pl.semaphore_signal(barrier, inc=1, device_id={"dp": other}, device_id_type=MESH)
-    pl.semaphore_wait(barrier, 3 + packs - 1)
+    load_grads = pltpu.make_async_copy(grads_in, grads, in_sem)
+    load_grads.start()
+
+    def near(k):
+        to = lax.rem(mate + k, mates)
+        return {"dp": ring.chip * 2 + to % 2, "rep": to // 2}
+
+    def far(k):
+        return {"dp": lax.rem(ring.chip + k, n) * 2 + ring.core}
+
+    for k in range(1, mates):
+        pl.semaphore_signal(barrier, inc=1, device_id=near(k), device_id_type=MESH)
+    for k in range(1, n):
+        pl.semaphore_signal(barrier, inc=1, device_id=far(k), device_id_type=MESH)
+    pl.semaphore_wait(barrier, mates + n - 2)
+    load_grads.wait()
 
     def place(t, d):
         return ring.chip_far(-t if d == 0 else t)
@@ -862,8 +1060,22 @@
 
     lax.fori_loop(1, n + 1, begin, 0)
 
-    def reduce_copy(t, d):
-        return remote(sent.at[d], landed.at[d, t % 2], rs_send.at[d], rs_recv.at[d, t % 2], ring.next[d])
+    def reduce_copy(t, d, u):
+        return remote(
+            sent.at[d, u],
+            landed.at[d, u, t % 2],
+            rs_send.at[d, u],
+            rs_recv.at[d, u, t % 2],
+            ring.next[d],
+        )
+
+    def output_copy(t, d):
+        return remote(
+            o_sent.at[d], o_landed.at[d, t % 2], o_send.at[d], o_recv.at[d, t % 2], ring.next[d]
+        )
+
+    def give_credit(sem, d):
+        pl.semaphore_signal(sem, inc=1, device_id={"dp": ring.back[d]}, device_id_type=MESH)
 
     def mine(t, d):
         start = (place(t, d) * 2 + ring.core) * rows + d * half
@@ -898,11 +1110,46 @@
             device_id_type=MESH,
         )
 
-    parts[...] = jnp.zeros_like(parts)
-    for i in range(3):
-        joined[pl.ds(i * r, r), :] = weights[i]
-        joined[pl.ds((3 + i) * r, r), :] = partner_weights[i]
     middle = n // 2
+
+    def output_step(t):
+        for d in (0, 1):
+            spot = lax.rem(ring.place + (n - t if d == 0 else t), n)
+            at = pl.ds(pl.multiple_of(spot * share, share), share)
+            columns = pl.ds(d * (features // 2), features // 2)
+            total = output_mine[at, columns].astype(F32)
+            for there in output_there:
+                total += there[at, columns].astype(F32)
+
+            @pl.when(t == 1)
+            def _():
+                o_sent[d] = total.astype(LOW)
+                output_copy(t, d).start()
+
+            @pl.when(t >= 2)
+            def _():
+                output_copy(t - 1, d).wait_recv()
+                more = total + o_landed[d, (t - 1) % 2].astype(F32)
+
+                @pl.when(t <= n - 2)
+                def _():
+                    give_credit(o_credit.at[d], d)
+
+                output_copy(t - 1, d).wait_send()
+
+                @pl.when(t < n)
+                def _():
+                    o_sent[d] = more.astype(LOW)
+
+                    @pl.when(t >= 3)
+                    def _():
+                        pl.semaphore_wait(o_credit.at[d], 1)
+
+                    output_copy(t, d).start()
+
+                @pl.when(t == n)
+                def _():
+                    output_grad[:, columns] = more.astype(LOW)
 
     def step(t, carry):
         @pl.when(t <= middle)
@@ -916,36 +1163,40 @@
             for d in (0, 1):
                 swap(t, d).wait_recv()
 
-        out[...] = dot_nn(block_grads(t), joined[...])
-
-        for d in (0, 1):
-            part = pl.ds(d * half, half)
-
-            @pl.when(t >= 2)
-            def _():
-                reduce_copy(t - 1, d).wait_recv()
-                out[part, :] += landed[d, (t - 1) % 2].astype(F32)
-
-                @pl.when(t <= n - 2)
+        block = block_grads(t)
+        for u in (0, 1):
+            columns = pl.ds(u * (features // 2), features // 2)
+            out[:, columns] = dot_nn(block, joined[:, columns])
+            for d in (0, 1):
+                part = pl.ds(d * half, half), columns
+
+                @pl.when(t >= 2)
                 def _():
-                    pl.semaphore_signal(
-                        credit.at[d], inc=1, device_id={"dp": ring.back[d]}, device_id_type=MESH
-                    )
-
-                reduce_copy(t - 1, d).wait_send()
-
-            @pl.when(t < n)
-            def _():
-                sent[d] = out[part, :].astype(LOW)
-
-                @pl.when(t >= 3)
+                    reduce_copy(t - 1, d, u).wait_recv()
+                    out[part] += landed[d, u, (t - 1) % 2].astype(F32)
+
+                    @pl.when(t <= n - 2)
+                    def _():
+                        give_credit(credit.at[d, u], d)
+
+                    reduce_copy(t - 1, d, u).wait_send()
+
+                @pl.when(t < n)
                 def _():
-                    pl.semaphore_wait(credit.at[d], 1)
-
-                reduce_copy(t, d).start()
+                    sent[d, u] = out[part].astype(LOW)
+
+                    @pl.when(t >= 3)
+                    def _():
+                        pl.semaphore_wait(credit.at[d, u], 1)
+
+                    reduce_copy(t, d, u).start()
+
+        output_step(t)
 
         @pl.when(t == 1)
         def _():
+            parts[...] = jnp.zeros_like(parts)
+
             def arrived(k, carry):
                 for d in (0, 1):
                     swap(k, d).wait_recv()
@@ -977,7 +1228,8 @@
 
     lax.fori_loop(1, n + 1, step, 0)
 
-    gain_part[...] = jnp.zeros_like(gain_part)
+    near_part[0:1, :] = jnp.zeros((1, features), F32)
+    near_part[1:2, :] = dense_gain_part[...]
 
     def close(i, carry):
         span = pl.ds(pl.multiple_of(i * 16, 16), 16)
@@ -987,96 +1239,16 @@
         scaled = grad * gain[...]
         shift = jnp.mean(value * scaled, axis=1, keepdims=True)
         out[span, :] = grad_mixed[span, :] + scale * scaled - value * (scale * scale * scale * shift)
-        gain_part[...] += jnp.sum(grad * value * scale, axis=0, keepdims=True)
+        near_part[0:1, :] += jnp.sum(grad * value * scale, axis=0, keepdims=True)
         return carry
 
     lax.fori_loop(0, rows // 16, close, 0)
 
-    def finish(t, carry):
-        for d in (0, 1):
-            swap(t, d).wait_send()
-        return carry
-
-    lax.fori_loop(1, n + 1, finish, 0)
-    for k in range(1, packs):
-        rep_copy(k).wait()
-    for i, total in enumerate((query_total, key_total, value_total)):
-        value = rep_land[lax.rem(pack + packs - 1, packs), i].astype(F32)
-        for q in range(1, packs):
-            value += rep_land[lax.rem(pack + 2 * packs - q - 1, packs), i].astype(F32)
-        total[...] = value
-
-
-def normed_back(grads, weights, partner_weights, hidden_in, gain, grad_mixed, normed_all):
-    tokens, r = grads.shape[1:]
-    features = weights.shape[2]
-    devices = lax.axis_size("dp")
-    packs = lax.axis_size("rep")
-    n = devices // 2
-    rows = tokens // devices
-    half = rows // 2
-    vmem = pl.BlockSpec(memory_space=pltpu.VMEM)
-    dma = pltpu.SemaphoreType.DMA
-    return pl.pallas_call(
-        normed_back_kernel,
-        out_shape=(
-            jax.ShapeDtypeStruct((rows, features), F32),
-            jax.ShapeDtypeStruct((1, features), F32),
-        )
-        + (jax.ShapeDtypeStruct((r, features), F32),) * 3,
-        in_specs=[vmem] * 6 + [pl.BlockSpec(memory_space=pl.ANY)],
-        out_specs=(vmem,) * 5,
-        scratch_shapes=[
-            pltpu.VMEM((3, n, rows, r), LOW),
-            pltpu.VMEM((2, half, features), LOW),
-            pltpu.VMEM((2, 2, half, features), LOW),
-            pltpu.VMEM((2, rows, features), LOW),
-            pltpu.VMEM((6 * r, features), F32),
-            pltpu.VMEM((6 * r, features), LOW),
-            pltpu.VMEM((3, r, features), LOW),
-            pltpu.VMEM((3, r, features), LOW),
-            pltpu.VMEM((packs, 3, r, features), LOW),
-            dma((2, n)), dma((2, n)), dma((2,)), dma((2, 2)),
-            pltpu.SemaphoreType.REGULAR((2,)),
-            dma((2, 2)), dma((2,)), dma((packs - 1,)), dma((packs - 1,)),
-        ],
-        compiler_params=pltpu.CompilerParams(
-            collective_id=3, has_side_effects=True, vmem_limit_bytes=56 * MIB
-        ),
-        cost_estimate=pl.CostEstimate(
-            flops=2 * n * rows * features * 12 * r, bytes_accessed=320 * MIB, transcendentals=0
-        ),
-        name="normed_back",
-    )(grads, weights, partner_weights, hidden_in, gain, grad_mixed, normed_all)
-
-
-def gain_total_kernel(part, out, near_land, near_sum, far_land, near_send, near_recv, far_send, far_recv):
-    packs = lax.axis_size("rep")
-    chips = lax.axis_size("dp") // 2
-    mates = 2 * packs
-    me, pack = lax.axis_index("dp"), lax.axis_index("rep")
-    core, chip = me % 2, me // 2
-    mate = pack * 2 + core
-    barrier = pltpu.get_barrier_semaphore()
-
-    def near(k):
-        to = lax.rem(mate + k, mates)
-        return {"dp": chip * 2 + to % 2, "rep": to // 2}
-
-    def far(k):
-        return {"dp": lax.rem(chip + k, chips) * 2 + core}
-
-    for k in range(1, mates):
-        pl.semaphore_signal(barrier, inc=1, device_id=near(k), device_id_type=MESH)
-    for k in range(1, chips):
-        pl.semaphore_signal(barrier, inc=1, device_id=far(k), device_id_type=MESH)
-    pl.semaphore_wait(barrier, mates + chips - 2)
-
-    def exchange(src, landed, own, send_sem, recv_sem, device, count):
+    def exchange(src, land, own, send_sem, recv_sem, device, count):
         copies = [
             pltpu.make_async_remote_copy(
                 src_ref=src,
-                dst_ref=landed.at[own],
+                dst_ref=land.at[own],
                 send_sem=send_sem.at[k],
                 recv_sem=recv_sem.at[k],
                 device_id=device(k),
@@ -1086,47 +1258,95 @@
         ]
         for copy in copies:
             copy.start()
-        landed[own] = src[...]
+        land[own] = src[...]
         for copy in copies:
             copy.wait()
-        total = landed[0]
+        total = land[0]
         for k in range(1, count):
-            total += landed[k]
+            total += land[k]
         return total
 
-    near_sum[...] = exchange(part, near_land, mate, near_send, near_recv, near, mates)
-    out[...] = exchange(near_sum, far_land, chip, far_send, far_recv, far, chips)
-
-
-def gain_total(part):
-    mates, chips = 2 * lax.axis_size("rep"), lax.axis_size("dp") // 2
+    near_sum[...] = exchange(near_part, near_land, mate, near_send, near_recv, near, mates)
+    gains[...] = exchange(near_sum, far_land, ring.chip, far_send, far_recv, far, n)
+
+    def finish(t, carry):
+        for d in (0, 1):
+            swap(t, d).wait_send()
+        return carry
+
+    lax.fori_loop(1, n + 1, finish, 0)
+    for k in range(1, packs):
+        rep_copy(k).wait()
+    for i, total in enumerate((query_total, key_total, value_total)):
+        value = rep_land[lax.rem(pack + packs - 1, packs), i].astype(F32)
+        for q in range(1, packs):
+            value += rep_land[lax.rem(pack + 2 * packs - q - 1, packs), i].astype(F32)
+        total[...] = value
+
+
+def normed_back(
+    grads, joined, hidden_in, gain, grad_mixed, dense_gain_part, normed_all, output_mine, output_there
+):
+    tokens, r = grads.shape[1:]
+    features = joined.shape[1]
+    devices = lax.axis_size("dp")
+    packs = lax.axis_size("rep")
+    n = devices // 2
+    rows = tokens // devices
+    half = rows // 2
+    share = output_mine.shape[0] // n
+    mates = 2 * packs
     vmem = pl.BlockSpec(memory_space=pltpu.VMEM)
+    hbm = pl.BlockSpec(memory_space=pl.ANY)
     dma = pltpu.SemaphoreType.DMA
     return pl.pallas_call(
-        gain_total_kernel,
-        out_shape=jax.ShapeDtypeStruct(part.shape, F32),
-        in_specs=[vmem],
-        out_specs=vmem,
+        functools.partial(normed_back_kernel, packs),
+        out_shape=(
+            jax.ShapeDtypeStruct((rows, features), F32),
+            jax.ShapeDtypeStruct((2, features), F32),
+        )
+        + (jax.ShapeDtypeStruct((r, features), F32),) * 3
+        + (jax.ShapeDtypeStruct((share, features), LOW),),
+        in_specs=[hbm] + [vmem] * 5 + [hbm] + [vmem] * packs,
+        out_specs=(vmem,) * 6,
         scratch_shapes=[
-            pltpu.VMEM((mates,) + part.shape, F32),
-            pltpu.VMEM(part.shape, F32),
-            pltpu.VMEM((chips,) + part.shape, F32),
-            dma((mates,)), dma((mates,)), dma((chips,)), dma((chips,)),
+            pltpu.VMEM(grads.shape, LOW),
+            pltpu.VMEM((3, n, rows, r), LOW),
+            pltpu.VMEM((2, 2, half, features // 2), LOW),
+            pltpu.VMEM((2, 2, 2, half, features // 2), LOW),
+            pltpu.VMEM((2, rows, features), LOW),
+            pltpu.VMEM((6 * r, features), F32),
+            pltpu.VMEM((3, r, features), LOW),
+            pltpu.VMEM((3, r, features), LOW),
+            pltpu.VMEM((packs, 3, r, features), LOW),
+            pltpu.VMEM((2, share, features // 2), LOW),
+            pltpu.VMEM((2, 2, share, features // 2), LOW),
+            pltpu.VMEM((2, features), F32),
+            pltpu.VMEM((mates, 2, features), F32),
+            pltpu.VMEM((2, features), F32),
+            pltpu.VMEM((n, 2, features), F32),
+            dma, dma((2, n)), dma((2, n)), dma((2, 2)), dma((2, 2, 2)),
+            pltpu.SemaphoreType.REGULAR((2, 2)),
+            dma((2, 2)), dma((2,)), dma((packs - 1,)), dma((packs - 1,)),
+            dma((2,)), dma((2, 2)), pltpu.SemaphoreType.REGULAR((2,)),
+            dma((mates,)), dma((mates,)), dma((n,)), dma((n,)),
         ],
-        compiler_params=pltpu.CompilerParams(collective_id=4, has_side_effects=True),
-        name="gain_total",
-    )(part)
+        compiler_params=pltpu.CompilerParams(
+            collective_id=3, has_side_effects=True, vmem_limit_bytes=56 * MIB
+        ),
+        cost_estimate=pl.CostEstimate(
+            flops=2 * n * rows * features * 12 * r, bytes_accessed=320 * MIB, transcendentals=0
+        ),
+        name="normed_back",
+    )(
+        grads, joined, hidden_in, gain, grad_mixed, dense_gain_part, normed_all, output_mine, *output_there
+    )
 
 
 def rms(values, norm_gain):
     return (
         values * lax.rsqrt(jnp.mean(values * values, axis=-1, keepdims=True) + EPSILON) * norm_gain
     )
-
-
-def rms_back(values, norm_gain, grads):
-    _, pullback = jax.vjp(rms, values, norm_gain)
-    return pullback(grads)
 
 
 def from_partner(value):
@@ -1197,21 +1417,18 @@
     order = ring_order(chips)
     walk = [2 * chip + k for chip in order for k in (0, 1)]
     lanes = [[2 * chip + k for chip in order] for k in (0, 1)]
-    full_output = full_output.reshape(-1, output_weight.shape[1])
     grad_low = cotangent[0]
-    first_half, second_half = grad_low[: tok_dev // 2], grad_low[tok_dev // 2 :]
-    second_half, _ = together(second_half, qkv)
-    cotangents = [
-        lax.all_gather(part, "dp", axis=0, axis_index_groups=lanes)
-        for part in (first_half, second_half)
-    ]
+    early, late = grad_low[: tok_dev // 4], grad_low[tok_dev // 4 :]
+    early = lax.all_gather(early, "dp", axis=0, axis_index_groups=lanes)
+    qkv, early, late = together(qkv, early, late)
+    cotangents = (early, lax.all_gather(late, "dp", axis=0, axis_index_groups=lanes))
     gate_other, up_other, down_other = (
         from_partner(gate_weight),
         from_partner(up_weight),
         from_partner(down_weight),
     )
-    qkv_weight = jnp.stack([query_weight, key_weight, value_weight])
-    qkv_other = from_partner(qkv_weight)
+    qkv_weight = jnp.concatenate([query_weight, key_weight, value_weight], 0)
+    joined = jnp.concatenate([qkv_weight, from_partner(qkv_weight)], 0)
 
     attended, log_total = attend(first, tail, qkv)
     attended_blocks = lax.all_to_all(
@@ -1223,10 +1440,18 @@
         axis_index_groups=[walk],
     )
     attended_here = attended_blocks.transpose(1, 0, 2).reshape(tok_dev, -1)
-    mixed = hidden_in + dot_nn(attended_here, full_output)
+    mixed = hidden_in + dot_nn(attended_here, full_output.reshape(-1, output_weight.shape[1]))
     normed_two = rms(mixed, dense_gain).astype(LOW)
 
-    grad_normed_two, out_parts, _, gate_low, up_low, down_low = dense(
+    packs, pack = lax.axis_size("rep"), lax.axis_index("rep")
+    attended_shares = (
+        attended_here.reshape(tok_dev, chips, 2, packs, r // packs)
+        .transpose(2, 3, 0, 1, 4)
+        .reshape(2, packs, tok_dev, -1)
+    )
+    normed_two, joined, attended_shares = together(normed_two, joined, attended_shares)
+
+    grad_normed_two, out_parts, _, gate_low, up_a, up_b, down_low = dense(
         normed_two,
         cotangents,
         (gate_weight, up_weight, down_weight),
@@ -1241,51 +1466,23 @@
     )
     gate_there = pack_swap(gate_low)
 
-    grad_mixed_norm, dense_gain_part = rms_back(mixed, dense_gain, grad_normed_two)
-    grad_mixed = grad_low.astype(F32) + grad_mixed_norm
-    grad_mixed_low = grad_mixed.astype(LOW)
-    grad_attended = dot_nt(grad_mixed_low, full_output).astype(LOW)
-    grad_heads = lax.all_to_all(
-        grad_attended.reshape(tok_dev, devices, r).transpose(1, 0, 2),
-        "dp",
-        split_axis=0,
-        concat_axis=0,
-        tiled=True,
-        axis_index_groups=[walk],
-    ).reshape(pack_tok, r)
-
-    packs, pack = lax.axis_size("rep"), lax.axis_index("rep")
-    core = lax.axis_index("dp") % 2
-    share = r // packs
-    by_share = attended_here.reshape(tok_dev, chips, 2, packs, share)
-
-    def output_rows(from_core, from_pack):
-        left = lax.dynamic_index_in_dim(by_share, from_core, axis=2, keepdims=False)
-        left = lax.dynamic_index_in_dim(left, from_pack, axis=2, keepdims=False)
-        return dot_tn(left.reshape(tok_dev, chips * share), grad_mixed_low)
-
-    others = [lax.rem(pack + k, packs) for k in range(1, packs)]
-    output_mine = (
-        output_rows(core, pack)
-        + from_partner(output_rows(1 - core, pack).astype(LOW)).astype(F32)
-    ).astype(LOW)
+    grad_mixed, dense_gain_part, grad_heads, output_mine, *output_low = mixed_back(
+        mixed, grad_normed_two, grad_low, dense_gain[None], full_output, attended_shares
+    )
     output_there = [
-        lax.ppermute(
-            (
-                output_rows(core, other)
-                + from_partner(output_rows(1 - core, other).astype(LOW)).astype(F32)
-            ).astype(LOW),
-            "rep",
-            [(i, (i + k) % packs) for i in range(packs)],
-        )
-        for k, other in enumerate(others, 1)
+        lax.ppermute(low, "rep", [(i, (i + k) % packs) for i in range(packs)])
+        for k, low in enumerate(output_low, 1)
     ]
-    grad_heads, gate_there = together(grad_heads, gate_there)
+    grad_heads, gate_there, output_mine = together(grad_heads, gate_there, output_mine)
+    up_a, _ = together(up_a, grad_heads)
+    up_a_there = pack_swap(up_a)
     grads = attend_back(first, tail, qkv, grad_heads, attended, log_total, cos_t, sin_t)
-    grads, output_there, out_sum, up_low, down_low = together(
-        grads, output_there, out_sum, up_low, down_low
-    )
-    up_there = pack_swap(up_low)
+    grads, output_there, out_sum, up_a_there, up_b, down_low = together(
+        grads, output_there, out_sum, up_a_there, up_b, down_low
+    )
+    up_b_there = pack_swap(up_b)
+    down_there = pack_swap(down_low)
+    up_b_there = pack_swap(up_b)
     down_there = pack_swap(down_low)
     output_grad = lax.psum_scatter(
         sum((there.astype(F32) for there in output_there), output_mine.astype(F32)).astype(LOW),
@@ -1294,11 +1491,19 @@
         tiled=True,
         axis_index_groups=lanes,
     )
-    input_grad, attention_gain_part, query_total, key_total, value_total = normed_back(
-        grads, qkv_weight, qkv_other, tokens[0], attention_gain[None], grad_mixed, normed_all
-    )
-    input_grad, out_sum, gate_there, up_there, down_there, output_grad = together(
-        input_grad, out_sum, gate_there, up_there, down_there, output_grad
+    input_grad, gain_totals, query_total, key_total, value_total, output_grad = normed_back(
+        grads,
+        joined,
+        tokens[0],
+        attention_gain[None],
+        grad_mixed,
+        dense_gain_part,
+        normed_all,
+        output_mine,
+        output_there,
+    )
+    input_grad, out_sum, gate_there, up_a_there, up_b_there, down_there = together(
+        input_grad, out_sum, gate_there, up_a_there, up_b_there, down_there
     )
     output_total = lax.all_gather(output_grad, "rep", axis=0, tiled=True)
     if packs == 2:
@@ -1308,8 +1513,6 @@
             jnp.concatenate([output_grad, output_other], 0),
             jnp.concatenate([output_other, output_grad], 0),
         )
-    gain_parts = jnp.stack([attention_gain_part[0], dense_gain_part])
-    gain_totals = gain_total(gain_parts.reshape(-1, 128)).reshape(2, -1)
     layer_out = mixed + out_sum.astype(F32)
     return (
         layer_out[None].astype(LOW),
@@ -1321,7 +1524,7 @@
         output_total.astype(F32),
         gain_totals[1],
         pack_add(gate_low, gate_there),
-        pack_add(up_low, up_there),
+        jnp.concatenate([pack_add(up_a, up_a_there), pack_add(up_b, up_b_there)], 0),
         pack_add(down_low, down_there),
     )
 

time: 711 us -> 700 us (0.985)
  Pallas kernels: 516 us -> 575 us
  waiting for transfers between devices: 82.6 us -> 42.9 us
  matrix products: 23.1 us -> 5.21 us
  other arithmetic: 32.3 us -> 19.9 us
    pallas_call x2, Pallas kernels: 139 us -> 179 us  [the longest x1 133 us: normed_back(): pl.pallas_call(functools.partial(normed_back_kernel, packs), out_shape=(j...]
    all_gather x2, waiting for transfers between devices: 24.9 us -> 0.02 us  [the longest x1 0.02 us: body(): lax.all_gather(late, 'dp', axis=0, axis_index_groups=lanes)]
    all_to_all x1 -> x0, waiting for transfers between devices: 23.4 us -> none  [body(): lax.all_to_all(grad_attended.reshape(tok_dev, devices, r).transpose(1, 0,...]
    pallas_call x1, Pallas kernels: 114 us -> 133 us  [gather_project(): pl.pallas_call(gather_project_kernel, out_shape=(jax.ShapeDtypeStruct((3,...]
    dot_general x5 -> x0, matrix products: 17.7 us -> none  [the longest x4 11.9 us: dot_tn(): lax.dot_general(a, b, (((0,), (0,)), ((), ())), preferred_element_type=F32)]
    convert_element_type x2 -> x0, other arithmetic: 8.02 us -> none  [the longest x1 5.92 us: body(): sum((there.astype(F32) for there in output_there), output_mine.astype(F32))]
    unnamed x66 -> x58, local copies, waits for them, and re-layouts: 18.5 us -> 17.8 us
  transfers between devices with their start and end apart: 17 -> 14, of which waited for: 5 -> 5; matrix products, arithmetic and copies ran while one was open for 6% -> 3% of each run, Pallas kernels for 31% -> 57%
where the time goes in v5:
time: 700 us; the launch traced here: 699 us
  Pallas kernels  575 us (82%)
  waiting for transfers between devices  42.9 us (6%)
  local copies, waits for them, and re-layouts  29.1 us (4%)
  other arithmetic  19.9 us (3%)
  between operations  14.1 us (2%)
  starting transfers between devices  13.2 us (2%)
    pallas_call x1, Pallas kernels, dense(): pl.pallas_call(dense_kernel, out_shape=(jax.ShapeDtypeStruct((rows, featu...  179 us
    pallas_call x1, Pallas kernels, gather_project(): pl.pallas_call(gather_project_kernel, out_shape=(jax.ShapeDtypeStruct((3,...  133 us
    pallas_call x1, Pallas kernels, normed_back(): pl.pallas_call(functools.partial(normed_back_kernel, packs), out_shape=(j...  133 us
    pallas_call x1, Pallas kernels, mixed_back(): pl.pallas_call(functools.partial(mixed_back_kernel, packs), out_shape=(ja...  46.5 us
    pallas_call x1, Pallas kernels, attend_back(): pl.pallas_call(functools.partial(attend_back_kernel, lax.axis_size('dp')...  44.4 us
    pallas_call x1, Pallas kernels, attend(): pl.pallas_call(functools.partial(attend_kernel, lax.axis_size('dp') // 2)...  38.9 us
    all_to_all x1, waiting for transfers between devices, body(): lax.all_to_all(attended.reshape(devices, tok_dev, r), 'dp', split_axis=0,...  28.7 us
    unnamed x58, local copies, waits for them, and re-layouts  17.8 us
  transfers between devices with their start and end apart: 14, of which 5 were waited for; matrix products, arithmetic and copies ran while one was open for 3% of the time, Pallas kernels for 57%

profile of v5, /device:TPU:0, one launch (start us, length us, event | category | flops | bytes accessed | tf_op | source)
XLA Modules:
  0.0 699.0 jit_solution(17275349866858529631)
XLA Ops:
  7.3 1.8 slice.26
  10.2 2.1 slice_bitcast_fusion
  12.3 1.9 multiply_sine_fusion
  15.4 133.2 %gather_project.1 = (bf16[3,4096,128]{2,1,0:T(8,128)(2,1)S(1)}, bf16[8,256,2048]{2,1,0:T(8,128)(2,1)}, bf16[16,128,2048]{2,1,0:T(8,128)(2,1)}) custom-call(bf16[256,2048]{1,0:T(8,128)(2,1)S(1)} %bitcast.36, f32[1,2048]{1,0:T(1,128)S(1)} %bitcast.38, bf16[128,2048]{1,0:T(8,128)(2,1)S(1)} %copy-done, bf16[128,2048]{1,0:T(8,128)(2,1)S(1)} %copy-done.1, ...), custom_call_target="tpu_custom_call" | custom-call | flops 6442450944 | bytes 335544320 | tf_op jit(solution)/shard_map/gather_project/pallas_call | solution.py:338
  148.6 1.7 copy-done.8
  150.5 1.9 copy-done.9
  152.4 38.9 %attend.1 = (bf16[4096,128]{1,0:T(8,128)(2,1)}, f32[32,256]{1,0:T(8,128)S(1)}) custom-call(s32[32]{0:T(128)S(1)} %convert_reduce_fusion.first_ref, s32[32]{0:T(128)S(1)} %add_select_fusion.tail_ref, bf16[3,4096,128]{2,1,0:T(8,128)(2,1)S(1)} %copy-done.9), custom_call_target="tpu_custom_call" | custom-call | flops 17179869184 | bytes 125829120 | tf_op jit(solution)/shard_map/attend/pallas_call | solution.py:453
  191.4 6.2 all-to-all-start
  198.9 3.1 collective-permute-done
  201.9 1.8 pad_maximum_fusion.1.joined
  203.7 28.7 %all-to-all-done = bf16[16,256,128]{2,1,0:T(8,128)(2,1)} async-done(((bf16[16,256,128]{2,1,0:T(8,128)(2,1)}), bf16[16,256,128]{2,1,0:T(8,128)(2,1)}, u32[]{:S(2)}, u32[]{:S(2)}) %all-to-all-start) | async-done | bytes 1048608 | tf_op jit(solution)/shard_map/all_to_all | solution.py:1434
  232.5 2.4 copy.31
  234.8 2.3 copy.32
  237.1 5.2 multiply_reduce_fusion
  242.4 1.3 copy-done.12
  244.9 178.7 %dense.1 = (f32[256,2048]{1,0:T(8,128)}, bf16[8,256,2048]{2,1,0:T(8,128)(2,1)}, bf16[8,256,2048]{2,1,0:T(8,128)(2,1)}, bf16[512,2048]{1,0:T(8,128)(2,1)}, bf16[6...) custom-call(bf16[256,2048]{1,0:T(8,128)(2,1)} %multiply_convert_fusion.normed, ...), custom_call_target="tpu_custom_call" | custom-call | flops 77309411328 | bytes 524288000 | tf_op jit(solution)/shard_map/dense/pallas_call | solution.py:821
  424.9 1.3 copy.33.shares
  426.2 46.5 %mixed_back.1 = (f32[256,2048]{1,0:T(8,128)}, f32[1,2048]{1,0:T(1,128)}, bf16[4096,128]{1,0:T(8,128)(2,1)}, bf16[512,2048]{1,0:T(8,128)(2,1)}, bf16[512,2048]{1,0:T(8,128)(2,1)}) custom-call(f32[256,2048]{1,0:T(8,128)} %copy-done.12, f32[256,2048]{1,0:T(8,128)} %get-tuple-element.62.grad_in, bf16[256,2048]{1,0:T(8,128)(2,1)} %bitcast.43, ...), custom_call_target="tpu_custom_call" | custom-call | flops 4294967296 | bytes 136314880 | tf_op jit(solution)/shard_map/mixed_back/pallas_call | solution.py:974
  476.1 44.4 %attend_back.1.grads_in = bf16[3,4096,128]{2,1,0:T(8,128)(2,1)S(1)} custom-call(s32[32]{0:T(128)S(1)} %convert_reduce_fusion.first_ref, s32[32]{0:T(128)S(1)} %add_select_fusion.tail_ref, bf16[3,4096,128]{2,1,0:T(8,128)(2,1)S(1)} %copy-done.10, bf16[4096,128]{1,0:T(8,128)(2,1)S(1)} %copy-done.7, bf16[4096,128]{1,0:T(8,128)(2,1)} %get-tuple-element.57.attended, ...), custom_call_target="tpu_custom_call" | custom-call | flops 42949672960 | bytes 251658240 | tf_op jit(solution)/shard_map/attend_back/pallas_call | solution.py:555
  520.5 1.7 copy-done.11
  522.2 3.6 collective-permute-done.6
  525.7 2.5 reduce-scatter.2.cloned.1.call-done
  528.2 1.5 collective-permute-start.8
  530.2 132.9 %normed_back.1 = (f32[256,2048]{1,0:T(8,128)}, f32[2,2048]{1,0:T(2,128)}, f32[128,2048]{1,0:T(8,128)}, f32[128,2048]{1,0:T(8,128)}, f32[128,2048]{1,0:T(8,128)}, /*index=5*/bf16[64,2048]{1,0:T(8,128)(2,1)}) custom-call(bf16[3,4096,128]{2,1,0:T(8,128)(2,1)} %copy-done.11, bf16[768,2048]{1,0:T(8,128)(2,1)} %pad_maximum_fusion.1.joined, ...), custom_call_target="tpu_custom_call" | custom-call | flops 12884901888 | bytes 335544320 | tf_op jit(solution)/shard_map/normed_back/pallas_call | solution.py:1302
  663.1 1.5 collective-permute-start.9
  664.7 1.4 fusion.4
  666.1 4.9 collective-permute-done.9
  671.0 2.1 fusion.2
  675.1 1.3 fusion.1
  676.3 2.6 pad_maximum_fusion
  680.1 6.9 convert_add_fusion
  687.0 1.3 copy.38
  (88 shorter events, 17.4 us)
Async XLA Ops:
  7.2 7.0 copy-start.6
  7.2 7.0 copy-start
  7.2 7.0 copy-start.1
  7.2 7.0 copy-start.2
  7.2 7.0 copy-start.5
  7.2 143.0 %all-gather.4.cloned.1.call-start = ((), (), s32[]{:S(2)}) async-start(), calls=%async_computation.2 | async-start | bytes 2359296 | tf_op jit(solution)/shard_map/all_gather | solution.py:1422
  9.1 235.8 %all-gather.6.cloned.1.call-start = ((), (), s32[]{:S(2)}) async-start(), calls=%async_computation.4 | async-start | bytes 7077888 | tf_op jit(solution)/shard_map/all_gather | solution.py:1424
  15.4 134.9 %copy-start.25 = (s32[1,8]{1,0:T(1,128)S(1)}, s32[1,8]{1,0:T(1,128)}, u32[]{:S(2)}) copy-start(s32[1,8]{1,0:T(1,128)} %param.24) | copy-start | bytes 100
  15.4 134.9 %copy-start.26 = (s32[1,32]{1,0:T(1,128)S(1)}, s32[1,32]{1,0:T(1,128)}, u32[]{:S(2)}) copy-start(s32[1,32]{1,0:T(1,128)} %param.23) | copy-start | bytes 388
  150.5 1.9 copy-start.9
  191.4 41.1 %all-to-all-start = ((bf16[16,256,128]{2,1,0:T(8,128)(2,1)}), bf16[16,256,128]{2,1,0:T(8,128)(2,1)}, u32[]{:S(2)}, u32[]{:S(2)}) async-start(bf16[16,256,128]{2,1,0:T(8,128)(2,1)} %bitcast.7), calls=%async_computation | async-start | bytes 2097152 | tf_op jit(solution)/shard_map/all_to_all | solution.py:1434
  197.6 330.6 %reduce-scatter.2.cloned.1.call-start = ((), (), s32[]{:S(2)}) async-start(), calls=%async_computation.3 | async-start | bytes 9437184 | tf_op jit(solution)/shard_map/reduce_scatter | solution.py:1460
  197.8 4.1 collective-permute-start
  198.2 46.7 %collective-permute-start.1 = (bf16[512,2048]{1,0:T(8,128)(2,1)}, bf16[512,2048]{1,0:T(8,128)(2,1)}, u32[]{:S(2)}, u32[]{:S(2)}) collective-permute-start(bf16[512,2048]{1,0:T(8,128)(2,1)} %gate_w.1), channel_id=1, source_target_pairs={{0,2},{2,0},{4,6},{6,4},{8,10},{10,8},{12,14},{14,12},{16,18},{18,... | collective-permute-start | bytes 6291464 | tf_op jit(solution)/shard_map/ppermute | solution.py:1354
  198.3 46.5 %collective-permute-start.2 = (bf16[512,2048]{1,0:T(8,128)(2,1)}, bf16[512,2048]{1,0:T(8,128)(2,1)}, u32[]{:S(2)}, u32[]{:S(2)}) collective-permute-start(bf16[512,2048]{1,0:T(8,128)(2,1)} %up_w.1), channel_id=1, source_target_pairs={{0,2},{2,0},{4,6},{6,4},{8,10},{10,8},{12,14},{14,12},{16,18},{18,... | collective-permute-start | bytes 6291464 | tf_op jit(solution)/shard_map/ppermute | solution.py:1354
  198.7 46.2 %collective-permute-start.3 = (bf16[512,2048]{1,0:T(8,128)(2,1)}, bf16[512,2048]{1,0:T(8,128)(2,1)}, u32[]{:S(2)}, u32[]{:S(2)}) collective-permute-start(bf16[512,2048]{1,0:T(8,128)(2,1)} %down_w.1), channel_id=1, source_target_pairs={{0,2},{2,0},{4,6},{6,4},{8,10},{10,8},{12,14},{14,12},{16,18},{18,... | collective-permute-start | bytes 6291464 | tf_op jit(solution)/shard_map/ppermute | solution.py:1354
  232.5 4.7 copy-start.4
  237.1 6.5 copy-start.24
  423.7 50.1 %collective-permute-start.4 = (bf16[512,2048]{1,0:T(8,128)(2,1)}, bf16[512,2048]{1,0:T(8,128)(2,1)}, u32[]{:S(2)}, u32[]{:S(2)}) collective-permute-start(bf16[512,2048]{1,0:T(8,128)(2,1)} %get-tuple-element.65), channel_id=1, source_target_pairs={{0,1},{1,0},{2,3},{3,2},{4,5},{5,4},{6,7},{7,6},{8,9},{9,8},{10,11... | collective-permute-start | bytes 6291464 | tf_op jit(solution)/shard_map/ppermute | solution.py:1359
  426.2 47.6 %copy-start.23 = (bf16[64,2048]{1,0:T(8,128)(2,1)S(1)}, bf16[64,2048]{1,0:T(8,128)(2,1)}, u32[]{:S(2)}) copy-start(bf16[64,2048]{1,0:T(8,128)(2,1)} %get-tuple-element.72) | copy-start | bytes 786436
  426.2 48.6 %copy-start.10 = (bf16[3,4096,128]{2,1,0:T(8,128)(2,1)S(1)}, bf16[3,4096,128]{2,1,0:T(8,128)(2,1)}, u32[]{:S(2)}) copy-start(bf16[3,4096,128]{2,1,0:T(8,128)(2,1)} %copy-done.8) | copy-start | bytes 9437188
  472.7 49.4 %collective-permute-start.5 = (bf16[512,2048]{1,0:T(8,128)(2,1)}, bf16[512,2048]{1,0:T(8,128)(2,1)}, u32[]{:S(2)}, u32[]{:S(2)}) collective-permute-start(bf16[512,2048]{1,0:T(8,128)(2,1)} %get-tuple-element.69), channel_id=1, source_target_pairs={{0,1},{1,0},{2,3},{3,2},{4,5},{5,4},{6,7},{7,6},{8,9},{9,8},{10,11... | collective-permute-start | bytes 6291464 | tf_op jit(solution)/shard_map/ppermute | solution.py:1473
  473.8 52.0 %collective-permute-start.6 = (bf16[64,2048]{1,0:T(8,128)(2,1)S(1)}, bf16[64,2048]{1,0:T(8,128)(2,1)S(1)}, u32[]{:S(2)}, u32[]{:S(2)}) collective-permute-start(bf16[64,2048]{1,0:T(8,128)(2,1)S(1)} %copy-done.23), channel_id=1, source_target_pairs={{0,1},{1,0},{2,3},{3,2},{4,5},{5,4},{6,7},{7,6},{8,9},{9,8},{10,11... | collective-permute-start | bytes 786440 | tf_op jit(solution)/shard_map/ppermute | solution.py:1359
  528.2 144.9 %collective-permute-start.8 = (bf16[512,2048]{1,0:T(8,128)(2,1)}, bf16[512,2048]{1,0:T(8,128)(2,1)S(1)}, u32[]{:S(2)}, u32[]{:S(2)}) collective-permute-start(bf16[512,2048]{1,0:T(8,128)(2,1)} %get-tuple-element.87), channel_id=1, source_target_pairs={{0,1},{1,0},{2,3},{3,2},{4,5},{5,4},{6,7},{7,6},{8,9},{9,8},{10,11... | collective-permute-start | bytes 6291464 | tf_op jit(solution)/shard_map/ppermute | solution.py:1359
  529.7 143.5 %collective-permute-start.7 = (bf16[448,2048]{1,0:T(8,128)(2,1)}, bf16[448,2048]{1,0:T(8,128)(2,1)S(1)}, u32[]{:S(2)}, u32[]{:S(2)}) collective-permute-start(bf16[448,2048]{1,0:T(8,128)(2,1)} %get-tuple-element.86), channel_id=1, source_target_pairs={{0,1},{1,0},{2,3},{3,2},{4,5},{5,4},{6,7},{7,6},{8,9},{9,8},{10,11... | collective-permute-start | bytes 5505032 | tf_op jit(solution)/shard_map/ppermute | solution.py:1359
  663.1 10.1 %copy-start.18 = (bf16[448,2048]{1,0:T(8,128)(2,1)S(1)}, bf16[448,2048]{1,0:T(8,128)(2,1)}, u32[]{:S(2)}) copy-start(bf16[448,2048]{1,0:T(8,128)(2,1)} %get-tuple-element.86) | copy-start | bytes 5505028
  663.1 7.9 %collective-permute-start.9 = (bf16[64,2048]{1,0:T(8,128)(2,1)}, bf16[64,2048]{1,0:T(8,128)(2,1)S(1)}, u32[]{:S(2)}, u32[]{:S(2)}) collective-permute-start(bf16[64,2048]{1,0:T(8,128)(2,1)} %get-tuple-element.94), channel_id=1, source_target_pairs={{0,1},{1,0},{2,3},{3,2},{4,5},{5,4},{6,7},{7,6},{8,9},{9,8},{10,11... | collective-permute-start | bytes 786440 | tf_op jit(solution)/shard_map/ppermute | solution.py:1510
  676.3 2.6 copy-start.16
  676.3 3.7 copy-start.17
  680.1 6.9 copy-start.15
  687.0 2.0 copy-start.21
  688.9 2.6 copy-start.19
  (9 other events, 13.4 us)
Sparse Core Ops, SparseCore 0:
  10.2 50.1 all-gather.3
  150.4 84.9 all-gather.5
  423.8 104.3 reduce-scatter.1

commit v6 on v5

--- a/solution.py
+++ b/solution.py
@@ -114,9 +114,9 @@
 
 
 def gather_project_kernel(
-    tokens, gain, query_w, key_w, value_w, output_w, cos_t, sin_t, qkv, gathered, output_all,
-    normed, partner_weights, x_buf, staged,
-    ag_send, ag_recv, w_send, w_recv, q_send, q_recv, local_sem,
+    tokens_in, gain, query_w, key_w, value_w, output_w, cos_t, sin_t, qkv, gathered, output_all,
+    tokens, own_weights, normed, partner_weights, x_buf, staged,
+    in_sem, ag_send, ag_recv, w_send, w_recv, q_send, q_recv, local_sem,
     o_send, o_recv, pair_send, pair_recv, rep_send, rep_recv, far_send, far_recv,
 ):
     ring = Ring()
@@ -125,7 +125,14 @@
     rows = normed.shape[0]
     half = rows // 2
     r = qkv.shape[2]
-    own_weights = (query_w, key_w, value_w)
+    sources = (query_w, key_w, value_w)
+    load_tokens = pltpu.make_async_copy(tokens_in, tokens, in_sem.at[3])
+    load_tokens.start()
+    load_weights = [
+        pltpu.make_async_copy(source, own_weights.at[i], in_sem.at[i]) for i, source in enumerate(sources)
+    ]
+    for load in load_weights:
+        load.start()
     barrier = pltpu.get_barrier_semaphore()
     for k in range(1, packs):
         pl.semaphore_signal(
@@ -134,6 +141,8 @@
     for other in (ring.next[0], ring.next[1], ring.partner):
         pl.semaphore_signal(barrier, inc=1, device_id={"dp": other}, device_id_type=MESH)
     pl.semaphore_wait(barrier, 3 + packs - 1)
+
+    load_tokens.wait()
 
     def normalize(i, carry):
         span = pl.ds(pl.multiple_of(i * 32, 32), 32)
@@ -206,7 +215,7 @@
     own_keep = pltpu.make_async_copy(output_w, output_all.at[spot], local_sem.at[5])
     own_keep.start()
     swaps = [
-        remote(own_weights[i], partner_weights.at[i], w_send.at[i], w_recv.at[i], ring.partner)
+        remote(sources[i], partner_weights.at[i], w_send.at[i], w_recv.at[i], ring.partner)
         for i in range(3)
     ]
     for swap in swaps:
@@ -237,7 +246,7 @@
                 value.astype(LOW),
             )
 
-        for i, value in enumerate(heads(own_weights)):
+        for i, value in enumerate(heads([own_weights.at[i] for i in range(3)])):
             for d in (0, 1):
                 qkv[i, pl.ds(starts[d], half), :] = value[d * half : (d + 1) * half]
         if from_input:
@@ -254,6 +263,8 @@
                 ring.partner,
             ).start()
 
+    for load in load_weights:
+        load.wait()
     project_block(0, True)
 
     def step(t, carry):
@@ -335,6 +346,7 @@
     n = devices // 2
     vmem = pl.BlockSpec(memory_space=pltpu.VMEM)
     dma = pltpu.SemaphoreType.DMA
+    hbm = pl.BlockSpec(memory_space=pl.ANY)
     return pl.pallas_call(
         gather_project_kernel,
         out_shape=(
@@ -342,20 +354,23 @@
             jax.ShapeDtypeStruct((n, rows, features), LOW),
             jax.ShapeDtypeStruct((devices,) + output_weight.shape, LOW),
         ),
-        in_specs=[vmem] * 8,
+        in_specs=[hbm, vmem] + [hbm] * 4 + [vmem] * 2,
         out_specs=(vmem, pl.BlockSpec(memory_space=pl.ANY), pl.BlockSpec(memory_space=pl.ANY)),
         scratch_shapes=[
             pltpu.VMEM((rows, features), LOW),
             pltpu.VMEM((3, r, features), LOW),
             pltpu.VMEM((rows, features), LOW),
+            pltpu.VMEM((3, r, features), LOW),
+            pltpu.VMEM((rows, features), LOW),
             pltpu.VMEM((n, 3, rows, r), LOW),
+            dma((4,)),
             dma((2, n)), dma((2, n)), dma((3,)), dma((3,)), dma((2, n)), dma((2, n)), dma((6,)),
             dma((2, n)), dma((2, n)), dma((2, n)), dma((2, n)),
             dma((packs - 1, 2, n)), dma((packs - 1, 2, n)),
             dma((packs - 1, 2, n)), dma((packs - 1, 2, n)),
         ],
         compiler_params=pltpu.CompilerParams(
-            collective_id=1, has_side_effects=True, vmem_limit_bytes=40 * MIB
+            collective_id=1, has_side_effects=True, vmem_limit_bytes=60 * MIB
         ),
         cost_estimate=pl.CostEstimate(
             flops=4 * n * rows * features * 3 * r, bytes_accessed=320 * MIB, transcendentals=0
@@ -572,8 +587,131 @@
     )(first, tail, qkv, grad_out, attended, log_total, cos_t, sin_t)
 
 
+def mixed_kernel(
+    attended, tokens_in, gain, output_all, mixed, normed, blocks,
+    tokens, weights, sem, w_sem, send_sem, recv_sem,
+):
+    ring = Ring()
+    n = ring.chips
+    devices = 2 * n
+    rows, features = mixed.shape
+    r = attended.shape[1]
+    spot = ring.place * 2 + ring.core
+    load = pltpu.make_async_copy(tokens_in, tokens, sem)
+    load.start()
+
+    def place_at(j):
+        return lax.rem(ring.place + (j % 2) * ((j + 1) // 2) + (1 - j % 2) * (n - j // 2), n)
+
+    def chip_weights(j):
+        place = place_at(j)
+        return pltpu.make_async_copy(
+            output_all.at[pl.ds(place * 2, 2)], weights.at[pl.ds(place * 2, 2)], w_sem.at[j]
+        )
+
+    def fetch(j, carry):
+        chip_weights(j).start()
+        return carry
+
+    lax.fori_loop(0, n, fetch, 0)
+    barrier = pltpu.get_barrier_semaphore()
+
+    def to(k):
+        other = lax.rem(spot + k, devices)
+        return chip_at(other // 2, n) * 2 + other % 2
+
+    def greet(k, carry):
+        pl.semaphore_signal(barrier, inc=1, device_id={"dp": to(k)}, device_id_type=MESH)
+        return carry
+
+    lax.fori_loop(1, devices, greet, 0)
+    pl.semaphore_wait(barrier, devices - 1)
+
+    def rows_of(at):
+        return pl.ds(pl.multiple_of(at * rows, rows), rows)
+
+    def copy(k):
+        return remote(
+            attended.at[rows_of(lax.rem(spot + k, devices))],
+            blocks.at[spot],
+            send_sem.at[k],
+            recv_sem.at[k],
+            to(k),
+        )
+
+    def begin(k, carry):
+        copy(k).start()
+        return carry
+
+    lax.fori_loop(1, devices, begin, 0)
+    blocks[spot] = attended[rows_of(spot), :]
+    load.wait()
+    mixed[...] = tokens[...].astype(F32)
+
+    def add(j, carry):
+        chip_weights(j).wait()
+        place = place_at(j)
+        for core in (0, 1):
+            k = lax.rem(spot + devices - place * 2 - core, devices)
+
+            @pl.when(k > 0)
+            def _():
+                copy(k).wait_recv()
+
+        both = jnp.concatenate([blocks[place * 2 + core] for core in (0, 1)], 1)
+        mixed[...] += dot_nn(both, weights[pl.ds(place * 2, 2)].reshape(2 * r, features))
+        return carry
+
+    lax.fori_loop(0, n, add, 0)
+
+    def normalize(i, carry):
+        span = pl.ds(pl.multiple_of(i * 32, 32), 32)
+        value = mixed[span, :]
+        scale = lax.rsqrt(jnp.mean(value * value, axis=1, keepdims=True) + EPSILON)
+        normed[span, :] = (value * scale * gain[...]).astype(LOW)
+        return carry
+
+    lax.fori_loop(0, rows // 32, normalize, 0)
+
+    def finish(k, carry):
+        copy(k).wait_send()
+        return carry
+
+    lax.fori_loop(1, devices, finish, 0)
+
+
+def mix(attended, tokens, gain, output_all):
+    rows, features = tokens.shape
+    devices, r = output_all.shape[:2]
+    vmem = pl.BlockSpec(memory_space=pltpu.VMEM)
+    hbm = pl.BlockSpec(memory_space=pl.ANY)
+    dma = pltpu.SemaphoreType.DMA
+    return pl.pallas_call(
+        mixed_kernel,
+        out_shape=(
+            jax.ShapeDtypeStruct((rows, features), F32),
+            jax.ShapeDtypeStruct((rows, features), LOW),
+            jax.ShapeDtypeStruct((devices, rows, r), LOW),
+        ),
+        in_specs=[vmem, hbm, vmem, hbm],
+        out_specs=(vmem,) * 3,
+        scratch_shapes=[
+            pltpu.VMEM((rows, features), LOW),
+            pltpu.VMEM((devices, r, features), LOW),
+            dma, dma((devices // 2,)), dma((devices,)), dma((devices,)),
+        ],
+        compiler_params=pltpu.CompilerParams(
+            collective_id=5, has_side_effects=True, vmem_limit_bytes=56 * MIB
+        ),
+        cost_estimate=pl.CostEstimate(
+            flops=2 * rows * features * features, bytes_accessed=100 * MIB, transcendentals=0
+        ),
+        name="mix",
+    )(attended, tokens, gain, output_all)
+
+
 def dense_kernel(
-    normed, cotangents_a, cotangents_b, gate_w, up_w, down_w, gate_p, up_p, down_p,
+    normed, cotangents, gate_w, up_w, down_w, gate_p, up_p, down_p,
     grad_sum, out_parts, gathered, gate_grad, up_a, up_b, down_grad,
     weights, totals, x_buf, g_buf, out_acc, grad_acc, sent, landed, cast_buf, pair_land,
     ag_send, ag_recv, rs_send, rs_recv, credit, local_sem, w_sem, cast_sem, pair_send, pair_recv,
@@ -582,7 +720,6 @@
     n = ring.chips
     rows, features = normed.shape
     half = rows // 2
-    early = cotangents_a.shape[1]
     own = gate_w.shape[0]
     tiles = 2 * own // FF_TILE
     loads = []
@@ -623,33 +760,31 @@
             cast_buf.at[t % 2, part], out_parts.at[source(t, d), part], cast_sem.at[t % 2, d]
         )
 
+    def pass_on(t):
+        for d in (0, 1):
+            send(t, d, False).wait_recv()
+
+        @pl.when(t < n - 1)
+        def _():
+            for d in (0, 1):
+                send(t + 1, d, False).start()
+
     def step(t, carry):
-        copies = [
-            pltpu.make_async_copy(cotangents_a.at[source(t, 0)], g_buf.at[pl.ds(0, early)], local_sem.at[0]),
-            pltpu.make_async_copy(
-                cotangents_b.at[source(t, 0), pl.ds(0, half - early)],
-                g_buf.at[pl.ds(early, half - early)],
-                local_sem.at[1],
-            ),
-            pltpu.make_async_copy(
-                cotangents_b.at[source(t, 1), pl.ds(half - early, half)],
-                g_buf.at[pl.ds(half, half)],
-                local_sem.at[4],
-            ),
-        ]
+        copies = []
+        for d in (0, 1):
+            part = half_rows(d, rows)
+            copies.append(
+                pltpu.make_async_copy(cotangents.at[source(t, d), part], g_buf.at[part], local_sem.at[d])
+            )
         for copy in copies:
             copy.start()
 
+        @pl.when(t > 1)
+        def _():
+            pass_on(t)
+
         @pl.when(t > 0)
         def _():
-            for d in (0, 1):
-                send(t, d, False).wait_recv()
-
-            @pl.when(t < n - 1)
-            def _():
-                for d in (0, 1):
-                    send(t + 1, d, False).start()
-
             more = []
             for d in (0, 1):
                 part = half_rows(d, rows)
@@ -671,6 +806,10 @@
         grad_acc[...] = jnp.zeros_like(grad_acc)
 
         def tile(i, carry):
+            @pl.when((t == 0) & (i == tiles - 1))
+            def _():
+                pass_on(1)
+
             span = pl.ds(pl.multiple_of(i * FF_TILE, FF_TILE), FF_TILE)
             x = x_buf[...]
             g = g_buf[...]
@@ -825,11 +964,11 @@
             jax.ShapeDtypeStruct((n, rows, features), LOW),
             jax.ShapeDtypeStruct((n, rows, features), LOW),
             jax.ShapeDtypeStruct((own, features), LOW),
-            jax.ShapeDtypeStruct((own // 8, features), LOW),
-            jax.ShapeDtypeStruct((own - own // 8, features), LOW),
+            jax.ShapeDtypeStruct((own // 4, features), LOW),
+            jax.ShapeDtypeStruct((own - own // 4, features), LOW),
             jax.ShapeDtypeStruct((own, features), LOW),
         ),
-        in_specs=[vmem] + [hbm] * 8,
+        in_specs=[vmem] + [hbm] * 7,
         out_specs=(vmem,) + (hbm,) * 6,
         scratch_shapes=[
             pltpu.VMEM((3, 2 * own, features), LOW),
@@ -844,7 +983,7 @@
             pltpu.VMEM((own_tiles, FF_TILE, features), LOW),
             dma((2, n)), dma((2, n)), dma((2,)), dma((2, 2)),
             pltpu.SemaphoreType.REGULAR((2,)),
-            dma((5,)), dma((6,)), dma((2, 2)), dma((2,)), dma((own_tiles,)),
+            dma((4,)), dma((6,)), dma((2, 2)), dma((2,)), dma((own_tiles,)),
         ],
         compiler_params=pltpu.CompilerParams(
             collective_id=2, has_side_effects=True, vmem_limit_bytes=62 * MIB
@@ -853,16 +992,23 @@
             flops=2 * 9 * n * rows * features * 2 * own, bytes_accessed=500 * MIB, transcendentals=0
         ),
         name="dense",
-    )(normed, *cotangents, *own_weights, *partner_weights)
+    )(normed, cotangents, *own_weights, *partner_weights)
+
+
+def output_split(r, packs):
+    plain = r // 4 if (r - r // 4) // packs % 16 == 0 else 0
+    return (r - plain) // packs, plain
 
 
 def mixed_back_kernel(
-    packs, mixed_in, grad_in, cotangent_in, gain, output_all, shares, grad_mixed, gain_part, grad_heads, *rest
+    packs, mixed_in, grad_in, cotangent_in, gain, output_all, blocks, grad_mixed, gain_part, grad_heads, *rest
 ):
     sums = rest[:packs]
-    mixed, grad_two, cotangent, low, weights, staged, given, taken, sem, w_sem, send_sem, recv_sem, g_sem, t_sem = (
-        rest[packs:]
-    )
+    given, taken = rest[packs : 2 * packs], rest[2 * packs : 3 * packs]
+    (
+        mixed, grad_two, cotangent, low, weights, staged, product,
+        sem, w_sem, send_sem, recv_sem, g_sem, t_sem,
+    ) = rest[3 * packs :]
     ring = Ring()
     n = ring.chips
     devices = 2 * n
@@ -942,15 +1088,42 @@
     grad_heads[pl.ds(pl.multiple_of(spot * rows, rows), rows), :] = staged[0]
 
     def give(k):
-        return remote(given.at[k], taken.at[k], g_sem.at[k], t_sem.at[k], ring.partner)
-
+        return remote(given[k], taken[k], g_sem.at[k], t_sem.at[k], ring.partner)
+
+    share, plain = output_split(r, packs)
+
+    def spots(k, place, first, count):
+        width = share + plain if k == 0 else share
+        return pl.ds(pl.multiple_of(place * width + first, 16), count)
+
+    def products(place, core, use):
+        product[...] = dot_tn(blocks[place * 2 + core], low[...])
+        for k in range(packs):
+            at = pl.multiple_of(lax.rem(pack + k, packs) * share, share)
+            use(k, spots(k, place, 0, share), product[pl.ds(at, share), :])
+        if plain:
+            use(0, spots(0, place, share, plain), product[pl.ds(r - plain, plain), :])
+
+    def put(k, at, value):
+        given[k][at, :] = value.astype(LOW)
+
+    def total(k, at, value):
+        sums[k][at, :] = (value + taken[k][at, :].astype(F32)).astype(LOW)
+
+    def for_partner(place, carry):
+        products(place, 1 - ring.core, put)
+        return carry
+
+    def for_self(place, carry):
+        products(place, ring.core, total)
+        return carry
+
+    lax.fori_loop(0, n, for_partner, 0)
     for k in range(packs):
-        given[k] = dot_tn(shares[1 - ring.core, lax.rem(pack + k, packs)], low[...]).astype(LOW)
         give(k).start()
     for k in range(packs):
-        own = dot_tn(shares[ring.core, lax.rem(pack + k, packs)], low[...])
         give(k).wait_recv()
-        sums[k][...] = (own + taken[k].astype(F32)).astype(LOW)
+    lax.fori_loop(0, n, for_self, 0)
 
     def finish(k, carry):
         copy(k).wait_send()
@@ -962,12 +1135,13 @@
         give(k).wait_send()
 
 
-def mixed_back(mixed, grad_two, cotangent, gain, output_all, shares):
+def mixed_back(mixed, grad_two, cotangent, gain, output_all, blocks):
     rows, features = mixed.shape
     devices, r = output_all.shape[:2]
     packs = lax.axis_size("rep")
     n = devices // 2
-    total = shares.shape[3]
+    share, plain = output_split(r, packs)
+    sizes = [n * (share + plain)] + [n * share] * (packs - 1)
     vmem = pl.BlockSpec(memory_space=pltpu.VMEM)
     hbm = pl.BlockSpec(memory_space=pl.ANY)
     dma = pltpu.SemaphoreType.DMA
@@ -978,18 +1152,18 @@
             jax.ShapeDtypeStruct((1, features), F32),
             jax.ShapeDtypeStruct((devices * rows, r), LOW),
         )
-        + (jax.ShapeDtypeStruct((total, features), LOW),) * packs,
+        + tuple(jax.ShapeDtypeStruct((size, features), LOW) for size in sizes),
         in_specs=[hbm] * 3 + [vmem, hbm, vmem],
         out_specs=(vmem,) * (3 + packs),
-        scratch_shapes=[
+        scratch_shapes=[pltpu.VMEM((size, features), LOW) for size in sizes + sizes]
+        + [
             pltpu.VMEM((rows, features), F32),
             pltpu.VMEM((rows, features), F32),
             pltpu.VMEM((rows, features), LOW),
             pltpu.VMEM((rows, features), LOW),
             pltpu.VMEM((devices, r, features), LOW),
             pltpu.VMEM((devices, rows, r), LOW),
-            pltpu.VMEM((packs, total, features), LOW),
-            pltpu.VMEM((packs, total, features), LOW),
+            pltpu.VMEM((r, features), F32),
             dma((3,)), dma((n,)), dma((devices,)), dma((devices,)), dma((packs,)), dma((packs,)),
         ],
         compiler_params=pltpu.CompilerParams(
@@ -999,32 +1173,38 @@
             flops=4 * rows * features * features, bytes_accessed=130 * MIB, transcendentals=0
         ),
         name="mixed_back",
-    )(mixed, grad_two, cotangent, gain, output_all, shares)
+    )(mixed, grad_two, cotangent, gain, output_all, blocks)
 
 
 def normed_back_kernel(
-    packs, grads_in, joined, hidden_in, gain, grad_mixed, dense_gain_part, normed_all, output_mine, *rest
+    packs, grads_in, query_w, key_w, value_w, partner_w, hidden_in, gain, grad_mixed, dense_gain_part, normed_all, output_mine, *rest
 ):
     output_there = rest[: packs - 1]
     (
-        out, gains, query_total, key_total, value_total, output_grad,
-        grads, partner_grads, sent, landed, x_buf, parts, pair_out, pair_land, rep_land,
+        out, gains, rep_land, o_packs,
+        grads, joined, partner_grads, sent, landed, x_buf, parts, pair_out, pair_land,
         o_sent, o_landed, near_part, near_land, near_sum, far_land,
-        in_sem, p_send, p_recv, rs_send, rs_recv, credit, x_sem, pair_sem, rep_send, rep_recv,
-        o_send, o_recv, o_credit, near_send, near_recv, far_send, far_recv,
+        in_sem, w_sem, p_send, p_recv, rs_send, rs_recv, credit, x_sem, pair_sem, rep_send, rep_recv,
+        o_send, o_recv, o_credit, swap_send, swap_recv, near_send, near_recv, far_send, far_recv,
     ) = rest[packs - 1 :]
     ring = Ring()
     n = ring.chips
     rows, features = out.shape
     half = rows // 2
     r = grads.shape[2]
-    share = output_grad.shape[0]
+    share, plain = output_split(r, packs)
     pack = lax.axis_index("rep")
     mates = 2 * packs
     mate = pack * 2 + ring.core
     barrier = pltpu.get_barrier_semaphore()
     load_grads = pltpu.make_async_copy(grads_in, grads, in_sem)
     load_grads.start()
+    load_weights = [
+        pltpu.make_async_copy(src, joined.at[pl.ds(i * r, src.shape[0])], w_sem.at[i])
+        for i, src in enumerate((query_w, key_w, value_w, partner_w))
+    ]
+    for load in load_weights:
+        load.start()
 
     def near(k):
         to = lax.rem(mate + k, mates)
@@ -1062,16 +1242,20 @@
 
     def reduce_copy(t, d, u):
         return remote(
-            sent.at[d, u],
+            sent.at[d, u, t % 2],
             landed.at[d, u, t % 2],
-            rs_send.at[d, u],
+            rs_send.at[d, u, t % 2],
             rs_recv.at[d, u, t % 2],
             ring.next[d],
         )
 
     def output_copy(t, d):
         return remote(
-            o_sent.at[d], o_landed.at[d, t % 2], o_send.at[d], o_recv.at[d, t % 2], ring.next[d]
+            o_sent.at[d, t % 2],
+            o_landed.at[d, t % 2],
+            o_send.at[d, t % 2],
+            o_recv.at[d, t % 2],
+            ring.next[d],
         )
 
     def give_credit(sem, d):
@@ -1081,7 +1265,7 @@
         start = (place(t, d) * 2 + ring.core) * rows + d * half
         return pl.ds(pl.multiple_of(start, half), half)
 
-    def load(t, d):
+    def load_rows(t, d):
         part = half_rows(d, rows)
         return pltpu.make_async_copy(normed_all.at[place(t, d), part], x_buf.at[t % 2, part], x_sem.at[t % 2, d])
 
@@ -1094,7 +1278,7 @@
 
     def weight_parts(t):
         for d in (0, 1):
-            load(t, d).wait()
+            load_rows(t, d).wait()
         parts[...] += dot_tn(block_grads(t), x_buf[t % 2])
 
     def pair_copy():
@@ -1115,16 +1299,27 @@
     def output_step(t):
         for d in (0, 1):
             spot = lax.rem(ring.place + (n - t if d == 0 else t), n)
-            at = pl.ds(pl.multiple_of(spot * share, share), share)
             columns = pl.ds(d * (features // 2), features // 2)
-            total = output_mine[at, columns].astype(F32)
+            own = pl.multiple_of(spot * (share + plain), 16)
+            total = output_mine[pl.ds(own, share), columns].astype(F32)
             for there in output_there:
-                total += there[at, columns].astype(F32)
+                total += there[pl.ds(pl.multiple_of(spot * share, share), share), columns].astype(F32)
+            if plain:
+                rest_rows = pl.ds(pl.multiple_of(own + share, 16), plain)
+                total = jnp.concatenate([total, output_mine[rest_rows, columns].astype(F32)], 0)
+
+            def pass_on(value):
+                @pl.when(t >= 3)
+                def _():
+                    output_copy(t - 2, d).wait_send()
+                    pl.semaphore_wait(o_credit.at[d], 1)
+
+                o_sent[d, t % 2] = value.astype(LOW)
+                output_copy(t, d).start()
 
             @pl.when(t == 1)
             def _():
-                o_sent[d] = total.astype(LOW)
-                output_copy(t, d).start()
+                pass_on(total)
 
             @pl.when(t >= 2)
             def _():
@@ -1135,38 +1330,37 @@
                 def _():
                     give_credit(o_credit.at[d], d)
 
-                output_copy(t - 1, d).wait_send()
-
                 @pl.when(t < n)
                 def _():
-                    o_sent[d] = more.astype(LOW)
-
-                    @pl.when(t >= 3)
-                    def _():
-                        pl.semaphore_wait(o_credit.at[d], 1)
-
-                    output_copy(t, d).start()
+                    pass_on(more)
 
                 @pl.when(t == n)
                 def _():
-                    output_grad[:, columns] = more.astype(LOW)
+                    o_packs[packs - 1, :, columns] = more.astype(LOW)
+
+    def output_swap(k):
+        return pltpu.make_async_remote_copy(
+            src_ref=o_packs.at[packs - 1],
+            dst_ref=o_packs.at[k - 1],
+            send_sem=swap_send.at[k - 1],
+            recv_sem=swap_recv.at[k - 1],
+            device_id={"rep": lax.rem(pack + k, packs)},
+            device_id_type=MESH,
+        )
 
     def step(t, carry):
         @pl.when(t <= middle)
         def _():
             for d in (0, 1):
-                load(2 * t - 1, d).start()
-                load(2 * t, d).start()
-
-        @pl.when(t == 1)
-        def _():
-            for d in (0, 1):
-                swap(t, d).wait_recv()
-
-        block = block_grads(t)
+                load_rows(2 * t - 1, d).start()
+                load_rows(2 * t, d).start()
+
+        @pl.when(2 * t - 1 <= n)
+        def _():
+            output_step(2 * t - 1)
+
         for u in (0, 1):
             columns = pl.ds(u * (features // 2), features // 2)
-            out[:, columns] = dot_nn(block, joined[:, columns])
             for d in (0, 1):
                 part = pl.ds(d * half, half), columns
 
@@ -1179,19 +1373,24 @@
                     def _():
                         give_credit(credit.at[d, u], d)
 
-                    reduce_copy(t - 1, d, u).wait_send()
-
                 @pl.when(t < n)
                 def _():
-                    sent[d, u] = out[part].astype(LOW)
-
                     @pl.when(t >= 3)
                     def _():
+                        reduce_copy(t - 2, d, u).wait_send()
                         pl.semaphore_wait(credit.at[d, u], 1)
 
+                    sent[d, u, t % 2] = out[part].astype(LOW)
                     reduce_copy(t, d, u).start()
 
-        output_step(t)
+        @pl.when(2 * t <= n)
+        def _():
+            output_step(2 * t)
+
+        @pl.when(2 * t == n)
+        def _():
+            for k in range(1, packs):
+                output_swap(k).start()
 
         @pl.when(t == 1)
         def _():
@@ -1224,9 +1423,23 @@
                 rep_copy(k).start()
             rep_land[packs - 1] = pair_out[...]
 
-        return carry
-
+        @pl.when(t < n)
+        def _():
+            out[...] = dot_nn(block_grads(t + 1), joined[...])
+
+        return carry
+
+    for d in (0, 1):
+        swap(1, d).wait_recv()
+    for load in load_weights:
+        load.wait()
+    out[...] = dot_nn(block_grads(1), joined[...])
     lax.fori_loop(1, n + 1, step, 0)
+    for t in (n - 2, n - 1):
+        for d in (0, 1):
+            output_copy(t, d).wait_send()
+            for u in (0, 1):
+                reduce_copy(t, d, u).wait_send()
 
     near_part[0:1, :] = jnp.zeros((1, features), F32)
     near_part[1:2, :] = dense_gain_part[...]
@@ -1277,24 +1490,21 @@
     lax.fori_loop(1, n + 1, finish, 0)
     for k in range(1, packs):
         rep_copy(k).wait()
-    for i, total in enumerate((query_total, key_total, value_total)):
-        value = rep_land[lax.rem(pack + packs - 1, packs), i].astype(F32)
-        for q in range(1, packs):
-            value += rep_land[lax.rem(pack + 2 * packs - q - 1, packs), i].astype(F32)
-        total[...] = value
+        output_swap(k).wait()
 
 
 def normed_back(
-    grads, joined, hidden_in, gain, grad_mixed, dense_gain_part, normed_all, output_mine, output_there
+    grads, weights, partner_weights, hidden_in, gain, grad_mixed, dense_gain_part, normed_all, output_mine, output_there
 ):
     tokens, r = grads.shape[1:]
-    features = joined.shape[1]
+    features = partner_weights.shape[1]
     devices = lax.axis_size("dp")
     packs = lax.axis_size("rep")
     n = devices // 2
     rows = tokens // devices
     half = rows // 2
-    share = output_mine.shape[0] // n
+    share, plain = output_split(r, packs)
+    carried = share + plain
     mates = 2 * packs
     vmem = pl.BlockSpec(memory_space=pltpu.VMEM)
     hbm = pl.BlockSpec(memory_space=pl.ANY)
@@ -1305,31 +1515,33 @@
             jax.ShapeDtypeStruct((rows, features), F32),
             jax.ShapeDtypeStruct((2, features), F32),
         )
-        + (jax.ShapeDtypeStruct((r, features), F32),) * 3
-        + (jax.ShapeDtypeStruct((share, features), LOW),),
-        in_specs=[hbm] + [vmem] * 5 + [hbm] + [vmem] * packs,
-        out_specs=(vmem,) * 6,
+        + (
+            jax.ShapeDtypeStruct((packs, 3, r, features), LOW),
+            jax.ShapeDtypeStruct((packs, carried, features), LOW),
+        ),
+        in_specs=[hbm] * 5 + [vmem] * 4 + [hbm] + [vmem] * packs,
+        out_specs=(vmem,) * 4,
         scratch_shapes=[
             pltpu.VMEM(grads.shape, LOW),
+            pltpu.VMEM((6 * r, features), LOW),
             pltpu.VMEM((3, n, rows, r), LOW),
-            pltpu.VMEM((2, 2, half, features // 2), LOW),
+            pltpu.VMEM((2, 2, 2, half, features // 2), LOW),
             pltpu.VMEM((2, 2, 2, half, features // 2), LOW),
             pltpu.VMEM((2, rows, features), LOW),
             pltpu.VMEM((6 * r, features), F32),
             pltpu.VMEM((3, r, features), LOW),
             pltpu.VMEM((3, r, features), LOW),
-            pltpu.VMEM((packs, 3, r, features), LOW),
-            pltpu.VMEM((2, share, features // 2), LOW),
-            pltpu.VMEM((2, 2, share, features // 2), LOW),
+            pltpu.VMEM((2, 2, carried, features // 2), LOW),
+            pltpu.VMEM((2, 2, carried, features // 2), LOW),
             pltpu.VMEM((2, features), F32),
             pltpu.VMEM((mates, 2, features), F32),
             pltpu.VMEM((2, features), F32),
             pltpu.VMEM((n, 2, features), F32),
-            dma, dma((2, n)), dma((2, n)), dma((2, 2)), dma((2, 2, 2)),
+            dma, dma((4,)), dma((2, n)), dma((2, n)), dma((2, 2, 2)), dma((2, 2, 2)),
             pltpu.SemaphoreType.REGULAR((2, 2)),
             dma((2, 2)), dma((2,)), dma((packs - 1,)), dma((packs - 1,)),
-            dma((2,)), dma((2, 2)), pltpu.SemaphoreType.REGULAR((2,)),
-            dma((mates,)), dma((mates,)), dma((n,)), dma((n,)),
+            dma((2, 2)), dma((2, 2)), pltpu.SemaphoreType.REGULAR((2,)),
+            dma((packs - 1,)), dma((packs - 1,)), dma((mates,)), dma((mates,)), dma((n,)), dma((n,)),
         ],
         compiler_params=pltpu.CompilerParams(
             collective_id=3, has_side_effects=True, vmem_limit_bytes=56 * MIB
@@ -1339,13 +1551,8 @@
         ),
         name="normed_back",
     )(
-        grads, joined, hidden_in, gain, grad_mixed, dense_gain_part, normed_all, output_mine, *output_there
-    )
-
-
-def rms(values, norm_gain):
-    return (
-        values * lax.rsqrt(jnp.mean(values * values, axis=-1, keepdims=True) + EPSILON) * norm_gain
+        grads, *weights, partner_weights, hidden_in, gain, grad_mixed, dense_gain_part, normed_all,
+        output_mine, *output_there,
     )
 
 
@@ -1387,8 +1594,7 @@
 ):
     devices = lax.axis_size("dp")
     chips = devices // 2
-    hidden_in = tokens[0].astype(F32)
-    tok_dev = hidden_in.shape[0]
+    tok_dev = tokens.shape[1]
     pack_tok = tok_dev * devices
 
     documents, tails = block_document[0], document_tail[0]
@@ -1415,41 +1621,22 @@
     )
 
     order = ring_order(chips)
-    walk = [2 * chip + k for chip in order for k in (0, 1)]
     lanes = [[2 * chip + k for chip in order] for k in (0, 1)]
     grad_low = cotangent[0]
-    early, late = grad_low[: tok_dev // 4], grad_low[tok_dev // 4 :]
-    early = lax.all_gather(early, "dp", axis=0, axis_index_groups=lanes)
-    qkv, early, late = together(qkv, early, late)
-    cotangents = (early, lax.all_gather(late, "dp", axis=0, axis_index_groups=lanes))
+    qkv, grad_late = together(qkv, grad_low)
+    cotangents = lax.all_gather(grad_late, "dp", axis=0, axis_index_groups=lanes)
     gate_other, up_other, down_other = (
         from_partner(gate_weight),
         from_partner(up_weight),
         from_partner(down_weight),
     )
     qkv_weight = jnp.concatenate([query_weight, key_weight, value_weight], 0)
-    joined = jnp.concatenate([qkv_weight, from_partner(qkv_weight)], 0)
 
     attended, log_total = attend(first, tail, qkv)
-    attended_blocks = lax.all_to_all(
-        attended.reshape(devices, tok_dev, r),
-        "dp",
-        split_axis=0,
-        concat_axis=0,
-        tiled=True,
-        axis_index_groups=[walk],
-    )
-    attended_here = attended_blocks.transpose(1, 0, 2).reshape(tok_dev, -1)
-    mixed = hidden_in + dot_nn(attended_here, full_output.reshape(-1, output_weight.shape[1]))
-    normed_two = rms(mixed, dense_gain).astype(LOW)
-
+    mixed, normed_two, attended_blocks = mix(attended, tokens[0], dense_gain[None], full_output)
+    normed_two, qkv_weight = together(normed_two, qkv_weight)
+    qkv_other = from_partner(qkv_weight)
     packs, pack = lax.axis_size("rep"), lax.axis_index("rep")
-    attended_shares = (
-        attended_here.reshape(tok_dev, chips, 2, packs, r // packs)
-        .transpose(2, 3, 0, 1, 4)
-        .reshape(2, packs, tok_dev, -1)
-    )
-    normed_two, joined, attended_shares = together(normed_two, joined, attended_shares)
 
     grad_normed_two, out_parts, _, gate_low, up_a, up_b, down_low = dense(
         normed_two,
@@ -1467,7 +1654,7 @@
     gate_there = pack_swap(gate_low)
 
     grad_mixed, dense_gain_part, grad_heads, output_mine, *output_low = mixed_back(
-        mixed, grad_normed_two, grad_low, dense_gain[None], full_output, attended_shares
+        mixed, grad_normed_two, grad_low, dense_gain[None], full_output, attended_blocks
     )
     output_there = [
         lax.ppermute(low, "rep", [(i, (i + k) % packs) for i in range(packs)])
@@ -1477,23 +1664,15 @@
     up_a, _ = together(up_a, grad_heads)
     up_a_there = pack_swap(up_a)
     grads = attend_back(first, tail, qkv, grad_heads, attended, log_total, cos_t, sin_t)
-    grads, output_there, out_sum, up_a_there, up_b, down_low = together(
-        grads, output_there, out_sum, up_a_there, up_b, down_low
+    grads, output_there, up_a_there, up_b, down_low = together(
+        grads, output_there, up_a_there, up_b, down_low
     )
     up_b_there = pack_swap(up_b)
     down_there = pack_swap(down_low)
-    up_b_there = pack_swap(up_b)
-    down_there = pack_swap(down_low)
-    output_grad = lax.psum_scatter(
-        sum((there.astype(F32) for there in output_there), output_mine.astype(F32)).astype(LOW),
-        "dp",
-        scatter_dimension=0,
-        tiled=True,
-        axis_index_groups=lanes,
-    )
-    input_grad, gain_totals, query_total, key_total, value_total, output_grad = normed_back(
+    input_grad, gain_totals, qkv_packs, output_packs = normed_back(
         grads,
-        joined,
+        (query_weight, key_weight, value_weight),
+        qkv_other,
         tokens[0],
         attention_gain[None],
         grad_mixed,
@@ -1505,14 +1684,18 @@
     input_grad, out_sum, gate_there, up_a_there, up_b_there, down_there = together(
         input_grad, out_sum, gate_there, up_a_there, up_b_there, down_there
     )
-    output_total = lax.all_gather(output_grad, "rep", axis=0, tiled=True)
-    if packs == 2:
-        output_other = lax.ppermute(output_grad, "rep", [(0, 1), (1, 0)])
-        output_total = jnp.where(
-            pack == 0,
-            jnp.concatenate([output_grad, output_other], 0),
-            jnp.concatenate([output_other, output_grad], 0),
-        )
+    slots = [lax.rem(pack + 2 * packs - q - 1, packs) for q in range(packs)]
+    query_total, key_total, value_total = [
+        sum(qkv_packs[slot, i].astype(F32) for slot in (slots if packs > 2 else range(2)))
+        for i in range(3)
+    ]
+    share, plain = output_split(r, packs)
+    output_total = jnp.concatenate([output_packs[slot, :share] for slot in slots], 0).astype(F32)
+    if plain:
+        plain_total = sum(
+            output_packs[slot, share:].astype(F32) for slot in (slots if packs > 2 else range(2))
+        )
+        output_total = jnp.concatenate([output_total, plain_total], 0)
     layer_out = mixed + out_sum.astype(F32)
     return (
         layer_out[None].astype(LOW),
@@ -1521,7 +1704,7 @@
         query_total,
         key_total,
         value_total,
-        output_total.astype(F32),
+        output_total,
         gain_totals[1],
         pack_add(gate_low, gate_there),
         jnp.concatenate([pack_add(up_a, up_a_there), pack_add(up_b, up_b_there)], 0),

time: 700 us -> 678 us (0.969)
  Pallas kernels: 575 us -> 605 us
  waiting for transfers between devices: 42.9 us -> 17.9 us
  local copies, waits for them, and re-layouts: 29.1 us -> 10.2 us
    pallas_call x0 -> x1, Pallas kernels: none -> 43.2 us  [mix(): pl.pallas_call(mixed_kernel, out_shape=(jax.ShapeDtypeStruct((rows, featu...]
    all_to_all x1 -> x0, waiting for transfers between devices: 28.7 us -> none  [body(): lax.all_to_all(attended.reshape(devices, tok_dev, r), 'dp', split_axis=0,...]
    all_gather x2 -> x1, waiting for transfers between devices: 0.02 us -> 17.8 us  [body(): lax.all_gather(grad_late, 'dp', axis=0, axis_index_groups=lanes)]
    pallas_call x1, Pallas kernels: 133 us -> 117 us  [gather_project(): pl.pallas_call(gather_project_kernel, out_shape=(jax.ShapeDtypeStruct((3,...]
    unnamed x58 -> x43, local copies, waits for them, and re-layouts: 17.8 us -> 8.42 us
  transfers between devices with their start and end apart: 14 -> 11, of which waited for: 5 -> 1; matrix products, arithmetic and copies ran while one was open for 3% -> 1% of each run, Pallas kernels for 57% -> 45%
where the time goes in v6:
time: 678 us; the launch traced here: 677 us
  Pallas kernels  605 us (89%)
  other arithmetic  23.1 us (3%)
  waiting for transfers between devices  17.9 us (3%)
  between operations  14.3 us (2%)
  local copies, waits for them, and re-layouts  10.2 us (2%)
    pallas_call x1, Pallas kernels, dense(): pl.pallas_call(dense_kernel, out_shape=(jax.ShapeDtypeStruct((rows, featu...  184 us
    pallas_call x1, Pallas kernels, normed_back(): pl.pallas_call(functools.partial(normed_back_kernel, packs), out_shape=(j...  132 us
    pallas_call x1, Pallas kernels, gather_project(): pl.pallas_call(gather_project_kernel, out_shape=(jax.ShapeDtypeStruct((3,...  117 us
    pallas_call x1, Pallas kernels, mixed_back(): pl.pallas_call(functools.partial(mixed_back_kernel, packs), out_shape=(ja...  46.8 us
    pallas_call x1, Pallas kernels, attend_back(): pl.pallas_call(functools.partial(attend_back_kernel, lax.axis_size('dp')...  43.8 us
    pallas_call x1, Pallas kernels, mix(): pl.pallas_call(mixed_kernel, out_shape=(jax.ShapeDtypeStruct((rows, featu...  43.2 us
    pallas_call x1, Pallas kernels, attend(): pl.pallas_call(functools.partial(attend_kernel, lax.axis_size('dp') // 2)...  38.1 us
    all_gather x1, waiting for transfers between devices, body(): lax.all_gather(grad_late, 'dp', axis=0, axis_index_groups=lanes)  17.8 us
  transfers between devices with their start and end apart: 11, of which 1 were waited for; matrix products, arithmetic and copies ran while one was open for 1% of the time, Pallas kernels for 45%

profile of v6, /device:TPU:0, one launch (start us, length us, event | category | flops | bytes accessed | tf_op | source)
XLA Modules:
  0.0 677.2 jit_solution(8702215535428103860)
XLA Ops:
  7.2 0.9 convert_reduce_fusion.first_ref
  8.2 2.8 multiply_sine_fusion
  11.0 116.8 %gather_project.1 = (bf16[3,4096,128]{2,1,0:T(8,128)(2,1)}, bf16[8,256,2048]{2,1,0:T(8,128)(2,1)}, bf16[16,128,2048]{2,1,0:T(8,128)(2,1)}) custom-call(bf16[256,2048]{1,0:T(8,128)(2,1)} %bitcast.31, f32[1,2048]{1,0:T(1,128)} %bitcast.41, bf16[128,2048]{1,0:T(8,128)(2,1)} %query_w.3, bf16[128,2048]{1,0:T(8,128)(2,1)} %key_w.3, bf16[128,2048]{1,0:T(8,128)(2,1)} %value_w.3, ...), custom_call_target="tpu_custom_call" | custom-call | flops 6442450944 | bytes 335544320 | tf_op jit(solution)/shard_map/gather_project/pallas_call | solution.py:350
  127.9 0.4 collective-permute-start
  128.3 0.2 collective-permute-start.1
  128.4 0.4 collective-permute-start.2
  129.0 1.9 copy-done.5
  130.9 38.1 %attend.1 = (bf16[4096,128]{1,0:T(8,128)(2,1)S(1)}, f32[32,256]{1,0:T(8,128)S(1)}) custom-call(s32[32]{0:T(128)S(1)} %convert_reduce_fusion.first_ref, s32[32]{0:T(128)S(1)} %add_select_fusion.tail_ref, bf16[3,4096,128]{2,1,0:T(8,128)(2,1)S(1)} %copy-done.5), custom_call_target="tpu_custom_call" | custom-call | flops 17179869184 | bytes 125829120 | tf_op jit(solution)/shard_map/attend/pallas_call | solution.py:468
  169.1 1.0 copy-done
  170.1 43.2 %mix.1 = (f32[256,2048]{1,0:T(8,128)}, bf16[256,2048]{1,0:T(8,128)(2,1)}, bf16[16,256,128]{2,1,0:T(8,128)(2,1)}) custom-call(bf16[4096,128]{1,0:T(8,128)(2,1)} %copy-done, bf16[256,2048]{1,0:T(8,128)(2,1)} %bitcast.32, f32[1,2048]{1,0:T(1,128)} %bitcast.38, bf16[16,128,2048]{2,1,0:T(8,128)(2,1)} %get-tuple-element.56.output_all), custom_call_target="tpu_custom_call" | custom-call | flops 2147483648 | bytes 104857600 | tf_op jit(solution)/shard_map/mix/pallas_call | solution.py:689
  213.3 1.3 pad_maximum_fusion.1
  214.6 17.8 %all-gather.3.cloned.1.call-done = bf16[2048,2048]{1,0:T(8,128)(2,1)} async-done(((bf16[256,2048]{1,0:T(8,128)(2,1)}), bf16[2048,2048]{1,0:T(8,128)(2,1)}) %all-gather.3.cloned.1.call-update) | async-done | bytes 8388624 | tf_op jit(solution)/shard_map/all_gather | solution.py:1627
  232.5 184.2 %dense.1 = (f32[256,2048]{1,0:T(8,128)}, bf16[8,256,2048]{2,1,0:T(8,128)(2,1)}, bf16[8,256,2048]{2,1,0:T(8,128)(2,1)}, bf16[512,2048]{1,0:T(8,128)(2,1)}, bf16[1...) custom-call(bf16[256,2048]{1,0:T(8,128)(2,1)} %get-tuple-element.59.normed, ...), custom_call_target="tpu_custom_call" | custom-call | flops 77309411328 | bytes 524288000 | tf_op jit(solution)/shard_map/dense/pallas_call | solution.py:960
  416.7 1.5 collective-permute-start.3
  418.2 46.8 %mixed_back.1 = (f32[256,2048]{1,0:T(8,128)}, f32[1,2048]{1,0:T(1,128)}, bf16[4096,128]{1,0:T(8,128)(2,1)}, bf16[640,2048]{1,0:T(8,128)(2,1)}, bf16[384,2048]{1,0:T(8,128)(2,1)}) custom-call(f32[256,2048]{1,0:T(8,128)} %get-tuple-element.57.mixed_in, f32[256,2048]{1,0:T(8,128)} %get-tuple-element.61.grad_in, bf16[256,2048]{1,0:T(8,128)(2,1)} %bitcast.35, ...), custom_call_target="tpu_custom_call" | custom-call | flops 4294967296 | bytes 136314880 | tf_op jit(solution)/shard_map/mixed_back/pallas_call | solution.py:1148
  465.1 2.0 collective-permute-start.5
  467.1 1.2 copy-done.4
  468.4 43.8 %attend_back.1.grads_in = bf16[3,4096,128]{2,1,0:T(8,128)(2,1)S(1)} custom-call(s32[32]{0:T(128)S(1)} %convert_reduce_fusion.first_ref, s32[32]{0:T(128)S(1)} %add_select_fusion.tail_ref, bf16[3,4096,128]{2,1,0:T(8,128)(2,1)S(1)} %copy-done.6, bf16[4096,128]{1,0:T(8,128)(2,1)S(1)} %copy-done.4, bf16[4096,128]{1,0:T(8,128)(2,1)S(1)} %copy-done.1, ...), custom_call_target="tpu_custom_call" | custom-call | flops 42949672960 | bytes 251658240 | tf_op jit(solution)/shard_map/attend_back/pallas_call | solution.py:570
  512.2 1.7 copy-done.7
  513.9 1.1 copy-done.18
  515.1 2.0 collective-permute-start.7
  517.0 132.1 %normed_back.1 = (f32[256,2048]{1,0:T(8,128)}, f32[2,2048]{1,0:T(2,128)}, bf16[2,3,128,2048]{3,2,1,0:T(8,128)(2,1)}, bf16[2,80,2048]{2,1,0:T(8,128)(2,1)}) custom-call(bf16[3,4096,128]{2,1,0:T(8,128)(2,1)} %copy-done.7, bf16[128,2048]{1,0:T(8,128)(2,1)} %query_w.3, bf16[128,2048]{1,0:T(8,128)(2,1)} %key_w.3, bf16[128,2048]{1,0:T(8,128)(2,1)} %value_w.3, ...), custom_call_target="tpu_custom_call" | custom-call | flops 12884901888 | bytes 335544320 | tf_op jit(solution)/shard_map/normed_back/pallas_call | solution.py:1512
  649.1 1.0 add_bitcast_fusion.3
  650.2 1.2 dynamic-slice_bitcast_fusion.1
  651.4 1.1 pad_maximum_fusion.2
  652.5 0.6 fusion.1
  653.1 1.8 add_bitcast_fusion
  655.1 2.6 convert_add_fusion.2
  657.9 1.3 fusion
  659.2 2.5 pad_maximum_fusion
  661.7 7.3 %convert_add_fusion = (f32[512,2048]{1,0:T(8,128)}, f32[512,2048]{1,0:T(8,128)}) fusion(bf16[512,2048]{1,0:T(8,128)(2,1)S(1)} %collective-permute-done.8, bf16[512,2048]{1,0:T(8,128)(2,1)} %get-tuple-element.85, bf16[512,2048]{1,0:T(8,128)(2,1)} %collective-permute-done.3, bf16[512,2048]{1,0:T(8,128)(2,1)S(1)} %copy-done.11), kind=kLoop, calls=%fused_computation.1 | loop fusion | flops 6291456 | bytes 16777216 | tf_op jit(solution)/shard_map/add | solution.py:1572
  669.0 1.3 copy.25
  (62 shorter events, 1.0 us)
Async XLA Ops:
  7.2 225.3 %all-gather.3.cloned.1.call-start = ((), (), s32[]{:S(2)}) async-start(), calls=%async_computation.2 | async-start | bytes 9437184 | tf_op jit(solution)/shard_map/all_gather | solution.py:1627
  11.0 117.8 %copy-start.19 = (s32[1,8]{1,0:T(1,128)S(1)}, s32[1,8]{1,0:T(1,128)}, u32[]{:S(2)}) copy-start(s32[1,8]{1,0:T(1,128)} %param.24) | copy-start | bytes 100
  11.0 117.8 %copy-start.20 = (s32[1,32]{1,0:T(1,128)S(1)}, s32[1,32]{1,0:T(1,128)}, u32[]{:S(2)}) copy-start(s32[1,32]{1,0:T(1,128)} %param.23) | copy-start | bytes 388
  127.8 527.1 %reduce-scatter.2.cloned.1.call-start = ((), (), s32[]{:S(2)}) async-start(), calls=%async_computation.1 | async-start | bytes 9437184 | tf_op jit(solution)/shard_map/reduce_scatter | solution.py:1647
  127.9 86.8 %collective-permute-start = (bf16[512,2048]{1,0:T(8,128)(2,1)}, bf16[512,2048]{1,0:T(8,128)(2,1)}, u32[]{:S(2)}, u32[]{:S(2)}) collective-permute-start(bf16[512,2048]{1,0:T(8,128)(2,1)} %gate_w.1), channel_id=1, source_target_pairs={{0,2},{2,0},{4,6},{6,4},{8,10},{10,8},{12,14},{14,12},{16,18},{18,... | collective-permute-start | bytes 6291464 | tf_op jit(solution)/shard_map/ppermute | solution.py:1561
  128.3 86.3 %collective-permute-start.1 = (bf16[512,2048]{1,0:T(8,128)(2,1)}, bf16[512,2048]{1,0:T(8,128)(2,1)}, u32[]{:S(2)}, u32[]{:S(2)}) collective-permute-start(bf16[512,2048]{1,0:T(8,128)(2,1)} %up_w.1), channel_id=1, source_target_pairs={{0,2},{2,0},{4,6},{6,4},{8,10},{10,8},{12,14},{14,12},{16,18},{18,... | collective-permute-start | bytes 6291464 | tf_op jit(solution)/shard_map/ppermute | solution.py:1561
  128.4 86.2 %collective-permute-start.2 = (bf16[512,2048]{1,0:T(8,128)(2,1)}, bf16[512,2048]{1,0:T(8,128)(2,1)}, u32[]{:S(2)}, u32[]{:S(2)}) collective-permute-start(bf16[512,2048]{1,0:T(8,128)(2,1)} %down_w.1), channel_id=1, source_target_pairs={{0,2},{2,0},{4,6},{6,4},{8,10},{10,8},{12,14},{14,12},{16,18},{18,... | collective-permute-start | bytes 6291464 | tf_op jit(solution)/shard_map/ppermute | solution.py:1561
  129.0 1.9 copy-start.5
  169.1 1.0 copy-start
  170.1 43.2 %copy-start.13 = (bf16[128,2048]{1,0:T(8,128)(2,1)S(1)}, bf16[128,2048]{1,0:T(8,128)(2,1)}, u32[]{:S(2)}) copy-start(bf16[128,2048]{1,0:T(8,128)(2,1)} %query_w.3) | copy-start | bytes 1572868
  170.1 43.2 %copy-start.14 = (bf16[128,2048]{1,0:T(8,128)(2,1)S(1)}, bf16[128,2048]{1,0:T(8,128)(2,1)}, u32[]{:S(2)}) copy-start(bf16[128,2048]{1,0:T(8,128)(2,1)} %key_w.3) | copy-start | bytes 1572868
  170.1 43.2 %copy-start.15 = (bf16[128,2048]{1,0:T(8,128)(2,1)S(1)}, bf16[128,2048]{1,0:T(8,128)(2,1)}, u32[]{:S(2)}) copy-start(bf16[128,2048]{1,0:T(8,128)(2,1)} %value_w.3) | copy-start | bytes 1572868
  416.7 48.4 %collective-permute-start.3 = (bf16[512,2048]{1,0:T(8,128)(2,1)}, bf16[512,2048]{1,0:T(8,128)(2,1)}, u32[]{:S(2)}, u32[]{:S(2)}) collective-permute-start(bf16[512,2048]{1,0:T(8,128)(2,1)} %get-tuple-element.64), channel_id=1, source_target_pairs={{0,1},{1,0},{2,3},{3,2},{4,5},{5,4},{6,7},{7,6},{8,9},{9,8},{10,11... | collective-permute-start | bytes 6291464 | tf_op jit(solution)/shard_map/ppermute | solution.py:1566
  418.2 98.9 %collective-permute-start.6 = (bf16[384,2048]{1,0:T(8,128)(2,1)}, bf16[384,2048]{1,0:T(8,128)(2,1)}, u32[]{:S(2)}, u32[]{:S(2)}) collective-permute-start(bf16[384,2048]{1,0:T(8,128)(2,1)} %pad_maximum_fusion.1), channel_id=1, source_target_pairs={{0,2},{2,0},{4,6},{6,4},{8,10},{10,8},{12,14},{14,12},{16,18},{18,... | collective-permute-start | bytes 4718600 | tf_op jit(solution)/shard_map/ppermute | solution.py:1561
  418.2 46.9 %copy-start.16 = (bf16[128,2048]{1,0:T(8,128)(2,1)S(1)}, bf16[128,2048]{1,0:T(8,128)(2,1)}, u32[]{:S(2)}) copy-start(bf16[128,2048]{1,0:T(8,128)(2,1)} %get-tuple-element.70) | copy-start | bytes 1572868
  418.2 48.9 %copy-start.1 = (bf16[4096,128]{1,0:T(8,128)(2,1)S(1)}, bf16[4096,128]{1,0:T(8,128)(2,1)}, u32[]{:S(2)}) copy-start(bf16[4096,128]{1,0:T(8,128)(2,1)} %copy-done) | copy-start | bytes 3145732
  418.2 48.9 %copy-start.2 = (f32[32,4096]{1,0:T(8,128)S(1)}, f32[32,4096]{1,0:T(8,128)}, u32[]{:S(2)}) copy-start(f32[32,4096]{1,0:T(8,128)} %get-tuple-element.100.sin_t) | copy-start | bytes 1572868
  418.2 48.9 %copy-start.3 = (f32[32,4096]{1,0:T(8,128)S(1)}, f32[32,4096]{1,0:T(8,128)}, u32[]{:S(2)}) copy-start(f32[32,4096]{1,0:T(8,128)} %get-tuple-element.101.cos_t) | copy-start | bytes 1572868
  418.2 48.9 %copy-start.6 = (bf16[3,4096,128]{2,1,0:T(8,128)(2,1)S(1)}, bf16[3,4096,128]{2,1,0:T(8,128)(2,1)}, u32[]{:S(2)}) copy-start(bf16[3,4096,128]{2,1,0:T(8,128)(2,1)} %get-tuple-element.54.qkv) | copy-start | bytes 9437188
  465.0 48.8 %collective-permute-start.4 = (bf16[384,2048]{1,0:T(8,128)(2,1)}, bf16[384,2048]{1,0:T(8,128)(2,1)S(1)}, u32[]{:S(2)}, u32[]{:S(2)}) collective-permute-start(bf16[384,2048]{1,0:T(8,128)(2,1)} %get-tuple-element.68), channel_id=1, source_target_pairs={{0,1},{1,0},{2,3},{3,2},{4,5},{5,4},{6,7},{7,6},{8,9},{9,8},{10,11... | collective-permute-start | bytes 4718600 | tf_op jit(solution)/shard_map/ppermute | solution.py:1660
  465.1 48.7 %collective-permute-start.5 = (bf16[128,2048]{1,0:T(8,128)(2,1)S(1)}, bf16[128,2048]{1,0:T(8,128)(2,1)S(1)}, u32[]{:S(2)}, u32[]{:S(2)}) collective-permute-start(bf16[128,2048]{1,0:T(8,128)(2,1)S(1)} %copy-done.16), channel_id=1, source_target_pairs={{0,1},{1,0},{2,3},{3,2},{4,5},{5,4},{6,7},{7,6},{8,9},{9,8},{10,11... | collective-permute-start | bytes 1572872 | tf_op jit(solution)/shard_map/ppermute | solution.py:1566
  467.1 1.3 copy-start.4
  512.2 1.7 copy-start.7
  513.9 1.1 copy-start.18
  515.0 139.9 %collective-permute-start.8 = (bf16[512,2048]{1,0:T(8,128)(2,1)}, bf16[512,2048]{1,0:T(8,128)(2,1)S(1)}, u32[]{:S(2)}, u32[]{:S(2)}) collective-permute-start(bf16[512,2048]{1,0:T(8,128)(2,1)} %get-tuple-element.85), channel_id=1, source_target_pairs={{0,1},{1,0},{2,3},{3,2},{4,5},{5,4},{6,7},{7,6},{8,9},{9,8},{10,11... | collective-permute-start | bytes 6291464 | tf_op jit(solution)/shard_map/ppermute | solution.py:1566
  515.1 139.9 %collective-permute-start.7 = (bf16[384,2048]{1,0:T(8,128)(2,1)}, bf16[384,2048]{1,0:T(8,128)(2,1)}, u32[]{:S(2)}, u32[]{:S(2)}) collective-permute-start(bf16[384,2048]{1,0:T(8,128)(2,1)} %get-tuple-element.84), channel_id=1, source_target_pairs={{0,1},{1,0},{2,3},{3,2},{4,5},{5,4},{6,7},{7,6},{8,9},{9,8},{10,11... | collective-permute-start | bytes 4718600 | tf_op jit(solution)/shard_map/ppermute | solution.py:1566
  650.1 2.4 copy-start.17
  650.1 3.0 copy-start.8
  655.1 2.7 copy-start.9
  655.1 2.8 copy-start.12
  659.2 2.5 copy-start.11
  661.7 7.3 %copy-start.10 = (f32[256,2048]{1,0:T(8,128)S(1)}, f32[256,2048]{1,0:T(8,128)}, u32[]{:S(2)}) copy-start(f32[256,2048]{1,0:T(8,128)} %get-tuple-element.87) | copy-start | bytes 6291460
Sparse Core Ops, SparseCore 0:
  127.9 104.4 all-gather.2
  416.8 103.9 reduce-scatter.1

commit v7 on v6

--- a/solution.py
+++ b/solution.py
@@ -13,6 +13,7 @@
 BLOCK = 128
 CHUNK = 512
 FF_TILE = 256
+STRIPE = 64
 EPSILON = 1e-05
 ROPE_BASE = 130000.0
 MASKED_SCORE = -1e30
@@ -901,23 +902,21 @@
     for i in (own_tiles - 2, own_tiles - 1):
         pair_copy(i).wait_send()
 
-    pieces = ((gate_grad,), (up_a, up_b), (down_grad,))
-
     def total_copies(i):
         matrix, low = i // (own // FF_TILE), (i % (own // FF_TILE)) * FF_TILE
-        copies, begin = [], 0
-        for piece in pieces[matrix]:
-            end = begin + piece.shape[0]
-            first, last = max(begin, low), min(end, low + FF_TILE)
-            if first < last:
+        if matrix != 1:
+            target = (gate_grad, None, down_grad)[matrix].at[pl.ds(low, FF_TILE)]
+            return [pltpu.make_async_copy(cast_buf.at[i % 2], target, cast_sem.at[i % 2, 0])]
+        copies = []
+        for j in range(FF_TILE // STRIPE):
+            for target, first, count in ((up_a, 0, STRIPE // 4), (up_b, STRIPE // 4, 3 * STRIPE // 4)):
                 copies.append(
                     pltpu.make_async_copy(
-                        cast_buf.at[i % 2, pl.ds(first - low, last - first)],
-                        piece.at[pl.ds(first - begin, last - first)],
+                        cast_buf.at[i % 2, pl.ds(j * STRIPE + first, count)],
+                        target.at[pl.ds((low // STRIPE + j) * count, count)],
                         cast_sem.at[i % 2, len(copies)],
                     )
                 )
-            begin = end
         return copies
 
     for i in range(own_tiles):
@@ -983,7 +982,7 @@
             pltpu.VMEM((own_tiles, FF_TILE, features), LOW),
             dma((2, n)), dma((2, n)), dma((2,)), dma((2, 2)),
             pltpu.SemaphoreType.REGULAR((2,)),
-            dma((4,)), dma((6,)), dma((2, 2)), dma((2,)), dma((own_tiles,)),
+            dma((4,)), dma((6,)), dma((2, 2 * FF_TILE // STRIPE)), dma((2,)), dma((own_tiles,)),
         ],
         compiler_params=pltpu.CompilerParams(
             collective_id=2, has_side_effects=True, vmem_limit_bytes=62 * MIB
@@ -1183,7 +1182,7 @@
     (
         out, gains, rep_land, o_packs,
         grads, joined, partner_grads, sent, landed, x_buf, parts, pair_out, pair_land,
-        o_sent, o_landed, near_part, near_land, near_sum, far_land,
+        o_sent, o_landed, far_part, far_land, near_part, near_land,
         in_sem, w_sem, p_send, p_recv, rs_send, rs_recv, credit, x_sem, pair_sem, rep_send, rep_recv,
         o_send, o_recv, o_credit, swap_send, swap_recv, near_send, near_recv, far_send, far_recv,
     ) = rest[packs - 1 :]
@@ -1348,6 +1347,42 @@
             device_id_type=MESH,
         )
 
+    def copies_to(src, land, own, send_sem, recv_sem, device, count):
+        return [
+            pltpu.make_async_remote_copy(
+                src_ref=src,
+                dst_ref=land.at[own],
+                send_sem=send_sem.at[k],
+                recv_sem=recv_sem.at[k],
+                device_id=device(k),
+                device_id_type=MESH,
+            )
+            for k in range(1, count)
+        ]
+
+    def far_copies():
+        return copies_to(far_part, far_land, ring.chip, far_send, far_recv, far, n)
+
+    def near_copies():
+        return copies_to(near_part, near_land, mate, near_send, near_recv, near, mates)
+
+    def collect(copies, src, land, own, count):
+        land[own] = src[...]
+        for copy in copies:
+            copy.wait()
+        total = land[0]
+        for k in range(1, count):
+            total += land[k]
+        return total
+
+    def first_gain():
+        def add(i, total):
+            at = pl.ds(pl.multiple_of(i * 64, 64), 64)
+            product = joined[at, :].astype(F32) * parts[at, :]
+            return total + jnp.sum(product, axis=0, keepdims=True)
+
+        return lax.fori_loop(0, 6 * r // 64, add, jnp.zeros((1, features), F32)) / gain[...]
+
     def step(t, carry):
         @pl.when(t <= middle)
         def _():
@@ -1355,10 +1390,6 @@
                 load_rows(2 * t - 1, d).start()
                 load_rows(2 * t, d).start()
 
-        @pl.when(2 * t - 1 <= n)
-        def _():
-            output_step(2 * t - 1)
-
         for u in (0, 1):
             columns = pl.ds(u * (features // 2), features // 2)
             for d in (0, 1):
@@ -1383,9 +1414,9 @@
                     sent[d, u, t % 2] = out[part].astype(LOW)
                     reduce_copy(t, d, u).start()
 
-        @pl.when(2 * t <= n)
-        def _():
-            output_step(2 * t)
+            @pl.when(2 * t - 1 + u <= n)
+            def _():
+                output_step(2 * t - 1 + u)
 
         @pl.when(2 * t == n)
         def _():
@@ -1413,6 +1444,10 @@
             for i in range(3):
                 pair_out[i] = parts[pl.ds((3 + i) * r, r), :].astype(LOW)
             pair_copy().start()
+            far_part[0:1, :] = first_gain()
+            far_part[1:2, :] = dense_gain_part[...]
+            for copy in far_copies():
+                copy.start()
 
         @pl.when(t == middle + 1)
         def _():
@@ -1422,6 +1457,12 @@
             for k in range(1, packs):
                 rep_copy(k).start()
             rep_land[packs - 1] = pair_out[...]
+
+        @pl.when(t == middle + 2)
+        def _():
+            near_part[...] = collect(far_copies(), far_part, far_land, ring.chip, n)
+            for copy in near_copies():
+                copy.start()
 
         @pl.when(t < n)
         def _():
@@ -1441,9 +1482,6 @@
             for u in (0, 1):
                 reduce_copy(t, d, u).wait_send()
 
-    near_part[0:1, :] = jnp.zeros((1, features), F32)
-    near_part[1:2, :] = dense_gain_part[...]
-
     def close(i, carry):
         span = pl.ds(pl.multiple_of(i * 16, 16), 16)
         value = hidden_in[span, :].astype(F32)
@@ -1452,35 +1490,9 @@
         scaled = grad * gain[...]
         shift = jnp.mean(value * scaled, axis=1, keepdims=True)
         out[span, :] = grad_mixed[span, :] + scale * scaled - value * (scale * scale * scale * shift)
-        near_part[0:1, :] += jnp.sum(grad * value * scale, axis=0, keepdims=True)
         return carry
 
     lax.fori_loop(0, rows // 16, close, 0)
-
-    def exchange(src, land, own, send_sem, recv_sem, device, count):
-        copies = [
-            pltpu.make_async_remote_copy(
-                src_ref=src,
-                dst_ref=land.at[own],
-                send_sem=send_sem.at[k],
-                recv_sem=recv_sem.at[k],
-                device_id=device(k),
-                device_id_type=MESH,
-            )
-            for k in range(1, count)
-        ]
-        for copy in copies:
-            copy.start()
-        land[own] = src[...]
-        for copy in copies:
-            copy.wait()
-        total = land[0]
-        for k in range(1, count):
-            total += land[k]
-        return total
-
-    near_sum[...] = exchange(near_part, near_land, mate, near_send, near_recv, near, mates)
-    gains[...] = exchange(near_sum, far_land, ring.chip, far_send, far_recv, far, n)
 
     def finish(t, carry):
         for d in (0, 1):
@@ -1488,6 +1500,7 @@
         return carry
 
     lax.fori_loop(1, n + 1, finish, 0)
+    gains[...] = collect(near_copies(), near_part, near_land, mate, mates)
     for k in range(1, packs):
         rep_copy(k).wait()
         output_swap(k).wait()
@@ -1534,9 +1547,9 @@
             pltpu.VMEM((2, 2, carried, features // 2), LOW),
             pltpu.VMEM((2, 2, carried, features // 2), LOW),
             pltpu.VMEM((2, features), F32),
+            pltpu.VMEM((n, 2, features), F32),
+            pltpu.VMEM((2, features), F32),
             pltpu.VMEM((mates, 2, features), F32),
-            pltpu.VMEM((2, features), F32),
-            pltpu.VMEM((n, 2, features), F32),
             dma, dma((4,)), dma((2, n)), dma((2, n)), dma((2, 2, 2)), dma((2, 2, 2)),
             pltpu.SemaphoreType.REGULAR((2, 2)),
             dma((2, 2)), dma((2,)), dma((packs - 1,)), dma((packs - 1,)),
@@ -1556,6 +1569,71 @@
     )
 
 
+def last_sums_kernel(packs, *refs):
+    gate, up_a, up_b, down, gate_o, up_a_o, up_b_o, down_o, qkv, mixed, out_sum, grad_in, output = refs[:13]
+    gate_t, up_t, down_t, query_t, key_t, value_t, layer, grad, output_t = refs[13:]
+
+    def add(low, other):
+        if packs == 2:
+            return low[...].astype(F32) + other[...].astype(F32)
+        return other[...].astype(F32)
+
+    gate_t[...] = add(gate, gate_o)
+    down_t[...] = add(down, down_o)
+    up_t[...] = jnp.concatenate([add(up_a, up_a_o), add(up_b, up_b_o)], 0)
+    pack = lax.axis_index("rep")
+    slots = [lax.rem(pack + 2 * packs - q - 1, packs) for q in range(packs)]
+    for i, target in enumerate((query_t, key_t, value_t)):
+        total = qkv[slots[0], i].astype(F32)
+        for slot in slots[1:]:
+            total += qkv[slot, i].astype(F32)
+        target[...] = total
+
+    @pl.when(pl.program_id(0) == 0)
+    def _():
+        r = output_t.shape[0]
+        share, plain = output_split(r, packs)
+        for q, slot in enumerate(slots):
+            output_t[q * share : (q + 1) * share, :] = output[slot, :share].astype(F32)
+        if plain:
+            total = output[slots[0], share:].astype(F32)
+            for slot in slots[1:]:
+                total += output[slot, share:].astype(F32)
+            output_t[r - plain :, :] = total
+
+    layer[...] = (mixed[...] + out_sum[...].astype(F32)).astype(LOW)
+    grad[...] = grad_in[...]
+
+
+def last_sums(lows, others, qkv, mixed, out_sum, grad_in, output):
+    own, features = lows[0].shape
+    rows, r = mixed.shape[0], qkv.shape[2]
+    packs = qkv.shape[0]
+    steps = own // STRIPE
+
+    def striped(array):
+        return pl.BlockSpec((array.shape[0] // steps, features), lambda i: (i, 0))
+
+    wide = jax.ShapeDtypeStruct((own, features), F32)
+    narrow = jax.ShapeDtypeStruct((r, features), F32)
+    layer = jax.ShapeDtypeStruct((rows, features), LOW)
+    out_shape = (wide,) * 3 + (narrow,) * 3 + (layer, grad_in, narrow)
+    return pl.pallas_call(
+        functools.partial(last_sums_kernel, packs),
+        out_shape=tuple(jax.ShapeDtypeStruct(a.shape, a.dtype) for a in out_shape),
+        grid=(steps,),
+        in_specs=[striped(a) for a in (*lows, *others)]
+        + [pl.BlockSpec((packs, 3, r // steps, features), lambda i: (0, 0, i, 0))]
+        + [striped(a) for a in (mixed, out_sum, grad_in)]
+        + [pl.BlockSpec(output.shape, lambda i: (0, 0, 0))],
+        out_specs=tuple(striped(a) for a in out_shape[:-1])
+        + (pl.BlockSpec((r, features), lambda i: (0, 0)),),
+        compiler_params=pltpu.CompilerParams(vmem_limit_bytes=62 * MIB),
+        cost_estimate=pl.CostEstimate(flops=8 * own * features, bytes_accessed=40 * MIB, transcendentals=0),
+        name="last_sums",
+    )(*lows, *others, qkv, mixed, out_sum, grad_in, output)
+
+
 def from_partner(value):
     devices = lax.axis_size("dp")
     return lax.ppermute(value, "dp", [(i, i ^ 1) for i in range(devices)])
@@ -1565,12 +1643,6 @@
     if lax.axis_size("rep") == 2:
         return lax.ppermute(low, "rep", [(0, 1), (1, 0)])
     return lax.psum(low, "rep")
-
-
-def pack_add(low, other):
-    if lax.axis_size("rep") == 2:
-        return low.astype(F32) + other.astype(F32)
-    return other.astype(F32)
 
 
 def together(*values):
@@ -1605,10 +1677,13 @@
     tail = jnp.where(last, own_tail, BLOCK).astype(jnp.int32)
     block_index = jnp.arange(documents.shape[0], dtype=jnp.int32)
     inside = jnp.arange(BLOCK, dtype=jnp.int32)
-    position = ((block_index - first)[:, None] * BLOCK + inside[None, :]).reshape(-1)
     frequency = ROPE_BASE ** (-(jnp.arange(HALF, dtype=F32) * (2.0 / HEAD_DIM)))
-    angles = position.astype(F32)[None, :] * frequency[:, None]
-    cos_t, sin_t = jnp.cos(angles), jnp.sin(angles)
+    start = ((block_index - first) * BLOCK).astype(F32)[None, :] * frequency[:, None]
+    within = inside.astype(F32)[None, :] * frequency[:, None]
+    cos_a, sin_a = jnp.cos(start)[:, :, None], jnp.sin(start)[:, :, None]
+    cos_b, sin_b = jnp.cos(within)[:, None, :], jnp.sin(within)[:, None, :]
+    cos_t = (cos_a * cos_b - sin_a * sin_b).reshape(HALF, -1)
+    sin_t = (sin_a * cos_b + cos_a * sin_b).reshape(HALF, -1)
     r = query_weight.shape[0]
 
     qkv, normed_all, full_output = gather_project(
@@ -1684,21 +1759,19 @@
     input_grad, out_sum, gate_there, up_a_there, up_b_there, down_there = together(
         input_grad, out_sum, gate_there, up_a_there, up_b_there, down_there
     )
-    slots = [lax.rem(pack + 2 * packs - q - 1, packs) for q in range(packs)]
-    query_total, key_total, value_total = [
-        sum(qkv_packs[slot, i].astype(F32) for slot in (slots if packs > 2 else range(2)))
-        for i in range(3)
-    ]
-    share, plain = output_split(r, packs)
-    output_total = jnp.concatenate([output_packs[slot, :share] for slot in slots], 0).astype(F32)
-    if plain:
-        plain_total = sum(
-            output_packs[slot, share:].astype(F32) for slot in (slots if packs > 2 else range(2))
-        )
-        output_total = jnp.concatenate([output_total, plain_total], 0)
-    layer_out = mixed + out_sum.astype(F32)
+    (
+        gate_total, up_total, down_total, query_total, key_total, value_total, layer_out, input_grad, output_total
+    ) = last_sums(
+        (gate_low, up_a, up_b, down_low),
+        (gate_there, up_a_there, up_b_there, down_there),
+        qkv_packs,
+        mixed,
+        out_sum,
+        input_grad,
+        output_packs,
+    )
     return (
-        layer_out[None].astype(LOW),
+        layer_out[None],
         input_grad[None],
         gain_totals[0],
         query_total,
@@ -1706,9 +1779,9 @@
         value_total,
         output_total,
         gain_totals[1],
-        pack_add(gate_low, gate_there),
-        jnp.concatenate([pack_add(up_a, up_a_there), pack_add(up_b, up_b_there)], 0),
-        pack_add(down_low, down_there),
+        gate_total,
+        up_total,
+        down_total,
     )
 
 

time: 678 us -> 664 us (0.979)
  other arithmetic: 23.1 us -> 1.97 us
  Pallas kernels: 605 us -> 612 us
    pallas_call x0 -> x1, Pallas kernels: none -> 15.9 us  [last_sums(): pl.pallas_call(functools.partial(last_sums_kernel, packs), out_shape=tupl...]
    add x5 -> x1, other arithmetic: 12.9 us -> 0.35 us  [body(): sin_t = (sin_a * cos_b + cos_a * sin_b).reshape(HALF, -1)]
    pallas_call x1, Pallas kernels: 132 us -> 123 us  [normed_back(): pl.pallas_call(functools.partial(normed_back_kernel, packs), out_shape=(j...]
  transfers between devices with their start and end apart: 11 -> 11, of which waited for: 1 -> 1; matrix products, arithmetic and copies ran while one was open for 1% -> 0% of each run, Pallas kernels for 45% -> 45%
where the time goes in v7:
time: 664 us; the launch traced here: 663 us
  Pallas kernels  612 us (92%)
  waiting for transfers between devices  19 us (3%)
  between operations  14.3 us (2%)
  local copies, waits for them, and re-layouts  8.79 us (1%)
  starting transfers between devices  6.7 us (1%)
    pallas_call x1, Pallas kernels, dense(): pl.pallas_call(dense_kernel, out_shape=(jax.ShapeDtypeStruct((rows, featu...  184 us
    pallas_call x1, Pallas kernels, normed_back(): pl.pallas_call(functools.partial(normed_back_kernel, packs), out_shape=(j...  123 us
    pallas_call x1, Pallas kernels, gather_project(): pl.pallas_call(gather_project_kernel, out_shape=(jax.ShapeDtypeStruct((3,...  117 us
    pallas_call x1, Pallas kernels, mixed_back(): pl.pallas_call(functools.partial(mixed_back_kernel, packs), out_shape=(ja...  46.7 us
    pallas_call x1, Pallas kernels, attend_back(): pl.pallas_call(functools.partial(attend_back_kernel, lax.axis_size('dp')...  43.8 us
    pallas_call x1, Pallas kernels, mix(): pl.pallas_call(mixed_kernel, out_shape=(jax.ShapeDtypeStruct((rows, featu...  43.2 us
    pallas_call x1, Pallas kernels, attend(): pl.pallas_call(functools.partial(attend_kernel, lax.axis_size('dp') // 2)...  38.1 us
    all_gather x1, waiting for transfers between devices, body(): lax.all_gather(grad_late, 'dp', axis=0, axis_index_groups=lanes)  19 us
  transfers between devices with their start and end apart: 11, of which 1 were waited for; matrix products, arithmetic and copies ran while one was open for 0% of the time, Pallas kernels for 45%

profile of v7, /device:TPU:0, one launch (start us, length us, event | category | flops | bytes accessed | tf_op | source)
XLA Modules:
  0.0 663.0 jit_solution(4682267656073161571)
XLA Ops:
  7.2 0.9 convert_reduce_fusion.first_ref
  8.2 0.1 multiply_cosine_fusion
  8.3 0.1 multiply_cosine_fusion.1
  8.5 0.4 multiply_add_fusion
  8.8 1.6 copy_bitcast_fusion
  10.4 116.8 %gather_project.1 = (bf16[3,4096,128]{2,1,0:T(8,128)(2,1)}, bf16[8,256,2048]{2,1,0:T(8,128)(2,1)}, bf16[16,128,2048]{2,1,0:T(8,128)(2,1)}) custom-call(bf16[256,2048]{1,0:T(8,128)(2,1)} %bitcast.23, f32[1,2048]{1,0:T(1,128)} %bitcast.35, bf16[128,2048]{1,0:T(8,128)(2,1)} %query_w.3, bf16[128,2048]{1,0:T(8,128)(2,1)} %key_w.3, bf16[128,2048]{1,0:T(8,128)(2,1)} %value_w.3, ...), custom_call_target="tpu_custom_call" | custom-call | flops 6442450944 | bytes 335544320 | tf_op jit(solution)/shard_map/gather_project/pallas_call | solution.py:351
  127.2 0.0 reduce-scatter.2.cloned.1.call-start
  127.3 0.4 collective-permute-start
  127.7 0.2 collective-permute-start.1
  127.8 0.4 collective-permute-start.2
  128.2 0.1 select_reduce_fusion
  128.3 0.1 compare_bitcast_fusion
  128.4 0.1 add_select_fusion.tail_ref
  128.5 1.9 copy-done.5
  130.3 38.1 %attend.1 = (bf16[4096,128]{1,0:T(8,128)(2,1)S(1)}, f32[32,256]{1,0:T(8,128)S(1)}) custom-call(s32[32]{0:T(128)S(1)} %convert_reduce_fusion.first_ref, s32[32]{0:T(128)S(1)} %add_select_fusion.tail_ref, bf16[3,4096,128]{2,1,0:T(8,128)(2,1)S(1)} %copy-done.5), custom_call_target="tpu_custom_call" | custom-call | flops 17179869184 | bytes 125829120 | tf_op jit(solution)/shard_map/attend/pallas_call | solution.py:469
  168.5 1.0 copy-done
  169.5 43.2 %mix.1 = (f32[256,2048]{1,0:T(8,128)}, bf16[256,2048]{1,0:T(8,128)(2,1)}, bf16[16,256,128]{2,1,0:T(8,128)(2,1)}) custom-call(bf16[4096,128]{1,0:T(8,128)(2,1)} %copy-done, bf16[256,2048]{1,0:T(8,128)(2,1)} %bitcast.24, f32[1,2048]{1,0:T(1,128)} %bitcast.30, bf16[16,128,2048]{2,1,0:T(8,128)(2,1)} %get-tuple-element.65.output_all), custom_call_target="tpu_custom_call" | custom-call | flops 2147483648 | bytes 104857600 | tf_op jit(solution)/shard_map/mix/pallas_call | solution.py:690
  212.7 0.2 pad_maximum_fusion
  212.9 19.0 %all-gather.3.cloned.1.call-done = bf16[2048,2048]{1,0:T(8,128)(2,1)} async-done(((bf16[256,2048]{1,0:T(8,128)(2,1)}), bf16[2048,2048]{1,0:T(8,128)(2,1)}) %all-gather.3.cloned.1.call-update) | async-done | bytes 8388624 | tf_op jit(solution)/shard_map/all_gather | solution.py:1702
  231.9 184.3 %dense.1 = (f32[256,2048]{1,0:T(8,128)}, bf16[8,256,2048]{2,1,0:T(8,128)(2,1)}, bf16[8,256,2048]{2,1,0:T(8,128)(2,1)}, bf16[512,2048]{1,0:T(8,128)(2,1)}, bf16[1...) custom-call(bf16[256,2048]{1,0:T(8,128)(2,1)} %get-tuple-element.67.normed, ...), custom_call_target="tpu_custom_call" | custom-call | flops 77309411328 | bytes 524288000 | tf_op jit(solution)/shard_map/dense/pallas_call | solution.py:959
  416.2 1.5 collective-permute-start.3
  417.7 46.7 %mixed_back.1 = (f32[256,2048]{1,0:T(8,128)}, f32[1,2048]{1,0:T(1,128)}, bf16[4096,128]{1,0:T(8,128)(2,1)}, bf16[640,2048]{1,0:T(8,128)(2,1)}, bf16[384,2048]{1,0:T(8,128)(2,1)}) custom-call(f32[256,2048]{1,0:T(8,128)} %get-tuple-element.71.mixed_in.refs_9_, f32[256,2048]{1,0:T(8,128)} %get-tuple-element.72.grad_in, bf16[256,2048]{1,0:T(8,128)(2,1)} %bitcast.27, ...), custom_call_target="tpu_custom_call" | custom-call | flops 4294967296 | bytes 136314880 | tf_op jit(solution)/shard_map/mixed_back/pallas_call | solution.py:1147
  464.4 0.1 collective-permute-start.4
  464.5 2.0 collective-permute-start.5
  466.5 1.2 copy-done.4
  467.8 43.8 %attend_back.1.grads_in = bf16[3,4096,128]{2,1,0:T(8,128)(2,1)S(1)} custom-call(s32[32]{0:T(128)S(1)} %convert_reduce_fusion.first_ref, s32[32]{0:T(128)S(1)} %add_select_fusion.tail_ref, bf16[3,4096,128]{2,1,0:T(8,128)(2,1)S(1)} %copy-done.6, bf16[4096,128]{1,0:T(8,128)(2,1)S(1)} %copy-done.4, bf16[4096,128]{1,0:T(8,128)(2,1)S(1)} %copy-done.1, ...), custom_call_target="tpu_custom_call" | custom-call | flops 42949672960 | bytes 251658240 | tf_op jit(solution)/shard_map/attend_back/pallas_call | solution.py:571
  511.6 1.7 copy-done.7
  513.3 0.1 collective-permute-start.8
  513.4 2.0 collective-permute-start.7
  515.4 123.5 %normed_back.1 = (f32[256,2048]{1,0:T(8,128)}, f32[2,2048]{1,0:T(2,128)}, bf16[2,3,128,2048]{3,2,1,0:T(8,128)(2,1)}, bf16[2,80,2048]{2,1,0:T(8,128)(2,1)}) custom-call(bf16[3,4096,128]{2,1,0:T(8,128)(2,1)} %copy-done.7, bf16[128,2048]{1,0:T(8,128)(2,1)} %query_w.3, bf16[128,2048]{1,0:T(8,128)(2,1)} %key_w.3, bf16[128,2048]{1,0:T(8,128)(2,1)} %value_w.3, ...), custom_call_target="tpu_custom_call" | custom-call | flops 12884901888 | bytes 335544320 | tf_op jit(solution)/shard_map/normed_back/pallas_call | solution.py:1525
  638.9 1.4 fusion
  640.3 15.9 %last_sums.1 = (f32[512,2048]{1,0:T(8,128)}, f32[512,2048]{1,0:T(8,128)}, f32[512,2048]{1,0:T(8,128)}, f32[128,2048]{1,0:T(8,128)}, f32[128,2048]{1,0:T(8,128)},...) custom-call(bf16[512,2048]{1,0:T(8,128)(2,1)} %get-tuple-element.69.refs_0_, ...), custom_call_target="tpu_custom_call" | custom-call | flops 8388608 | bytes 41943040 | tf_op jit(solution)/shard_map/last_sums/pallas_call | solution.py:1621
  (43 shorter events, 0.2 us)
Async XLA Ops:
  7.2 224.7 %all-gather.3.cloned.1.call-start = ((), (), s32[]{:S(2)}) async-start(), calls=%async_computation.2 | async-start | bytes 9437184 | tf_op jit(solution)/shard_map/all_gather | solution.py:1702
  10.4 117.8 %copy-start.13 = (s32[1,8]{1,0:T(1,128)S(1)}, s32[1,8]{1,0:T(1,128)}, u32[]{:S(2)}) copy-start(s32[1,8]{1,0:T(1,128)} %param.24) | copy-start | bytes 100
  10.4 117.8 %copy-start.14 = (s32[1,32]{1,0:T(1,128)S(1)}, s32[1,32]{1,0:T(1,128)}, u32[]{:S(2)}) copy-start(s32[1,32]{1,0:T(1,128)} %param.23) | copy-start | bytes 388
  127.2 513.1 %reduce-scatter.2.cloned.1.call-start = ((), (), s32[]{:S(2)}) async-start(), calls=%async_computation.1 | async-start | bytes 9437184 | tf_op jit(solution)/shard_map/reduce_scatter | solution.py:1722
  127.3 85.6 %collective-permute-start = (bf16[512,2048]{1,0:T(8,128)(2,1)}, bf16[512,2048]{1,0:T(8,128)(2,1)}, u32[]{:S(2)}, u32[]{:S(2)}) collective-permute-start(bf16[512,2048]{1,0:T(8,128)(2,1)} %gate_w.1), channel_id=1, source_target_pairs={{0,2},{2,0},{4,6},{6,4},{8,10},{10,8},{12,14},{14,12},{16,18},{18,... | collective-permute-start | bytes 6291464 | tf_op jit(solution)/shard_map/ppermute | solution.py:1639
  127.7 85.2 %collective-permute-start.1 = (bf16[512,2048]{1,0:T(8,128)(2,1)}, bf16[512,2048]{1,0:T(8,128)(2,1)}, u32[]{:S(2)}, u32[]{:S(2)}) collective-permute-start(bf16[512,2048]{1,0:T(8,128)(2,1)} %up_w.1), channel_id=1, source_target_pairs={{0,2},{2,0},{4,6},{6,4},{8,10},{10,8},{12,14},{14,12},{16,18},{18,... | collective-permute-start | bytes 6291464 | tf_op jit(solution)/shard_map/ppermute | solution.py:1639
  127.8 85.0 %collective-permute-start.2 = (bf16[512,2048]{1,0:T(8,128)(2,1)}, bf16[512,2048]{1,0:T(8,128)(2,1)}, u32[]{:S(2)}, u32[]{:S(2)}) collective-permute-start(bf16[512,2048]{1,0:T(8,128)(2,1)} %down_w.1), channel_id=1, source_target_pairs={{0,2},{2,0},{4,6},{6,4},{8,10},{10,8},{12,14},{14,12},{16,18},{18,... | collective-permute-start | bytes 6291464 | tf_op jit(solution)/shard_map/ppermute | solution.py:1639
  128.5 1.9 copy-start.5
  168.5 1.0 copy-start
  169.5 43.2 %copy-start.8 = (bf16[128,2048]{1,0:T(8,128)(2,1)S(1)}, bf16[128,2048]{1,0:T(8,128)(2,1)}, u32[]{:S(2)}) copy-start(bf16[128,2048]{1,0:T(8,128)(2,1)} %query_w.3) | copy-start | bytes 1572868
  169.5 43.2 %copy-start.9 = (bf16[128,2048]{1,0:T(8,128)(2,1)S(1)}, bf16[128,2048]{1,0:T(8,128)(2,1)}, u32[]{:S(2)}) copy-start(bf16[128,2048]{1,0:T(8,128)(2,1)} %key_w.3) | copy-start | bytes 1572868
  169.5 43.2 %copy-start.10 = (bf16[128,2048]{1,0:T(8,128)(2,1)S(1)}, bf16[128,2048]{1,0:T(8,128)(2,1)}, u32[]{:S(2)}) copy-start(bf16[128,2048]{1,0:T(8,128)(2,1)} %value_w.3) | copy-start | bytes 1572868
  416.2 48.3 %collective-permute-start.3 = (bf16[512,2048]{1,0:T(8,128)(2,1)}, bf16[512,2048]{1,0:T(8,128)(2,1)}, u32[]{:S(2)}, u32[]{:S(2)}) collective-permute-start(bf16[512,2048]{1,0:T(8,128)(2,1)} %get-tuple-element.69.refs_0_), channel_id=1, source_target_pairs={{0,1},{1,0},{2,3},{3,2},{4,5},{5,4},{6,7},{7,6},{8,9},{9,8},{10,11... | collective-permute-start | bytes 6291464 | tf_op jit(solution)/shard_map/ppermute | solution.py:1644
  417.7 97.7 %collective-permute-start.6 = (bf16[384,2048]{1,0:T(8,128)(2,1)S(1)}, bf16[384,2048]{1,0:T(8,128)(2,1)}, u32[]{:S(2)}, u32[]{:S(2)}) collective-permute-start(bf16[384,2048]{1,0:T(8,128)(2,1)S(1)} %pad_maximum_fusion), channel_id=1, source_target_pairs={{0,2},{2,0},{4,6},{6,4},{8,10},{10,8},{12,14},{14,12},{16,18},{18,... | collective-permute-start | bytes 4718600 | tf_op jit(solution)/shard_map/ppermute | solution.py:1639
  417.7 48.8 %copy-start.1 = (bf16[4096,128]{1,0:T(8,128)(2,1)S(1)}, bf16[4096,128]{1,0:T(8,128)(2,1)}, u32[]{:S(2)}) copy-start(bf16[4096,128]{1,0:T(8,128)(2,1)} %copy-done) | copy-start | bytes 3145732
  417.7 48.8 %copy-start.2 = (f32[32,4096]{1,0:T(8,128)S(1)}, f32[32,4096]{1,0:T(8,128)}, u32[]{:S(2)}) copy-start(f32[32,4096]{1,0:T(8,128)} %get-tuple-element.121.sin_t) | copy-start | bytes 1572868
  417.7 48.8 %copy-start.3 = (f32[32,4096]{1,0:T(8,128)S(1)}, f32[32,4096]{1,0:T(8,128)}, u32[]{:S(2)}) copy-start(f32[32,4096]{1,0:T(8,128)} %get-tuple-element.122.cos_t) | copy-start | bytes 1572868
  417.7 48.8 %copy-start.6 = (bf16[3,4096,128]{2,1,0:T(8,128)(2,1)S(1)}, bf16[3,4096,128]{2,1,0:T(8,128)(2,1)}, u32[]{:S(2)}) copy-start(bf16[3,4096,128]{2,1,0:T(8,128)(2,1)} %get-tuple-element.63.qkv) | copy-start | bytes 9437188
  464.4 48.8 %collective-permute-start.4 = (bf16[384,2048]{1,0:T(8,128)(2,1)}, bf16[384,2048]{1,0:T(8,128)(2,1)S(1)}, u32[]{:S(2)}, u32[]{:S(2)}) collective-permute-start(bf16[384,2048]{1,0:T(8,128)(2,1)} %get-tuple-element.79), channel_id=1, source_target_pairs={{0,1},{1,0},{2,3},{3,2},{4,5},{5,4},{6,7},{7,6},{8,9},{9,8},{10,11... | collective-permute-start | bytes 4718600 | tf_op jit(solution)/shard_map/ppermute | solution.py:1735
  464.5 48.8 %collective-permute-start.5 = (bf16[128,2048]{1,0:T(8,128)(2,1)}, bf16[128,2048]{1,0:T(8,128)(2,1)S(1)}, u32[]{:S(2)}, u32[]{:S(2)}) collective-permute-start(bf16[128,2048]{1,0:T(8,128)(2,1)} %get-tuple-element.77.refs_1_), channel_id=1, source_target_pairs={{0,1},{1,0},{2,3},{3,2},{4,5},{5,4},{6,7},{7,6},{8,9},{9,8},{10,11... | collective-permute-start | bytes 1572872 | tf_op jit(solution)/shard_map/ppermute | solution.py:1644
  466.5 1.3 copy-start.4
  511.6 1.7 copy-start.7
  513.3 2.1 copy-start.12
  513.3 2.1 copy-start.11
  513.3 127.0 %collective-permute-start.8 = (bf16[512,2048]{1,0:T(8,128)(2,1)}, bf16[512,2048]{1,0:T(8,128)(2,1)}, u32[]{:S(2)}, u32[]{:S(2)}) collective-permute-start(bf16[512,2048]{1,0:T(8,128)(2,1)} %get-tuple-element.83.refs_3_), channel_id=1, source_target_pairs={{0,1},{1,0},{2,3},{3,2},{4,5},{5,4},{6,7},{7,6},{8,9},{9,8},{10,11... | collective-permute-start | bytes 6291464 | tf_op jit(solution)/shard_map/ppermute | solution.py:1644
  513.4 126.9 %collective-permute-start.7 = (bf16[384,2048]{1,0:T(8,128)(2,1)}, bf16[384,2048]{1,0:T(8,128)(2,1)}, u32[]{:S(2)}, u32[]{:S(2)}) collective-permute-start(bf16[384,2048]{1,0:T(8,128)(2,1)} %get-tuple-element.82.refs_2_), channel_id=1, source_target_pairs={{0,1},{1,0},{2,3},{3,2},{4,5},{5,4},{6,7},{7,6},{8,9},{9,8},{10,11... | collective-permute-start | bytes 4718600 | tf_op jit(solution)/shard_map/ppermute | solution.py:1644
Sparse Core Ops, SparseCore 0:
  127.3 104.4 all-gather.2
  416.3 103.9 reduce-scatter.1

commit v8 on v7

--- a/solution.py
+++ b/solution.py
@@ -13,7 +13,7 @@
 BLOCK = 128
 CHUNK = 512
 FF_TILE = 256
-STRIPE = 64
+STRIPE = 128
 EPSILON = 1e-05
 ROPE_BASE = 130000.0
 MASKED_SCORE = -1e30
@@ -1570,8 +1570,8 @@
 
 
 def last_sums_kernel(packs, *refs):
-    gate, up_a, up_b, down, gate_o, up_a_o, up_b_o, down_o, qkv, mixed, out_sum, grad_in, output = refs[:13]
-    gate_t, up_t, down_t, query_t, key_t, value_t, layer, grad, output_t = refs[13:]
+    gate, up_a, up_b, down, gate_o, up_a_o, up_b_o, down_o, qkv, mixed, out_sum, grad_in, output, gains = refs[:14]
+    gate_t, up_t, down_t, query_t, key_t, value_t, layer, grad, output_t, first_gain, second_gain = refs[14:]
 
     def add(low, other):
         if packs == 2:
@@ -1591,6 +1591,8 @@
 
     @pl.when(pl.program_id(0) == 0)
     def _():
+        first_gain[...] = gains[0, :]
+        second_gain[...] = gains[1, :]
         r = output_t.shape[0]
         share, plain = output_split(r, packs)
         for q, slot in enumerate(slots):
@@ -1605,7 +1607,7 @@
     grad[...] = grad_in[...]
 
 
-def last_sums(lows, others, qkv, mixed, out_sum, grad_in, output):
+def last_sums(lows, others, qkv, mixed, out_sum, grad_in, output, gains):
     own, features = lows[0].shape
     rows, r = mixed.shape[0], qkv.shape[2]
     packs = qkv.shape[0]
@@ -1617,7 +1619,8 @@
     wide = jax.ShapeDtypeStruct((own, features), F32)
     narrow = jax.ShapeDtypeStruct((r, features), F32)
     layer = jax.ShapeDtypeStruct((rows, features), LOW)
-    out_shape = (wide,) * 3 + (narrow,) * 3 + (layer, grad_in, narrow)
+    line = jax.ShapeDtypeStruct((features,), F32)
+    out_shape = (wide,) * 3 + (narrow,) * 3 + (layer, grad_in, narrow, line, line)
     return pl.pallas_call(
         functools.partial(last_sums_kernel, packs),
         out_shape=tuple(jax.ShapeDtypeStruct(a.shape, a.dtype) for a in out_shape),
@@ -1625,13 +1628,14 @@
         in_specs=[striped(a) for a in (*lows, *others)]
         + [pl.BlockSpec((packs, 3, r // steps, features), lambda i: (0, 0, i, 0))]
         + [striped(a) for a in (mixed, out_sum, grad_in)]
-        + [pl.BlockSpec(output.shape, lambda i: (0, 0, 0))],
-        out_specs=tuple(striped(a) for a in out_shape[:-1])
-        + (pl.BlockSpec((r, features), lambda i: (0, 0)),),
+        + [pl.BlockSpec(output.shape, lambda i: (0, 0, 0)), pl.BlockSpec(gains.shape, lambda i: (0, 0))],
+        out_specs=tuple(striped(a) for a in out_shape[:-3])
+        + (pl.BlockSpec((r, features), lambda i: (0, 0)),)
+        + (pl.BlockSpec((features,), lambda i: (0,)),) * 2,
         compiler_params=pltpu.CompilerParams(vmem_limit_bytes=62 * MIB),
         cost_estimate=pl.CostEstimate(flops=8 * own * features, bytes_accessed=40 * MIB, transcendentals=0),
         name="last_sums",
-    )(*lows, *others, qkv, mixed, out_sum, grad_in, output)
+    )(*lows, *others, qkv, mixed, out_sum, grad_in, output, gains)
 
 
 def from_partner(value):
@@ -1760,7 +1764,8 @@
         input_grad, out_sum, gate_there, up_a_there, up_b_there, down_there
     )
     (
-        gate_total, up_total, down_total, query_total, key_total, value_total, layer_out, input_grad, output_total
+        gate_total, up_total, down_total, query_total, key_total, value_total,
+        layer_out, input_grad, output_total, first_gain, second_gain,
     ) = last_sums(
         (gate_low, up_a, up_b, down_low),
         (gate_there, up_a_there, up_b_there, down_there),
@@ -1769,16 +1774,17 @@
         out_sum,
         input_grad,
         output_packs,
+        gain_totals,
     )
     return (
         layer_out[None],
         input_grad[None],
-        gain_totals[0],
+        first_gain,
         query_total,
         key_total,
         value_total,
         output_total,
-        gain_totals[1],
+        second_gain,
         gate_total,
         up_total,
         down_total,

time: 664 us -> 662 us (level)
  no operation moved by 1% of the time
where the time goes in v8:
time: 662 us; the launch traced here: 661 us
  Pallas kernels  610 us (92%)
  waiting for transfers between devices  17.9 us (3%)
  between operations  14.3 us (2%)
  local copies, waits for them, and re-layouts  8.61 us (1%)
  starting transfers between devices  6.68 us (1%)
    pallas_call x1, Pallas kernels, dense(): pl.pallas_call(dense_kernel, out_shape=(jax.ShapeDtypeStruct((rows, featu...  184 us
    pallas_call x1, Pallas kernels, normed_back(): pl.pallas_call(functools.partial(normed_back_kernel, packs), out_shape=(j...  123 us
    pallas_call x1, Pallas kernels, gather_project(): pl.pallas_call(gather_project_kernel, out_shape=(jax.ShapeDtypeStruct((3,...  117 us
    pallas_call x1, Pallas kernels, mixed_back(): pl.pallas_call(functools.partial(mixed_back_kernel, packs), out_shape=(ja...  46.7 us
    pallas_call x1, Pallas kernels, attend_back(): pl.pallas_call(functools.partial(attend_back_kernel, lax.axis_size('dp')...  43.8 us
    pallas_call x1, Pallas kernels, mix(): pl.pallas_call(mixed_kernel, out_shape=(jax.ShapeDtypeStruct((rows, featu...  43.2 us
    pallas_call x1, Pallas kernels, attend(): pl.pallas_call(functools.partial(attend_kernel, lax.axis_size('dp') // 2)...  38.1 us
    all_gather x1, waiting for transfers between devices, body(): lax.all_gather(grad_late, 'dp', axis=0, axis_index_groups=lanes)  17.8 us
  transfers between devices with their start and end apart: 11, of which 1 were waited for; matrix products, arithmetic and copies ran while one was open for 0% of the time, Pallas kernels for 45%

profile of v8, /device:TPU:0, one launch (start us, length us, event | category | flops | bytes accessed | tf_op | source)
XLA Modules:
  0.0 660.5 jit_solution(8221233552741592130)
XLA Ops:
  7.2 0.9 convert_reduce_fusion.first_ref
  8.2 0.1 multiply_cosine_fusion
  8.3 0.1 multiply_cosine_fusion.1
  8.5 0.4 multiply_add_fusion
  8.8 1.6 copy_bitcast_fusion
  10.4 116.8 %gather_project.1 = (bf16[3,4096,128]{2,1,0:T(8,128)(2,1)}, bf16[8,256,2048]{2,1,0:T(8,128)(2,1)}, bf16[16,128,2048]{2,1,0:T(8,128)(2,1)}) custom-call(bf16[256,2048]{1,0:T(8,128)(2,1)} %bitcast.21, f32[1,2048]{1,0:T(1,128)} %bitcast.31, bf16[128,2048]{1,0:T(8,128)(2,1)} %query_w.3, bf16[128,2048]{1,0:T(8,128)(2,1)} %key_w.3, bf16[128,2048]{1,0:T(8,128)(2,1)} %value_w.3, ...), custom_call_target="tpu_custom_call" | custom-call | flops 6442450944 | bytes 335544320 | tf_op jit(solution)/shard_map/gather_project/pallas_call | solution.py:351
  127.2 0.0 reduce-scatter.2.cloned.1.call-start
  127.3 0.4 collective-permute-start
  127.7 0.2 collective-permute-start.1
  127.8 0.4 collective-permute-start.2
  128.2 0.1 select_reduce_fusion
  128.3 0.1 compare_bitcast_fusion
  128.4 0.1 add_select_fusion.tail_ref
  128.4 1.9 copy-done.5
  130.3 38.1 %attend.1 = (bf16[4096,128]{1,0:T(8,128)(2,1)S(1)}, f32[32,256]{1,0:T(8,128)S(1)}) custom-call(s32[32]{0:T(128)S(1)} %convert_reduce_fusion.first_ref, s32[32]{0:T(128)S(1)} %add_select_fusion.tail_ref, bf16[3,4096,128]{2,1,0:T(8,128)(2,1)S(1)} %copy-done.5), custom_call_target="tpu_custom_call" | custom-call | flops 17179869184 | bytes 125829120 | tf_op jit(solution)/shard_map/attend/pallas_call | solution.py:469
  168.5 1.0 copy-done
  169.5 43.2 %mix.1 = (f32[256,2048]{1,0:T(8,128)}, bf16[256,2048]{1,0:T(8,128)(2,1)}, bf16[16,256,128]{2,1,0:T(8,128)(2,1)}) custom-call(bf16[4096,128]{1,0:T(8,128)(2,1)} %copy-done, bf16[256,2048]{1,0:T(8,128)(2,1)} %bitcast.22, f32[1,2048]{1,0:T(1,128)} %bitcast.26, bf16[16,128,2048]{2,1,0:T(8,128)(2,1)} %get-tuple-element.67.output_all), custom_call_target="tpu_custom_call" | custom-call | flops 2147483648 | bytes 104857600 | tf_op jit(solution)/shard_map/mix/pallas_call | solution.py:690
  212.7 1.3 pad_maximum_fusion
  214.0 17.8 %all-gather.3.cloned.1.call-done = bf16[2048,2048]{1,0:T(8,128)(2,1)} async-done(((bf16[256,2048]{1,0:T(8,128)(2,1)}), bf16[2048,2048]{1,0:T(8,128)(2,1)}) %all-gather.3.cloned.1.call-update) | async-done | bytes 8388624 | tf_op jit(solution)/shard_map/all_gather | solution.py:1706
  231.9 184.2 %dense.1 = (f32[256,2048]{1,0:T(8,128)}, bf16[8,256,2048]{2,1,0:T(8,128)(2,1)}, bf16[8,256,2048]{2,1,0:T(8,128)(2,1)}, bf16[512,2048]{1,0:T(8,128)(2,1)}, bf16[1...) custom-call(bf16[256,2048]{1,0:T(8,128)(2,1)} %get-tuple-element.69.normed, ...), custom_call_target="tpu_custom_call" | custom-call | flops 77309411328 | bytes 524288000 | tf_op jit(solution)/shard_map/dense/pallas_call | solution.py:959
  416.1 1.5 collective-permute-start.3
  417.7 46.7 %mixed_back.1 = (f32[256,2048]{1,0:T(8,128)}, f32[1,2048]{1,0:T(1,128)}, bf16[4096,128]{1,0:T(8,128)(2,1)}, bf16[640,2048]{1,0:T(8,128)(2,1)}, bf16[384,2048]{1,0:T(8,128)(2,1)}) custom-call(f32[256,2048]{1,0:T(8,128)} %get-tuple-element.73.mixed_in.refs_9_, f32[256,2048]{1,0:T(8,128)} %get-tuple-element.74.grad_in, bf16[256,2048]{1,0:T(8,128)(2,1)} %bitcast.25, ...), custom_call_target="tpu_custom_call" | custom-call | flops 4294967296 | bytes 136314880 | tf_op jit(solution)/shard_map/mixed_back/pallas_call | solution.py:1147
  464.4 0.1 collective-permute-start.4
  464.5 2.0 collective-permute-start.5
  466.5 1.2 copy-done.4
  467.8 43.8 %attend_back.1.grads_in = bf16[3,4096,128]{2,1,0:T(8,128)(2,1)S(1)} custom-call(s32[32]{0:T(128)S(1)} %convert_reduce_fusion.first_ref, s32[32]{0:T(128)S(1)} %add_select_fusion.tail_ref, bf16[3,4096,128]{2,1,0:T(8,128)(2,1)S(1)} %copy-done.6, bf16[4096,128]{1,0:T(8,128)(2,1)S(1)} %copy-done.4, bf16[4096,128]{1,0:T(8,128)(2,1)S(1)} %copy-done.1, ...), custom_call_target="tpu_custom_call" | custom-call | flops 42949672960 | bytes 251658240 | tf_op jit(solution)/shard_map/attend_back/pallas_call | solution.py:571
  511.5 1.7 copy-done.7
  513.2 0.1 collective-permute-start.8
  513.4 1.9 collective-permute-start.7
  515.3 123.5 %normed_back.1 = (f32[256,2048]{1,0:T(8,128)}, f32[2,2048]{1,0:T(2,128)}, bf16[2,3,128,2048]{3,2,1,0:T(8,128)(2,1)}, bf16[2,80,2048]{2,1,0:T(8,128)(2,1)}) custom-call(bf16[3,4096,128]{2,1,0:T(8,128)(2,1)} %copy-done.7, bf16[128,2048]{1,0:T(8,128)(2,1)} %query_w.3, bf16[128,2048]{1,0:T(8,128)(2,1)} %key_w.3, bf16[128,2048]{1,0:T(8,128)(2,1)} %value_w.3, ...), custom_call_target="tpu_custom_call" | custom-call | flops 12884901888 | bytes 335544320 | tf_op jit(solution)/shard_map/normed_back/pallas_call | solution.py:1525
  638.8 1.2 copy-done.9
  640.0 13.6 %last_sums.1 = (f32[512,2048]{1,0:T(8,128)}, f32[512,2048]{1,0:T(8,128)}, f32[512,2048]{1,0:T(8,128)}, f32[128,2048]{1,0:T(8,128)}, f32[128,2048]{1,0:T(8,128)},...) custom-call(bf16[512,2048]{1,0:T(8,128)(2,1)} %get-tuple-element.71., ...), custom_call_target="tpu_custom_call" | custom-call | flops 8388608 | bytes 41943040 | tf_op jit(solution)/shard_map/last_sums/pallas_call | solution.py:1624
  (46 shorter events, 0.2 us)
Async XLA Ops:
  7.2 224.7 %all-gather.3.cloned.1.call-start = ((), (), s32[]{:S(2)}) async-start(), calls=%async_computation.2 | async-start | bytes 9437184 | tf_op jit(solution)/shard_map/all_gather | solution.py:1706
  10.4 117.8 %copy-start.15 = (s32[1,8]{1,0:T(1,128)S(1)}, s32[1,8]{1,0:T(1,128)}, u32[]{:S(2)}) copy-start(s32[1,8]{1,0:T(1,128)} %param.24) | copy-start | bytes 100
  10.4 117.8 %copy-start.16 = (s32[1,32]{1,0:T(1,128)S(1)}, s32[1,32]{1,0:T(1,128)}, u32[]{:S(2)}) copy-start(s32[1,32]{1,0:T(1,128)} %param.23) | copy-start | bytes 388
  127.2 512.8 %reduce-scatter.2.cloned.1.call-start = ((), (), s32[]{:S(2)}) async-start(), calls=%async_computation.1 | async-start | bytes 9437184 | tf_op jit(solution)/shard_map/reduce_scatter | solution.py:1726
  127.3 86.7 %collective-permute-start = (bf16[512,2048]{1,0:T(8,128)(2,1)}, bf16[512,2048]{1,0:T(8,128)(2,1)}, u32[]{:S(2)}, u32[]{:S(2)}) collective-permute-start(bf16[512,2048]{1,0:T(8,128)(2,1)} %gate_w.1), channel_id=1, source_target_pairs={{0,2},{2,0},{4,6},{6,4},{8,10},{10,8},{12,14},{14,12},{16,18},{18,... | collective-permute-start | bytes 6291464 | tf_op jit(solution)/shard_map/ppermute | solution.py:1643
  127.7 86.3 %collective-permute-start.1 = (bf16[512,2048]{1,0:T(8,128)(2,1)}, bf16[512,2048]{1,0:T(8,128)(2,1)}, u32[]{:S(2)}, u32[]{:S(2)}) collective-permute-start(bf16[512,2048]{1,0:T(8,128)(2,1)} %up_w.1), channel_id=1, source_target_pairs={{0,2},{2,0},{4,6},{6,4},{8,10},{10,8},{12,14},{14,12},{16,18},{18,... | collective-permute-start | bytes 6291464 | tf_op jit(solution)/shard_map/ppermute | solution.py:1643
  127.8 86.2 %collective-permute-start.2 = (bf16[512,2048]{1,0:T(8,128)(2,1)}, bf16[512,2048]{1,0:T(8,128)(2,1)}, u32[]{:S(2)}, u32[]{:S(2)}) collective-permute-start(bf16[512,2048]{1,0:T(8,128)(2,1)} %down_w.1), channel_id=1, source_target_pairs={{0,2},{2,0},{4,6},{6,4},{8,10},{10,8},{12,14},{14,12},{16,18},{18,... | collective-permute-start | bytes 6291464 | tf_op jit(solution)/shard_map/ppermute | solution.py:1643
  128.4 1.9 copy-start.5
  168.5 1.0 copy-start
  169.5 43.2 %copy-start.11 = (bf16[128,2048]{1,0:T(8,128)(2,1)S(1)}, bf16[128,2048]{1,0:T(8,128)(2,1)}, u32[]{:S(2)}) copy-start(bf16[128,2048]{1,0:T(8,128)(2,1)} %query_w.3) | copy-start | bytes 1572868
  169.5 43.2 %copy-start.12 = (bf16[128,2048]{1,0:T(8,128)(2,1)S(1)}, bf16[128,2048]{1,0:T(8,128)(2,1)}, u32[]{:S(2)}) copy-start(bf16[128,2048]{1,0:T(8,128)(2,1)} %key_w.3) | copy-start | bytes 1572868
  169.5 43.2 %copy-start.13 = (bf16[128,2048]{1,0:T(8,128)(2,1)S(1)}, bf16[128,2048]{1,0:T(8,128)(2,1)}, u32[]{:S(2)}) copy-start(bf16[128,2048]{1,0:T(8,128)(2,1)} %value_w.3) | copy-start | bytes 1572868
  416.1 48.3 %collective-permute-start.3 = (bf16[512,2048]{1,0:T(8,128)(2,1)}, bf16[512,2048]{1,0:T(8,128)(2,1)}, u32[]{:S(2)}, u32[]{:S(2)}) collective-permute-start(bf16[512,2048]{1,0:T(8,128)(2,1)} %get-tuple-element.71.refs_0_), channel_id=1, source_target_pairs={{0,1},{1,0},{2,3},{3,2},{4,5},{5,4},{6,7},{7,6},{8,9},{9,8},{10,11... | collective-permute-start | bytes 6291464 | tf_op jit(solution)/shard_map/ppermute | solution.py:1648
  417.6 97.7 %collective-permute-start.6 = (bf16[384,2048]{1,0:T(8,128)(2,1)}, bf16[384,2048]{1,0:T(8,128)(2,1)}, u32[]{:S(2)}, u32[]{:S(2)}) collective-permute-start(bf16[384,2048]{1,0:T(8,128)(2,1)} %pad_maximum_fusion), channel_id=1, source_target_pairs={{0,2},{2,0},{4,6},{6,4},{8,10},{10,8},{12,14},{14,12},{16,18},{18,... | collective-permute-start | bytes 4718600 | tf_op jit(solution)/shard_map/ppermute | solution.py:1643
  417.6 48.8 %copy-start.1 = (bf16[4096,128]{1,0:T(8,128)(2,1)S(1)}, bf16[4096,128]{1,0:T(8,128)(2,1)}, u32[]{:S(2)}) copy-start(bf16[4096,128]{1,0:T(8,128)(2,1)} %copy-done) | copy-start | bytes 3145732
  417.7 48.8 %copy-start.2 = (f32[32,4096]{1,0:T(8,128)S(1)}, f32[32,4096]{1,0:T(8,128)}, u32[]{:S(2)}) copy-start(f32[32,4096]{1,0:T(8,128)} %get-tuple-element.123.sin_t) | copy-start | bytes 1572868
  417.7 48.8 %copy-start.3 = (f32[32,4096]{1,0:T(8,128)S(1)}, f32[32,4096]{1,0:T(8,128)}, u32[]{:S(2)}) copy-start(f32[32,4096]{1,0:T(8,128)} %get-tuple-element.124.cos_t) | copy-start | bytes 1572868
  417.7 48.8 %copy-start.6 = (bf16[3,4096,128]{2,1,0:T(8,128)(2,1)S(1)}, bf16[3,4096,128]{2,1,0:T(8,128)(2,1)}, u32[]{:S(2)}) copy-start(bf16[3,4096,128]{2,1,0:T(8,128)(2,1)} %get-tuple-element.65.qkv) | copy-start | bytes 9437188
  464.4 48.8 %collective-permute-start.4 = (bf16[384,2048]{1,0:T(8,128)(2,1)}, bf16[384,2048]{1,0:T(8,128)(2,1)S(1)}, u32[]{:S(2)}, u32[]{:S(2)}) collective-permute-start(bf16[384,2048]{1,0:T(8,128)(2,1)} %get-tuple-element.81), channel_id=1, source_target_pairs={{0,1},{1,0},{2,3},{3,2},{4,5},{5,4},{6,7},{7,6},{8,9},{9,8},{10,11... | collective-permute-start | bytes 4718600 | tf_op jit(solution)/shard_map/ppermute | solution.py:1739
  464.5 48.7 %collective-permute-start.5 = (bf16[128,2048]{1,0:T(8,128)(2,1)}, bf16[128,2048]{1,0:T(8,128)(2,1)S(1)}, u32[]{:S(2)}, u32[]{:S(2)}) collective-permute-start(bf16[128,2048]{1,0:T(8,128)(2,1)} %get-tuple-element.79.refs_1_), channel_id=1, source_target_pairs={{0,1},{1,0},{2,3},{3,2},{4,5},{5,4},{6,7},{7,6},{8,9},{9,8},{10,11... | collective-permute-start | bytes 1572872 | tf_op jit(solution)/shard_map/ppermute | solution.py:1648
  466.5 1.3 copy-start.4
  467.8 45.6 %copy-start.8 = (bf16[384,2048]{1,0:T(8,128)(2,1)S(1)}, bf16[384,2048]{1,0:T(8,128)(2,1)}, u32[]{:S(2)}) copy-start(bf16[384,2048]{1,0:T(8,128)(2,1)} %get-tuple-element.84.refs_2_) | copy-start | bytes 4718596
  511.5 1.7 copy-start.7
  513.2 2.1 copy-start.14
  513.2 2.1 copy-start.10
  513.2 126.8 %collective-permute-start.8 = (bf16[512,2048]{1,0:T(8,128)(2,1)}, bf16[512,2048]{1,0:T(8,128)(2,1)}, u32[]{:S(2)}, u32[]{:S(2)}) collective-permute-start(bf16[512,2048]{1,0:T(8,128)(2,1)} %get-tuple-element.85.refs_3_), channel_id=1, source_target_pairs={{0,1},{1,0},{2,3},{3,2},{4,5},{5,4},{6,7},{7,6},{8,9},{9,8},{10,11... | collective-permute-start | bytes 6291464 | tf_op jit(solution)/shard_map/ppermute | solution.py:1648
  513.4 125.4 %collective-permute-start.7 = (bf16[384,2048]{1,0:T(8,128)(2,1)S(1)}, bf16[384,2048]{1,0:T(8,128)(2,1)S(1)}, u32[]{:S(2)}, u32[]{:S(2)}) collective-permute-start(bf16[384,2048]{1,0:T(8,128)(2,1)S(1)} %copy-done.8), channel_id=1, source_target_pairs={{0,1},{1,0},{2,3},{3,2},{4,5},{5,4},{6,7},{7,6},{8,9},{9,8},{10,11... | collective-permute-start | bytes 4718600 | tf_op jit(solution)/shard_map/ppermute | solution.py:1648
  638.8 1.2 copy-start.9
Sparse Core Ops, SparseCore 0:
  127.3 104.4 all-gather.2
  416.3 103.9 reduce-scatter.1

commit v9 on v8

--- a/solution.py
+++ b/solution.py
@@ -740,7 +740,30 @@
         return remote(src, gathered.at[place, part], ag_send.at[d, t - 1], ag_recv.at[d, t - 1], ring.next[d])
 
     def reduce_copy(t, d):
-        return remote(sent.at[d], landed.at[d, t % 2], rs_send.at[d], rs_recv.at[d, t % 2], ring.next[d])
+        return remote(
+            sent.at[d, t % 2], landed.at[d, t % 2], rs_send.at[d, t % 2], rs_recv.at[d, t % 2], ring.next[d]
+        )
+
+    def reduce_on(t):
+        for d in (0, 1):
+            @pl.when(t >= 2)
+            def _():
+                reduce_copy(t - 1, d).wait_recv()
+                sent[d, t % 2] = (
+                    sent[d, t % 2].astype(F32) + landed[d, (t - 1) % 2].astype(F32)
+                ).astype(LOW)
+
+                @pl.when(t <= n - 2)
+                def _():
+                    pl.semaphore_signal(
+                        credit.at[d], inc=1, device_id={"dp": ring.back[d]}, device_id_type=MESH
+                    )
+
+            @pl.when(t >= 3)
+            def _():
+                pl.semaphore_wait(credit.at[d], 1)
+
+            reduce_copy(t, d).start()
 
     for d in (0, 1):
         send(1, d, True).start()
@@ -810,6 +833,10 @@
             @pl.when((t == 0) & (i == tiles - 1))
             def _():
                 pass_on(1)
+
+            @pl.when((t >= 2) & (i == tiles // 2))
+            def _():
+                reduce_on(t - 1)
 
             span = pl.ds(pl.multiple_of(i * FF_TILE, FF_TILE), FF_TILE)
             x = x_buf[...]
@@ -848,32 +875,16 @@
         @pl.when(t > 0)
         def _():
             for d in (0, 1):
-                part = pl.ds(d * half, half)
-
-                @pl.when(t >= 2)
-                def _():
-                    reduce_copy(t - 1, d).wait_recv()
-                    grad_acc[part, :] += landed[d, (t - 1) % 2].astype(F32)
-
-                    @pl.when(t <= n - 2)
-                    def _():
-                        pl.semaphore_signal(
-                            credit.at[d], inc=1, device_id={"dp": ring.back[d]}, device_id_type=MESH
-                        )
-
-                    reduce_copy(t - 1, d).wait_send()
-
-                sent[d] = grad_acc[part, :].astype(LOW)
-
                 @pl.when(t >= 3)
                 def _():
-                    pl.semaphore_wait(credit.at[d], 1)
-
-                reduce_copy(t, d).start()
+                    reduce_copy(t - 2, d).wait_send()
+
+                sent[d, t % 2] = grad_acc[pl.ds(d * half, half), :].astype(LOW)
 
         return carry
 
     lax.fori_loop(0, n, step, 0)
+    reduce_on(n - 1)
     for t in (n - 2, n - 1):
         for d in (0, 1):
             out_copy(t, d).wait()
@@ -933,6 +944,7 @@
         part = pl.ds(d * half, half)
         reduce_copy(n - 1, d).wait_recv()
         grad_sum[part, :] += landed[d, (n - 1) % 2].astype(F32)
+        reduce_copy(n - 2, d).wait_send()
         reduce_copy(n - 1, d).wait_send()
 
     for i in (own_tiles - 2, own_tiles - 1):
@@ -976,11 +988,11 @@
             pltpu.VMEM((rows, features), LOW),
             pltpu.VMEM((rows, features), F32),
             pltpu.VMEM((rows, features), F32),
-            pltpu.VMEM((2, half, features), LOW),
+            pltpu.VMEM((2, 2, half, features), LOW),
             pltpu.VMEM((2, 2, half, features), LOW),
             pltpu.VMEM((2, FF_TILE, features), LOW),
             pltpu.VMEM((own_tiles, FF_TILE, features), LOW),
-            dma((2, n)), dma((2, n)), dma((2,)), dma((2, 2)),
+            dma((2, n)), dma((2, n)), dma((2, 2)), dma((2, 2)),
             pltpu.SemaphoreType.REGULAR((2,)),
             dma((4,)), dma((6,)), dma((2, 2 * FF_TILE // STRIPE)), dma((2,)), dma((own_tiles,)),
         ],
@@ -1176,16 +1188,19 @@
 
 
 def normed_back_kernel(
-    packs, grads_in, query_w, key_w, value_w, partner_w, hidden_in, gain, grad_mixed, dense_gain_part, normed_all, output_mine, *rest
+    packs, grads_in, query_w, key_w, value_w, partner_w, tokens_in, gain, mixed_in, dense_gain_part, normed_all, output_mine, *rest
 ):
-    output_there = rest[: packs - 1]
+    outputs_in = (output_mine, *rest[: packs - 1])
     (
         out, gains, rep_land, o_packs,
+        hidden_in, grad_mixed, output_mine, *output_there
+    ) = rest[packs - 1 : 2 * packs + 5]
+    (
         grads, joined, partner_grads, sent, landed, x_buf, parts, pair_out, pair_land,
         o_sent, o_landed, far_part, far_land, near_part, near_land,
         in_sem, w_sem, p_send, p_recv, rs_send, rs_recv, credit, x_sem, pair_sem, rep_send, rep_recv,
         o_send, o_recv, o_credit, swap_send, swap_recv, near_send, near_recv, far_send, far_recv,
-    ) = rest[packs - 1 :]
+    ) = rest[2 * packs + 5 :]
     ring = Ring()
     n = ring.chips
     rows, features = out.shape
@@ -1202,7 +1217,15 @@
         pltpu.make_async_copy(src, joined.at[pl.ds(i * r, src.shape[0])], w_sem.at[i])
         for i, src in enumerate((query_w, key_w, value_w, partner_w))
     ]
-    for load in load_weights:
+    load_outputs = [
+        pltpu.make_async_copy(src, dst, w_sem.at[4 + i])
+        for i, (src, dst) in enumerate(zip(outputs_in, (output_mine, *output_there)))
+    ]
+    load_late = [
+        pltpu.make_async_copy(tokens_in, hidden_in, w_sem.at[4 + packs]),
+        pltpu.make_async_copy(mixed_in, grad_mixed, w_sem.at[5 + packs]),
+    ]
+    for load in load_weights + load_outputs + load_late:
         load.start()
 
     def near(k):
@@ -1472,7 +1495,7 @@
 
     for d in (0, 1):
         swap(1, d).wait_recv()
-    for load in load_weights:
+    for load in load_weights + load_outputs:
         load.wait()
     out[...] = dot_nn(block_grads(1), joined[...])
     lax.fori_loop(1, n + 1, step, 0)
@@ -1481,6 +1504,9 @@
             output_copy(t, d).wait_send()
             for u in (0, 1):
                 reduce_copy(t, d, u).wait_send()
+
+    for load in load_late:
+        load.wait()
 
     def close(i, carry):
         span = pl.ds(pl.multiple_of(i * 16, 16), 16)
@@ -1532,9 +1558,10 @@
             jax.ShapeDtypeStruct((packs, 3, r, features), LOW),
             jax.ShapeDtypeStruct((packs, carried, features), LOW),
         ),
-        in_specs=[hbm] * 5 + [vmem] * 4 + [hbm] + [vmem] * packs,
+        in_specs=[hbm] * 6 + [vmem, hbm, vmem] + [hbm] * (1 + packs),
         out_specs=(vmem,) * 4,
-        scratch_shapes=[
+        scratch_shapes=[pltpu.VMEM(a.shape, a.dtype) for a in (hidden_in, grad_mixed, output_mine, *output_there)]
+        + [
             pltpu.VMEM(grads.shape, LOW),
             pltpu.VMEM((6 * r, features), LOW),
             pltpu.VMEM((3, n, rows, r), LOW),
@@ -1550,7 +1577,7 @@
             pltpu.VMEM((n, 2, features), F32),
             pltpu.VMEM((2, features), F32),
             pltpu.VMEM((mates, 2, features), F32),
-            dma, dma((4,)), dma((2, n)), dma((2, n)), dma((2, 2, 2)), dma((2, 2, 2)),
+            dma, dma((6 + packs,)), dma((2, n)), dma((2, n)), dma((2, 2, 2)), dma((2, 2, 2)),
             pltpu.SemaphoreType.REGULAR((2, 2)),
             dma((2, 2)), dma((2,)), dma((packs - 1,)), dma((packs - 1,)),
             dma((2, 2)), dma((2, 2)), pltpu.SemaphoreType.REGULAR((2,)),

time: 662 us -> 660 us (level)
  no operation moved by 1% of the time
where the time goes in v9:
time: 660 us; the launch traced here: 659 us
  Pallas kernels  609 us (92%)
  waiting for transfers between devices  17.9 us (3%)
  between operations  14.3 us (2%)
  local copies, waits for them, and re-layouts  8.61 us (1%)
  starting transfers between devices  6.69 us (1%)
    pallas_call x1, Pallas kernels, dense(): pl.pallas_call(dense_kernel, out_shape=(jax.ShapeDtypeStruct((rows, featu...  183 us
    pallas_call x1, Pallas kernels, normed_back(): pl.pallas_call(functools.partial(normed_back_kernel, packs), out_shape=(j...  123 us
    pallas_call x1, Pallas kernels, gather_project(): pl.pallas_call(gather_project_kernel, out_shape=(jax.ShapeDtypeStruct((3,...  117 us
    pallas_call x1, Pallas kernels, mixed_back(): pl.pallas_call(functools.partial(mixed_back_kernel, packs), out_shape=(ja...  46.7 us
    pallas_call x1, Pallas kernels, attend_back(): pl.pallas_call(functools.partial(attend_back_kernel, lax.axis_size('dp')...  43.8 us
    pallas_call x1, Pallas kernels, mix(): pl.pallas_call(mixed_kernel, out_shape=(jax.ShapeDtypeStruct((rows, featu...  43.2 us
    pallas_call x1, Pallas kernels, attend(): pl.pallas_call(functools.partial(attend_kernel, lax.axis_size('dp') // 2)...  37.9 us
    all_gather x1, waiting for transfers between devices, body(): lax.all_gather(grad_late, 'dp', axis=0, axis_index_groups=lanes)  17.9 us
  transfers between devices with their start and end apart: 11, of which 1 were waited for; matrix products, arithmetic and copies ran while one was open for 0% of the time, Pallas kernels for 45%

profile of v9, /device:TPU:0, one launch (start us, length us, event | category | flops | bytes accessed | tf_op | source)
XLA Modules:
  0.0 659.4 jit_solution(11969727901475561275)
XLA Ops:
  7.2 0.9 convert_reduce_fusion.first_ref
  8.2 0.1 multiply_cosine_fusion
  8.3 0.1 multiply_cosine_fusion.1
  8.5 0.4 multiply_add_fusion
  8.8 1.6 copy_bitcast_fusion
  10.4 116.8 %gather_project.1 = (bf16[3,4096,128]{2,1,0:T(8,128)(2,1)}, bf16[8,256,2048]{2,1,0:T(8,128)(2,1)}, bf16[16,128,2048]{2,1,0:T(8,128)(2,1)}) custom-call(bf16[256,2048]{1,0:T(8,128)(2,1)} %bitcast.21, f32[1,2048]{1,0:T(1,128)} %bitcast.31, bf16[128,2048]{1,0:T(8,128)(2,1)} %query_w.3, bf16[128,2048]{1,0:T(8,128)(2,1)} %key_w.3, bf16[128,2048]{1,0:T(8,128)(2,1)} %value_w.3, ...), custom_call_target="tpu_custom_call" | custom-call | flops 6442450944 | bytes 335544320 | tf_op jit(solution)/shard_map/gather_project/pallas_call | solution.py:351
  127.2 0.2 reduce-scatter.2.cloned.1.call-start
  127.4 0.4 collective-permute-start
  127.9 0.2 collective-permute-start.1
  128.0 0.4 collective-permute-start.2
  128.4 0.1 select_reduce_fusion
  128.5 0.1 compare_bitcast_fusion
  128.5 0.1 add_select_fusion.tail_ref
  128.6 1.9 copy-done.5
  130.5 37.9 %attend.1 = (bf16[4096,128]{1,0:T(8,128)(2,1)S(1)}, f32[32,256]{1,0:T(8,128)S(1)}) custom-call(s32[32]{0:T(128)S(1)} %convert_reduce_fusion.first_ref, s32[32]{0:T(128)S(1)} %add_select_fusion.tail_ref, bf16[3,4096,128]{2,1,0:T(8,128)(2,1)S(1)} %copy-done.5), custom_call_target="tpu_custom_call" | custom-call | flops 17179869184 | bytes 125829120 | tf_op jit(solution)/shard_map/attend/pallas_call | solution.py:469
  168.5 1.0 copy-done
  169.4 43.2 %mix.1 = (f32[256,2048]{1,0:T(8,128)}, bf16[256,2048]{1,0:T(8,128)(2,1)}, bf16[16,256,128]{2,1,0:T(8,128)(2,1)}) custom-call(bf16[4096,128]{1,0:T(8,128)(2,1)} %copy-done, bf16[256,2048]{1,0:T(8,128)(2,1)} %bitcast.22, f32[1,2048]{1,0:T(1,128)} %bitcast.26, bf16[16,128,2048]{2,1,0:T(8,128)(2,1)} %get-tuple-element.67.output_all), custom_call_target="tpu_custom_call" | custom-call | flops 2147483648 | bytes 104857600 | tf_op jit(solution)/shard_map/mix/pallas_call | solution.py:690
  212.7 1.3 pad_maximum_fusion
  214.0 17.9 %all-gather.3.cloned.1.call-done = bf16[2048,2048]{1,0:T(8,128)(2,1)} async-done(((bf16[256,2048]{1,0:T(8,128)(2,1)}), bf16[2048,2048]{1,0:T(8,128)(2,1)}) %all-gather.3.cloned.1.call-update) | async-done | bytes 8388624 | tf_op jit(solution)/shard_map/all_gather | solution.py:1733
  231.9 183.2 %dense.1 = (f32[256,2048]{1,0:T(8,128)}, bf16[8,256,2048]{2,1,0:T(8,128)(2,1)}, bf16[8,256,2048]{2,1,0:T(8,128)(2,1)}, bf16[512,2048]{1,0:T(8,128)(2,1)}, bf16[1...) custom-call(bf16[256,2048]{1,0:T(8,128)(2,1)} %get-tuple-element.69.normed, ...), custom_call_target="tpu_custom_call" | custom-call | flops 77309411328 | bytes 524288000 | tf_op jit(solution)/shard_map/dense/pallas_call | solution.py:971
  415.1 1.3 collective-permute-start.3
  416.5 46.7 %mixed_back.1 = (f32[256,2048]{1,0:T(8,128)}, f32[1,2048]{1,0:T(1,128)}, bf16[4096,128]{1,0:T(8,128)(2,1)}, bf16[640,2048]{1,0:T(8,128)(2,1)}, bf16[384,2048]{1,0:T(8,128)(2,1)}) custom-call(f32[256,2048]{1,0:T(8,128)} %get-tuple-element.73.mixed_in.refs_9_, f32[256,2048]{1,0:T(8,128)} %get-tuple-element.74.grad_in, bf16[256,2048]{1,0:T(8,128)(2,1)} %bitcast.25, ...), custom_call_target="tpu_custom_call" | custom-call | flops 4294967296 | bytes 136314880 | tf_op jit(solution)/shard_map/mixed_back/pallas_call | solution.py:1159
  463.2 0.2 collective-permute-start.4
  463.4 1.9 collective-permute-start.5
  465.3 1.2 copy-done.4
  466.6 43.8 %attend_back.1.grads_in = bf16[3,4096,128]{2,1,0:T(8,128)(2,1)S(1)} custom-call(s32[32]{0:T(128)S(1)} %convert_reduce_fusion.first_ref, s32[32]{0:T(128)S(1)} %add_select_fusion.tail_ref, bf16[3,4096,128]{2,1,0:T(8,128)(2,1)S(1)} %copy-done.6, bf16[4096,128]{1,0:T(8,128)(2,1)S(1)} %copy-done.4, bf16[4096,128]{1,0:T(8,128)(2,1)S(1)} %copy-done.1, ...), custom_call_target="tpu_custom_call" | custom-call | flops 42949672960 | bytes 251658240 | tf_op jit(solution)/shard_map/attend_back/pallas_call | solution.py:571
  510.4 1.7 copy-done.7
  512.1 0.2 collective-permute-start.8
  512.2 1.9 collective-permute-start.7
  514.2 123.5 %normed_back.1 = (f32[256,2048]{1,0:T(8,128)}, f32[2,2048]{1,0:T(2,128)}, bf16[2,3,128,2048]{3,2,1,0:T(8,128)(2,1)}, bf16[2,80,2048]{2,1,0:T(8,128)(2,1)}) custom-call(bf16[3,4096,128]{2,1,0:T(8,128)(2,1)} %copy-done.7, bf16[128,2048]{1,0:T(8,128)(2,1)} %query_w.3, bf16[128,2048]{1,0:T(8,128)(2,1)} %key_w.3, bf16[128,2048]{1,0:T(8,128)(2,1)} %value_w.3, ...), custom_call_target="tpu_custom_call" | custom-call | flops 12884901888 | bytes 335544320 | tf_op jit(solution)/shard_map/normed_back/pallas_call | solution.py:1551
  637.7 1.2 copy-done.9
  638.9 13.6 %last_sums.1 = (f32[512,2048]{1,0:T(8,128)}, f32[512,2048]{1,0:T(8,128)}, f32[512,2048]{1,0:T(8,128)}, f32[128,2048]{1,0:T(8,128)}, f32[128,2048]{1,0:T(8,128)},...) custom-call(bf16[512,2048]{1,0:T(8,128)(2,1)} %get-tuple-element.71., ...), custom_call_target="tpu_custom_call" | custom-call | flops 8388608 | bytes 41943040 | tf_op jit(solution)/shard_map/last_sums/pallas_call | solution.py:1651
  (46 shorter events, 0.2 us)
Async XLA Ops:
  7.2 224.7 %all-gather.3.cloned.1.call-start = ((), (), s32[]{:S(2)}) async-start(), calls=%async_computation.2 | async-start | bytes 9437184 | tf_op jit(solution)/shard_map/all_gather | solution.py:1733
  10.4 118.0 %copy-start.15 = (s32[1,8]{1,0:T(1,128)S(1)}, s32[1,8]{1,0:T(1,128)}, u32[]{:S(2)}) copy-start(s32[1,8]{1,0:T(1,128)} %param.24) | copy-start | bytes 100
  10.4 118.0 %copy-start.16 = (s32[1,32]{1,0:T(1,128)S(1)}, s32[1,32]{1,0:T(1,128)}, u32[]{:S(2)}) copy-start(s32[1,32]{1,0:T(1,128)} %param.23) | copy-start | bytes 388
  127.2 511.7 %reduce-scatter.2.cloned.1.call-start = ((), (), s32[]{:S(2)}) async-start(), calls=%async_computation.1 | async-start | bytes 9437184 | tf_op jit(solution)/shard_map/reduce_scatter | solution.py:1753
  127.4 86.5 %collective-permute-start = (bf16[512,2048]{1,0:T(8,128)(2,1)}, bf16[512,2048]{1,0:T(8,128)(2,1)}, u32[]{:S(2)}, u32[]{:S(2)}) collective-permute-start(bf16[512,2048]{1,0:T(8,128)(2,1)} %gate_w.1), channel_id=1, source_target_pairs={{0,2},{2,0},{4,6},{6,4},{8,10},{10,8},{12,14},{14,12},{16,18},{18,... | collective-permute-start | bytes 6291464 | tf_op jit(solution)/shard_map/ppermute | solution.py:1670
  127.9 86.1 %collective-permute-start.1 = (bf16[512,2048]{1,0:T(8,128)(2,1)}, bf16[512,2048]{1,0:T(8,128)(2,1)}, u32[]{:S(2)}, u32[]{:S(2)}) collective-permute-start(bf16[512,2048]{1,0:T(8,128)(2,1)} %up_w.1), channel_id=1, source_target_pairs={{0,2},{2,0},{4,6},{6,4},{8,10},{10,8},{12,14},{14,12},{16,18},{18,... | collective-permute-start | bytes 6291464 | tf_op jit(solution)/shard_map/ppermute | solution.py:1670
  128.0 86.0 %collective-permute-start.2 = (bf16[512,2048]{1,0:T(8,128)(2,1)}, bf16[512,2048]{1,0:T(8,128)(2,1)}, u32[]{:S(2)}, u32[]{:S(2)}) collective-permute-start(bf16[512,2048]{1,0:T(8,128)(2,1)} %down_w.1), channel_id=1, source_target_pairs={{0,2},{2,0},{4,6},{6,4},{8,10},{10,8},{12,14},{14,12},{16,18},{18,... | collective-permute-start | bytes 6291464 | tf_op jit(solution)/shard_map/ppermute | solution.py:1670
  128.6 1.9 copy-start.5
  168.5 1.0 copy-start
  169.4 43.2 %copy-start.11 = (bf16[128,2048]{1,0:T(8,128)(2,1)S(1)}, bf16[128,2048]{1,0:T(8,128)(2,1)}, u32[]{:S(2)}) copy-start(bf16[128,2048]{1,0:T(8,128)(2,1)} %query_w.3) | copy-start | bytes 1572868
  169.4 43.2 %copy-start.12 = (bf16[128,2048]{1,0:T(8,128)(2,1)S(1)}, bf16[128,2048]{1,0:T(8,128)(2,1)}, u32[]{:S(2)}) copy-start(bf16[128,2048]{1,0:T(8,128)(2,1)} %key_w.3) | copy-start | bytes 1572868
  169.4 43.2 %copy-start.13 = (bf16[128,2048]{1,0:T(8,128)(2,1)S(1)}, bf16[128,2048]{1,0:T(8,128)(2,1)}, u32[]{:S(2)}) copy-start(bf16[128,2048]{1,0:T(8,128)(2,1)} %value_w.3) | copy-start | bytes 1572868
  415.1 48.3 %collective-permute-start.3 = (bf16[512,2048]{1,0:T(8,128)(2,1)}, bf16[512,2048]{1,0:T(8,128)(2,1)}, u32[]{:S(2)}, u32[]{:S(2)}) collective-permute-start(bf16[512,2048]{1,0:T(8,128)(2,1)} %get-tuple-element.71.refs_0_), channel_id=1, source_target_pairs={{0,1},{1,0},{2,3},{3,2},{4,5},{5,4},{6,7},{7,6},{8,9},{9,8},{10,11... | collective-permute-start | bytes 6291464 | tf_op jit(solution)/shard_map/ppermute | solution.py:1675
  416.4 97.7 %collective-permute-start.6 = (bf16[384,2048]{1,0:T(8,128)(2,1)}, bf16[384,2048]{1,0:T(8,128)(2,1)}, u32[]{:S(2)}, u32[]{:S(2)}) collective-permute-start(bf16[384,2048]{1,0:T(8,128)(2,1)} %pad_maximum_fusion), channel_id=1, source_target_pairs={{0,2},{2,0},{4,6},{6,4},{8,10},{10,8},{12,14},{14,12},{16,18},{18,... | collective-permute-start | bytes 4718600 | tf_op jit(solution)/shard_map/ppermute | solution.py:1670
  416.5 48.9 %copy-start.1 = (bf16[4096,128]{1,0:T(8,128)(2,1)S(1)}, bf16[4096,128]{1,0:T(8,128)(2,1)}, u32[]{:S(2)}) copy-start(bf16[4096,128]{1,0:T(8,128)(2,1)} %copy-done) | copy-start | bytes 3145732
  416.5 48.9 %copy-start.2 = (f32[32,4096]{1,0:T(8,128)S(1)}, f32[32,4096]{1,0:T(8,128)}, u32[]{:S(2)}) copy-start(f32[32,4096]{1,0:T(8,128)} %get-tuple-element.123.sin_t) | copy-start | bytes 1572868
  416.5 48.9 %copy-start.3 = (f32[32,4096]{1,0:T(8,128)S(1)}, f32[32,4096]{1,0:T(8,128)}, u32[]{:S(2)}) copy-start(f32[32,4096]{1,0:T(8,128)} %get-tuple-element.124.cos_t) | copy-start | bytes 1572868
  416.5 48.9 %copy-start.6 = (bf16[3,4096,128]{2,1,0:T(8,128)(2,1)S(1)}, bf16[3,4096,128]{2,1,0:T(8,128)(2,1)}, u32[]{:S(2)}) copy-start(bf16[3,4096,128]{2,1,0:T(8,128)(2,1)} %get-tuple-element.65.qkv) | copy-start | bytes 9437188
  463.2 48.8 %collective-permute-start.4 = (bf16[384,2048]{1,0:T(8,128)(2,1)}, bf16[384,2048]{1,0:T(8,128)(2,1)S(1)}, u32[]{:S(2)}, u32[]{:S(2)}) collective-permute-start(bf16[384,2048]{1,0:T(8,128)(2,1)} %get-tuple-element.81), channel_id=1, source_target_pairs={{0,1},{1,0},{2,3},{3,2},{4,5},{5,4},{6,7},{7,6},{8,9},{9,8},{10,11... | collective-permute-start | bytes 4718600 | tf_op jit(solution)/shard_map/ppermute | solution.py:1766
  463.4 48.7 %collective-permute-start.5 = (bf16[128,2048]{1,0:T(8,128)(2,1)}, bf16[128,2048]{1,0:T(8,128)(2,1)S(1)}, u32[]{:S(2)}, u32[]{:S(2)}) collective-permute-start(bf16[128,2048]{1,0:T(8,128)(2,1)} %get-tuple-element.79.refs_1_), channel_id=1, source_target_pairs={{0,1},{1,0},{2,3},{3,2},{4,5},{5,4},{6,7},{7,6},{8,9},{9,8},{10,11... | collective-permute-start | bytes 1572872 | tf_op jit(solution)/shard_map/ppermute | solution.py:1675
  465.3 1.3 copy-start.4
  466.6 45.7 %copy-start.8 = (bf16[384,2048]{1,0:T(8,128)(2,1)S(1)}, bf16[384,2048]{1,0:T(8,128)(2,1)}, u32[]{:S(2)}) copy-start(bf16[384,2048]{1,0:T(8,128)(2,1)} %get-tuple-element.84.refs_2_) | copy-start | bytes 4718596
  510.4 1.7 copy-start.7
  512.0 2.1 copy-start.14
  512.0 2.1 copy-start.10
  512.1 126.8 %collective-permute-start.8 = (bf16[512,2048]{1,0:T(8,128)(2,1)}, bf16[512,2048]{1,0:T(8,128)(2,1)}, u32[]{:S(2)}, u32[]{:S(2)}) collective-permute-start(bf16[512,2048]{1,0:T(8,128)(2,1)} %get-tuple-element.85.refs_3_), channel_id=1, source_target_pairs={{0,1},{1,0},{2,3},{3,2},{4,5},{5,4},{6,7},{7,6},{8,9},{9,8},{10,11... | collective-permute-start | bytes 6291464 | tf_op jit(solution)/shard_map/ppermute | solution.py:1675
  512.2 125.4 %collective-permute-start.7 = (bf16[384,2048]{1,0:T(8,128)(2,1)S(1)}, bf16[384,2048]{1,0:T(8,128)(2,1)S(1)}, u32[]{:S(2)}, u32[]{:S(2)}) collective-permute-start(bf16[384,2048]{1,0:T(8,128)(2,1)S(1)} %copy-done.8), channel_id=1, source_target_pairs={{0,1},{1,0},{2,3},{3,2},{4,5},{5,4},{6,7},{7,6},{8,9},{9,8},{10,11... | collective-permute-start | bytes 4718600 | tf_op jit(solution)/shard_map/ppermute | solution.py:1675
  637.6 1.2 copy-start.9
Sparse Core Ops, SparseCore 0:
  127.3 104.4 all-gather.2
  415.3 103.3 reduce-scatter.1

commit v10 on v9

--- a/solution.py
+++ b/solution.py
@@ -494,7 +494,7 @@
 
 def attend_back_kernel(
     chips, first_ref, tail_ref, qkv, grad_out, attended, log_total, cos_t, sin_t, grads,
-    key_t, grad_key, grad_value, staged, store_sem,
+    key_t, grad_key, grad_value,
 ):
     tokens, r = qkv.shape[1:]
     tok_dev = tokens // (2 * chips)
@@ -543,25 +543,19 @@
             grad_query,
         )
         turned = unrotate(join_heads(grad_query) * scale, cos_t[:, here], sin_t[:, here])
-        staged[0, here, :] = turned.T.astype(LOW)
+        grads[0, here, :] = turned.T.astype(LOW)
         return carry
 
     lax.fori_loop(0, tokens // BLOCK, block, 0)
-    query_store = pltpu.make_async_copy(staged.at[0], grads.at[0], store_sem.at[0])
-    query_store.start()
 
     def close(b, carry):
         here = pl.ds(pl.multiple_of(b * BLOCK, BLOCK), BLOCK)
         turned = unrotate(grad_key[here, :].T * scale, cos_t[:, here], sin_t[:, here])
-        staged[1, here, :] = turned.T.astype(LOW)
-        staged[2, here, :] = grad_value[here, :].astype(LOW)
+        grads[1, here, :] = turned.T.astype(LOW)
+        grads[2, here, :] = grad_value[here, :].astype(LOW)
         return carry
 
     lax.fori_loop(0, tokens // BLOCK, close, 0)
-    rest_store = pltpu.make_async_copy(staged.at[pl.ds(1, 2)], grads.at[pl.ds(1, 2)], store_sem.at[1])
-    rest_store.start()
-    query_store.wait()
-    rest_store.wait()
 
 
 def attend_back(first, tail, qkv, grad_out, attended, log_total, cos_t, sin_t):
@@ -572,13 +566,11 @@
         functools.partial(attend_back_kernel, lax.axis_size("dp") // 2),
         out_shape=jax.ShapeDtypeStruct((3, tokens, r), LOW),
         in_specs=[smem, smem] + [vmem] * 6,
-        out_specs=pl.BlockSpec(memory_space=pl.ANY),
+        out_specs=vmem,
         scratch_shapes=[
             pltpu.VMEM((r, tokens), LOW),
             pltpu.VMEM((tokens, r), F32),
             pltpu.VMEM((tokens, r), F32),
-            pltpu.VMEM((3, tokens, r), LOW),
-            pltpu.SemaphoreType.DMA((2,)),
         ],
         compiler_params=pltpu.CompilerParams(vmem_limit_bytes=40 * MIB),
         cost_estimate=pl.CostEstimate(
@@ -1188,7 +1180,7 @@
 
 
 def normed_back_kernel(
-    packs, grads_in, query_w, key_w, value_w, partner_w, tokens_in, gain, mixed_in, dense_gain_part, normed_all, output_mine, *rest
+    packs, grads, query_w, key_w, value_w, partner_w, tokens_in, gain, mixed_in, dense_gain_part, normed_all, output_mine, *rest
 ):
     outputs_in = (output_mine, *rest[: packs - 1])
     (
@@ -1196,9 +1188,9 @@
         hidden_in, grad_mixed, output_mine, *output_there
     ) = rest[packs - 1 : 2 * packs + 5]
     (
-        grads, joined, partner_grads, sent, landed, x_buf, parts, pair_out, pair_land,
+        joined, partner_grads, sent, landed, x_buf, parts, pair_out, pair_land,
         o_sent, o_landed, far_part, far_land, near_part, near_land,
-        in_sem, w_sem, p_send, p_recv, rs_send, rs_recv, credit, x_sem, pair_sem, rep_send, rep_recv,
+        w_sem, p_send, p_recv, rs_send, rs_recv, credit, x_sem, pair_sem, rep_send, rep_recv,
         o_send, o_recv, o_credit, swap_send, swap_recv, near_send, near_recv, far_send, far_recv,
     ) = rest[2 * packs + 5 :]
     ring = Ring()
@@ -1211,8 +1203,6 @@
     mates = 2 * packs
     mate = pack * 2 + ring.core
     barrier = pltpu.get_barrier_semaphore()
-    load_grads = pltpu.make_async_copy(grads_in, grads, in_sem)
-    load_grads.start()
     load_weights = [
         pltpu.make_async_copy(src, joined.at[pl.ds(i * r, src.shape[0])], w_sem.at[i])
         for i, src in enumerate((query_w, key_w, value_w, partner_w))
@@ -1240,7 +1230,6 @@
     for k in range(1, n):
         pl.semaphore_signal(barrier, inc=1, device_id=far(k), device_id_type=MESH)
     pl.semaphore_wait(barrier, mates + n - 2)
-    load_grads.wait()
 
     def place(t, d):
         return ring.chip_far(-t if d == 0 else t)
@@ -1558,11 +1547,10 @@
             jax.ShapeDtypeStruct((packs, 3, r, features), LOW),
             jax.ShapeDtypeStruct((packs, carried, features), LOW),
         ),
-        in_specs=[hbm] * 6 + [vmem, hbm, vmem] + [hbm] * (1 + packs),
+        in_specs=[vmem] + [hbm] * 5 + [vmem, hbm, vmem] + [hbm] * (1 + packs),
         out_specs=(vmem,) * 4,
         scratch_shapes=[pltpu.VMEM(a.shape, a.dtype) for a in (hidden_in, grad_mixed, output_mine, *output_there)]
         + [
-            pltpu.VMEM(grads.shape, LOW),
             pltpu.VMEM((6 * r, features), LOW),
             pltpu.VMEM((3, n, rows, r), LOW),
             pltpu.VMEM((2, 2, 2, half, features // 2), LOW),
@@ -1577,14 +1565,14 @@
             pltpu.VMEM((n, 2, features), F32),
             pltpu.VMEM((2, features), F32),
             pltpu.VMEM((mates, 2, features), F32),
-            dma, dma((6 + packs,)), dma((2, n)), dma((2, n)), dma((2, 2, 2)), dma((2, 2, 2)),
+            dma((6 + packs,)), dma((2, n)), dma((2, n)), dma((2, 2, 2)), dma((2, 2, 2)),
             pltpu.SemaphoreType.REGULAR((2, 2)),
             dma((2, 2)), dma((2,)), dma((packs - 1,)), dma((packs - 1,)),
             dma((2, 2)), dma((2, 2)), pltpu.SemaphoreType.REGULAR((2,)),
             dma((packs - 1,)), dma((packs - 1,)), dma((mates,)), dma((mates,)), dma((n,)), dma((n,)),
         ],
         compiler_params=pltpu.CompilerParams(
-            collective_id=3, has_side_effects=True, vmem_limit_bytes=56 * MIB
+            collective_id=3, has_side_effects=True, vmem_limit_bytes=44 * MIB
         ),
         cost_estimate=pl.CostEstimate(
             flops=2 * n * rows * features * 12 * r, bytes_accessed=320 * MIB, transcendentals=0

time: 660 us -> 661 us (level)
  no operation moved by 1% of the time
where the time goes in v10:
time: 661 us; the launch traced here: 660 us
  Pallas kernels  606 us (92%)
  waiting for transfers between devices  17.4 us (3%)
  between operations  14.3 us (2%)
  local copies, waits for them, and re-layouts  12 us (2%)
  starting transfers between devices  6.81 us (1%)
    pallas_call x1, Pallas kernels, dense(): pl.pallas_call(dense_kernel, out_shape=(jax.ShapeDtypeStruct((rows, featu...  182 us
    pallas_call x1, Pallas kernels, normed_back(): pl.pallas_call(functools.partial(normed_back_kernel, packs), out_shape=(j...  122 us
    pallas_call x1, Pallas kernels, gather_project(): pl.pallas_call(gather_project_kernel, out_shape=(jax.ShapeDtypeStruct((3,...  117 us
    pallas_call x1, Pallas kernels, mixed_back(): pl.pallas_call(functools.partial(mixed_back_kernel, packs), out_shape=(ja...  46.1 us
    pallas_call x1, Pallas kernels, attend_back(): pl.pallas_call(functools.partial(attend_back_kernel, lax.axis_size('dp')...  43.7 us
    pallas_call x1, Pallas kernels, mix(): pl.pallas_call(mixed_kernel, out_shape=(jax.ShapeDtypeStruct((rows, featu...  43.2 us
    pallas_call x1, Pallas kernels, attend(): pl.pallas_call(functools.partial(attend_kernel, lax.axis_size('dp') // 2)...  38.5 us
    all_gather x1, waiting for transfers between devices, body(): lax.all_gather(grad_late, 'dp', axis=0, axis_index_groups=lanes)  17.3 us
  transfers between devices with their start and end apart: 11, of which 1 were waited for; matrix products, arithmetic and copies ran while one was open for 0% of the time, Pallas kernels for 45%

profile of v10, /device:TPU:0, one launch (start us, length us, event | category | flops | bytes accessed | tf_op | source)
XLA Modules:
  0.0 660.0 jit_solution(17272020647948191005)
XLA Ops:
  7.2 0.9 convert_reduce_fusion.first_ref
  8.2 0.1 multiply_cosine_fusion
  8.3 0.1 multiply_cosine_fusion.1
  8.5 0.4 multiply_add_fusion
  8.8 1.6 copy_bitcast_fusion
  10.4 116.8 %gather_project.1 = (bf16[3,4096,128]{2,1,0:T(8,128)(2,1)}, bf16[8,256,2048]{2,1,0:T(8,128)(2,1)}, bf16[16,128,2048]{2,1,0:T(8,128)(2,1)}) custom-call(bf16[256,2048]{1,0:T(8,128)(2,1)} %bitcast.18, f32[1,2048]{1,0:T(1,128)} %bitcast.21, bf16[128,2048]{1,0:T(8,128)(2,1)} %query_w.3, bf16[128,2048]{1,0:T(8,128)(2,1)} %key_w.3, bf16[128,2048]{1,0:T(8,128)(2,1)} %value_w.3, ...), custom_call_target="tpu_custom_call" | custom-call | flops 6442450944 | bytes 335544320 | tf_op jit(solution)/shard_map/gather_project/pallas_call | solution.py:351
  127.2 0.2 reduce-scatter.2.cloned.1.call-start
  127.4 0.4 collective-permute-start
  127.8 0.2 collective-permute-start.1
  128.0 0.4 collective-permute-start.2
  128.4 0.1 select_reduce_fusion
  128.5 0.1 add_select_fusion.tail_ref
  128.6 1.9 copy-done.13
  130.5 38.5 %attend.1 = (bf16[4096,128]{1,0:T(8,128)(2,1)S(1)}, f32[32,256]{1,0:T(8,128)S(1)}) custom-call(s32[32]{0:T(128)S(1)} %convert_reduce_fusion.first_ref, s32[32]{0:T(128)S(1)} %add_select_fusion.tail_ref, bf16[3,4096,128]{2,1,0:T(8,128)(2,1)S(1)} %copy-done.13), custom_call_target="tpu_custom_call" | custom-call | flops 17179869184 | bytes 125829120 | tf_op jit(solution)/shard_map/attend/pallas_call | solution.py:469
  169.0 1.0 copy-done.2
  170.0 43.2 %mix.1 = (f32[256,2048]{1,0:T(8,128)}, bf16[256,2048]{1,0:T(8,128)(2,1)}, bf16[16,256,128]{2,1,0:T(8,128)(2,1)}) custom-call(bf16[4096,128]{1,0:T(8,128)(2,1)} %copy-done.2, bf16[256,2048]{1,0:T(8,128)(2,1)} %bitcast.19, f32[1,2048]{1,0:T(1,128)} %bitcast.28, bf16[16,128,2048]{2,1,0:T(8,128)(2,1)} %get-tuple-element.67.output_all), custom_call_target="tpu_custom_call" | custom-call | flops 2147483648 | bytes 104857600 | tf_op jit(solution)/shard_map/mix/pallas_call | solution.py:682
  213.2 1.3 pad_maximum_fusion
  214.5 17.3 %all-gather.3.cloned.1.call-done = bf16[2048,2048]{1,0:T(8,128)(2,1)} async-done(((bf16[256,2048]{1,0:T(8,128)(2,1)}), bf16[2048,2048]{1,0:T(8,128)(2,1)}) %all-gather.3.cloned.1.call-update) | async-done | bytes 8388624 | tf_op jit(solution)/shard_map/all_gather | solution.py:1721
  231.8 182.0 %dense.1 = (f32[256,2048]{1,0:T(8,128)}, bf16[8,256,2048]{2,1,0:T(8,128)(2,1)}, bf16[8,256,2048]{2,1,0:T(8,128)(2,1)}, bf16[512,2048]{1,0:T(8,128)(2,1)}, bf16[1...) custom-call(bf16[256,2048]{1,0:T(8,128)(2,1)} %get-tuple-element.69.normed, ...), custom_call_target="tpu_custom_call" | custom-call | flops 77309411328 | bytes 524288000 | tf_op jit(solution)/shard_map/dense/pallas_call | solution.py:963
  413.9 1.5 collective-permute-start.3
  415.4 46.1 %mixed_back.1 = (f32[256,2048]{1,0:T(8,128)}, f32[1,2048]{1,0:T(1,128)}, bf16[4096,128]{1,0:T(8,128)(2,1)}, bf16[640,2048]{1,0:T(8,128)(2,1)}, bf16[384,2048]{1,0:T(8,128)(2,1)}) custom-call(f32[256,2048]{1,0:T(8,128)} %get-tuple-element.73.mixed_in.refs_9_, f32[256,2048]{1,0:T(8,128)} %get-tuple-element.74.grad_in, bf16[256,2048]{1,0:T(8,128)(2,1)} %bitcast.27, ...), custom_call_target="tpu_custom_call" | custom-call | flops 4294967296 | bytes 136314880 | tf_op jit(solution)/shard_map/mixed_back/pallas_call | solution.py:1151
  461.6 2.0 collective-permute-start.5
  463.6 1.3 copy-done.12
  464.8 1.9 copy-done.14
  466.7 43.7 %attend_back.1.grads = bf16[3,4096,128]{2,1,0:T(8,128)(2,1)S(1)} custom-call(s32[32]{0:T(128)S(1)} %convert_reduce_fusion.first_ref, s32[32]{0:T(128)S(1)} %add_select_fusion.tail_ref, bf16[3,4096,128]{2,1,0:T(8,128)(2,1)S(1)} %copy-done.14, bf16[4096,128]{1,0:T(8,128)(2,1)S(1)} %copy-done.12, bf16[4096,128]{1,0:T(8,128)(2,1)S(1)} %copy-done.3, ...), custom_call_target="tpu_custom_call" | custom-call | flops 42949672960 | bytes 251658240 | tf_op jit(solution)/shard_map/attend_back/pallas_call | solution.py:565
  510.4 1.7 copy-done.16
  512.2 2.0 collective-permute-start.7
  514.2 122.5 %normed_back.1 = (f32[256,2048]{1,0:T(8,128)S(1)}, f32[2,2048]{1,0:T(2,128)S(1)}, bf16[2,3,128,2048]{3,2,1,0:T(8,128)(2,1)}, bf16[2,80,2048]{2,1,0:T(8,128)(2,1)S(1)}) custom-call(bf16[3,4096,128]{2,1,0:T(8,128)(2,1)} %copy-done.16, bf16[128,2048]{1,0:T(8,128)(2,1)S(1)} %copy-done.5, bf16[128,2048]{1,0:T(8,128)(2,1)S(1)} %copy-done.6, ...), custom_call_target="tpu_custom_call" | custom-call | flops 12884901888 | bytes 335544320 | tf_op jit(solution)/shard_map/normed_back/pallas_call | solution.py:1540
  636.7 1.3 copy-done
  638.0 0.9 copy-done.4
  638.9 0.6 copy-done.10
  639.5 13.7 %last_sums.1 = (f32[512,2048]{1,0:T(8,128)}, f32[512,2048]{1,0:T(8,128)}, f32[512,2048]{1,0:T(8,128)}, f32[128,2048]{1,0:T(8,128)}, f32[128,2048]{1,0:T(8,128)},...) custom-call(bf16[512,2048]{1,0:T(8,128)(2,1)} %get-tuple-element.71., ...), custom_call_target="tpu_custom_call" | custom-call | flops 8388608 | bytes 41943040 | tf_op jit(solution)/shard_map/last_sums/pallas_call | solution.py:1639
  (56 shorter events, 0.4 us)
Async XLA Ops:
  7.2 224.7 %all-gather.3.cloned.1.call-start = ((), (), s32[]{:S(2)}) async-start(), calls=%async_computation.2 | async-start | bytes 9437184 | tf_op jit(solution)/shard_map/all_gather | solution.py:1721
  10.4 118.0 %copy-start.20 = (s32[1,8]{1,0:T(1,128)S(1)}, s32[1,8]{1,0:T(1,128)}, u32[]{:S(2)}) copy-start(s32[1,8]{1,0:T(1,128)} %param.24) | copy-start | bytes 100
  10.4 118.0 %copy-start.21 = (s32[1,32]{1,0:T(1,128)S(1)}, s32[1,32]{1,0:T(1,128)}, u32[]{:S(2)}) copy-start(s32[1,32]{1,0:T(1,128)} %param.23) | copy-start | bytes 388
  127.2 512.3 %reduce-scatter.2.cloned.1.call-start = ((), (), s32[]{:S(2)}) async-start(), calls=%async_computation.1 | async-start | bytes 9437184 | tf_op jit(solution)/shard_map/reduce_scatter | solution.py:1741
  127.4 87.1 %collective-permute-start = (bf16[512,2048]{1,0:T(8,128)(2,1)}, bf16[512,2048]{1,0:T(8,128)(2,1)}, u32[]{:S(2)}, u32[]{:S(2)}) collective-permute-start(bf16[512,2048]{1,0:T(8,128)(2,1)} %gate_w.1), channel_id=1, source_target_pairs={{0,2},{2,0},{4,6},{6,4},{8,10},{10,8},{12,14},{14,12},{16,18},{18,... | collective-permute-start | bytes 6291464 | tf_op jit(solution)/shard_map/ppermute | solution.py:1658
  127.8 86.7 %collective-permute-start.1 = (bf16[512,2048]{1,0:T(8,128)(2,1)}, bf16[512,2048]{1,0:T(8,128)(2,1)}, u32[]{:S(2)}, u32[]{:S(2)}) collective-permute-start(bf16[512,2048]{1,0:T(8,128)(2,1)} %up_w.1), channel_id=1, source_target_pairs={{0,2},{2,0},{4,6},{6,4},{8,10},{10,8},{12,14},{14,12},{16,18},{18,... | collective-permute-start | bytes 6291464 | tf_op jit(solution)/shard_map/ppermute | solution.py:1658
  128.0 86.5 %collective-permute-start.2 = (bf16[512,2048]{1,0:T(8,128)(2,1)}, bf16[512,2048]{1,0:T(8,128)(2,1)}, u32[]{:S(2)}, u32[]{:S(2)}) collective-permute-start(bf16[512,2048]{1,0:T(8,128)(2,1)} %down_w.1), channel_id=1, source_target_pairs={{0,2},{2,0},{4,6},{6,4},{8,10},{10,8},{12,14},{14,12},{16,18},{18,... | collective-permute-start | bytes 6291464 | tf_op jit(solution)/shard_map/ppermute | solution.py:1658
  128.6 1.9 copy-start.13
  169.0 1.0 copy-start.2
  170.0 43.2 %copy-start.5 = (bf16[128,2048]{1,0:T(8,128)(2,1)S(1)}, bf16[128,2048]{1,0:T(8,128)(2,1)}, u32[]{:S(2)}) copy-start(bf16[128,2048]{1,0:T(8,128)(2,1)} %query_w.3) | copy-start | bytes 1572868
  170.0 43.2 %copy-start.6 = (bf16[128,2048]{1,0:T(8,128)(2,1)S(1)}, bf16[128,2048]{1,0:T(8,128)(2,1)}, u32[]{:S(2)}) copy-start(bf16[128,2048]{1,0:T(8,128)(2,1)} %key_w.3) | copy-start | bytes 1572868
  170.0 43.2 %copy-start.7 = (bf16[128,2048]{1,0:T(8,128)(2,1)S(1)}, bf16[128,2048]{1,0:T(8,128)(2,1)}, u32[]{:S(2)}) copy-start(bf16[128,2048]{1,0:T(8,128)(2,1)} %value_w.3) | copy-start | bytes 1572868
  413.9 47.7 %collective-permute-start.3 = (bf16[512,2048]{1,0:T(8,128)(2,1)}, bf16[512,2048]{1,0:T(8,128)(2,1)}, u32[]{:S(2)}, u32[]{:S(2)}) collective-permute-start(bf16[512,2048]{1,0:T(8,128)(2,1)} %get-tuple-element.71.refs_0_), channel_id=1, source_target_pairs={{0,1},{1,0},{2,3},{3,2},{4,5},{5,4},{6,7},{7,6},{8,9},{9,8},{10,11... | collective-permute-start | bytes 6291464 | tf_op jit(solution)/shard_map/ppermute | solution.py:1663
  415.3 98.8 %collective-permute-start.6 = (bf16[384,2048]{1,0:T(8,128)(2,1)}, bf16[384,2048]{1,0:T(8,128)(2,1)S(1)}, u32[]{:S(2)}, u32[]{:S(2)}) collective-permute-start(bf16[384,2048]{1,0:T(8,128)(2,1)} %pad_maximum_fusion), channel_id=1, source_target_pairs={{0,2},{2,0},{4,6},{6,4},{8,10},{10,8},{12,14},{14,12},{16,18},{18,... | collective-permute-start | bytes 4718600 | tf_op jit(solution)/shard_map/ppermute | solution.py:1658
  415.3 46.2 %copy-start.18 = (bf16[128,2048]{1,0:T(8,128)(2,1)S(1)}, bf16[128,2048]{1,0:T(8,128)(2,1)}, u32[]{:S(2)}) copy-start(bf16[128,2048]{1,0:T(8,128)(2,1)} %get-tuple-element.79.refs_1_) | copy-start | bytes 1572868
  415.3 48.2 %copy-start.3 = (bf16[4096,128]{1,0:T(8,128)(2,1)S(1)}, bf16[4096,128]{1,0:T(8,128)(2,1)}, u32[]{:S(2)}) copy-start(bf16[4096,128]{1,0:T(8,128)(2,1)} %copy-done.2) | copy-start | bytes 3145732
  415.3 48.2 %copy-start.8 = (f32[32,4096]{1,0:T(8,128)S(1)}, f32[32,4096]{1,0:T(8,128)}, u32[]{:S(2)}) copy-start(f32[32,4096]{1,0:T(8,128)} %get-tuple-element.123.sin_t) | copy-start | bytes 1572868
  415.3 48.2 %copy-start.9 = (f32[32,4096]{1,0:T(8,128)S(1)}, f32[32,4096]{1,0:T(8,128)}, u32[]{:S(2)}) copy-start(f32[32,4096]{1,0:T(8,128)} %get-tuple-element.124.cos_t) | copy-start | bytes 1572868
  461.5 50.6 %collective-permute-start.4 = (bf16[384,2048]{1,0:T(8,128)(2,1)}, bf16[384,2048]{1,0:T(8,128)(2,1)S(1)}, u32[]{:S(2)}, u32[]{:S(2)}) collective-permute-start(bf16[384,2048]{1,0:T(8,128)(2,1)} %get-tuple-element.81), channel_id=1, source_target_pairs={{0,1},{1,0},{2,3},{3,2},{4,5},{5,4},{6,7},{7,6},{8,9},{9,8},{10,11... | collective-permute-start | bytes 4718600 | tf_op jit(solution)/shard_map/ppermute | solution.py:1754
  461.6 50.5 %collective-permute-start.5 = (bf16[128,2048]{1,0:T(8,128)(2,1)S(1)}, bf16[128,2048]{1,0:T(8,128)(2,1)S(1)}, u32[]{:S(2)}, u32[]{:S(2)}) collective-permute-start(bf16[128,2048]{1,0:T(8,128)(2,1)S(1)} %copy-done.18), channel_id=1, source_target_pairs={{0,1},{1,0},{2,3},{3,2},{4,5},{5,4},{6,7},{7,6},{8,9},{9,8},{10,11... | collective-permute-start | bytes 1572872 | tf_op jit(solution)/shard_map/ppermute | solution.py:1663
  463.6 1.3 copy-start.12
  464.8 1.9 copy-start.14
  466.7 45.4 %copy-start.17 = (bf16[512,2048]{1,0:T(8,128)(2,1)S(1)}, bf16[512,2048]{1,0:T(8,128)(2,1)}, u32[]{:S(2)}) copy-start(bf16[512,2048]{1,0:T(8,128)(2,1)} %get-tuple-element.85.refs_3_) | copy-start | bytes 6291460
  466.7 47.5 %copy-start.1 = (bf16[1,256,2048]{2,1,0:T(8,128)(2,1)S(1)}, bf16[1,256,2048]{2,1,0:T(8,128)(2,1)}, u32[]{:S(2)}) copy-start(bf16[1,256,2048]{2,1,0:T(8,128)(2,1)} %param.13) | copy-start | bytes 3145732
  466.7 47.5 %copy-start.11 = (f32[2048]{0:T(1024)S(1)}, f32[2048]{0:T(1024)}, u32[]{:S(2)}) copy-start(f32[2048]{0:T(1024)} %param.14) | copy-start | bytes 24580
  466.7 47.5 %copy-start.15 = (f32[1,2048]{1,0:T(1,128)S(1)}, f32[1,2048]{1,0:T(1,128)}, u32[]{:S(2)}) copy-start(f32[1,2048]{1,0:T(1,128)} %get-tuple-element.89.dense_gain_part) | copy-start | bytes 24580
  510.4 1.7 copy-start.16
  512.1 124.6 %copy-start.19 = (bf16[128,2048]{1,0:T(8,128)(2,1)}, bf16[128,2048]{1,0:T(8,128)(2,1)S(1)}, u32[]{:S(2)}) copy-start(bf16[128,2048]{1,0:T(8,128)(2,1)S(1)} %collective-permute-done.5.refs_5_) | copy-start | bytes 1572868
  512.1 127.4 %collective-permute-start.8 = (bf16[512,2048]{1,0:T(8,128)(2,1)S(1)}, bf16[512,2048]{1,0:T(8,128)(2,1)}, u32[]{:S(2)}, u32[]{:S(2)}) collective-permute-start(bf16[512,2048]{1,0:T(8,128)(2,1)S(1)} %copy-done.17), channel_id=1, source_target_pairs={{0,1},{1,0},{2,3},{3,2},{4,5},{5,4},{6,7},{7,6},{8,9},{9,8},{10,11... | collective-permute-start | bytes 6291464 | tf_op jit(solution)/shard_map/ppermute | solution.py:1663
  512.2 127.3 %collective-permute-start.7 = (bf16[384,2048]{1,0:T(8,128)(2,1)}, bf16[384,2048]{1,0:T(8,128)(2,1)}, u32[]{:S(2)}, u32[]{:S(2)}) collective-permute-start(bf16[384,2048]{1,0:T(8,128)(2,1)} %get-tuple-element.84.refs_2_), channel_id=1, source_target_pairs={{0,1},{1,0},{2,3},{3,2},{4,5},{5,4},{6,7},{7,6},{8,9},{9,8},{10,11... | collective-permute-start | bytes 4718600 | tf_op jit(solution)/shard_map/ppermute | solution.py:1663
  636.7 1.3 copy-start
  638.0 0.9 copy-start.4
  (1 other events, 0.6 us)
Sparse Core Ops, SparseCore 0:
  127.3 104.4 all-gather.2
  414.0 103.5 reduce-scatter.1
